TPU v7x, 128 devices: a whole 4x4x4 slice. The times are simulated.
128 devices in a mesh: group: 4 (over y_lo, core), rep: 32 (over x, z, y_hi).
Axes of the slice: x: 4, y: 4 (y_hi: 2, y_lo: 2; y = y_hi * 2 + y_lo), z: 4, core: 2. Of those that a mesh axis runs over, the one named last changes fastest.
Arguments:
- tokens: bfloat16 [32, 1024, 768], P('rep', 'group'), may hold values from -6 to 6
- segments: int32 [32, 1024], P('rep', 'group'), may hold values from 0 to 4, as said below
- cotangent: bfloat16 [32, 1024, 768], P('rep', 'group'), may hold values from -6 to 6
- gain_in: bfloat16 [768], P('group'), may hold values from 0.5 to 1.5
- w_in: bfloat16 [768, 3352], P('group'), may hold values from -0.25 to 0.25
- kernel: bfloat16 [4, 1792], P(None, 'group'), may hold values from -3 to 3
- conv_bias: bfloat16 [1792], P('group'), may hold values from -1.5 to 1.5
- dt_bias: bfloat16 [24], P('group'), may hold values from -5 to -3
- a_log: bfloat16 [24], P('group'), may hold values from -6 to 0
- skip_gain: bfloat16 [24], P('group'), may hold values from 0.5 to 1.5
- gain_out: bfloat16 [1536], P('group'), may hold values from 0.5 to 1.5
- w_out: bfloat16 [1536, 768], P('group'), may hold values from -0.2 to 0.2
Outputs:
- layer_out: bfloat16 [32, 1024, 768], P('rep', 'group')
- grad_tokens: float32 [32, 1024, 768], P('rep', 'group')
- grad_gain_in: float32 [768], P('group')
- grad_w_in: float32 [768, 3352], P('group')
- grad_kernel: float32 [4, 1792], P(None, 'group')
- grad_conv_bias: float32 [1792], P('group')
- grad_dt_bias: float32 [24], P('group')
- grad_a_log: float32 [24], P('group')
- grad_skip_gain: float32 [24], P('group')
- grad_gain_out: float32 [1536], P('group')
- grad_w_out: float32 [1536, 768], P('group')
Inputs may be any that keep to these rules, and one draw needn't show every extreme that they name: `segments`: along each sequence the numbers never fall.
All inputs are finite; a program needn't handle non-finite values.
Results may differ from a plain program's by a relative error of at most 0.024.
Values may be sent and summed in bfloat16 or wider, within the bound.
No kernel may reach another device: no remote copies, remote signals or barrier semaphores. Data moves between devices by JAX's collectives and lax.ppermute only.
A program may use at most 192 MiB of HBM per device.

v0:
```python
from functools import partial

import jax
import jax.numpy as jnp
from jax import lax
from jax.sharding import PartitionSpec as P

NH = 24
HP = 64
NS = 128
KC = 4
DI = 1536
CW = 1792
SPAN = 128


epsilon = 1e-05
highest = lax.Precision.HIGHEST
sentinel = 1000000000.0


def shifted(block, axis, distance):
    devices = range(lax.axis_size(axis))
    route = [(i - distance, i) for i in devices if i - distance in devices]
    return lax.ppermute(block, axis, route)


def entering(value, axis, join, neutral, backward):
    count, mine = (lax.axis_size(axis), lax.axis_index(axis))
    pieces = jax.tree.map(lambda part: lax.all_gather(part, axis), value)
    if backward:
        pieces = jax.tree.map(lambda part: part[::-1], pieces)
        mine = count - 1 - mine
    total = jax.tree.map(
        lambda part, zero: jnp.full_like(part, 0) + jnp.asarray(zero, part.dtype), value, neutral
    )

    def step(position, total):
        longer = join(total, jax.tree.map(lambda part: part[position], pieces))
        return jax.tree.map(lambda new, old: jnp.where(position < mine, new, old), longer, total)

    return lax.fori_loop(0, count - 1, step, total)


def norm_rows(values, gain_values):
    return (
        values
        * lax.rsqrt(jnp.mean(values * values, axis=-1, keepdims=True) + epsilon)
        * gain_values
    )


def conv_silu(extended, extended_ids, kernel_values, bias_values, row_count):
    tap_count = kernel_values.shape[0]
    current = extended_ids[tap_count - 1 :]
    summed = jnp.zeros((row_count, extended.shape[1]), extended.dtype) + bias_values[None, :]
    for offset in range(tap_count):
        window = lax.slice_in_dim(extended, offset, offset + row_count, axis=0)
        same_doc = (
            lax.slice_in_dim(extended_ids, offset, offset + row_count, axis=0) == current
        ).astype(extended.dtype)
        summed = summed + window * kernel_values[offset][None, :] * same_doc[:, None]
    return jax.nn.silu(summed)


def ssd_block(rate_values, carried_in, block_items):
    state_now, prior_id = carried_in
    heads_x, b_rows, c_rows, step_rows, block_ids = block_items
    cumulated = jnp.cumsum(step_rows * rate_values[None, :], axis=0)
    block_len = block_ids.shape[0]
    positions = jnp.arange(block_len)
    allowed = (block_ids[:, None] == block_ids[None, :]) & (
        positions[:, None] >= positions[None, :]
    )
    spread = jnp.minimum(cumulated[:, None, :] - cumulated[None, :, :], 0.0)
    decays = jnp.where(allowed[:, :, None], jnp.exp(spread), 0.0)
    scores = jnp.einsum("tn,sn->ts", c_rows, b_rows, precision=highest)
    mixing = decays * scores[:, :, None] * step_rows[None, :, :]
    inner_part = jnp.einsum("tsh,shp->thp", mixing, heads_x, precision=highest)
    linked = (block_ids == prior_id).astype(state_now.dtype)
    carried = jnp.exp(cumulated) * linked[:, None]
    outer_part = (
        jnp.einsum("tn,hpn->thp", c_rows, state_now, precision=highest) * carried[:, :, None]
    )
    last_id = block_ids[block_len - 1]
    tail_weights = (
        jnp.where(
            (block_ids == last_id)[:, None],
            jnp.exp(cumulated[block_len - 1][None, :] - cumulated),
            0.0,
        )
        * step_rows
    )
    fresh_state = jnp.einsum("sh,shp,sn->hpn", tail_weights, heads_x, b_rows, precision=highest)
    state_next = carried[block_len - 1][:, None, None] * state_now + fresh_state
    return ((state_next, last_id), inner_part + outer_part)


def mixer_front(proj_f, prior_rows, kernel_f, bias_f, dt_bias_f, a_log_f, seg_ids, prior_ids):
    row_count = proj_f.shape[0]
    gate_rows = proj_f[:, :DI]
    extended = jnp.concatenate([prior_rows, proj_f[:, DI : DI + CW]], axis=0)
    extended_ids = jnp.concatenate([prior_ids, seg_ids])
    conv_rows = conv_silu(extended, extended_ids, kernel_f, bias_f, row_count)
    heads_x = conv_rows[:, :DI].reshape(row_count, NH, HP)
    b_rows = conv_rows[:, DI : DI + NS]
    c_rows = conv_rows[:, DI + NS :]
    step_rows = jax.nn.softplus(proj_f[:, DI + CW :] + dt_bias_f[None, :])
    rate_values = -jnp.exp(a_log_f)
    blocks = row_count // SPAN
    pieces = (
        heads_x.reshape(blocks, SPAN, NH, HP),
        b_rows.reshape(blocks, SPAN, NS),
        c_rows.reshape(blocks, SPAN, NS),
        step_rows.reshape(blocks, SPAN, NH),
        seg_ids.reshape(blocks, SPAN),
    )
    initial = (jnp.zeros((NH, HP, NS), jnp.float32), seg_ids[0])
    (state_end, _), outputs = lax.scan(partial(ssd_block, rate_values), initial, pieces)
    local_y = outputs.reshape(row_count, NH, HP)
    cumulated = jnp.cumsum(step_rows * rate_values[None, :], axis=0)
    from_start = jnp.exp(cumulated) * (seg_ids == seg_ids[0]).astype(jnp.float32)[:, None]
    return (gate_rows, heads_x, c_rows, local_y, from_start, state_end, from_start[row_count - 1])


def mixer_back(gate_rows, heads_x, c_rows, local_y, from_start, skip_f, gain_out_f, state_in):
    row_count = gate_rows.shape[0]
    incoming = (
        jnp.einsum("tn,hpn->thp", c_rows, state_in, precision=highest) * from_start[:, :, None]
    )
    total_y = local_y + incoming + skip_f[None, :, None] * heads_x
    gated = total_y.reshape(row_count, DI) * jax.nn.silu(gate_rows)
    return norm_rows(gated, gain_out_f)


def link_combine(earlier, later):
    first_a, last_a, decay_a, state_a = earlier
    first_b, last_b, decay_b, state_b = later
    joined = ((first_b == last_a) | (last_a < -0.5 * sentinel) | (first_b > 0.5 * sentinel)).astype(
        jnp.float32
    )
    through = decay_b * joined
    return (
        jnp.minimum(first_a, first_b),
        jnp.maximum(last_a, last_b),
        decay_a * through,
        through[:, None, None] * state_a + state_b,
    )


def grad_combine(earlier, later):
    mult_a, vector_a = earlier
    mult_b, vector_b = later
    return (mult_a * mult_b, vector_b + mult_b[:, None, None] * vector_a)


def local(
    tokens,
    segments,
    cotangent,
    gain_in,
    w_in,
    kernel,
    conv_bias,
    dt_bias,
    a_log,
    skip_gain,
    gain_out,
    w_out,
):
    row_count = tokens.shape[1]
    model_width = tokens.shape[2]
    inputs_f = tokens.reshape(row_count, model_width).astype(jnp.float32)
    seg_ids = segments.reshape(row_count)
    cot_low = cotangent.reshape(row_count, model_width)
    gathered = (
        lax.all_gather(gain_in, "group", axis=0, tiled=True),
        lax.all_gather(w_in, "group", axis=0, tiled=True),
        lax.all_gather(kernel, "group", axis=1, tiled=True),
        lax.all_gather(conv_bias, "group", axis=0, tiled=True),
        lax.all_gather(dt_bias, "group", axis=0, tiled=True),
        lax.all_gather(a_log, "group", axis=0, tiled=True),
        lax.all_gather(skip_gain, "group", axis=0, tiled=True),
        lax.all_gather(gain_out, "group", axis=0, tiled=True),
        lax.all_gather(w_out, "group", axis=0, tiled=True),
    )
    (
        full_gain_in,
        full_w_in,
        full_kernel,
        full_bias,
        full_dt_bias,
        full_a_log,
        full_skip,
        full_gain_out,
        full_w_out,
    ) = gathered
    normed, norm_pull = jax.vjp(norm_rows, inputs_f, full_gain_in.astype(jnp.float32))
    normed_low = normed.astype(jnp.bfloat16)
    proj_low = jnp.dot(normed_low, full_w_in, preferred_element_type=jnp.float32).astype(
        jnp.bfloat16
    )
    margin = KC - 1
    tail_rows = proj_low[row_count - margin :, DI : DI + CW].astype(jnp.float32)
    tail_ids = seg_ids[row_count - margin :].astype(jnp.float32)
    prior_rows, prior_ids = shifted((tail_rows, tail_ids), "group", 1)
    front = partial(mixer_front, seg_ids=seg_ids, prior_ids=prior_ids.astype(jnp.int32))
    front_out, front_pull = jax.vjp(
        front,
        proj_low.astype(jnp.float32),
        prior_rows,
        full_kernel.astype(jnp.float32),
        full_bias.astype(jnp.float32),
        full_dt_bias.astype(jnp.float32),
        full_a_log.astype(jnp.float32),
    )
    gate_rows, heads_x, c_rows, local_y, from_start, state_end, decay_dev = front_out
    first_id = seg_ids[0:1].astype(jnp.float32)
    last_id = seg_ids[row_count - 1 :].astype(jnp.float32)
    identity = (
        jnp.full((1,), sentinel, jnp.float32),
        jnp.full((1,), -sentinel, jnp.float32),
        jnp.ones((NH,), jnp.float32),
        jnp.zeros((NH, HP, NS), jnp.float32),
    )
    prefix = entering(
        (first_id, last_id, decay_dev, state_end), "group", link_combine, identity, False
    )
    connect = (first_id == prefix[1]).astype(jnp.float32)
    state_in = connect[:, None, None] * prefix[3]
    back_out, back_pull = jax.vjp(
        mixer_back,
        gate_rows,
        heads_x,
        c_rows,
        local_y,
        from_start,
        full_skip.astype(jnp.float32),
        full_gain_out.astype(jnp.float32),
        state_in,
    )
    out_low = back_out.astype(jnp.bfloat16)
    branch = jnp.dot(out_low, full_w_out, preferred_element_type=jnp.float32)
    layer_out = (inputs_f + branch).astype(jnp.bfloat16).reshape(1, row_count, model_width)
    back_w_in, back_w_out = (
        lax.all_gather(w_in, "group", axis=0, tiled=True),
        lax.all_gather(w_out, "group", axis=0, tiled=True),
    )
    contract_last = (((1,), (1,)), ((), ()))
    contract_first = (((0,), (0,)), ((), ()))
    d_normed_out = lax.dot_general(
        cot_low, back_w_out, contract_last, preferred_element_type=jnp.float32
    )
    grad_w_out_local = lax.dot_general(
        out_low, cot_low, contract_first, preferred_element_type=jnp.float32
    )
    d_gate, d_heads, d_crows, d_local, d_from, d_skip, d_gain_out, d_state_in = back_pull(
        d_normed_out
    )
    mult_own = connect * decay_dev
    vector_own = connect[:, None, None] * d_state_in
    ident_back = (jnp.ones((NH,), jnp.float32), jnp.zeros((NH, HP, NS), jnp.float32))
    later_grads = entering((mult_own, vector_own), "group", grad_combine, ident_back, True)
    d_state_end = later_grads[1]
    d_decay_dev = jnp.sum(d_state_end * state_in, axis=(1, 2))
    d_proj, d_prior, d_kernel, d_bias, d_dt_bias, d_a_log = front_pull(
        (d_gate, d_heads, d_crows, d_local, d_from, d_state_end, d_decay_dev)
    )
    returned = shifted(d_prior, "group", -1)
    d_proj = d_proj.at[row_count - margin :, DI : DI + CW].add(returned)
    d_proj_low = d_proj.astype(jnp.bfloat16)
    d_normed = lax.dot_general(
        d_proj_low, back_w_in, contract_last, preferred_element_type=jnp.float32
    )
    grad_w_in_local = lax.dot_general(
        normed_low, d_proj_low, contract_first, preferred_element_type=jnp.float32
    )
    d_inputs, d_gain_in = norm_pull(d_normed)
    grad_tokens = (cot_low.astype(jnp.float32) + d_inputs).reshape(1, row_count, model_width)
    local_grads = (
        d_gain_in,
        grad_w_in_local,
        d_kernel,
        d_bias,
        d_dt_bias,
        d_a_log,
        d_skip,
        d_gain_out,
        grad_w_out_local,
    )
    owned = (
        lax.psum_scatter(local_grads[0], "group", scatter_dimension=0, tiled=True),
        lax.psum_scatter(local_grads[1], "group", scatter_dimension=0, tiled=True),
        lax.psum_scatter(local_grads[2], "group", scatter_dimension=1, tiled=True),
        lax.psum_scatter(local_grads[3], "group", scatter_dimension=0, tiled=True),
        lax.psum_scatter(local_grads[4], "group", scatter_dimension=0, tiled=True),
        lax.psum_scatter(local_grads[5], "group", scatter_dimension=0, tiled=True),
        lax.psum_scatter(local_grads[6], "group", scatter_dimension=0, tiled=True),
        lax.psum_scatter(local_grads[7], "group", scatter_dimension=0, tiled=True),
        lax.psum_scatter(local_grads[8], "group", scatter_dimension=0, tiled=True),
    )
    summed = lax.psum(
        (owned[0], owned[1], owned[2], owned[3], owned[4], owned[5], owned[6], owned[7], owned[8]),
        "rep",
    )
    return (layer_out, grad_tokens) + tuple(summed)


def solution(mesh):
    placed = (
        P("rep", "group", None),
        P("rep", "group"),
        P("rep", "group", None),
        P("group"),
        P("group", None),
        P(None, "group"),
        P("group"),
        P("group"),
        P("group"),
        P("group"),
        P("group"),
        P("group", None),
    )
    return jax.shard_map(
        local,
        mesh=mesh,
        in_specs=placed,
        out_specs=(
            P("rep", "group", None),
            P("rep", "group", None),
            P("group"),
            P("group", None),
            P(None, "group"),
            P("group"),
            P("group"),
            P("group"),
            P("group"),
            P("group"),
            P("group", None),
        ),
        check_vma=False,
    )
```

profile of v0, /device:TPU:0, one launch (start us, length us, event | category | flops | bytes accessed | tf_op | source)
XLA Modules:
  0.0 1009.4 jit_solution(17749694502246609696)
XLA Ops:
  17.7 8.6 all-reduce.34
  26.4 5.4 all-gather.2
  37.2 30.3 %all-gather.11.cloned.1.call-done = bf16[768,3352]{1,0:T(8,128)(2,1)} async-done(((bf16[192,3352]{1,0:T(8,128)(2,1)}), bf16[768,3352]{1,0:T(8,128)(2,1)}) %all-gather.11.cloned.1.call-update) | async-done | bytes 5148688 | tf_op jit(solution)/shard_map/all_gather | solution.py:178
  67.5 6.4 fusion.192
  75.6 3.0 collective-permute-start
  83.1 8.0 fusion.120
  101.1 82.4 %while.110 = (s32[]{:T(128)}, f32[24,64,128]{2,1,0:T(8,128)S(1)}, s32[]{:T(128)}, f32[2,128,24,64]{1,0,3,2:T(2,128)}, f32[2,128,128,24]{2,3,1,0:T(8,128)}, /*ind...) while((s32[]{:T(128)}, f32[24,64,128]{2,1,0:T(8,128)S(1)}, ...), condition=%wide.region_3.4_spmd.clone, body=%wide.region_1.3_spmd.clone.sunk | while | flops 938877568 | bytes 24205132 | solution.py:119
  104.2 3.7 fusion.245
  112.4 3.3 fusion.244
  115.7 19.0 %dynamic_update_slice.223 = f32[2,128,24,64]{1,0,3,2:T(2,128)} dynamic-update-slice(f32[2,128,24,64]{1,0,3,2:T(2,128)} %get-tuple-element.2528, f32[1,128,24,64]{1,0,3,2:T(1,128)S(1)} %bitcast.570, s32[]{:T(128)} %get-tuple-element.2525, s32[]{:T(128)} %constant.277.clone.1..sunk, s32[]{:T(128)} %constant.277.clone.1..sunk, s32[]{:T(128)} %constant.277.clone.1..sunk) | dynamic-update-slice | bytes 1572868 | tf_op jit(solution)/shard_map/jvp()/while/body/jit(dynamic_update_index_in_dim)/dynamic_update_slice | solution.py:119
  145.5 3.7 fusion.245
  153.6 3.3 fusion.244
  156.9 19.0 %dynamic_update_slice.223 = f32[2,128,24,64]{1,0,3,2:T(2,128)} dynamic-update-slice(f32[2,128,24,64]{1,0,3,2:T(2,128)} %get-tuple-element.2528, f32[1,128,24,64]{1,0,3,2:T(1,128)S(1)} %bitcast.570, s32[]{:T(128)} %get-tuple-element.2525, s32[]{:T(128)} %constant.277.clone.1..sunk, s32[]{:T(128)} %constant.277.clone.1..sunk, s32[]{:T(128)} %constant.277.clone.1..sunk) | dynamic-update-slice | bytes 1572868 | tf_op jit(solution)/shard_map/jvp()/while/body/jit(dynamic_update_index_in_dim)/dynamic_update_slice | solution.py:119
  187.9 5.8 all-reduce.33
  195.0 5.1 all-gather.4
  202.7 5.5 all-gather.3
  208.2 3.3 reshape.606
  211.5 11.7 %all-gather.15.cloned.1.call-done = f32[96,64,128]{2,1,0:T(8,128)} async-done(((f32[24,64,128]{2,1,0:T(8,128)}), f32[96,64,128]{2,1,0:T(8,128)}) %all-gather.15.cloned.1.call-update) | async-done | bytes 3145744 | tf_op jit(solution)/shard_map/all_gather | solution.py:30
  223.2 11.2 %while.111 = (s32[]{:T(128)}, f32[1]{0:T(128)}, f32[24,64,128]{2,1,0:T(8,128)S(1)}, s32[]{:T(128)}, f32[4,1]{0,1:T(1,128)S(1)}, /*index=5*/f32[4,24]{1,0:T(4,128...) while((s32[]{:T(128)}, f32[1]{0:T(128)}, ...), condition=%wide.region_7.8_spmd.clone, body=%wide.region_6.7_spmd.clone.sunk | while | flops 786468 | bytes 2359816 | solution.py:42
  234.4 2.6 fusion.155
  239.6 3.8 multiply_reduce_fusion.8
  243.3 13.8 %all-gather.13.cloned.1.call-done = bf16[1536,768]{1,0:T(8,128)(2,1)} async-done(((bf16[384,768]{1,0:T(8,128)(2,1)}), bf16[1536,768]{1,0:T(8,128)(2,1)}) %all-gather.13.cloned.1.call-update) | async-done | bytes 2359312 | tf_op jit(solution)/shard_map/all_gather | solution.py:185
  257.2 3.8 multiply_reduce_fusion.4
  261.1 4.4 multiply_reduce_fusion.5
  270.7 5.0 all-gather.5
  278.2 2.9 fusion.157
  281.2 25.3 %all-gather.17.cloned.1.call-done = f32[96,64,128]{2,1,0:T(8,128)} async-done(((f32[24,64,128]{2,1,0:T(8,128)}), f32[96,64,128]{2,1,0:T(8,128)}) %all-gather.17.cloned.1.call-update) | async-done | bytes 3145744 | tf_op jit(solution)/shard_map/all_gather | solution.py:30
  306.5 4.0 rev.6
  310.5 4.0 while.112
  318.5 131.9 %while.113 = (s32[]{:T(128)}, f32[24]{0:T(128)}, f32[24,64,128]{2,1,0:T(8,128)S(1)}, f32[2,128,24,64]{1,0,3,2:T(2,128)}, f32[2,128,128]{2,1,0:T(8,128)}, /*index...) while((s32[]{:T(128)}, f32[24]{0:T(128)}, ...), condition=%wide.region_26.27_spmd.clone, body=%wide.region_16.26_spmd.clone.sunk | while | flops 1869405184 | bytes 99822048 | solution.py:119
  329.4 3.7 fusion.262
  353.6 2.7 convolution_bitcast_fusion.5
  363.2 19.0 %dynamic_update_slice.227 = f32[2,128,24,64]{1,0,3,2:T(2,128)} dynamic-update-slice(f32[2,128,24,64]{1,0,3,2:T(2,128)} %get-tuple-element.2684, f32[1,128,24,64]{1,0,3,2:T(1,128)} %bitcast.566, s32[]{:T(128)S(6)} %sub.231, s32[]{:T(128)} %constant.277.clone.1..sunk.3, s32[]{:T(128)} %constant.277.clone.1..sunk.3, s32[]{:T(128)} %constant.277.clone.1..sunk.3) | dynamic-update-slice | bytes 1572868 | tf_op jit(solution)/shard_map/transpose(jvp())/while/body/jit(dynamic_update_index_in_dim)/dynamic_update_slice | solution.py:119
  394.8 3.7 fusion.262
  419.5 2.7 convolution_bitcast_fusion.5
  429.2 19.0 %dynamic_update_slice.227 = f32[2,128,24,64]{1,0,3,2:T(2,128)} dynamic-update-slice(f32[2,128,24,64]{1,0,3,2:T(2,128)} %get-tuple-element.2684, f32[1,128,24,64]{1,0,3,2:T(1,128)} %bitcast.566, s32[]{:T(128)S(6)} %sub.231, s32[]{:T(128)} %constant.277.clone.1..sunk.3, s32[]{:T(128)} %constant.277.clone.1..sunk.3, s32[]{:T(128)} %constant.277.clone.1..sunk.3) | dynamic-update-slice | bytes 1572868 | tf_op jit(solution)/shard_map/transpose(jvp())/while/body/jit(dynamic_update_index_in_dim)/dynamic_update_slice | solution.py:119
  452.6 3.3 fusion.136
  458.6 5.8 multiply_reduce_fusion.2
  479.4 4.8 pad_add_fusion.1
  490.5 6.3 scatter-add.4
  496.8 7.8 fusion.141
  506.8 97.5 %reduce-scatter.6.cloned.1.call-done = f32[192,3352]{1,0:T(8,128)} async-done(((f32[768,3352]{1,0:T(8,128)}), f32[192,3352]{1,0:T(8,128)}) %reduce-scatter.6.cloned.1.call-update) | async-done | bytes 2574352 | tf_op jit(solution)/shard_map/reduce_scatter | solution.py:293
  607.3 3.5 fusion.132
  610.9 4.4 fusion.146
  615.3 11.2 %all-reduce.32 = (f32[768]{0:T(1024)S(1)}, f32[1792]{0:T(1024)S(1)}, f32[24]{0:T(128)S(1)}, f32[24]{0:T(128)S(1)}, f32[24]{0:T(128)S(1)}, /*index=5*/f32[1536]{0:T(1024)S(1)}) all-reduce(f32[768]{0:T(1024)S(1)} %get-tuple-element.1729, f32[1792]{0:T(1024)S(1)} %copy-done.102, ...), channel_id=4, replica_groups=mesh['group'=4,'rep'=32] {'group'}, use_global_device_ids=true, to_apply=%region_29.30.clone | all-reduce | flops 4168 | bytes 33344
  629.5 183.8 %all-reduce.30 = (f32[192]{0:T(256)}, f32[4,448]{1,0:T(4,128)}, f32[448]{0:T(512)}, f32[6]{0:T(128)}, f32[6]{0:T(128)}, /*index=5*/f32[6]{0:T(128)}, f32[384]{0:T(512)}) all-reduce(f32[192]{0:T(256)S(1)} %dynamic-slice.16, f32[4,448]{1,0:T(4,128)S(1)} %copy.258, ...), channel_id=1, replica_groups=mesh['group'=4,'rep'=32] {'rep'}, use_global_device_ids=true, to_apply=%region_30.31 | all-reduce | flops 2834 | bytes 22672 | tf_op jit(solution)/shard_map/psum | solution.py:302
  813.3 184.3 %all-reduce.37.cloned.1.call-done = (f32[192,3352]{1,0:T(8,128)}, f32[384,768]{1,0:T(8,128)}) async-done(((f32[192,3352]{1,0:T(8,128)}, f32[384,768]{1,0:T(8,128)}), (f32[192,3352]{1,0:T(8,128)}, f32[384,768]{1,0:T(8,128)})) %all-reduce.37.cloned.1.call-update) | async-done | bytes 3754000 | tf_op jit(solution)/shard_map/psum | solution.py:302
  997.6 3.5 copy.533
  (618 shorter events, 201.2 us)
Async XLA Ops:
  7.2 26.6 %copy-start.28 = (bf16[1,256,768]{2,1,0:T(8,128)(2,1)S(1)}, bf16[1,256,768]{2,1,0:T(8,128)(2,1)}, u32[]{:S(2)}) copy-start(bf16[1,256,768]{2,1,0:T(8,128)(2,1)} %param.22) | copy-start | bytes 1179652
  7.2 60.3 %all-gather.11.cloned.1.call-start = ((), (), s32[]{:S(2)}) async-start(), calls=%async_computation.3 | async-start | bytes 6635520 | tf_op jit(solution)/shard_map/all_gather | solution.py:178
  7.9 215.3 %all-gather.15.cloned.1.call-start = ((), (), s32[]{:S(2)}) async-start(), calls=%async_computation.7 | async-start | bytes 3932160 | tf_op jit(solution)/shard_map/all_gather | solution.py:30
  8.7 25.9 %collective-permute-start.1 = (f32[3]{0:T(128)S(1)}, f32[3]{0:T(128)S(1)}, u32[]{:S(2)}, u32[]{:S(2)}) collective-permute-start(f32[3]{0:T(128)S(1)} %convert_bitcast_fusion), channel_id=1, source_target_pairs={{0,32},{32,64},{64,96},{1,33},{33,65},{65,97},{2,34},{34,66},{66,9... | collective-permute-start | bytes 44 | tf_op jit(solution)/shard_map/ppermute | solution.py:25
  26.4 47.6 %copy-start.119 = (bf16[24]{0:T(256)(128)(2,1)}, bf16[24]{0:T(256)(128)(2,1)S(1)}, u32[]{:S(2)}) copy-start(bf16[24]{0:T(256)(128)(2,1)S(1)} %get-tuple-element.1903) | copy-start | bytes 148
  26.4 47.6 %copy-start.63 = (f32[768]{0:T(1024)}, f32[768]{0:T(1024)S(1)}, u32[]{:S(2)}) copy-start(f32[768]{0:T(1024)S(1)} %convert_element_type.117) | copy-start | bytes 9220
  31.8 46.7 %copy-start.114 = (f32[24]{0:T(128)}, f32[24]{0:T(128)S(1)}, u32[]{:S(2)}) copy-start(f32[24]{0:T(128)S(1)} %convert_element_type.121) | copy-start | bytes 292
  33.8 49.2 %copy-start.83 = (f32[1792]{0:T(1024)}, f32[1792]{0:T(1024)S(1)}, u32[]{:S(2)}) copy-start(f32[1792]{0:T(1024)S(1)} %get-tuple-element.1731) | copy-start | bytes 21508
  33.8 49.2 %copy-start.85 = (f32[1792]{0:T(1024)}, f32[1792]{0:T(1024)S(1)}, u32[]{:S(2)}) copy-start(f32[1792]{0:T(1024)S(1)} %get-tuple-element.1732) | copy-start | bytes 21508
  33.8 49.2 %copy-start.87 = (f32[1792]{0:T(1024)}, f32[1792]{0:T(1024)S(1)}, u32[]{:S(2)}) copy-start(f32[1792]{0:T(1024)S(1)} %get-tuple-element.1733) | copy-start | bytes 21508
  33.9 49.2 %copy-start.89 = (f32[1792]{0:T(1024)}, f32[1792]{0:T(1024)S(1)}, u32[]{:S(2)}) copy-start(f32[1792]{0:T(1024)S(1)} %get-tuple-element.1734) | copy-start | bytes 21508
  34.0 39.9 %copy-start.110 = (f32[256]{0:T(256)}, f32[256]{0:T(256)S(1)}, u32[]{:S(2)}) copy-start(f32[256]{0:T(256)S(1)} %fusion.149) | copy-start | bytes 3076
  34.5 44.1 %copy-start.116 = (f32[24]{0:T(128)}, f32[24]{0:T(128)S(1)}, u32[]{:S(2)}) copy-start(f32[24]{0:T(128)S(1)} %get-tuple-element.1966) | copy-start | bytes 292
  34.6 39.4 %copy-start.93 = (f32[256]{0:T(256)}, f32[256]{0:T(256)S(1)}, u32[]{:S(2)}) copy-start(f32[256]{0:T(256)S(1)} %fusion.177) | copy-start | bytes 3076
  37.2 45.9 %copy-start.104 = (f32[256]{0:T(256)}, f32[256]{0:T(256)S(1)}, u32[]{:S(2)}) copy-start(f32[256]{0:T(256)S(1)} %get-tuple-element.1957) | copy-start | bytes 3076
  37.2 45.9 %copy-start.106 = (f32[256]{0:T(256)}, f32[256]{0:T(256)S(1)}, u32[]{:S(2)}) copy-start(f32[256]{0:T(256)S(1)} %get-tuple-element.1958) | copy-start | bytes 3076
  37.2 45.9 %copy-start.108 = (f32[256]{0:T(256)}, f32[256]{0:T(256)S(1)}, u32[]{:S(2)}) copy-start(f32[256]{0:T(256)S(1)} %get-tuple-element.1959) | copy-start | bytes 3076
  75.6 7.1 collective-permute-start
  83.0 8.1 copy-start.36
  101.1 9.5 copy-start.24
  142.3 9.5 copy-start.24
  183.6 28.0 %copy-start.26 = (f32[2,128,128]{2,1,0:T(8,128)}, f32[2,128,128]{2,1,0:T(8,128)S(1)}, u32[]{:S(2)}) copy-start(f32[2,128,128]{2,1,0:T(8,128)S(1)} %get-tuple-element.2783) | copy-start | bytes 393220
  184.5 72.7 %all-gather.13.cloned.1.call-start = ((), (), s32[]{:S(2)}) async-start(), calls=%async_computation.4 | async-start | bytes 2949120 | tf_op jit(solution)/shard_map/all_gather | solution.py:185
  185.2 121.3 %all-gather.17.cloned.1.call-start = ((), (), s32[]{:S(2)}) async-start(), calls=%async_computation.8 | async-start | bytes 3932160 | tf_op jit(solution)/shard_map/all_gather | solution.py:30
  200.2 78.0 %copy-start.61 = (f32[1536]{0:T(1024)}, f32[1536]{0:T(1024)S(1)}, u32[]{:S(2)}) copy-start(f32[1536]{0:T(1024)S(1)} %reshape.661) | copy-start | bytes 18436
  201.5 21.7 %copy-start.59 = (f32[24,2,128]{2,0,1:T(8,128)}, f32[24,2,128]{2,0,1:T(8,128)S(1)}, u32[]{:S(2)}) copy-start(f32[24,2,128]{2,0,1:T(8,128)S(1)} %reduce-window.14) | copy-start | bytes 73732
  201.7 21.5 %copy-start.112 = (f32[24,2]{0,1:T(2,128)}, f32[24,2]{0,1:T(2,128)S(1)}, u32[]{:S(2)}) copy-start(f32[24,2]{0,1:T(2,128)S(1)} %slice.141) | copy-start | bytes 580
  202.5 68.1 %copy-start.55 = (f32[256,24]{0,1:T(8,128)}, f32[256,24]{0,1:T(8,128)S(1)}, u32[]{:S(2)}) copy-start(f32[256,24]{0,1:T(8,128)S(1)} %fusion.175) | copy-start | bytes 73732
  239.6 17.6 %copy-start.41 = (bf16[1,256,768]{2,1,0:T(8,128)(2,1)S(1)}, bf16[1,256,768]{2,1,0:T(8,128)(2,1)}, u32[]{:S(2)}) copy-start(bf16[1,256,768]{2,1,0:T(8,128)(2,1)} %param.24) | copy-start | bytes 1179652
  243.3 34.9 %copy-start.95 = (f32[256]{0:T(256)}, f32[256]{0:T(256)S(1)}, u32[]{:S(2)}) copy-start(f32[256]{0:T(256)S(1)} %fusion.178) | copy-start | bytes 3076
  265.4 10.4 %copy-start.3 = (f32[256,1536]{0,1:T(8,128)}, f32[256,1536]{0,1:T(8,128)S(1)}, u32[]{:S(2)}) copy-start(f32[256,1536]{0,1:T(8,128)S(1)} %get-tuple-element.1912) | copy-start | bytes 4718596
  267.8 239.0 %reduce-scatter.8.cloned.1.call-start = ((), (), s32[]{:S(2)}) async-start(), calls=%async_computation.6 | async-start | bytes 5898240 | tf_op jit(solution)/shard_map/reduce_scatter | solution.py:300
  281.2 323.1 %reduce-scatter.6.cloned.1.call-start = ((), (), s32[]{:S(2)}) async-start(), calls=%async_computation.5 | async-start | bytes 13271040 | tf_op jit(solution)/shard_map/reduce_scatter | solution.py:293
  353.5 7.1 copy-start.77
  353.5 7.1 copy-start.1
  353.5 7.1 copy-start.2
  360.6 21.6 %copy-start.123 = (f32[2,24,1,1]{1,3,2,0:T(1,128)S(1)}, f32[2,24,1,1]{1,3,2,0:T(1,128)}, u32[]{:S(2)}) copy-start(f32[2,24,1,1]{1,3,2,0:T(1,128)} %get-tuple-element.2738) | copy-start | bytes 580 | tf_op jit(solution)/shard_map/transpose(jvp())/while
  419.5 7.1 copy-start.1
  426.5 21.6 %copy-start.123 = (f32[2,24,1,1]{1,3,2,0:T(1,128)S(1)}, f32[2,24,1,1]{1,3,2,0:T(1,128)}, u32[]{:S(2)}) copy-start(f32[2,24,1,1]{1,3,2,0:T(1,128)} %get-tuple-element.2738) | copy-start | bytes 580 | tf_op jit(solution)/shard_map/transpose(jvp())/while
  469.7 9.0 copy-start.56
  471.8 16.1 %collective-permute-start.2 = (f32[3,1792]{1,0:T(4,128)}, f32[3,1792]{1,0:T(4,128)}, u32[]{:S(2)}, u32[]{:S(2)}) collective-permute-start(f32[3,1792]{1,0:T(4,128)} %copy.239), channel_id=1, source_target_pairs={{32,0},{64,32},{96,64},{33,1},{65,33},{97,65},{34,2},{66,34},{98,6... | collective-permute-start | bytes 64520 | tf_op jit(solution)/shard_map/ppermute | solution.py:25
  489.0 7.8 copy-start.29
  489.0 7.8 copy-start.64
  489.0 7.8 copy-start.94
  504.7 123.8 %reduce-scatter.10.cloned.1.call-start = ((), (), s32[]{:S(2)}) async-start(), calls=%async_computation.9 | async-start | bytes 1146880
  506.7 490.9 %all-reduce.37.cloned.1.call-start = ((), (), s32[]{:S(2)}) async-start(), calls=%async_computation.10 | async-start | bytes 7667712 | tf_op jit(solution)/shard_map/psum | solution.py:302
  610.8 16.1 %copy-start.111 = (f32[256]{0:T(256)S(1)}, f32[256]{0:T(256)}, u32[]{:S(2)}) copy-start(f32[256]{0:T(256)} %copy-done.110) | copy-start | bytes 3076
  610.9 16.1 %copy-start.43 = (bf16[1,256,768]{2,1,0:T(8,128)(2,1)S(1)}, bf16[1,256,768]{2,1,0:T(8,128)(2,1)}, u32[]{:S(2)}) copy-start(bf16[1,256,768]{2,1,0:T(8,128)(2,1)} %param.24) | copy-start | bytes 1179652
  (128 other events, 352.2 us)
Sparse Core Ops, SparseCore 0:
  9.7 57.7 all-gather.10
  184.6 38.5 all-gather.14
  224.9 32.2 all-gather.12
  267.9 38.5 all-gather.16
  308.8 50.8 reduce-scatter.7
  504.8 99.4 reduce-scatter.5
  607.4 21.0 reduce-scatter.9
  631.3 366.2 all-reduce.36
where the time goes:
time: 1020 us; the launch traced here: 1010 us
  waiting for transfers between devices  365 us (36%)
  blocking collectives  230 us (23%)
  local copies, waits for them, and re-layouts  187 us (18%)
  other arithmetic  106 us (10%)
  matrix products  85.2 us (8%)
  between operations  22.3 us (2%)
    psum x1, waiting for transfers between devices, local(): lax.psum((owned[0], owned[1], owned[2], owned[3], owned[4], owned[5], own...  184 us
    psum x1, blocking collectives, local(): lax.psum((owned[0], owned[1], owned[2], owned[3], owned[4], owned[5], own...  184 us
    reduce_scatter x1, waiting for transfers between devices, local(): lax.psum_scatter(local_grads[1], 'group', scatter_dimension=0, tiled=True)  97.5 us
    dynamic_update_slice x22, local copies, waits for them, and re-layouts, mixer_front(): lax.scan(partial(ssd_block, rate_values), initial, pieces)  79.6 us
    all_gather x2, waiting for transfers between devices, entering(): pieces = jax.tree.map(lambda part: lax.all_gather(part, axis), value)  37 us
    all_gather x1, waiting for transfers between devices, local(): lax.all_gather(w_in, 'group', axis=0, tiled=True)  30.3 us
    unnamed x3, blocking collectives  25.6 us
    unnamed x197, local copies, waits for them, and re-layouts  25.5 us
  transfers between devices with their start and end apart: 11, of which 7 were waited for; matrix products, arithmetic and copies ran while one was open for 24% of the time, Pallas kernels for 0%

commit v1 on v0

v1 whole, which is shorter than its diff:
```python
import jax
import jax.numpy as jnp
import numpy as np
from jax import lax
from jax.experimental import pallas as pl
from jax.experimental.pallas import tpu as pltpu
from jax.sharding import PartitionSpec as P

D = 768
NH = 24
HP = 64
NS = 128
DI = 1536
CW = 1792
SPAN = 128
ROWS = 256
HL = 6
XW = HL * HP
CL = XW + 2 * NS
PW = XW + CL + 128
CHUNK = 288
epsilon = 1e-05
f32 = jnp.float32
bf16 = jnp.bfloat16
NN = ((1,), (0,))
NT = ((1,), (1,))
TN = ((0,), (0,))
vmem_bytes = 56 * 1024 * 1024


def mm(a, b, dims):
    return lax.dot_general(
        a.astype(bf16), b.astype(bf16), (dims, ((), ())), preferred_element_type=f32
    )


def mm_exact(a, b, dims):
    return lax.dot_general(
        a, b, (dims, ((), ())), preferred_element_type=f32, precision=lax.Precision.HIGHEST
    )


def to_columns(rows):
    short = SPAN - rows.shape[0]
    return jnp.concatenate([rows, jnp.zeros((short, SPAN), f32)], axis=0).T


def softplus(v):
    return jnp.maximum(v, 0.0) + jnp.log1p(jnp.exp(-jnp.abs(v)))


def over_lanes(column):
    return jnp.broadcast_to(column, (SPAN, SPAN))


def span_decays(dt_rows, rate, pos_rows):
    row_at = lax.broadcasted_iota(jnp.int32, (SPAN, SPAN), 0)
    lane_at = lax.broadcasted_iota(jnp.int32, (SPAN, SPAN), 1)
    pos = to_columns(pos_rows)
    step = softplus(dt_rows)
    cum = mm_exact((row_at >= lane_at).astype(f32), step * rate, NN)
    cum_t = cum.T
    step_t = step.T
    allowed = (over_lanes(pos[:, 0:1]) == pos_rows[0:1, :]) & (row_at >= lane_at)
    low = lane_at < HP
    cums = [over_lanes(cum[:, h : h + 1]) for h in range(HL)]
    linked = pos[:, 4:5]
    tail = pos[:, 5:6]
    carried, tails = [], []
    for p in range(HL // 2):
        both = jnp.where(low, cums[2 * p], cums[2 * p + 1])
        steps = jnp.where(
            low, over_lanes(step[:, 2 * p : 2 * p + 1]), over_lanes(step[:, 2 * p + 1 : 2 * p + 2])
        )
        carried.append(jnp.exp(both) * linked)
        tails.append(jnp.exp(both[SPAN - 1 :, :] - both) * tail * steps)

    def decay(h):
        return jnp.where(allowed, jnp.exp(jnp.minimum(cums[h] - cum_t[h : h + 1, :], 0.0)), 0.0)

    return pos, step, step_t, cum, decay, carried, tails, low


def pick(index, sources, target):
    for d, source in enumerate(sources):

        @pl.when(index == d)
        def _(source=source):
            target[...] = source[...]


def put(index, targets, value):
    for d, target in enumerate(targets):

        @pl.when(index == d)
        def _(target=target):
            target[...] = value


def forward_kernel(
    me, t0, t1, t2, t3, c0, c1, c2, c3, w0, w1, w2, w3,
    pos, gain_in, taps, bias, dtb, rate, skip, gain_out, w_out,
    w_full, normed, proj, v_out, states, y_out, dno_out, stats, o0, o1, o2, o3,
    tok, cot, state, ext,
):
    i = pl.program_id(0)
    g = me[0]

    @pl.when(i == 0)
    def _():
        for d, part in enumerate((w0, w1, w2, w3)):
            w_full[pl.ds(pl.multiple_of((g ^ d) * 192, 64), 192), :] = part[...]
        state[...] = jnp.zeros_like(state)
        ext[0:8, :] = jnp.zeros((8, CL), f32)

    pick(g ^ i, (t0, t1, t2, t3), tok)
    pick(g ^ i, (c0, c1, c2, c3), cot)
    x = tok[...].astype(f32)
    rms = lax.rsqrt(jnp.mean(x * x, axis=-1, keepdims=True) + epsilon)
    low_rows = (x * rms * gain_in[...]).astype(bf16)
    normed[...] = low_rows
    proj[...] = mm(low_rows, w_full[...], NN).astype(bf16)
    dno_out[...] = mm(cot[...], w_out[...], NT)
    ext[8 : 8 + ROWS, :] = proj[:, XW : XW + CL].astype(f32)
    weighted = []
    for s in range(ROWS // SPAN):
        at = s * SPAN
        rows = slice(at, at + SPAN)
        dt_rows = proj[rows, XW + CL :].astype(f32) + dtb[...]
        pos_rows = pos[s]
        cols, step, step_t, cum, decay, carried, tails, low = span_decays(
            dt_rows, rate[...], pos_rows
        )
        v = bias[...] + taps[3:4, :] * ext[8 + at : 8 + at + SPAN, :]
        for lag in range(1, 4):
            window = ext[8 + at - lag : 8 + at - lag + SPAN, :]
            v = v + (taps[3 - lag : 4 - lag, :] * cols[:, lag : lag + 1]) * window
        v_out[rows, :] = v
        conv = v * jax.nn.sigmoid(v)
        b_rows, c_rows = conv[:, XW : XW + NS], conv[:, XW + NS :]
        scores = mm(c_rows, b_rows, NT)
        states[s] = state[...]
        from_state = mm(c_rows, state[...], NN)
        ys, ends, decays_end = [], [], []
        for p in range(HL // 2):
            lanes = slice(p * SPAN, (p + 1) * SPAN)
            xp = conv[:, lanes]
            mixing = [
                decay(h) * scores * step_t[h : h + 1, :] for h in (2 * p, 2 * p + 1)
            ]
            inner = mm(
                jnp.concatenate(mixing, axis=1),
                jnp.concatenate([jnp.where(low, xp, 0.0), jnp.where(low, 0.0, xp)], axis=0),
                NN,
            )
            ys.append(inner + carried[p] * from_state[:, lanes] + skip[:, lanes] * xp)
            ends.append(tails[p] * xp)
            decays_end.append(carried[p][SPAN - 1 :, :])
        y = jnp.concatenate(ys, axis=1)
        y_out[rows, :] = y
        state[...] = jnp.concatenate(decays_end, axis=1) * state[...] + mm(
            b_rows, jnp.concatenate(ends, axis=1), TN
        )
        gate = proj[rows, :XW].astype(f32)
        gated = y * (gate * jax.nn.sigmoid(gate))
        scaled = gated * gain_out[...]
        weighted.append(scaled.astype(bf16))
        squares = jnp.sum(gated * gated, axis=-1, keepdims=True)
        products = jnp.sum(scaled * dno_out[rows, :], axis=-1, keepdims=True)
        lane_at = lax.broadcasted_iota(jnp.int32, (SPAN, SPAN), 1)
        both = jnp.where(lane_at == 0, squares, jnp.where(lane_at == 1, products, 0.0))
        stats[s] = both.T[0:8, :]
    ext[0:8, :] = ext[ROWS : ROWS + 8, :]
    branch = mm(jnp.concatenate(weighted, axis=0), w_out[...], NN)
    put(g ^ i, (o0, o1, o2, o3), branch.astype(bf16))


def split_sum(rows, ones):
    high = rows.astype(bf16)
    rest = rows - high.astype(f32)
    return mm(high, ones, NN) + mm(rest, ones, NN)


def backward_kernel(
    me, c0, c1, c2, c3, w_full, normed, proj, v_in, states, y_in, dno_in, stats,
    pos, taps, dtb, rate, skip, gain_out, ones,
    bundle, n0, n1, n2, n3,
    cot, d_state, ext, d_proj, normed_out, acc_in, acc_dt, acc_out, acc_small, small,
):
    i = pl.num_programs(0) - 1 - pl.program_id(0)
    g = me[0]

    @pl.when(pl.program_id(0) == 0)
    def _():
        for ref in (d_state, acc_in, acc_dt, acc_out, acc_small, small):
            ref[...] = jnp.zeros_like(ref)
        ext[ROWS:, :] = jnp.zeros((8, CL), f32)

    pick(g ^ i, (c0, c1, c2, c3), cot)
    row_at = lax.broadcasted_iota(jnp.int32, (SPAN, SPAN), 0)
    lane_at = lax.broadcasted_iota(jnp.int32, (SPAN, SPAN), 1)
    later = (row_at <= lane_at).astype(f32)

    def add(row, value):
        width = value.shape[1]
        acc_small[row : row + 1, :width] += value

    def down(value):
        return jnp.sum(value, axis=0, keepdims=True)

    for s in reversed(range(ROWS // SPAN)):
        at = s * SPAN
        rows = slice(at, at + SPAN)
        sums = to_columns(stats[s])
        rms = lax.rsqrt(sums[:, 0:1] * (1.0 / DI) + epsilon)
        mean = rms * rms * rms * sums[:, 1:2] * (1.0 / DI)
        gate = proj[rows, :XW].astype(f32)
        sig = jax.nn.sigmoid(gate)
        silu = gate * sig
        y = y_in[rows, :]
        gated = y * silu
        scaled = gated * rms
        normed_out[rows, :] = (scaled * gain_out[...]).astype(bf16)
        dno = dno_in[rows, :]
        add(0, down(dno * scaled))
        d_gated = rms * gain_out[...] * dno - gated * mean
        dy = d_gated * silu
        d_proj[rows, :XW] = (d_gated * y * (sig * (1.0 + gate * (1.0 - sig)))).astype(bf16)

        dt_rows = proj[rows, XW + CL :].astype(f32) + dtb[...]
        cols, step, step_t, cum, decay, carried, tails, low = span_decays(
            dt_rows, rate[...], pos[s]
        )
        v = v_in[rows, :]
        sig_v = jax.nn.sigmoid(v)
        conv = v * sig_v
        x, b_rows, c_rows = conv[:, :XW], conv[:, XW : XW + NS], conv[:, XW + NS :]
        add(1, down(dy * x))
        state = states[s]
        state_grad = d_state[...]
        scores = mm(c_rows, b_rows, NT)
        from_state = mm(c_rows, state, NN)
        from_grad = mm(b_rows, state_grad, NN)
        carried_all = jnp.concatenate(carried, axis=1)
        tails_all = jnp.concatenate(tails, axis=1)
        dy_carried = dy * carried_all
        x_tail = x * tails_all
        d_scores = jnp.zeros((SPAN, SPAN), f32)
        row_sums = jnp.zeros((SPAN, SPAN), f32)
        col_sums, dxs = [], []
        for p in range(HL // 2):
            lanes = slice(p * SPAN, (p + 1) * SPAN)
            xp, dyp = x[:, lanes], dy[:, lanes]
            halves = jnp.concatenate([jnp.where(low, dyp, 0.0), jnp.where(low, 0.0, dyp)], axis=0)
            d_mixing = mm(halves, xp, NT)
            mixing = []
            for k in range(2):
                h = 2 * p + k
                kept = decay(h)
                kept_step = kept * step_t[h : h + 1, :]
                mixing.append(kept_step * scores)
                d_mix = d_mixing[k * SPAN : (k + 1) * SPAN, :]
                d_scores = d_scores + d_mix * kept_step
                plain = d_mix * kept * scores
                col_sums.append(down(plain))
                row_sum = jnp.sum(plain * step_t[h : h + 1, :], axis=1, keepdims=True)
                row_sums = jnp.where(lane_at == h, row_sum, row_sums)
            inner = mm(jnp.concatenate(mixing, axis=0), halves, TN)
            dxs.append(inner + skip[:, lanes] * dyp + tails[p] * from_grad[:, lanes])
        dx = jnp.concatenate(dxs, axis=1)
        d_c = mm(d_scores, b_rows, NN) + mm(dy_carried, state, NT)
        d_b = mm(d_scores, c_rows, TN) + mm(x_tail, state_grad, NT)

        end_decay = carried_all[SPAN - 1 :, :]
        through = end_decay * down(state * state_grad)
        last = lax.broadcasted_iota(jnp.int32, (SPAN, XW), 0) == SPAN - 1
        from_start = split_sum(
            dy_carried * from_state + jnp.where(last, through, 0.0), ones[...]
        )
        to_end = split_sum(x * from_grad, ones[...])
        end_plain = jnp.exp(cum[SPAN - 1 :, :] - cum) * cols[:, 5:6]
        to_end_kept = to_end * end_plain
        to_end_step = to_end_kept * step
        col_sum = to_columns(jnp.concatenate(col_sums, axis=0))
        d_cum = row_sums - col_sum * step + from_start - to_end_step
        d_cum = d_cum + jnp.where(row_at == SPAN - 1, down(to_end_step), 0.0)
        d_log = mm_exact(later, d_cum, NN)
        d_step = col_sum + to_end_kept + rate[...] * d_log
        d_dt = d_step * jax.nn.sigmoid(dt_rows)
        add(2, down(d_dt))
        add(3, down(d_log * step) * rate[...])
        d_proj[rows, XW + CL :] = d_dt.astype(bf16)
        d_state[...] = end_decay * state_grad + mm(c_rows, dy_carried, TN)

        dv = jnp.concatenate([dx, d_b, d_c], axis=1) * (sig_v * (1.0 + v * (1.0 - sig_v)))
        ext[rows, :] = dv
        add(4, down(dv))
        conv_in = proj[rows, XW : XW + CL].astype(f32)
        add(8, down(dv * conv_in))
        d_conv = taps[3:4, :] * dv
        for lag in range(1, 4):
            window = ext[at + lag : at + lag + SPAN, :] * cols[:, 5 + lag : 6 + lag]
            d_conv = d_conv + taps[3 - lag : 4 - lag, :] * window
            add(8 - lag, down(window * conv_in))
        d_proj[rows, XW : XW + CL] = d_conv.astype(bf16)

    ext[ROWS:, :] = ext[0:8, :]
    d_normed = mm(d_proj[...], w_full[...], NT)
    put(g ^ i, (n0, n1, n2, n3), d_normed.astype(bf16))
    add(9, down(d_normed * normed[...].astype(f32)))
    acc_in[...] += mm(normed[...], d_proj[:, : XW + CL], TN)
    acc_dt[...] += mm(d_proj[:, XW + CL :], normed[...], TN)[0:8, :]
    acc_out[...] += mm(normed_out[...], cot[...], TN)

    @pl.when(i == 0)
    def _():
        for k in range(4):
            for tile in range(8):
                for q in range(4):
                    bundle[4 * tile + q, 48 * k : 48 * k + 48, :] = acc_in[
                        192 * k + 48 * q : 192 * k + 48 * q + 48, 128 * tile : 128 * tile + 128
                    ].astype(bf16)
            for h in range(HL):
                at = 16 * k + 2 * h
                small[at : at + 1, :] = acc_dt[h : h + 1, 192 * k : 192 * k + 128]
                small[at + 1 : at + 2, 0:64] = acc_dt[h : h + 1, 192 * k + 128 : 192 * k + 192]
        for piece in range(160):
            place = 192 + 16 * (piece % 5)
            if piece < 144:
                tile, q = piece // 24, piece % 24
                value = acc_out[16 * q : 16 * q + 16, 128 * tile : 128 * tile + 128].astype(bf16)
            else:
                value = jnp.zeros((16, 128), bf16)
            bundle[piece // 5, place : place + 16, :] = value

        def lay(start, row, tiles):
            for t in range(tiles):
                small[start + t : start + t + 1, :] = acc_small[
                    row : row + 1, 128 * t : 128 * t + 128
                ]

        for j in range(4):
            lay(64 + 5 * j, 5 + j, 5)
        lay(84, 4, 5)
        lay(89, 9, 6)
        lay(95, 0, 3)
        lay(98, 1, 3)
        lay(101, 2, 1)
        lay(102, 3, 1)
        for r in range(32):
            bundle[r, 272:288, :] = jnp.concatenate(
                [small[4 * r : 4 * r + 4, :], jnp.zeros((12, 128), f32)], axis=0
            ).astype(bf16)


def assemble_kernel(me, parts, grad_in, grad_out, small):
    g = me[0]
    for q in range(4):
        rows = slice(48 * q, 48 * q + 48)
        for tile in range(8):
            r = 4 * tile + q
            pieces = [parts[r, 48 * d : 48 * d + 48, :].astype(f32) for d in range(4)]
            if tile < 6:
                start = (tile // 3) * DI + (tile % 3) * 128
                for d in range(4):
                    column = pl.multiple_of(start + (g ^ d) * XW, 128)
                    grad_in[rows, pl.ds(column, 128)] = pieces[d]
            else:
                column = 2 * DI + (tile - 6) * 128
                grad_in[rows, column : column + 128] = (pieces[0] + pieces[1]) + (
                    pieces[2] + pieces[3]
                )
    grad_in[:, 2 * DI + 256 :] = jnp.zeros((192, NH), f32)
    for piece in range(144):
        tile, q = piece // 24, piece % 24
        place = 192 + 16 * (piece % 5)
        grad_out[16 * q : 16 * q + 16, 128 * tile : 128 * tile + 128] = parts[
            piece // 5, place : place + 16, :
        ].astype(f32)
    for r in range(32):
        values = parts[r, 272:288, :].astype(f32)
        for d in range(4):
            small[d, 4 * r : 4 * r + 4, :] = values[4 * d : 4 * d + 4, :]


def whole(shape):
    zeros = (0,) * len(shape)
    return pl.BlockSpec(shape, lambda i: zeros)


def blocked(shape, place):
    zeros = (0,) * (len(shape) - 1)
    return pl.BlockSpec(shape, lambda i: (place(i),) + zeros)


scalar_spec = pl.BlockSpec(memory_space=pltpu.SMEM)
params = pltpu.CompilerParams(
    vmem_limit_bytes=vmem_bytes, dimension_semantics=("arbitrary",)
)


def among(value, d):
    return lax.ppermute(value, "group", [(i, i ^ d) for i in range(4)])


def local(
    tokens, segments, cotangent, gain_in, w_in, kernel, conv_bias, dt_bias, a_log, skip_gain,
    gain_out, w_out,
):
    reps = lax.axis_size("rep")
    g = lax.axis_index("group")
    me = g.astype(jnp.int32).reshape(1)
    tok = tokens.reshape(ROWS, D)
    cot = cotangent.reshape(ROWS, D)

    t2 = among(tok, 2)
    t1 = among(tok, 1)
    columns = []
    for k in range(4):
        columns.append(
            jnp.concatenate(
                [
                    w_in[:, k * XW : (k + 1) * XW],
                    w_in[:, DI + k * XW : DI + (k + 1) * XW],
                    w_in[:, 2 * DI : DI + CW],
                    w_in[:, DI + CW + k * HL : DI + CW + (k + 1) * HL],
                    jnp.zeros((192, 128 - HL), bf16),
                ],
                axis=1,
            )
        )
    stacked = jnp.stack(columns)

    def share(d):
        return lax.dynamic_index_in_dim(stacked, g ^ d, 0, keepdims=False)

    def across(value, d):
        pairs = [(i * reps + r, (i ^ d) * reps + (r ^ 1)) for r in range(reps) for i in range(4)]
        return lax.ppermute(value, ("group", "rep"), pairs)

    w2, w3 = across(share(2), 2), across(share(3), 3)
    w1 = among(share(1), 1)
    w0 = share(0)
    c2 = among(cot, 2)
    c1 = among(cot, 1)
    t3 = among(t2, 1)
    c3 = among(c2, 1)

    packed = jnp.concatenate(
        [
            kernel.astype(f32).reshape(-1),
            conv_bias.astype(f32),
            gain_in.astype(f32),
            segments.reshape(-1).astype(f32),
        ]
    )
    gathered = lax.all_gather(packed, "group")
    taps_all = jnp.moveaxis(gathered[:, :CW].reshape(4, 4, 448), 0, 1).reshape(4, CW)
    both_all = jnp.concatenate([taps_all, gathered[:, CW : CW + 448].reshape(1, CW)], axis=0)
    both = jnp.concatenate(
        [lax.dynamic_slice_in_dim(both_all, g * XW, XW, axis=1), both_all[:, DI:]], axis=1
    )
    taps = jnp.concatenate([both[:4], jnp.zeros((4, CL), f32)], axis=0)
    bias = both[4:5]
    gain_in_all = gathered[:, CW + 448 : CW + 640].reshape(1, D)
    seg = gathered[:, CW + 640 :].reshape(-1)
    length = seg.shape[0]
    spans = length // SPAN
    before = jnp.concatenate([jnp.full((3,), -1.0, f32), seg])
    after = jnp.concatenate([seg, jnp.full((3,), -2.0, f32)])
    seg_rows = seg.reshape(spans, SPAN)
    ends = seg_rows[:, SPAN - 1 :]
    starts = jnp.concatenate([jnp.full((1, 1), -1.0, f32), ends[:-1]], axis=0)
    features = [seg_rows]
    features += [
        (before[3 - lag : 3 - lag + length] == seg).astype(f32).reshape(spans, SPAN)
        for lag in range(1, 4)
    ]
    features += [(seg_rows == starts).astype(f32), (seg_rows == ends).astype(f32)]
    features += [
        (after[lag : lag + length] == seg).astype(f32).reshape(spans, SPAN) for lag in range(1, 4)
    ]
    features += [jnp.zeros((spans, SPAN), f32)] * 7
    pos = jnp.stack(features, axis=1)

    dtb = jnp.pad(dt_bias.astype(f32), (0, 128 - HL)).reshape(1, 128)
    rate = jnp.pad(-jnp.exp(a_log.astype(f32)), (0, 128 - HL)).reshape(1, 128)
    skip = jnp.repeat(skip_gain.astype(f32), HP).reshape(1, XW)
    gain_o = gain_out.astype(f32).reshape(1, XW)

    blocks = 4
    part = whole((ROWS, D))

    def up(i):
        return i

    out_shapes = (
        jax.ShapeDtypeStruct((D, PW), bf16),
        jax.ShapeDtypeStruct((length, D), bf16),
        jax.ShapeDtypeStruct((length, PW), bf16),
        jax.ShapeDtypeStruct((length, CL), f32),
        jax.ShapeDtypeStruct((spans, NS, XW), f32),
        jax.ShapeDtypeStruct((length, XW), f32),
        jax.ShapeDtypeStruct((length, XW), f32),
        jax.ShapeDtypeStruct((spans, 8, SPAN), f32),
    ) + (jax.ShapeDtypeStruct((ROWS, D), bf16),) * 4
    (w_full, normed, proj, v_rows, states, y_rows, dno, stats, o0, o1, o2, o3) = pl.pallas_call(
        forward_kernel,
        grid=(blocks,),
        in_specs=[scalar_spec]
        + [part] * 8
        + [whole((192, PW))] * 4
        + [blocked((2, 16, SPAN), up)]
        + [
            whole((1, D)), whole((8, CL)), whole((1, CL)), whole((1, 128)), whole((1, 128)),
            whole((1, XW)), whole((1, XW)), whole((XW, D)),
        ],
        out_specs=[
            whole((D, PW)),
            blocked((ROWS, D), up),
            blocked((ROWS, PW), up),
            blocked((ROWS, CL), up),
            blocked((2, NS, XW), up),
            blocked((ROWS, XW), up),
            blocked((ROWS, XW), up),
            blocked((2, 8, SPAN), up),
        ]
        + [part] * 4,
        out_shape=out_shapes,
        scratch_shapes=[
            pltpu.VMEM((ROWS, D), bf16),
            pltpu.VMEM((ROWS, D), bf16),
            pltpu.VMEM((NS, XW), f32),
            pltpu.VMEM((ROWS + 8, CL), f32),
        ],
        compiler_params=params,
        name="forward",
    )(
        me, tok, t1, t2, t3, cot, c1, c2, c3, w0, w1, w2, w3,
        pos, gain_in_all, taps, bias, dtb, rate, skip, gain_o, w_out,
    )

    stats = lax.psum(stats, "group")
    branches = [o0, among(o1, 1), among(o2, 2), among(o3, 3)]

    def down(i):
        return blocks - 1 - i

    ones = jnp.asarray(np.arange(XW)[:, None] // HP == np.arange(128)[None, :], bf16)
    bundle, n0, n1, n2, n3 = pl.pallas_call(
        backward_kernel,
        grid=(blocks,),
        in_specs=[scalar_spec]
        + [part] * 4
        + [
            whole((D, PW)),
            blocked((ROWS, D), down),
            blocked((ROWS, PW), down),
            blocked((ROWS, CL), down),
            blocked((2, NS, XW), down),
            blocked((ROWS, XW), down),
            blocked((ROWS, XW), down),
            blocked((2, 8, SPAN), down),
            blocked((2, 16, SPAN), down),
            whole((8, CL)), whole((1, 128)), whole((1, 128)), whole((1, XW)), whole((1, XW)),
            whole((XW, 128)),
        ],
        out_specs=[whole((32, CHUNK, 128))] + [part] * 4,
        out_shape=(jax.ShapeDtypeStruct((32, CHUNK, 128), bf16),)
        + (jax.ShapeDtypeStruct((ROWS, D), bf16),) * 4,
        scratch_shapes=[
            pltpu.VMEM((ROWS, D), bf16),
            pltpu.VMEM((NS, XW), f32),
            pltpu.VMEM((ROWS + 8, CL), f32),
            pltpu.VMEM((ROWS, PW), bf16),
            pltpu.VMEM((ROWS, XW), bf16),
            pltpu.VMEM((D, XW + CL), f32),
            pltpu.VMEM((8, D), f32),
            pltpu.VMEM((XW, D), f32),
            pltpu.VMEM((16, D), f32),
            pltpu.VMEM((128, 128), f32),
        ],
        compiler_params=params,
        name="backward",
    )(
        me, cot, c1, c2, c3, w_full, normed, proj, v_rows, states, y_rows, dno, stats,
        pos, taps, dtb, rate, skip, gain_o, ones,
    )

    d_parts = [n0, among(n1, 1), among(n2, 2), among(n3, 3)]
    x = tok.astype(f32)
    squares = lax.dynamic_slice_in_dim(stats[:, 0, :].reshape(-1), g * ROWS, ROWS, axis=0)
    rms_out = lax.rsqrt(squares * (1.0 / DI) + epsilon)[:, None]
    branch = sum(value.astype(f32) for value in branches)
    layer_out = (x + rms_out * branch).astype(bf16).reshape(tokens.shape)
    d_normed = sum(value.astype(f32) for value in d_parts)
    rms_in = lax.rsqrt(jnp.mean(x * x, axis=-1, keepdims=True) + epsilon)
    scaled = d_normed * gain_in_all
    grad_tokens = (
        cot.astype(f32)
        + rms_in * scaled
        - x * (rms_in * rms_in * rms_in * jnp.mean(x * scaled, axis=-1, keepdims=True))
    ).reshape(tokens.shape)

    received = lax.all_to_all(bundle, "rep", 0, 0, tiled=True)
    reduced = jnp.sum(received.astype(f32), axis=0).astype(bf16)
    for_members = reduced[:192].reshape(4, 48, 128)
    small_part = reduced[272:276]
    pieces, smalls = [], []
    for d in range(4):
        piece = lax.dynamic_index_in_dim(for_members, g ^ d, 0, keepdims=False)
        both = jnp.concatenate([piece, small_part], axis=0)
        both = both if d == 0 else among(both, d)
        pieces.append(both[:48])
        smalls.append(both[48:])
    payload = jnp.concatenate(pieces + [reduced[192:272]] + smalls, axis=0)
    parts = lax.all_to_all(
        jnp.broadcast_to(payload[None], (reps, CHUNK, 128)), "rep", 0, 0, tiled=True
    )
    grad_w_in, grad_w_out, small = pl.pallas_call(
        assemble_kernel,
        in_specs=[scalar_spec, pl.BlockSpec(memory_space=pltpu.VMEM)],
        out_specs=[pl.BlockSpec(memory_space=pltpu.VMEM)] * 3,
        out_shape=(
            jax.ShapeDtypeStruct((192, 3352), f32),
            jax.ShapeDtypeStruct((XW, D), f32),
            jax.ShapeDtypeStruct((4, 128, 128), f32),
        ),
        compiler_params=pltpu.CompilerParams(vmem_limit_bytes=vmem_bytes),
        name="assemble",
    )(me, parts)
    own = small[0]
    ordered = small[jnp.arange(4) ^ g]
    mine = lax.dynamic_slice_in_dim(ordered, g * 16, 16, axis=1)[:, : 2 * HL]
    dt_grad = mine.reshape(NH, 256)[:, :192].T
    grad_w_in = lax.dynamic_update_slice(grad_w_in, dt_grad, (0, DI + CW))
    conv = ordered[:, 64:89].reshape(4, 5, CL)
    conv_x = jnp.moveaxis(conv[:, :, :XW], 0, 1).reshape(5, DI)
    conv_all = jnp.concatenate([conv_x, jnp.sum(conv[:, :, XW:], axis=0)], axis=1)
    conv_mine = lax.dynamic_slice_in_dim(conv_all, g * 448, 448, axis=1)
    gain_in_sum = jnp.sum(small[:, 89:95], axis=0).reshape(-1) / gain_in_all[0]
    grad_gain_in = lax.dynamic_slice_in_dim(gain_in_sum, g * 192, 192, axis=0)
    grad_gain_out = own[95:98].reshape(-1)
    grad_skip = jnp.sum(own[98:101].reshape(HL, HP), axis=1)
    return (
        layer_out,
        grad_tokens,
        grad_gain_in,
        grad_w_in,
        conv_mine[:4],
        conv_mine[4],
        own[101, :HL],
        own[102, :HL],
        grad_skip,
        grad_gain_out,
        grad_w_out,
    )


def solution(mesh):
    sequences = P("rep", "group", None)
    vector = P("group")
    matrix = P("group", None)
    return jax.shard_map(
        local,
        mesh=mesh,
        in_specs=(
            sequences, P("rep", "group"), sequences, vector, matrix, P(None, "group"),
            vector, vector, vector, vector, vector, matrix,
        ),
        out_specs=(
            sequences, sequences, vector, matrix, P(None, "group"), vector, vector, vector,
            vector, vector, matrix,
        ),
        check_vma=False,
    )
```

time: 1020 us -> 244 us (0.24)
  the two profiles are of different devices: /device:TPU:0 before, /device:TPU:1 now
where the time goes in v1:
time: 244 us; the launch traced here: 240 us
  waiting for transfers between devices  74.5 us (31%)
  blocking collectives  64.6 us (26%)
  Pallas kernels  48.3 us (20%)
  local copies, waits for them, and re-layouts  22.2 us (9%)
  starting transfers between devices  21.6 us (9%)
  other arithmetic  7.48 us (3%)
    ppermute x16, waiting for transfers between devices, among(): return lax.ppermute(value, 'group', [(i, i ^ d) for i in range(4)])  56.3 us
    all_to_all x1, blocking collectives, local(): received = lax.all_to_all(bundle, 'rep', 0, 0, tiled=True)  40.5 us
    pallas_call x1, Pallas kernels, local(): pl.pallas_call(backward_kernel, grid=(blocks,), in_specs=[scalar_spec] +...  27 us
    ppermute x2, waiting for transfers between devices, across(): return lax.ppermute(value, ('group', 'rep'), pairs)  18.2 us
    pallas_call x1, Pallas kernels, local(): pl.pallas_call(forward_kernel, grid=(blocks,), in_specs=[scalar_spec] + [...  17.4 us
    ppermute x16, starting transfers between devices, among(): return lax.ppermute(value, 'group', [(i, i ^ d) for i in range(4)])  14.1 us
    all_gather x1, blocking collectives, local(): gathered = lax.all_gather(packed, 'group')  12.6 us
    psum x1, blocking collectives, local(): stats = lax.psum(stats, 'group')  11.5 us
  transfers between devices with their start and end apart: 19, of which 8 were waited for; matrix products, arithmetic and copies ran while one was open for 7% of the time, Pallas kernels for 0%

profile of v1, /device:TPU:1, one launch (start us, length us, event | category | flops | bytes accessed | tf_op | source)
XLA Modules:
  0.0 239.7 jit_solution(9378934762503121956)
XLA Ops:
  0.7 2.2 collective-permute-start.4
  2.9 1.0 collective-permute-start.3
  4.2 2.1 fusion.11
  6.5 1.2 concatenate.54
  8.4 1.1 dynamic-slice_bitcast_fusion
  9.9 12.6 %all-gather.1 = f32[4,1,2688]{2,1,0:T(1,128)S(1)} all-gather(f32[1,1,2688]{2,1,0:T(1,128)S(1)} %reshape.370), channel_id=2, replica_groups=mesh['group'=4,'rep'=32] {'group'}, dimensions={0}, use_global_device_ids=true | all-gather | bytes 53760 | tf_op jit(solution)/shard_map/all_gather | solution.py:457
  23.4 0.6 slice.243.bias
  24.0 0.7 reshape.337.gain_in
  24.8 0.6 reshape_reshape.7.skip
  25.4 0.6 reshape.360.gain_out
  26.0 0.6 concatenate.64.taps
  26.8 1.3 stack.33.pos
  28.1 2.9 %collective-permute-start.7 = (bf16[192,1152]{1,0:T(8,128)(2,1)S(1)}, bf16[192,1152]{1,0:T(8,128)(2,1)S(1)}, u32[]{:S(2)}, u32[]{:S(2)}) collective-permute-start(bf16[192,1152]{1,0:T(8,128)(2,1)S(1)} %get-tuple-element.54), channel_id=1, source_target_pairs={{0,65},{32,97},{64,1},{96,33},{1,64},{33,96},{65,0},{97,32},{2,67}... | collective-permute-start | bytes 1327112 | tf_op jit(solution)/shard_map/ppermute | solution.py:439
  31.7 0.5 pad_bitcast_fusion.rate
  32.8 8.6 %collective-permute-done.7.w2 = bf16[192,1152]{1,0:T(8,128)(2,1)S(1)} collective-permute-done((bf16[192,1152]{1,0:T(8,128)(2,1)S(1)}, bf16[192,1152]{1,0:T(8,128)(2,1)S(1)}, u32[]{:S(2)}, u32[]{:S(2)}) %collective-permute-start.7) | collective-permute-done | bytes 442400 | tf_op jit(solution)/shard_map/ppermute | solution.py:439
  41.4 9.5 %collective-permute-done.8.w3 = bf16[192,1152]{1,0:T(8,128)(2,1)S(1)} collective-permute-done((bf16[192,1152]{1,0:T(8,128)(2,1)S(1)}, bf16[192,1152]{1,0:T(8,128)(2,1)S(1)}, u32[]{:S(2)}, u32[]{:S(2)}) %collective-permute-start.8) | collective-permute-done | bytes 442400 | tf_op jit(solution)/shard_map/ppermute | solution.py:439
  51.0 0.7 copy-done.10
  52.0 17.4 %forward.1 = (bf16[768,1152]{1,0:T(8,128)(2,1)}, bf16[1024,768]{1,0:T(8,128)(2,1)}, bf16[1024,1152]{1,0:T(8,128)(2,1)}, f32[1024,640]{1,0:T(8,128)}, f32[8,128,3...) custom-call(s32[1]{0:T(128)} %bitcast.1.me, ...), custom_call_target="tpu_custom_call" | custom-call | tf_op jit(solution)/shard_map/forward/pallas_call | solution.py:507
  69.3 11.5 %psum.7.stats = f32[8,8,128]{2,1,0:T(8,128)} all-reduce(f32[8,8,128]{2,1,0:T(8,128)} %get-tuple-element.31), channel_id=1, replica_groups=mesh['group'=4,'rep'=32] {'group'}, use_global_device_ids=true, to_apply=%region_0.1 | all-reduce | flops 8192 | bytes 65536 | tf_op jit(solution)/shard_map/psum | solution.py:543
  80.8 27.0 %backward.1 = (bf16[32,288,128]{2,1,0:T(8,128)(2,1)}, bf16[256,768]{1,0:T(8,128)(2,1)}, bf16[256,768]{1,0:T(8,128)(2,1)}, bf16[256,768]{1,0:T(8,128)(2,1)}, bf16[256,768]{1,0:T(8,128)(2,1)}) custom-call(s32[1]{0:T(128)} %bitcast.1.me, bf16[256,768]{1,0:T(8,128)(2,1)} %bitcast.82, bf16[256,768]{1,0:T(8,128)(2,1)} %copy-done.6, bf16[256,768]{1,0:T(8,128)(2,1)} %copy-done.5, ...), custom_call_target="tpu_custom_call" | custom-call | tf_op jit(solution)/shard_map/backward/pallas_call | solution.py:550
  107.9 40.5 %all_to_all.10 = bf16[32,288,128]{2,1,0:T(8,128)(2,1)S(1)} all-to-all(bf16[32,288,128]{2,1,0:T(8,128)(2,1)} %get-tuple-element.47), channel_id=1, replica_groups=mesh['group'=4,'rep'=32] {'rep'}, dimensions={0} | all-to-all | bytes 4718592 | tf_op jit(solution)/shard_map/all_to_all | solution.py:605
  148.8 3.7 %collective-permute-start.15 = (bf16[52,128]{1,0:T(8,128)(2,1)S(1)}, bf16[52,128]{1,0:T(8,128)(2,1)S(1)}, u32[]{:S(2)}, u32[]{:S(2)}) collective-permute-start(bf16[52,128]{1,0:T(8,128)(2,1)S(1)} %get-tuple-element.95), channel_id=1, source_target_pairs={{0,32},{32,0},{64,96},{96,64},{1,33},{33,1},{65,97},{97,65},{2,34}... | collective-permute-start | bytes 39944 | tf_op jit(solution)/shard_map/ppermute | solution.py:403
  152.5 0.8 collective-permute-start.16
  153.3 0.9 collective-permute-start.17
  154.2 0.8 collective-permute-done.16
  155.0 1.4 collective-permute-done.17
  156.6 1.7 broadcast_in_dim.5
  158.3 4.4 %all-to-all-start.1 = ((bf16[32,288,128]{2,1,0:T(8,128)(2,1)}), bf16[32,288,128]{2,1,0:T(8,128)(2,1)S(1)}, u32[]{:S(2)}, u32[]{:S(2)}) async-start(bf16[32,288,128]{2,1,0:T(8,128)(2,1)} %broadcast_in_dim.5), calls=%async_computation.1 | async-start | bytes 4718592 | tf_op jit(solution)/shard_map/all_to_all | solution.py:617
  162.7 0.7 collective-permute-start.12
  163.7 1.5 collective-permute-start.14
  165.6 1.6 collective-permute-start.11
  167.3 30.3 %collective-permute-done.13 = bf16[256,768]{1,0:T(8,128)(2,1)} collective-permute-done((bf16[256,768]{1,0:T(8,128)(2,1)}, bf16[256,768]{1,0:T(8,128)(2,1)}, u32[]{:S(2)}, u32[]{:S(2)}) %collective-permute-start.13) | collective-permute-done | bytes 393248 | tf_op jit(solution)/shard_map/ppermute | solution.py:403
  197.6 9.3 %collective-permute-done.14 = bf16[256,768]{1,0:T(8,128)(2,1)} collective-permute-done((bf16[256,768]{1,0:T(8,128)(2,1)}, bf16[256,768]{1,0:T(8,128)(2,1)}, u32[]{:S(2)}, u32[]{:S(2)}) %collective-permute-start.14) | collective-permute-done | bytes 393248 | tf_op jit(solution)/shard_map/ppermute | solution.py:403
  206.9 1.6 fusion.1
  208.6 5.8 %collective-permute-done.10 = bf16[256,768]{1,0:T(8,128)(2,1)S(1)} collective-permute-done((bf16[256,768]{1,0:T(8,128)(2,1)}, bf16[256,768]{1,0:T(8,128)(2,1)S(1)}, u32[]{:S(2)}, u32[]{:S(2)}) %collective-permute-start.10) | collective-permute-done | bytes 393248 | tf_op jit(solution)/shard_map/ppermute | solution.py:403
  214.3 8.7 %collective-permute-done.11 = bf16[256,768]{1,0:T(8,128)(2,1)S(1)} collective-permute-done((bf16[256,768]{1,0:T(8,128)(2,1)}, bf16[256,768]{1,0:T(8,128)(2,1)S(1)}, u32[]{:S(2)}, u32[]{:S(2)}) %collective-permute-start.11) | collective-permute-done | bytes 393248 | tf_op jit(solution)/shard_map/ppermute | solution.py:403
  223.1 2.9 %fusion.4 = (f32[1,256,768]{2,1,0:T(8,128)}, bf16[1,256,768]{2,1,0:T(8,128)(2,1)}) fusion(f32[256]{0:T(256)S(1)} %get-tuple-element.97, f32[256]{0:T(256)S(1)} %get-tuple-element.96, f32[768]{0:T(1024)S(1)} %mul.93, bf16[256,768]{1,0:T(8,128)(2,1)} %collective-permute-done.14, bf16[256,768]{1,0:T(8,128)(2,1)} %collective-permute-done.13, ...), kind=kLoop, calls=%fused_computation.10 | loop fusion | flops 4718592 | bytes 5117952 | tf_op jit(solution)/shard_map/reshape | solution.py:603
  226.0 1.4 copy-done
  227.4 3.9 %assemble.1 = (f32[192,3352]{1,0:T(8,128)}, f32[384,768]{1,0:T(8,128)}, f32[4,128,128]{2,1,0:T(8,128)}) custom-call(s32[1]{0:T(128)} %bitcast.1.me, bf16[32,288,128]{2,1,0:T(8,128)(2,1)} %copy-done), custom_call_target="tpu_custom_call" | custom-call | tf_op jit(solution)/shard_map/assemble/pallas_call | solution.py:620
  231.3 1.5 gather_fusion
  233.0 0.6 slice.258
  233.6 0.6 slice.259
  234.1 0.8 slice_bitcast_fusion
  235.0 0.7 slice_reduce_fusion.1
  235.7 1.3 slice_bitcast_fusion.1
  237.8 0.6 reduce_sum.62
  238.4 0.6 bitcast_dynamic-update-slice_fusion
  239.1 0.6 dynamic_slice.51
  (133 shorter events, 6.5 us)
Async XLA Ops:
  0.6 5.7 %copy-start.3 = (bf16[192,3352]{1,0:T(8,128)(2,1)S(1)}, bf16[192,3352]{1,0:T(8,128)(2,1)}, u32[]{:S(2)}) copy-start(bf16[192,3352]{1,0:T(8,128)(2,1)} %param.17) | copy-start | bytes 3861508
  0.7 27.4 %collective-permute-start.4 = (bf16[256,768]{1,0:T(8,128)(2,1)}, bf16[256,768]{1,0:T(8,128)(2,1)S(1)}, u32[]{:S(2)}, u32[]{:S(2)}) collective-permute-start(bf16[256,768]{1,0:T(8,128)(2,1)} %bitcast.79), channel_id=1, source_target_pairs={{0,64},{32,96},{64,0},{96,32},{1,65},{33,97},{65,1},{97,33},{2,66}... | collective-permute-start | bytes 1179656 | tf_op jit(solution)/shard_map/ppermute | solution.py:403
  2.9 28.1 %collective-permute-start.3 = (bf16[256,768]{1,0:T(8,128)(2,1)}, bf16[256,768]{1,0:T(8,128)(2,1)S(1)}, u32[]{:S(2)}, u32[]{:S(2)}) collective-permute-start(bf16[256,768]{1,0:T(8,128)(2,1)} %bitcast.80), channel_id=1, source_target_pairs={{0,32},{32,0},{64,96},{96,64},{1,33},{33,1},{65,97},{97,65},{2,34}... | collective-permute-start | bytes 1179656 | tf_op jit(solution)/shard_map/ppermute | solution.py:403
  3.8 27.4 %collective-permute-start.1 = (bf16[256,768]{1,0:T(8,128)(2,1)}, bf16[256,768]{1,0:T(8,128)(2,1)}, u32[]{:S(2)}, u32[]{:S(2)}) collective-permute-start(bf16[256,768]{1,0:T(8,128)(2,1)} %bitcast.76), channel_id=1, source_target_pairs={{0,64},{32,96},{64,0},{96,32},{1,65},{33,97},{65,1},{97,33},{2,66}... | collective-permute-start | bytes 1179656 | tf_op jit(solution)/shard_map/ppermute | solution.py:403
  3.9 27.7 %collective-permute-start = (bf16[256,768]{1,0:T(8,128)(2,1)}, bf16[256,768]{1,0:T(8,128)(2,1)}, u32[]{:S(2)}, u32[]{:S(2)}) collective-permute-start(bf16[256,768]{1,0:T(8,128)(2,1)} %bitcast.77), channel_id=1, source_target_pairs={{0,32},{32,0},{64,96},{96,64},{1,33},{33,1},{65,97},{97,65},{2,34}... | collective-permute-start | bytes 1179656 | tf_op jit(solution)/shard_map/ppermute | solution.py:403
  6.3 1.5 slice-start
  6.4 1.5 slice-start.1
  8.4 1.4 copy-start.13
  8.4 1.5 copy-start.15
  8.4 1.4 copy-start.14
  8.4 1.4 copy-start.17
  8.4 16.3 %copy-start.18 = (bf16[6]{0:T(256)(128)(2,1)S(1)}, bf16[6]{0:T(256)(128)(2,1)}, u32[]{:S(2)}) copy-start(bf16[6]{0:T(256)(128)(2,1)} %param.22) | copy-start | bytes 40
  8.4 17.0 %copy-start.16 = (bf16[384]{0:T(512)(128)(2,1)S(1)}, bf16[384]{0:T(512)(128)(2,1)}, u32[]{:S(2)}) copy-start(bf16[384]{0:T(512)(128)(2,1)} %param.23) | copy-start | bytes 2308
  8.4 23.3 %copy-start.19 = (bf16[6]{0:T(256)(128)(2,1)S(1)}, bf16[6]{0:T(256)(128)(2,1)}, u32[]{:S(2)}) copy-start(bf16[6]{0:T(256)(128)(2,1)} %param.21) | copy-start | bytes 40
  8.4 23.8 %copy-start.20 = (bf16[6]{0:T(256)(128)(2,1)S(1)}, bf16[6]{0:T(256)(128)(2,1)}, u32[]{:S(2)}) copy-start(bf16[6]{0:T(256)(128)(2,1)} %param.20) | copy-start | bytes 40
  9.5 23.2 %collective-permute-start.6 = (bf16[192,1152]{1,0:T(8,128)(2,1)}, bf16[192,1152]{1,0:T(8,128)(2,1)S(1)}, u32[]{:S(2)}, u32[]{:S(2)}) collective-permute-start(bf16[192,1152]{1,0:T(8,128)(2,1)} %get-tuple-element.55), channel_id=1, source_target_pairs={{0,32},{32,0},{64,96},{96,64},{1,33},{33,1},{65,97},{97,65},{2,34}... | collective-permute-start | bytes 1327112 | tf_op jit(solution)/shard_map/ppermute | solution.py:403
  28.1 22.8 %copy-start.5 = (bf16[256,768]{1,0:T(8,128)(2,1)}, bf16[256,768]{1,0:T(8,128)(2,1)S(1)}, u32[]{:S(2)}) copy-start(bf16[256,768]{1,0:T(8,128)(2,1)S(1)} %collective-permute-done.4.c2) | copy-start | bytes 1179652
  28.1 13.3 %collective-permute-start.7 = (bf16[192,1152]{1,0:T(8,128)(2,1)S(1)}, bf16[192,1152]{1,0:T(8,128)(2,1)S(1)}, u32[]{:S(2)}, u32[]{:S(2)}) collective-permute-start(bf16[192,1152]{1,0:T(8,128)(2,1)S(1)} %get-tuple-element.54), channel_id=1, source_target_pairs={{0,65},{32,97},{64,1},{96,33},{1,64},{33,96},{65,0},{97,32},{2,67}... | collective-permute-start | bytes 1327112 | tf_op jit(solution)/shard_map/ppermute | solution.py:439
  31.0 19.9 %copy-start.6 = (bf16[256,768]{1,0:T(8,128)(2,1)}, bf16[256,768]{1,0:T(8,128)(2,1)S(1)}, u32[]{:S(2)}) copy-start(bf16[256,768]{1,0:T(8,128)(2,1)S(1)} %collective-permute-done.3.c1) | copy-start | bytes 1179652
  31.0 19.9 %collective-permute-start.8 = (bf16[192,1152]{1,0:T(8,128)(2,1)S(1)}, bf16[192,1152]{1,0:T(8,128)(2,1)S(1)}, u32[]{:S(2)}, u32[]{:S(2)}) collective-permute-start(bf16[192,1152]{1,0:T(8,128)(2,1)S(1)} %get-tuple-element.53), channel_id=1, source_target_pairs={{0,97},{32,65},{64,33},{96,1},{1,96},{33,64},{65,32},{97,0},{2,99}... | collective-permute-start | bytes 1327112 | tf_op jit(solution)/shard_map/ppermute | solution.py:439
  31.2 19.7 %collective-permute-start.5 = (bf16[256,768]{1,0:T(8,128)(2,1)S(1)}, bf16[256,768]{1,0:T(8,128)(2,1)S(1)}, u32[]{:S(2)}, u32[]{:S(2)}) collective-permute-start(bf16[256,768]{1,0:T(8,128)(2,1)S(1)} %collective-permute-done.4.c2), channel_id=1, source_target_pairs={{0,32},{32,0},{64,96},{96,64},{1,33},{33,1},{65,97},{97,65},{2,34}... | collective-permute-start | bytes 1179656 | tf_op jit(solution)/shard_map/ppermute | solution.py:403
  31.6 19.3 %collective-permute-start.2 = (bf16[256,768]{1,0:T(8,128)(2,1)}, bf16[256,768]{1,0:T(8,128)(2,1)S(1)}, u32[]{:S(2)}, u32[]{:S(2)}) collective-permute-start(bf16[256,768]{1,0:T(8,128)(2,1)} %collective-permute-done.1.t2), channel_id=1, source_target_pairs={{0,32},{32,0},{64,96},{96,64},{1,33},{33,1},{65,97},{97,65},{2,34}... | collective-permute-start | bytes 1179656 | tf_op jit(solution)/shard_map/ppermute | solution.py:403
  32.7 18.2 %copy-start.8 = (bf16[192,1152]{1,0:T(8,128)(2,1)}, bf16[192,1152]{1,0:T(8,128)(2,1)S(1)}, u32[]{:S(2)}) copy-start(bf16[192,1152]{1,0:T(8,128)(2,1)S(1)} %collective-permute-done.6.w1) | copy-start | bytes 1327108
  41.4 9.6 %copy-start.9 = (bf16[192,1152]{1,0:T(8,128)(2,1)}, bf16[192,1152]{1,0:T(8,128)(2,1)S(1)}, u32[]{:S(2)}) copy-start(bf16[192,1152]{1,0:T(8,128)(2,1)S(1)} %collective-permute-done.7.w2) | copy-start | bytes 1327108
  50.9 0.8 copy-start.10
  50.9 0.9 copy-start.7
  50.9 1.0 copy-start.12
  148.8 5.4 %collective-permute-start.15 = (bf16[52,128]{1,0:T(8,128)(2,1)S(1)}, bf16[52,128]{1,0:T(8,128)(2,1)S(1)}, u32[]{:S(2)}, u32[]{:S(2)}) collective-permute-start(bf16[52,128]{1,0:T(8,128)(2,1)S(1)} %get-tuple-element.95), channel_id=1, source_target_pairs={{0,32},{32,0},{64,96},{96,64},{1,33},{33,1},{65,97},{97,65},{2,34}... | collective-permute-start | bytes 39944 | tf_op jit(solution)/shard_map/ppermute | solution.py:403
  152.5 2.6 %collective-permute-start.16 = (bf16[52,128]{1,0:T(8,128)(2,1)S(1)}, bf16[52,128]{1,0:T(8,128)(2,1)S(1)}, u32[]{:S(2)}, u32[]{:S(2)}) collective-permute-start(bf16[52,128]{1,0:T(8,128)(2,1)S(1)} %get-tuple-element.94), channel_id=1, source_target_pairs={{0,64},{32,96},{64,0},{96,32},{1,65},{33,97},{65,1},{97,33},{2,66}... | collective-permute-start | bytes 39944 | tf_op jit(solution)/shard_map/ppermute | solution.py:403
  153.3 3.1 %collective-permute-start.17 = (bf16[52,128]{1,0:T(8,128)(2,1)S(1)}, bf16[52,128]{1,0:T(8,128)(2,1)S(1)}, u32[]{:S(2)}, u32[]{:S(2)}) collective-permute-start(bf16[52,128]{1,0:T(8,128)(2,1)S(1)} %get-tuple-element.93), channel_id=1, source_target_pairs={{0,96},{32,64},{64,32},{96,0},{1,97},{33,65},{65,33},{97,1},{2,98}... | collective-permute-start | bytes 39944 | tf_op jit(solution)/shard_map/ppermute | solution.py:403
  158.3 8.9 %slice-start.2 = ((f32[8,8,128]{2,1,0:T(8,128)}), f32[8,1,128]{2,1,0:T(1,128)S(1)}, s32[]{:S(2)}) async-start(f32[8,8,128]{2,1,0:T(8,128)} %psum.7.stats), calls=%async_computation.4 | async-start | bytes 8192 | tf_op jit(solution)/shard_map/slice | solution.py:592
  158.3 48.6 %copy-start.1 = (bf16[1,256,768]{2,1,0:T(8,128)(2,1)S(1)}, bf16[1,256,768]{2,1,0:T(8,128)(2,1)}, u32[]{:S(2)}) copy-start(bf16[1,256,768]{2,1,0:T(8,128)(2,1)} %param.13) | copy-start | bytes 1179652
  158.3 48.6 %copy-start.4 = (bf16[256,768]{1,0:T(8,128)(2,1)S(1)}, bf16[256,768]{1,0:T(8,128)(2,1)}, u32[]{:S(2)}) copy-start(bf16[256,768]{1,0:T(8,128)(2,1)} %get-tuple-element.43) | copy-start | bytes 1179652
  158.3 67.7 %all-to-all-start.1 = ((bf16[32,288,128]{2,1,0:T(8,128)(2,1)}), bf16[32,288,128]{2,1,0:T(8,128)(2,1)S(1)}, u32[]{:S(2)}, u32[]{:S(2)}) async-start(bf16[32,288,128]{2,1,0:T(8,128)(2,1)} %broadcast_in_dim.5), calls=%async_computation.1 | async-start | bytes 4718592 | tf_op jit(solution)/shard_map/all_to_all | solution.py:617
  162.7 60.3 %copy-start.2 = (bf16[1,256,768]{2,1,0:T(8,128)(2,1)S(1)}, bf16[1,256,768]{2,1,0:T(8,128)(2,1)}, u32[]{:S(2)}) copy-start(bf16[1,256,768]{2,1,0:T(8,128)(2,1)} %param.15) | copy-start | bytes 1179652
  162.7 4.5 %collective-permute-start.12 = (bf16[256,768]{1,0:T(8,128)(2,1)}, bf16[256,768]{1,0:T(8,128)(2,1)}, u32[]{:S(2)}, u32[]{:S(2)}) collective-permute-start(bf16[256,768]{1,0:T(8,128)(2,1)} %get-tuple-element.44), channel_id=1, source_target_pairs={{0,32},{32,0},{64,96},{96,64},{1,33},{33,1},{65,97},{97,65},{2,34}... | collective-permute-start | bytes 1179656 | tf_op jit(solution)/shard_map/ppermute | solution.py:403
  163.5 34.1 %collective-permute-start.13 = (bf16[256,768]{1,0:T(8,128)(2,1)}, bf16[256,768]{1,0:T(8,128)(2,1)}, u32[]{:S(2)}, u32[]{:S(2)}) collective-permute-start(bf16[256,768]{1,0:T(8,128)(2,1)} %get-tuple-element.45), channel_id=1, source_target_pairs={{0,64},{32,96},{64,0},{96,32},{1,65},{33,97},{65,1},{97,33},{2,66}... | collective-permute-start | bytes 1179656 | tf_op jit(solution)/shard_map/ppermute | solution.py:403
  163.7 43.2 %collective-permute-start.14 = (bf16[256,768]{1,0:T(8,128)(2,1)}, bf16[256,768]{1,0:T(8,128)(2,1)}, u32[]{:S(2)}, u32[]{:S(2)}) collective-permute-start(bf16[256,768]{1,0:T(8,128)(2,1)} %get-tuple-element.46), channel_id=1, source_target_pairs={{0,96},{32,64},{64,32},{96,0},{1,97},{33,65},{65,33},{97,1},{2,98}... | collective-permute-start | bytes 1179656 | tf_op jit(solution)/shard_map/ppermute | solution.py:403
  165.3 57.8 %copy-start.11 = (bf16[256,768]{1,0:T(8,128)(2,1)S(1)}, bf16[256,768]{1,0:T(8,128)(2,1)}, u32[]{:S(2)}) copy-start(bf16[256,768]{1,0:T(8,128)(2,1)} %get-tuple-element.32) | copy-start | bytes 1179652
  165.3 49.1 %collective-permute-start.10 = (bf16[256,768]{1,0:T(8,128)(2,1)}, bf16[256,768]{1,0:T(8,128)(2,1)S(1)}, u32[]{:S(2)}, u32[]{:S(2)}) collective-permute-start(bf16[256,768]{1,0:T(8,128)(2,1)} %get-tuple-element.34), channel_id=1, source_target_pairs={{0,64},{32,96},{64,0},{96,32},{1,65},{33,97},{65,1},{97,33},{2,66}... | collective-permute-start | bytes 1179656 | tf_op jit(solution)/shard_map/ppermute | solution.py:403
  165.6 57.5 %collective-permute-start.11 = (bf16[256,768]{1,0:T(8,128)(2,1)}, bf16[256,768]{1,0:T(8,128)(2,1)S(1)}, u32[]{:S(2)}, u32[]{:S(2)}) collective-permute-start(bf16[256,768]{1,0:T(8,128)(2,1)} %get-tuple-element.35), channel_id=1, source_target_pairs={{0,96},{32,64},{64,32},{96,0},{1,97},{33,65},{65,33},{97,1},{2,98}... | collective-permute-start | bytes 1179656 | tf_op jit(solution)/shard_map/ppermute | solution.py:403
  167.2 55.8 %collective-permute-start.9 = (bf16[256,768]{1,0:T(8,128)(2,1)}, bf16[256,768]{1,0:T(8,128)(2,1)S(1)}, u32[]{:S(2)}, u32[]{:S(2)}) collective-permute-start(bf16[256,768]{1,0:T(8,128)(2,1)} %get-tuple-element.33), channel_id=1, source_target_pairs={{0,32},{32,0},{64,96},{96,64},{1,33},{33,1},{65,97},{97,65},{2,34}... | collective-permute-start | bytes 1179656 | tf_op jit(solution)/shard_map/ppermute | solution.py:403
  226.0 1.4 copy-start

commit v2 on v1

v2 whole, which is shorter than its diff:
```python
import jax
import jax.numpy as jnp
import numpy as np
from jax import lax
from jax.experimental import pallas as pl
from jax.experimental.pallas import tpu as pltpu
from jax.sharding import PartitionSpec as P

D = 768
NH = 24
HP = 64
NS = 128
DI = 1536
CW = 1792
SPAN = 128
ROWS = 256
HL = 6
XW = HL * HP
CL = XW + 2 * NS
PW = XW + CL + 128
epsilon = 1e-05
f32 = jnp.float32
bf16 = jnp.bfloat16
NN = ((1,), (0,))
NT = ((1,), (1,))
TN = ((0,), (0,))
vmem_bytes = 56 * 1024 * 1024


def mm(a, b, dims):
    return lax.dot_general(
        a.astype(bf16), b.astype(bf16), (dims, ((), ())), preferred_element_type=f32
    )


def mm_exact(a, b, dims):
    return lax.dot_general(
        a, b, (dims, ((), ())), preferred_element_type=f32, precision=lax.Precision.HIGHEST
    )


def to_columns(rows):
    short = SPAN - rows.shape[0]
    return jnp.concatenate([rows, jnp.zeros((short, SPAN), f32)], axis=0).T


def softplus(v):
    return jnp.maximum(v, 0.0) + jnp.log1p(jnp.exp(-jnp.abs(v)))


def over_lanes(column):
    return jnp.broadcast_to(column, (SPAN, SPAN))


def span_decays(dt_rows, rate, pos_rows):
    row_at = lax.broadcasted_iota(jnp.int32, (SPAN, SPAN), 0)
    lane_at = lax.broadcasted_iota(jnp.int32, (SPAN, SPAN), 1)
    pos = to_columns(pos_rows)
    step = softplus(dt_rows)
    cum = mm_exact((row_at >= lane_at).astype(f32), step * rate, NN)
    cum_t = cum.T
    step_t = step.T
    allowed = (over_lanes(pos[:, 0:1]) == pos_rows[0:1, :]) & (row_at >= lane_at)
    low = lane_at < HP
    cums = [over_lanes(cum[:, h : h + 1]) for h in range(HL)]
    linked = pos[:, 4:5]
    tail = pos[:, 5:6]
    carried, tails = [], []
    for p in range(HL // 2):
        both = jnp.where(low, cums[2 * p], cums[2 * p + 1])
        steps = jnp.where(
            low, over_lanes(step[:, 2 * p : 2 * p + 1]), over_lanes(step[:, 2 * p + 1 : 2 * p + 2])
        )
        carried.append(jnp.exp(both) * linked)
        tails.append(jnp.exp(both[SPAN - 1 :, :] - both) * tail * steps)

    def decay(h):
        return jnp.where(allowed, jnp.exp(jnp.minimum(cums[h] - cum_t[h : h + 1, :], 0.0)), 0.0)

    return pos, step, step_t, cum, decay, carried, tails, low


def pick(index, sources, target):
    for d, source in enumerate(sources):

        @pl.when(index == d)
        def _(source=source):
            target[...] = source[...]


def put(index, own, pair, across, value):
    low, high = pair.at[0:ROWS, :], pair.at[ROWS : 2 * ROWS, :]
    for d, target in enumerate((own, low, across, high)):

        @pl.when(index == d)
        def _(target=target):
            target[...] = value


def columns_kernel(me, w_in, tok, taps, bias, gain_in, seg, w0, w1, w2, w3, out, rows):
    g = me[0]
    for d, send in enumerate((w0, w1, w2, w3)):
        start = (g ^ d) * XW
        send[:, :XW] = w_in[:, pl.ds(pl.multiple_of(start, 128), XW)]
        send[:, XW : 2 * XW] = w_in[:, pl.ds(pl.multiple_of(DI + start, 128), XW)]
        send[:, 2 * XW : XW + CL] = w_in[:, 2 * DI : DI + CW]
        send[:, XW + CL :] = jnp.concatenate(
            [w_in[:, DI + CW :], jnp.zeros((192, 128 - NH), bf16)], axis=1
        )
    out[0:ROWS, :] = tok[...]
    rows[...] = jnp.zeros_like(rows)
    rows[0:4, 0:448] = taps[...].astype(f32)
    rows[4:5, 0:448] = bias[...].astype(f32).reshape(1, 448)
    rows[5:6, 0:192] = gain_in[...].astype(f32).reshape(1, 192)
    rows[6:7, 0:ROWS] = seg[...].astype(f32)
    out[ROWS : ROWS + 16, :] = rows[...].astype(bf16)


def gather_short(g, parts, taps, gain_in, pos, wide, seg):
    for d, part in enumerate(parts):
        rows = part[ROWS : ROWS + 16, :].astype(f32)
        for k in range(4):

            @pl.when((g ^ d) == k)
            def _(k=k, rows=rows):
                wide[0:5, 448 * k : 448 * k + 448] = rows[0:5, 0:448]
                gain_in[:, 192 * k : 192 * k + 192] = rows[5:6, 0:192]
                seg[2 * k : 2 * k + 1, :] = rows[6:7, 0:128]
                seg[2 * k + 1 : 2 * k + 2, :] = rows[6:7, 128:256]

    taps[...] = jnp.zeros_like(taps)
    taps[0:5, 0:XW] = wide[0:5, pl.ds(pl.multiple_of(g * XW, 128), XW)]
    taps[0:5, XW:] = wide[0:5, DI:]
    ids = seg[...]
    row_at = lax.broadcasted_iota(jnp.int32, (8, 128), 0)
    lane_at = lax.broadcasted_iota(jnp.int32, (8, 128), 1)
    one = jnp.full((1, 128), -1.0, f32)
    earlier = jnp.concatenate([one, ids[0:7]], axis=0)
    later = jnp.concatenate([ids[1:8], one], axis=0)
    ends = jnp.broadcast_to(ids[:, 127:128], (8, 128))
    starts = jnp.broadcast_to(earlier[:, 127:128], (8, 128))
    features = [ids]
    for lag in range(1, 4):
        shifted = jnp.where(
            lane_at >= lag, pltpu.roll(ids, lag, 1), pltpu.roll(earlier, lag, 1)
        )
        features.append((shifted == ids).astype(f32))
    features += [(ids == starts).astype(f32), (ids == ends).astype(f32)]
    for lag in range(1, 4):
        shifted = jnp.where(
            lane_at < 128 - lag, pltpu.roll(ids, 128 - lag, 1), pltpu.roll(later, 128 - lag, 1)
        )
        features.append((shifted == ids).astype(f32))
    pos[...] = jnp.zeros_like(pos)
    for j, feature in enumerate(features):
        for n in range(8):
            pos[n, j : j + 1, :] = feature[n : n + 1, :]


def forward_kernel(
    me, t0, t1, t2, t3, w0, w1, w2, w3, dtb, rate, skip,
    w_full, normed, proj, v_out, states, y_out, pos, taps, gain_in,
    tok, state, ext, wide, seg,
):
    i = pl.program_id(0)
    g = me[0]

    @pl.when(i == 0)
    def _():
        row_at = lax.broadcasted_iota(jnp.int32, (128, 128), 0)
        lane_at = lax.broadcasted_iota(jnp.int32, (128, 128), 1)
        chosen = ((row_at == lane_at + g * HL) & (lane_at < HL)).astype(bf16)
        for d, part in enumerate((w0, w1, w2, w3)):
            rows = pl.ds(pl.multiple_of((g ^ d) * 192, 64), 192)
            w_full[rows, : XW + CL] = part[:, : XW + CL]
            w_full[rows, XW + CL :] = mm(part[:, XW + CL :], chosen, NN).astype(bf16)
        state[...] = jnp.zeros_like(state)
        ext[0:8, :] = jnp.zeros((8, CL), f32)
        gather_short(g, (t0, t1, t2, t3), taps, gain_in, pos, wide, seg)

    for d, source in enumerate((t0, t1, t2, t3)):

        @pl.when((g ^ i) == d)
        def _(source=source):
            tok[...] = source[0:ROWS, :]

    x = tok[...].astype(f32)
    rms = lax.rsqrt(jnp.mean(x * x, axis=-1, keepdims=True) + epsilon)
    low_rows = (x * rms * gain_in[...]).astype(bf16)
    normed[...] = low_rows
    proj[...] = mm(low_rows, w_full[...], NN).astype(bf16)
    ext[8 : 8 + ROWS, :] = proj[:, XW : XW + CL].astype(f32)
    for s in range(ROWS // SPAN):
        at = s * SPAN
        rows = slice(at, at + SPAN)
        dt_rows = proj[rows, XW + CL :].astype(f32) + dtb[...]
        pos_rows = pos[2 * i + s]
        cols, step, step_t, cum, decay, carried, tails, low = span_decays(
            dt_rows, rate[...], pos_rows
        )
        v = taps[4:5, :] + taps[3:4, :] * ext[8 + at : 8 + at + SPAN, :]
        for lag in range(1, 4):
            window = ext[8 + at - lag : 8 + at - lag + SPAN, :]
            v = v + (taps[3 - lag : 4 - lag, :] * cols[:, lag : lag + 1]) * window
        v_out[rows, :] = v
        conv = v * jax.nn.sigmoid(v)
        b_rows, c_rows = conv[:, XW : XW + NS], conv[:, XW + NS :]
        scores = mm(c_rows, b_rows, NT)
        states[s] = state[...]
        from_state = mm(c_rows, state[...], NN)
        ys, ends, decays_end = [], [], []
        for p in range(HL // 2):
            lanes = slice(p * SPAN, (p + 1) * SPAN)
            xp = conv[:, lanes]
            mixing = [
                decay(h) * scores * step_t[h : h + 1, :] for h in (2 * p, 2 * p + 1)
            ]
            inner = mm(
                jnp.concatenate(mixing, axis=1),
                jnp.concatenate([jnp.where(low, xp, 0.0), jnp.where(low, 0.0, xp)], axis=0),
                NN,
            )
            ys.append(inner + carried[p] * from_state[:, lanes] + skip[:, lanes] * xp)
            ends.append(tails[p] * xp)
            decays_end.append(carried[p][SPAN - 1 :, :])
        y_out[rows, :] = jnp.concatenate(ys, axis=1)
        state[...] = jnp.concatenate(decays_end, axis=1) * state[...] + mm(
            b_rows, jnp.concatenate(ends, axis=1), TN
        )
    ext[0:8, :] = ext[ROWS : ROWS + 8, :]


def sums_kernel(me, c0, c1, c2, c3, gate_in, y_in, gain_out, w_out, dno_out, stats, cot):
    i = pl.program_id(0)
    pick(me[0] ^ i, (c0, c1, c2, c3), cot)
    dno = mm(cot[...], w_out[...], NT)
    dno_out[...] = dno
    gate = gate_in[...].astype(f32)
    gated = y_in[...] * (gate * jax.nn.sigmoid(gate))
    squares = jnp.sum(gated * gated, axis=-1, keepdims=True)
    products = jnp.sum(gated * gain_out[...] * dno, axis=-1, keepdims=True)
    lane_at = lax.broadcasted_iota(jnp.int32, (SPAN, SPAN), 1)
    both = jnp.zeros((SPAN, SPAN), f32)
    for s in range(ROWS // SPAN):
        rows = slice(s * SPAN, (s + 1) * SPAN)
        both = jnp.where(lane_at == 2 * s, squares[rows], both)
        both = jnp.where(lane_at == 2 * s + 1, products[rows], both)
    stats[0] = both.T[0:8, :]


def out_kernel(
    me, c0, c1, c2, c3, gate_in, y_in, dno_in, stats, gain_out, w_out, normed,
    bundle, d_gate, dy_out, sums, o_own, o_pair, o_across,
    cot, acc_out, acc_gate, acc_sum, normed_out,
):
    i = pl.program_id(0)
    g = me[0]

    @pl.when(i == 0)
    def _():
        for ref in (acc_out, acc_gate, acc_sum):
            ref[...] = jnp.zeros_like(ref)

    pick(g ^ i, (c0, c1, c2, c3), cot)
    totals = to_columns(stats[0])
    for s in range(ROWS // SPAN):
        rows = slice(s * SPAN, (s + 1) * SPAN)
        rms = lax.rsqrt(totals[:, 2 * s : 2 * s + 1] * (1.0 / DI) + epsilon)
        mean = rms * rms * rms * totals[:, 2 * s + 1 : 2 * s + 2] * (1.0 / DI)
        gate = gate_in[rows, :].astype(f32)
        sig = jax.nn.sigmoid(gate)
        silu = gate * sig
        y = y_in[rows, :]
        gated = y * silu
        scaled = gated * rms
        normed_out[rows, :] = (scaled * gain_out[...]).astype(bf16)
        dno = dno_in[rows, :]
        acc_sum[0:1, :] += jnp.sum(dno * scaled, axis=0, keepdims=True)
        d_gated = rms * gain_out[...] * dno - gated * mean
        dy_out[rows, :] = d_gated * silu
        d_gate[rows, :] = (d_gated * y * (sig * (1.0 + gate * (1.0 - sig)))).astype(bf16)
    acc_out[...] += mm(normed_out[...], cot[...], TN)
    acc_gate[...] += mm(normed[...], d_gate[...], TN)
    put(g ^ i, o_own, o_pair, o_across, mm(normed_out[...], w_out[...], NN).astype(bf16))

    @pl.when(i == pl.num_programs(0) - 1)
    def _():
        sums[...] = acc_sum[...]
        for k in range(4):
            for t in range(3):
                at = 576 * k + 192 * t
                bundle[at : at + 192, :] = acc_gate[
                    192 * k : 192 * k + 192, 128 * t : 128 * t + 128
                ].astype(bf16)
        for t in range(6):
            at = 2304 + XW * t
            bundle[at : at + XW, :] = acc_out[:, 128 * t : 128 * t + 128].astype(bf16)


def split_sum(rows, ones):
    high = rows.astype(bf16)
    rest = rows - high.astype(f32)
    return mm(high, ones, NN) + mm(rest, ones, NN)


def backward_block(
    w_full, normed, proj, v_in, states, dy_in, d_gate, pos, taps, dtb, rate, skip, ones,
    d_state, ext, acc_in, acc_dt, acc_small, d_proj,
):
    row_at = lax.broadcasted_iota(jnp.int32, (SPAN, SPAN), 0)
    lane_at = lax.broadcasted_iota(jnp.int32, (SPAN, SPAN), 1)
    later = (row_at <= lane_at).astype(f32)

    def add(row, value):
        width = value.shape[1]
        acc_small[row : row + 1, :width] += value

    def down(value):
        return jnp.sum(value, axis=0, keepdims=True)

    d_proj[:, :XW] = d_gate[...]
    for s in reversed(range(ROWS // SPAN)):
        at = s * SPAN
        rows = slice(at, at + SPAN)
        dy = dy_in[rows, :]
        dt_rows = proj[rows, XW + CL :].astype(f32) + dtb[...]
        cols, step, step_t, cum, decay, carried, tails, low = span_decays(
            dt_rows, rate[...], pos[s]
        )
        v = v_in[rows, :]
        sig_v = jax.nn.sigmoid(v)
        conv = v * sig_v
        x, b_rows, c_rows = conv[:, :XW], conv[:, XW : XW + NS], conv[:, XW + NS :]
        add(1, down(dy * x))
        state = states[s]
        state_grad = d_state[...]
        scores = mm(c_rows, b_rows, NT)
        from_state = mm(c_rows, state, NN)
        from_grad = mm(b_rows, state_grad, NN)
        carried_all = jnp.concatenate(carried, axis=1)
        tails_all = jnp.concatenate(tails, axis=1)
        dy_carried = dy * carried_all
        x_tail = x * tails_all
        d_scores = jnp.zeros((SPAN, SPAN), f32)
        row_sums = jnp.zeros((SPAN, SPAN), f32)
        col_sums, dxs = [], []
        for p in range(HL // 2):
            lanes = slice(p * SPAN, (p + 1) * SPAN)
            xp, dyp = x[:, lanes], dy[:, lanes]
            halves = jnp.concatenate([jnp.where(low, dyp, 0.0), jnp.where(low, 0.0, dyp)], axis=0)
            d_mixing = mm(halves, xp, NT)
            mixing = []
            for k in range(2):
                h = 2 * p + k
                kept = decay(h)
                kept_step = kept * step_t[h : h + 1, :]
                mixing.append(kept_step * scores)
                d_mix = d_mixing[k * SPAN : (k + 1) * SPAN, :]
                d_scores = d_scores + d_mix * kept_step
                plain = d_mix * kept * scores
                col_sums.append(down(plain))
                row_sum = jnp.sum(plain * step_t[h : h + 1, :], axis=1, keepdims=True)
                row_sums = jnp.where(lane_at == h, row_sum, row_sums)
            inner = mm(jnp.concatenate(mixing, axis=0), halves, TN)
            dxs.append(inner + skip[:, lanes] * dyp + tails[p] * from_grad[:, lanes])
        dx = jnp.concatenate(dxs, axis=1)
        d_c = mm(d_scores, b_rows, NN) + mm(dy_carried, state, NT)
        d_b = mm(d_scores, c_rows, TN) + mm(x_tail, state_grad, NT)

        end_decay = carried_all[SPAN - 1 :, :]
        through = end_decay * down(state * state_grad)
        last = lax.broadcasted_iota(jnp.int32, (SPAN, XW), 0) == SPAN - 1
        from_start = split_sum(
            dy_carried * from_state + jnp.where(last, through, 0.0), ones[...]
        )
        to_end = split_sum(x * from_grad, ones[...])
        end_plain = jnp.exp(cum[SPAN - 1 :, :] - cum) * cols[:, 5:6]
        to_end_kept = to_end * end_plain
        to_end_step = to_end_kept * step
        col_sum = to_columns(jnp.concatenate(col_sums, axis=0))
        d_cum = row_sums - col_sum * step + from_start - to_end_step
        d_cum = d_cum + jnp.where(row_at == SPAN - 1, down(to_end_step), 0.0)
        d_log = mm_exact(later, d_cum, NN)
        d_step = col_sum + to_end_kept + rate[...] * d_log
        d_dt = d_step * jax.nn.sigmoid(dt_rows)
        add(2, down(d_dt))
        add(3, down(d_log * step) * rate[...])
        d_proj[rows, XW + CL :] = d_dt.astype(bf16)
        d_state[...] = end_decay * state_grad + mm(c_rows, dy_carried, TN)

        dv = jnp.concatenate([dx, d_b, d_c], axis=1) * (sig_v * (1.0 + v * (1.0 - sig_v)))
        ext[rows, :] = dv
        add(4, down(dv))
        conv_in = proj[rows, XW : XW + CL].astype(f32)
        add(8, down(dv * conv_in))
        d_conv = taps[3:4, :] * dv
        for lag in range(1, 4):
            window = ext[at + lag : at + lag + SPAN, :] * cols[:, 5 + lag : 6 + lag]
            d_conv = d_conv + taps[3 - lag : 4 - lag, :] * window
            add(8 - lag, down(window * conv_in))
        d_proj[rows, XW : XW + CL] = d_conv.astype(bf16)

    ext[ROWS:, :] = ext[0:8, :]
    d_normed = mm(d_proj[...], w_full[...], NT)
    add(9, down(d_normed * normed[...].astype(f32)))
    acc_in[...] += mm(normed[...], d_proj[:, XW : XW + CL], TN)
    acc_dt[...] += mm(d_proj[:, XW + CL :], normed[...], TN)[0:8, :]
    return d_normed.astype(bf16)


def late_kernel(
    w_full, normed, proj, v_in, states, dy_in, d_gate, pos, taps, dtb, rate, skip, ones,
    d_state, edge, acc_in, acc_dt, acc_small, d_normed,
    ext, d_proj,
):
    @pl.when(pl.program_id(0) == 0)
    def _():
        for ref in (d_state, acc_in, acc_dt, acc_small):
            ref[...] = jnp.zeros_like(ref)
        ext[ROWS:, :] = jnp.zeros((8, CL), f32)

    d_normed[...] = backward_block(
        w_full, normed, proj, v_in, states, dy_in, d_gate, pos, taps, dtb, rate, skip, ones,
        d_state, ext, acc_in, acc_dt, acc_small, d_proj,
    )
    edge[...] = ext[ROWS:, :]


def early_kernel(
    me, w_full, normed, proj, v_in, states, dy_in, d_gate, pos, taps, dtb, rate, skip, ones,
    d_state_in, edge, acc_in_in, acc_dt_in, acc_small_in, d_normed_in, sums,
    bundle, n_own, n_pair, n_across,
    d_state, ext, acc_in, acc_dt, acc_small, d_proj, small,
):
    i = pl.num_programs(0) - 1 - pl.program_id(0)
    g = me[0]

    @pl.when(pl.program_id(0) == 0)
    def _():
        d_state[...] = d_state_in[...]
        ext[ROWS:, :] = edge[...]
        acc_in[...] = acc_in_in[...]
        acc_dt[...] = acc_dt_in[...]
        acc_small[...] = acc_small_in[...]
        small[...] = jnp.zeros_like(small)
        for j in range(2):
            put(g ^ (2 + j), n_own, n_pair, n_across, d_normed_in[ROWS * j : ROWS * j + ROWS, :])

    value = backward_block(
        w_full, normed, proj, v_in, states, dy_in, d_gate, pos, taps, dtb, rate, skip, ones,
        d_state, ext, acc_in, acc_dt, acc_small, d_proj,
    )
    put(g ^ i, n_own, n_pair, n_across, value)

    @pl.when(i == 0)
    def _():
        def place(k, piece, value):
            at = 32 * k + 16 * (piece % 2)
            bundle[piece // 2, at : at + 16, :] = value.astype(bf16)

        def lay(start, source, row, first, tiles):
            for t in range(tiles):
                lanes = slice(first + 128 * t, first + 128 * t + 128)
                small[start + t : start + t + 1, :] = source[row : row + 1, lanes]

        for j in range(4):
            lay(16 + 5 * j, acc_small, 5 + j, 0, 5)
        lay(36, acc_small, 4, 0, 5)
        lay(43, sums, 0, 0, 3)
        lay(46, acc_small, 1, 0, 3)
        lay(49, acc_small, 2, 0, 1)
        lay(50, acc_small, 3, 0, 1)
        for k in range(4):
            for tile in range(5):
                for q in range(12):
                    place(
                        k,
                        12 * tile + q,
                        acc_in[
                            192 * k + 16 * q : 192 * k + 16 * q + 16,
                            128 * tile : 128 * tile + 128,
                        ],
                    )
            for h in range(HL):
                small[2 * h : 2 * h + 1, :] = acc_dt[h : h + 1, 192 * k : 192 * k + 128]
                small[2 * h + 1 : 2 * h + 2, 0:64] = acc_dt[
                    h : h + 1, 192 * k + 128 : 192 * k + 192
                ]
            small[41:42, :] = acc_small[9:10, 192 * k : 192 * k + 128]
            small[42:43, 0:64] = acc_small[9:10, 192 * k + 128 : 192 * k + 192]
            for q in range(4):
                place(k, 60 + q, small[16 * q : 16 * q + 16, :])


def assemble_kernel(
    me, gates0, gates1, gates2, gates3, parts, gain_in,
    grad_in, grad_kernel, grad_bias, grad_gain_in, grad_gain_out, grad_skip,
    grad_dt, grad_log,
    wide, turned,
):
    g = me[0]

    def piece(k, row, count=192):
        return parts[k, row : row + count, :].astype(f32)

    for d, gates in enumerate((gates0, gates1, gates2, gates3)):
        for t in range(3):
            start = pl.multiple_of((g ^ d) * XW + 128 * t, 128)
            grad_in[:, pl.ds(start, 128)] = gates[192 * t : 192 * t + 192, :].astype(f32)
    for k in range(4):
        for t in range(3):
            lanes = slice(DI + k * XW + 128 * t, DI + k * XW + 128 * t + 128)
            grad_in[:, lanes] = piece(k, 192 * t)
    for t in range(3, 5):
        lanes = slice(2 * DI + 128 * (t - 3), 2 * DI + 128 * (t - 2))
        grad_in[:, lanes] = (piece(0, 192 * t) + piece(1, 192 * t)) + (
            piece(2, 192 * t) + piece(3, 192 * t)
        )

    turned[...] = jnp.zeros_like(turned)
    wide[...] = jnp.zeros_like(wide)
    gain = jnp.zeros((2, 128), f32)
    for k in range(4):
        rest = piece(k, 960, 64)
        for h in range(HL):
            at = HL * k + h
            turned[at : at + 1, 0:128] = rest[2 * h : 2 * h + 1, :]
            turned[at : at + 1, 128:256] = rest[2 * h + 1 : 2 * h + 2, :]
        for j in range(5):
            for t in range(3):
                lanes = slice(k * XW + 128 * t, k * XW + 128 * t + 128)
                wide[j : j + 1, lanes] = rest[16 + 5 * j + t : 17 + 5 * j + t, :]
            for t in range(3, 5):
                lanes = slice(DI + 128 * (t - 3), DI + 128 * (t - 2))
                wide[j : j + 1, lanes] += rest[16 + 5 * j + t : 17 + 5 * j + t, :]
        gain = gain + rest[41:43, :]
    grad_in[:, DI + CW :] = turned[...].T[0:192, 0:NH]
    grad_gain_in[:, 0:128] = gain[0:1, :] / gain_in[:, 0:128]
    grad_gain_in[:, 128:192] = gain[1:2, 0:64] / gain_in[:, 128:192]
    for k in range(4):

        @pl.when(g == k)
        def _(k=k):
            grad_kernel[...] = wide[0:4, 448 * k : 448 * k + 448]
            grad_bias[...] = wide[4:5, 448 * k : 448 * k + 448]

    own = parts[g, 960:1024, :].astype(f32)
    for t in range(3):
        grad_gain_out[:, 128 * t : 128 * t + 128] = own[43 + t : 44 + t, :]
    lane_at = lax.broadcasted_iota(jnp.int32, (1, 128), 1)
    skips = jnp.zeros((1, 128), f32)
    for t in range(3):
        row = own[46 + t : 47 + t, :]
        first = jnp.sum(jnp.where(lane_at < HP, row, 0.0), axis=1, keepdims=True)
        second = jnp.sum(jnp.where(lane_at < HP, 0.0, row), axis=1, keepdims=True)
        skips = jnp.where(lane_at == 2 * t, first, skips)
        skips = jnp.where(lane_at == 2 * t + 1, second, skips)
    grad_skip[...] = skips[:, 0:HL]
    grad_dt[...] = own[49:50, 0:HL]
    grad_log[...] = own[50:51, 0:HL]


def whole(shape):
    zeros = (0,) * len(shape)
    return pl.BlockSpec(shape, lambda i: zeros)


def blocked(shape, place):
    zeros = (0,) * (len(shape) - 1)
    return pl.BlockSpec(shape, lambda i: (place(i),) + zeros)


scalar_spec = pl.BlockSpec(memory_space=pltpu.SMEM)
vmem_spec = pl.BlockSpec(memory_space=pltpu.VMEM)


def shape(dims, dtype):
    return jax.ShapeDtypeStruct(dims, dtype)


def call(body, name, micros, **kwargs):
    return pl.pallas_call(
        body,
        name=name,
        compiler_params=pltpu.CompilerParams(vmem_limit_bytes=vmem_bytes),
        cost_estimate=pl.CostEstimate(
            flops=int(micros * 1e9), bytes_accessed=1 << 20, transcendentals=0
        ),
        **kwargs,
    )


def among(value, d):
    return lax.ppermute(value, "group", [(i, i ^ d) for i in range(4)])


def local(
    tokens, segments, cotangent, gain_in, w_in, kernel, conv_bias, dt_bias, a_log, skip_gain,
    gain_out, w_out,
):
    reps = lax.axis_size("rep")
    g = lax.axis_index("group")
    me = g.astype(jnp.int32).reshape(1)
    tok = tokens.reshape(ROWS, D)
    cot = cotangent.reshape(ROWS, D)
    part = whole((ROWS, D))
    blocks = 4

    w0, w1, w2, w3, both0 = call(
        columns_kernel,
        "columns",
        2,
        in_specs=[scalar_spec] + [vmem_spec] * 6,
        out_specs=[vmem_spec] * 5,
        out_shape=(shape((192, PW), bf16),) * 4 + (shape((ROWS + 16, D), bf16),),
        scratch_shapes=[pltpu.VMEM((16, D), f32)],
    )(
        me, w_in, tok, kernel, conv_bias, gain_in,
        segments.reshape(1, ROWS),
    )

    def across(value, d):
        pairs = [(i * reps + r, (i ^ d) * reps + (r ^ 1)) for r in range(reps) for i in range(4)]
        return lax.ppermute(value, ("group", "rep"), pairs)

    w2 = across(w2, 2)
    both2 = among(both0, 2)
    w3 = across(w3, 3)
    w1 = among(w1, 1)
    both1 = among(both0, 1)
    both2, cot_late = lax.optimization_barrier((both2, cot))
    both3 = among(both2, 1)
    c2 = among(cot_late, 2)
    c1 = among(cot_late, 1)
    c3 = among(c2, 1)
    length = blocks * ROWS
    spans = length // SPAN

    dtb = jnp.pad(dt_bias.astype(f32), (0, 128 - HL)).reshape(1, 128)
    rate = jnp.pad(-jnp.exp(a_log.astype(f32)), (0, 128 - HL)).reshape(1, 128)
    skip = jnp.repeat(skip_gain.astype(f32), HP).reshape(1, XW)
    gain_o = gain_out.astype(f32).reshape(1, XW)

    def up(i):
        return i

    by_owner_specs = [part, whole((2 * ROWS, D)), part]
    by_owner_shapes = tuple(shape((n * ROWS, D), bf16) for n in (1, 2, 1))

    def to_owner(own, pair, over):
        got = among(pair, 1).astype(f32)
        other = (over.astype(f32) + got[ROWS:]).astype(bf16)
        return own, got[:ROWS], among(other, 2)

    w_full, normed, proj, v_rows, states, y_rows, pos, taps, gain_in_all = call(
        forward_kernel,
        "forward",
        15,
        grid=(blocks,),
        in_specs=[scalar_spec]
        + [whole((ROWS + 16, D))] * 4
        + [whole((192, PW))] * 4
        + [whole((1, 128)), whole((1, 128)), whole((1, XW))],
        out_specs=[
            whole((D, PW)),
            blocked((ROWS, D), up),
            blocked((ROWS, PW), up),
            blocked((ROWS, CL), up),
            blocked((2, NS, XW), up),
            blocked((ROWS, XW), up),
            whole((8, 16, SPAN)),
            whole((8, CL)),
            whole((1, D)),
        ],
        out_shape=(
            shape((D, PW), bf16),
            shape((length, D), bf16),
            shape((length, PW), bf16),
            shape((length, CL), f32),
            shape((spans, NS, XW), f32),
            shape((length, XW), f32),
            shape((spans, 16, SPAN), f32),
            shape((8, CL), f32),
            shape((1, D), f32),
        ),
        scratch_shapes=[
            pltpu.VMEM((ROWS, D), bf16),
            pltpu.VMEM((NS, XW), f32),
            pltpu.VMEM((ROWS + 8, CL), f32),
            pltpu.VMEM((8, CW), f32),
            pltpu.VMEM((8, 128), f32),
        ],
    )(
        me, both0, both1, both2, both3, w0, w1, w2, w3, dtb, rate, skip,
    )

    gate_spec = pl.BlockSpec((ROWS, XW), lambda i: (i, 0))
    dno, stats = call(
        sums_kernel,
        "sums",
        4,
        grid=(blocks,),
        in_specs=[scalar_spec]
        + [part] * 4
        + [gate_spec, blocked((ROWS, XW), up), whole((1, XW)), whole((XW, D))],
        out_specs=[blocked((ROWS, XW), up), blocked((1, 8, SPAN), up)],
        out_shape=(shape((length, XW), f32), shape((blocks, 8, SPAN), f32)),
        scratch_shapes=[pltpu.VMEM((ROWS, D), bf16)],
    )(me, cot, c1, c2, c3, proj, y_rows, gain_o, w_out)
    stats = lax.psum(stats, "group")

    bundle1, d_gate, dy, sums, *o_parts = call(
        out_kernel,
        "out",
        7,
        grid=(blocks,),
        in_specs=[scalar_spec]
        + [part] * 4
        + [
            gate_spec, blocked((ROWS, XW), up), blocked((ROWS, XW), up),
            blocked((1, 8, SPAN), up), whole((1, XW)), whole((XW, D)), blocked((ROWS, D), up),
        ],
        out_specs=[
            whole((4608, 128)), blocked((ROWS, XW), up), blocked((ROWS, XW), up), whole((8, XW)),
        ]
        + by_owner_specs,
        out_shape=(
            shape((4608, 128), bf16), shape((length, XW), bf16), shape((length, XW), f32),
            shape((8, XW), f32),
        )
        + by_owner_shapes,
        scratch_shapes=[
            pltpu.VMEM((ROWS, D), bf16),
            pltpu.VMEM((XW, D), f32),
            pltpu.VMEM((D, XW), f32),
            pltpu.VMEM((8, XW), f32),
            pltpu.VMEM((ROWS, XW), bf16),
        ],
    )(me, cot, c1, c2, c3, proj, y_rows, dno, stats, gain_o, w_out, normed)

    def spread(value):
        return lax.all_to_all(value, "rep", 0, 0, tiled=True)

    received1 = spread(bundle1.reshape(reps, 144, 128))
    branches = to_owner(*o_parts)

    ones = jnp.asarray(np.arange(XW)[:, None] // HP == np.arange(128)[None, :], bf16)
    half = blocks // 2
    shared = [
        shape((NS, XW), f32), shape((8, CL), f32), shape((D, CL), f32), shape((8, D), f32),
        shape((16, D), f32),
    ]

    def backward_specs(last):
        def back(i):
            return last - i

        return [
            whole((D, PW)),
            blocked((ROWS, D), back),
            blocked((ROWS, PW), back),
            blocked((ROWS, CL), back),
            blocked((2, NS, XW), back),
            blocked((ROWS, XW), back),
            blocked((ROWS, XW), back),
            blocked((2, 16, SPAN), back),
            whole((8, CL)), whole((1, 128)), whole((1, 128)), whole((1, XW)), whole((XW, 128)),
        ]

    operands = (w_full, normed, proj, v_rows, states, dy, d_gate, pos, taps, dtb, rate, skip, ones)
    handed = call(
        late_kernel,
        "late",
        12,
        grid=(half,),
        in_specs=backward_specs(blocks - 1),
        out_specs=[whole(v.shape) for v in shared]
        + [blocked((ROWS, D), lambda i: half - 1 - i)],
        out_shape=shared + [shape((half * ROWS, D), bf16)],
        scratch_shapes=[pltpu.VMEM((ROWS + 8, CL), f32), pltpu.VMEM((ROWS, PW), bf16)],
    )(*operands)

    def total(received):
        return jnp.sum(received.astype(f32), axis=0).astype(bf16)

    reduced1 = total(received1)
    reduced1, handed, branches = lax.optimization_barrier((reduced1, handed, branches))
    flat1 = spread(jnp.broadcast_to(reduced1[None], (reps, 144, 128))).reshape(4608, 128)
    bundle2, *n_parts = call(
        early_kernel,
        "early",
        12,
        grid=(half,),
        in_specs=[scalar_spec]
        + backward_specs(half - 1)
        + [whole(v.shape) for v in shared]
        + [whole((half * ROWS, D)), whole((8, XW))],
        out_specs=[whole((32, 128, 128))] + by_owner_specs,
        out_shape=(shape((32, 128, 128), bf16),) + by_owner_shapes,
        scratch_shapes=[
            pltpu.VMEM((NS, XW), f32),
            pltpu.VMEM((ROWS + 8, CL), f32),
            pltpu.VMEM((D, CL), f32),
            pltpu.VMEM((8, D), f32),
            pltpu.VMEM((16, D), f32),
            pltpu.VMEM((ROWS, PW), bf16),
            pltpu.VMEM((64, 128), f32),
        ],
    )(me, *operands, *handed, sums)

    bundle2, flat1 = lax.optimization_barrier((bundle2, flat1))
    received2 = spread(bundle2)
    d_parts = to_owner(*n_parts)
    by_member = flat1[:2304].reshape(4, 576, 128)
    gates = [lax.dynamic_index_in_dim(by_member, g ^ d, 0, keepdims=False) for d in range(4)]
    gates = [gates[0]] + [among(gates[d], d) for d in range(1, 4)]
    reduced2, gates, d_parts = lax.optimization_barrier((total(received2), gates, d_parts))
    parts = lax.all_to_all(
        jnp.broadcast_to(reduced2.reshape(4, 1, 32, 128), (4, reps, 32, 128)).reshape(
            4 * reps, 32, 128
        ),
        ("group", "rep"), 0, 0, tiled=True,
    ).reshape(4, 32 * reps, 128)
    grad_w_out = flat1[2304:].reshape(6, XW, 128).transpose(1, 0, 2).reshape(XW, D).astype(f32)

    x = tok.astype(f32)
    branch = sum(value.astype(f32) for value in branches)
    layer_out = (x + branch).astype(bf16).reshape(tokens.shape)
    d_normed = sum(value.astype(f32) for value in d_parts)
    rms_in = lax.rsqrt(jnp.mean(x * x, axis=-1, keepdims=True) + epsilon)
    scaled = d_normed * gain_in_all
    grad_tokens = (
        cot.astype(f32)
        + rms_in * scaled
        - x * (rms_in * rms_in * rms_in * jnp.mean(x * scaled, axis=-1, keepdims=True))
    ).reshape(tokens.shape)

    grads = call(
        assemble_kernel,
        "assemble",
        4,
        in_specs=[scalar_spec] + [vmem_spec] * 6,
        out_specs=[vmem_spec] * 8,
        out_shape=(
            shape((192, 3352), f32), shape((4, 448), f32),
            shape((1, 448), f32), shape((1, 192), f32), shape((1, XW), f32), shape((1, HL), f32),
            shape((1, HL), f32), shape((1, HL), f32),
        ),
        scratch_shapes=[pltpu.VMEM((8, CW), f32), pltpu.VMEM((128, 256), f32)],
    )(me, *gates, parts, gain_in.astype(f32).reshape(1, 192))
    grad_w_in, grad_kernel, grad_bias, grad_gi, grad_go, grad_s, grad_d, grad_l = grads
    return (
        layer_out,
        grad_tokens,
        grad_gi.reshape(-1),
        grad_w_in,
        grad_kernel,
        grad_bias.reshape(-1),
        grad_d.reshape(-1),
        grad_l.reshape(-1),
        grad_s.reshape(-1),
        grad_go.reshape(-1),
        grad_w_out,
    )


def solution(mesh):
    sequences = P("rep", "group", None)
    vector = P("group")
    matrix = P("group", None)
    return jax.shard_map(
        local,
        mesh=mesh,
        in_specs=(
            sequences, P("rep", "group"), sequences, vector, matrix, P(None, "group"),
            vector, vector, vector, vector, vector, matrix,
        ),
        out_specs=(
            sequences, sequences, vector, matrix, P(None, "group"), vector, vector, vector,
            vector, vector, matrix,
        ),
        check_vma=False,
    )
```

time: 244 us -> 208 us (0.85); the launches traced: 240 us -> 207 us
  blocking collectives: 64.6 us -> 10.7 us
  starting transfers between devices: 21.6 us -> 57.5 us
  waiting for transfers between devices: 74.5 us -> 54.9 us
  Pallas kernels: 48.3 us -> 63.1 us
  local copies, waits for them, and re-layouts: 22.2 us -> 12.2 us
    all_to_all x1 -> x0, blocking collectives: 40.5 us -> none  [local(): received = lax.all_to_all(bundle, 'rep', 0, 0, tiled=True)]
    all_to_all x1 -> x4, starting transfers between devices: 4.44 us -> 41.5 us  [the longest x3 31 us: spread(): return lax.all_to_all(value, 'rep', 0, 0, tiled=True)]
    ppermute x16 -> x14, waiting for transfers between devices: 56.3 us -> 23.8 us  [among(): return lax.ppermute(value, 'group', [(i, i ^ d) for i in range(4)])]
    all_to_all x1 -> x4, waiting for transfers between devices: 0.01 us -> 29.8 us  [the longest x3 15.9 us: spread(): return lax.all_to_all(value, 'rep', 0, 0, tiled=True)]
    ppermute x2, waiting for transfers between devices: 18.2 us -> 1.33 us  [across(): return lax.ppermute(value, ('group', 'rep'), pairs)]
    pallas_call x3 -> x7, Pallas kernels: 48.3 us -> 63.1 us  [the longest x1 14.5 us: local(): call(early_kernel, 'early', 12, grid=(half,), in_specs=[scalar_spec] + ba...]
    all_gather x1 -> x0, blocking collectives: 12.6 us -> none  [local(): gathered = lax.all_gather(packed, 'group')]
    convert_element_type x2 -> x5, other arithmetic: 0.09 us -> 3.46 us  [the longest x2 2.02 us: to_owner(): other = (over.astype(f32) + got[ROWS:]).astype(bf16)]
  transfers between devices with their start and end apart: 19 -> 20, of which waited for: 8 -> 11; matrix products, arithmetic and copies ran while one was open for 7% -> 6% of each run, Pallas kernels for 0% -> 20%
where the time goes in v2:
time: 208 us; the launch traced here: 207 us
  Pallas kernels  63.1 us (30%)
  starting transfers between devices  57.5 us (28%)
  waiting for transfers between devices  54.9 us (26%)
  local copies, waits for them, and re-layouts  12.2 us (6%)
  blocking collectives  10.7 us (5%)
  other arithmetic  7.97 us (4%)
    all_to_all x3, starting transfers between devices, spread(): return lax.all_to_all(value, 'rep', 0, 0, tiled=True)  31 us
    ppermute x14, waiting for transfers between devices, among(): return lax.ppermute(value, 'group', [(i, i ^ d) for i in range(4)])  23.8 us
    all_to_all x3, waiting for transfers between devices, spread(): return lax.all_to_all(value, 'rep', 0, 0, tiled=True)  15.9 us
    pallas_call x1, Pallas kernels, local(): call(early_kernel, 'early', 12, grid=(half,), in_specs=[scalar_spec] + ba...  14.5 us
    pallas_call x1, Pallas kernels, local(): call(forward_kernel, 'forward', 15, grid=(blocks,), in_specs=[scalar_spec...  14.3 us
    all_to_all x1, waiting for transfers between devices, local(): lax.all_to_all(jnp.broadcast_to(reduced2.reshape(4, 1, 32, 128), (4, reps...  13.9 us
    pallas_call x1, Pallas kernels, local(): call(late_kernel, 'late', 12, grid=(half,), in_specs=backward_specs(block...  13.1 us
    ppermute x14, starting transfers between devices, among(): return lax.ppermute(value, 'group', [(i, i ^ d) for i in range(4)])  12.6 us
  transfers between devices with their start and end apart: 20, of which 11 were waited for; matrix products, arithmetic and copies ran while one was open for 6% of the time, Pallas kernels for 20%

profile of v2, /device:TPU:1, one launch (start us, length us, event | category | flops | bytes accessed | tf_op | source)
XLA Modules:
  0.0 207.3 jit_solution(17161136510572444409)
XLA Ops:
  0.7 2.9 %columns.1 = (bf16[192,1152]{1,0:T(8,128)(2,1)}, bf16[192,1152]{1,0:T(8,128)(2,1)}, bf16[192,1152]{1,0:T(8,128)(2,1)}, bf16[192,1152]{1,0:T(8,128)(2,1)}, bf16[272,768]{1,0:T(8,128)(2,1)}) custom-call(s32[1]{0:T(128)} %bitcast.1.me, bf16[192,3352]{1,0:T(8,128)(2,1)} %w_in.1, bf16[256,768]{1,0:T(8,128)(2,1)} %bitcast.46, bf16[4,448]{1,0:T(4,128)(2,1)} %taps.1, ...), custom_call_target="tpu_custom_call" | custom-call | flops 2000000000 | bytes 1048576 | tf_op jit(solution)/shard_map/columns/pallas_call | solution.py:609
  3.6 2.1 %collective-permute-start = (bf16[272,768]{1,0:T(8,128)(2,1)}, bf16[272,768]{1,0:T(8,128)(2,1)S(1)}, u32[]{:S(2)}, u32[]{:S(2)}) collective-permute-start(bf16[272,768]{1,0:T(8,128)(2,1)} %get-tuple-element.74.t0), channel_id=1, source_target_pairs={{0,64},{32,96},{64,0},{96,32},{1,65},{33,97},{65,1},{97,33},{2,66}... | collective-permute-start | bytes 1253384 | tf_op jit(solution)/shard_map/ppermute | solution.py:594
  5.7 1.0 collective-permute-start.4
  6.7 1.9 collective-permute-start.7
  8.6 1.4 collective-permute-start.8
  11.3 3.6 %collective-permute-done.t2 = bf16[272,768]{1,0:T(8,128)(2,1)S(1)} collective-permute-done((bf16[272,768]{1,0:T(8,128)(2,1)}, bf16[272,768]{1,0:T(8,128)(2,1)S(1)}, u32[]{:S(2)}, u32[]{:S(2)}) %collective-permute-start) | collective-permute-done | bytes 417824 | tf_op jit(solution)/shard_map/ppermute | solution.py:594
  14.9 1.6 collective-permute-start.5
  16.6 1.5 collective-permute-start.2
  19.4 7.9 %collective-permute-done.2.c2 = bf16[256,768]{1,0:T(8,128)(2,1)S(1)} collective-permute-done((bf16[256,768]{1,0:T(8,128)(2,1)S(1)}, bf16[256,768]{1,0:T(8,128)(2,1)S(1)}, u32[]{:S(2)}, u32[]{:S(2)}) %collective-permute-start.2) | collective-permute-done | bytes 393248 | tf_op jit(solution)/shard_map/ppermute | solution.py:594
  27.4 0.8 collective-permute-start.3
  28.2 1.3 collective-permute-done.8.w3
  29.5 0.7 copy-done.16
  30.4 14.3 %forward.1 = (bf16[768,1152]{1,0:T(8,128)(2,1)}, bf16[1024,768]{1,0:T(8,128)(2,1)}, bf16[1024,1152]{1,0:T(8,128)(2,1)}, f32[1024,640]{1,0:T(8,128)}, f32[8,128,3...) custom-call(s32[1]{0:T(128)} %bitcast.1.me, ...), custom_call_target="tpu_custom_call" | custom-call | flops 15000000512 | bytes 1048576 | tf_op jit(solution)/shard_map/forward/pallas_call | solution.py:655
  44.7 0.7 copy-done.21
  45.6 5.3 %sums.1 = (f32[1024,384]{1,0:T(8,128)}, f32[4,8,128]{2,1,0:T(8,128)}) custom-call(s32[1]{0:T(128)} %bitcast.1.me, bf16[256,768]{1,0:T(8,128)(2,1)} %bitcast.48, bf16[256,768]{1,0:T(8,128)(2,1)} %copy-done.21, bf16[256,768]{1,0:T(8,128)(2,1)} %copy-done.20, bf16[256,768]{1,0:T(8,128)(2,1)} %copy-done.22, bf16[1024,1152]{1,0:T(8,128)(2,1)} %get-tuple-element.81.gate_in.proj, ...), custom_call_target="tpu_custom_call" | custom-call | flops 4000000000 | bytes 1048576 | tf_op jit(solution)/shard_map/sums/pallas_call | solution.py:698
  50.8 10.7 %psum.7.stats = f32[4,8,128]{2,1,0:T(8,128)} all-reduce(f32[4,8,128]{2,1,0:T(8,128)} %get-tuple-element.84), channel_id=1, replica_groups=mesh['group'=4,'rep'=32] {'group'}, use_global_device_ids=true, to_apply=%region_0.1 | all-reduce | flops 4096 | bytes 32768 | tf_op jit(solution)/shard_map/psum | solution.py:710
  61.5 9.6 %out.1 = (bf16[4608,128]{1,0:T(8,128)(2,1)}, bf16[1024,384]{1,0:T(8,128)(2,1)}, f32[1024,384]{1,0:T(8,128)}, f32[8,384]{1,0:T(8,128)}, bf16[256,768]{1,0:T(8,128...) custom-call(s32[1]{0:T(128)} %bitcast.1.me, bf16[256,768]{1,0:T(8,128)(2,1)} %bitcast.49, ...), custom_call_target="tpu_custom_call" | custom-call | flops 7000000000 | bytes 1048576 | tf_op jit(solution)/shard_map/out/pallas_call | solution.py:712
  71.1 1.3 collective-permute-start.9
  72.4 10.4 %all-to-all-start = ((bf16[32,144,128]{2,1,0:T(8,128)(2,1)}), bf16[32,144,128]{2,1,0:T(8,128)(2,1)S(1)}, u32[]{:S(2)}, u32[]{:S(2)}) async-start(bf16[32,144,128]{2,1,0:T(8,128)(2,1)} %bitcast.47), calls=%async_computation | async-start | bytes 2359296 | tf_op jit(solution)/shard_map/all_to_all | solution.py:742
  82.9 0.9 copy-done.5
  84.1 13.1 %late.1 = (f32[128,384]{1,0:T(8,128)}, f32[8,640]{1,0:T(8,128)}, f32[768,640]{1,0:T(8,128)}, f32[8,768]{1,0:T(8,128)}, f32[16,768]{1,0:T(8,128)}, /*index=5*/bf16[512,768]{1,0:T(8,128)(2,1)}) custom-call(bf16[768,1152]{1,0:T(8,128)(2,1)} %get-tuple-element.87.w_full, bf16[1024,768]{1,0:T(8,128)(2,1)} %get-tuple-element.85.normed, ...), custom_call_target="tpu_custom_call" | custom-call | flops 12000000000 | bytes 1048576 | tf_op jit(solution)/shard_map/late/pallas_call | solution.py:771
  97.2 1.0 slice.24
  98.2 4.9 %all-to-all-done = bf16[32,144,128]{2,1,0:T(8,128)(2,1)S(1)} async-done(((bf16[32,144,128]{2,1,0:T(8,128)(2,1)}), bf16[32,144,128]{2,1,0:T(8,128)(2,1)S(1)}, u32[]{:S(2)}, u32[]{:S(2)}) %all-to-all-start) | async-done | bytes 1179680 | tf_op jit(solution)/shard_map/all_to_all | solution.py:742
  103.2 1.1 collective-permute-done.10
  104.4 1.2 broadcast_in_dim.9
  105.5 11.0 %all-to-all-start.1 = ((bf16[32,144,128]{2,1,0:T(8,128)(2,1)}), bf16[32,144,128]{2,1,0:T(8,128)(2,1)S(1)}, u32[]{:S(2)}, u32[]{:S(2)}) async-start(bf16[32,144,128]{2,1,0:T(8,128)(2,1)} %broadcast_in_dim.9), calls=%async_computation.1 | async-start | bytes 2359296 | tf_op jit(solution)/shard_map/all_to_all | solution.py:742
  116.5 14.5 %early.1 = (bf16[32,128,128]{2,1,0:T(8,128)(2,1)}, bf16[256,768]{1,0:T(8,128)(2,1)}, bf16[512,768]{1,0:T(8,128)(2,1)}, bf16[256,768]{1,0:T(8,128)(2,1)}) custom-call(s32[1]{0:T(128)} %bitcast.1.me, bf16[768,1152]{1,0:T(8,128)(2,1)} %get-tuple-element.87.w_full, bf16[1024,768]{1,0:T(8,128)(2,1)} %get-tuple-element.85.normed, ...), custom_call_target="tpu_custom_call" | custom-call | flops 12000000000 | bytes 1048576 | tf_op jit(solution)/shard_map/early/pallas_call | solution.py:789
  131.0 1.1 collective-permute-start.14
  132.2 2.1 %collective-permute-done.14 = bf16[512,768]{1,0:T(8,128)(2,1)S(1)} collective-permute-done((bf16[512,768]{1,0:T(8,128)(2,1)}, bf16[512,768]{1,0:T(8,128)(2,1)S(1)}, u32[]{:S(2)}, u32[]{:S(2)}) %collective-permute-start.14) | collective-permute-done | bytes 786464 | tf_op jit(solution)/shard_map/ppermute | solution.py:594
  134.3 1.3 convert_element_type.77
  135.5 9.6 %all-to-all-start.2 = ((bf16[32,128,128]{2,1,0:T(8,128)(2,1)}), bf16[32,128,128]{2,1,0:T(8,128)(2,1)S(1)}, u32[]{:S(2)}, u32[]{:S(2)}) async-start(bf16[32,128,128]{2,1,0:T(8,128)(2,1)} %get-tuple-element.115), calls=%async_computation.2 | async-start | bytes 2097152 | tf_op jit(solution)/shard_map/all_to_all | solution.py:742
  145.2 2.0 fusion.5
  147.2 0.9 fusion.9
  148.0 0.8 dynamic-slice_bitcast_fusion
  148.8 0.9 collective-permute-start.11
  149.7 1.5 collective-permute-start.12
  151.9 11.0 %all-to-all-done.2 = bf16[32,128,128]{2,1,0:T(8,128)(2,1)S(1)} async-done(((bf16[32,128,128]{2,1,0:T(8,128)(2,1)}), bf16[32,128,128]{2,1,0:T(8,128)(2,1)S(1)}, u32[]{:S(2)}, u32[]{:S(2)}) %all-to-all-start.2) | async-done | bytes 1048608 | tf_op jit(solution)/shard_map/all_to_all | solution.py:742
  163.1 2.1 %collective-permute-done.15 = bf16[256,768]{1,0:T(8,128)(2,1)S(1)} collective-permute-done((bf16[256,768]{1,0:T(8,128)(2,1)}, bf16[256,768]{1,0:T(8,128)(2,1)S(1)}, u32[]{:S(2)}, u32[]{:S(2)}) %collective-permute-start.15) | collective-permute-done | bytes 393248 | tf_op jit(solution)/shard_map/ppermute | solution.py:594
  165.2 3.3 %collective-permute-done.12.gates2 = bf16[576,128]{1,0:T(8,128)(2,1)} collective-permute-done((bf16[576,128]{1,0:T(8,128)(2,1)S(1)}, bf16[576,128]{1,0:T(8,128)(2,1)}, u32[]{:S(2)}, u32[]{:S(2)}) %collective-permute-start.12) | collective-permute-done | bytes 147488 | tf_op jit(solution)/shard_map/ppermute | solution.py:594
  168.5 3.7 %collective-permute-done.13.gates3 = bf16[576,128]{1,0:T(8,128)(2,1)} collective-permute-done((bf16[576,128]{1,0:T(8,128)(2,1)S(1)}, bf16[576,128]{1,0:T(8,128)(2,1)}, u32[]{:S(2)}, u32[]{:S(2)}) %collective-permute-start.13) | collective-permute-done | bytes 147488 | tf_op jit(solution)/shard_map/ppermute | solution.py:594
  172.2 1.1 broadcast_in_dim.21
  173.3 10.5 %all-to-all-start.3 = ((bf16[128,32,128]{2,1,0:T(8,128)(2,1)}), bf16[128,32,128]{2,1,0:T(8,128)(2,1)}, u32[]{:S(2)}, u32[]{:S(2)}) async-start(bf16[128,32,128]{2,1,0:T(8,128)(2,1)} %bitcast.16), calls=%async_computation.3 | async-start | bytes 2097152 | tf_op jit(solution)/shard_map/all_to_all | solution.py:818
  184.3 1.4 copy.25
  186.1 0.8 copy-done
  187.2 1.5 fusion.4
  188.6 13.9 %all-to-all-done.3 = bf16[128,32,128]{2,1,0:T(8,128)(2,1)} async-done(((bf16[128,32,128]{2,1,0:T(8,128)(2,1)}), bf16[128,32,128]{2,1,0:T(8,128)(2,1)}, u32[]{:S(2)}, u32[]{:S(2)}) %all-to-all-start.3) | async-done | bytes 1048608 | tf_op jit(solution)/shard_map/all_to_all | solution.py:818
  202.5 3.5 %assemble.1 = (f32[192,3352]{1,0:T(8,128)}, f32[4,448]{1,0:T(4,128)}, f32[1,448]{1,0:T(1,128)}, f32[1,192]{1,0:T(1,128)}, f32[1,384]{1,0:T(1,128)}, /*index=5*/f...) custom-call(s32[1]{0:T(128)} %bitcast.1.me, bf16[576,128]{1,0:T(8,128)(2,1)} %get-tuple-element.124.gates0, ...), custom_call_target="tpu_custom_call" | custom-call | flops 4000000000 | bytes 1048576 | tf_op jit(solution)/shard_map/assemble/pallas_call | solution.py:838
  206.0 1.3 reduce.3
  (79 shorter events, 5.6 us)
Async XLA Ops:
  0.7 9.4 %copy-start.13 = (bf16[6]{0:T(256)(128)(2,1)S(1)}, bf16[6]{0:T(256)(128)(2,1)}, u32[]{:S(2)}) copy-start(bf16[6]{0:T(256)(128)(2,1)} %param.22) | copy-start | bytes 40
  0.7 10.1 %copy-start.12 = (bf16[384]{0:T(512)(128)(2,1)S(1)}, bf16[384]{0:T(512)(128)(2,1)}, u32[]{:S(2)}) copy-start(bf16[384]{0:T(512)(128)(2,1)} %param.23) | copy-start | bytes 2308
  0.7 15.9 %copy-start.6 = (bf16[1,256,768]{2,1,0:T(8,128)(2,1)S(1)}, bf16[1,256,768]{2,1,0:T(8,128)(2,1)}, u32[]{:S(2)}) copy-start(bf16[1,256,768]{2,1,0:T(8,128)(2,1)} %param.15) | copy-start | bytes 1179652
  0.7 17.4 %copy-start.23 = (bf16[6]{0:T(256)(128)(2,1)S(1)}, bf16[6]{0:T(256)(128)(2,1)}, u32[]{:S(2)}) copy-start(bf16[6]{0:T(256)(128)(2,1)} %param.21) | copy-start | bytes 40
  0.7 17.9 %copy-start.24 = (bf16[6]{0:T(256)(128)(2,1)S(1)}, bf16[6]{0:T(256)(128)(2,1)}, u32[]{:S(2)}) copy-start(bf16[6]{0:T(256)(128)(2,1)} %param.20) | copy-start | bytes 40
  3.6 11.3 %collective-permute-start = (bf16[272,768]{1,0:T(8,128)(2,1)}, bf16[272,768]{1,0:T(8,128)(2,1)S(1)}, u32[]{:S(2)}, u32[]{:S(2)}) collective-permute-start(bf16[272,768]{1,0:T(8,128)(2,1)} %get-tuple-element.74.t0), channel_id=1, source_target_pairs={{0,64},{32,96},{64,0},{96,32},{1,65},{33,97},{65,1},{97,33},{2,66}... | collective-permute-start | bytes 1253384 | tf_op jit(solution)/shard_map/ppermute | solution.py:594
  5.7 10.8 %collective-permute-start.4 = (bf16[272,768]{1,0:T(8,128)(2,1)}, bf16[272,768]{1,0:T(8,128)(2,1)S(1)}, u32[]{:S(2)}, u32[]{:S(2)}) collective-permute-start(bf16[272,768]{1,0:T(8,128)(2,1)} %get-tuple-element.74.t0), channel_id=1, source_target_pairs={{0,32},{32,0},{64,96},{96,64},{1,33},{33,1},{65,97},{97,65},{2,34}... | collective-permute-start | bytes 1253384 | tf_op jit(solution)/shard_map/ppermute | solution.py:594
  6.7 12.4 %collective-permute-start.6 = (bf16[192,1152]{1,0:T(8,128)(2,1)}, bf16[192,1152]{1,0:T(8,128)(2,1)S(1)}, u32[]{:S(2)}, u32[]{:S(2)}) collective-permute-start(bf16[192,1152]{1,0:T(8,128)(2,1)} %get-tuple-element.78), channel_id=1, source_target_pairs={{0,32},{32,0},{64,96},{96,64},{1,33},{33,1},{65,97},{97,65},{2,34}... | collective-permute-start | bytes 1327112 | tf_op jit(solution)/shard_map/ppermute | solution.py:594
  6.7 21.5 %collective-permute-start.7 = (bf16[192,1152]{1,0:T(8,128)(2,1)}, bf16[192,1152]{1,0:T(8,128)(2,1)S(1)}, u32[]{:S(2)}, u32[]{:S(2)}) collective-permute-start(bf16[192,1152]{1,0:T(8,128)(2,1)} %get-tuple-element.79), channel_id=1, source_target_pairs={{0,65},{32,97},{64,1},{96,33},{1,64},{33,96},{65,0},{97,32},{2,67}... | collective-permute-start | bytes 1327112 | tf_op jit(solution)/shard_map/ppermute | solution.py:624
  8.6 20.9 %collective-permute-start.8 = (bf16[192,1152]{1,0:T(8,128)(2,1)}, bf16[192,1152]{1,0:T(8,128)(2,1)S(1)}, u32[]{:S(2)}, u32[]{:S(2)}) collective-permute-start(bf16[192,1152]{1,0:T(8,128)(2,1)} %get-tuple-element.80), channel_id=1, source_target_pairs={{0,97},{32,65},{64,33},{96,1},{1,96},{33,64},{65,32},{97,0},{2,99}... | collective-permute-start | bytes 1327112 | tf_op jit(solution)/shard_map/ppermute | solution.py:624
  14.9 14.6 %copy-start.17 = (bf16[272,768]{1,0:T(8,128)(2,1)}, bf16[272,768]{1,0:T(8,128)(2,1)S(1)}, u32[]{:S(2)}) copy-start(bf16[272,768]{1,0:T(8,128)(2,1)S(1)} %collective-permute-done.t2) | copy-start | bytes 1253380
  14.9 14.6 %collective-permute-start.5 = (bf16[272,768]{1,0:T(8,128)(2,1)S(1)}, bf16[272,768]{1,0:T(8,128)(2,1)S(1)}, u32[]{:S(2)}, u32[]{:S(2)}) collective-permute-start(bf16[272,768]{1,0:T(8,128)(2,1)S(1)} %collective-permute-done.t2), channel_id=1, source_target_pairs={{0,32},{32,0},{64,96},{96,64},{1,33},{33,1},{65,97},{97,65},{2,34}... | collective-permute-start | bytes 1253384 | tf_op jit(solution)/shard_map/ppermute | solution.py:594
  16.5 13.0 %copy-start.18 = (bf16[272,768]{1,0:T(8,128)(2,1)}, bf16[272,768]{1,0:T(8,128)(2,1)S(1)}, u32[]{:S(2)}) copy-start(bf16[272,768]{1,0:T(8,128)(2,1)S(1)} %collective-permute-done.4.t1) | copy-start | bytes 1253380
  16.6 10.8 %collective-permute-start.2 = (bf16[256,768]{1,0:T(8,128)(2,1)S(1)}, bf16[256,768]{1,0:T(8,128)(2,1)S(1)}, u32[]{:S(2)}, u32[]{:S(2)}) collective-permute-start(bf16[256,768]{1,0:T(8,128)(2,1)S(1)} %bitcast.50), channel_id=1, source_target_pairs={{0,64},{32,96},{64,0},{96,32},{1,65},{33,97},{65,1},{97,33},{2,66}... | collective-permute-start | bytes 1179656 | tf_op jit(solution)/shard_map/ppermute | solution.py:594
  19.1 10.4 %copy-start.14 = (bf16[192,1152]{1,0:T(8,128)(2,1)}, bf16[192,1152]{1,0:T(8,128)(2,1)S(1)}, u32[]{:S(2)}) copy-start(bf16[192,1152]{1,0:T(8,128)(2,1)S(1)} %collective-permute-done.6.w1) | copy-start | bytes 1327108
  19.1 25.6 %collective-permute-start.1 = (bf16[256,768]{1,0:T(8,128)(2,1)S(1)}, bf16[256,768]{1,0:T(8,128)(2,1)S(1)}, u32[]{:S(2)}, u32[]{:S(2)}) collective-permute-start(bf16[256,768]{1,0:T(8,128)(2,1)S(1)} %bitcast.51), channel_id=1, source_target_pairs={{0,32},{32,0},{64,96},{96,64},{1,33},{33,1},{65,97},{97,65},{2,34}... | collective-permute-start | bytes 1179656 | tf_op jit(solution)/shard_map/ppermute | solution.py:594
  27.4 17.3 %copy-start.20 = (bf16[256,768]{1,0:T(8,128)(2,1)}, bf16[256,768]{1,0:T(8,128)(2,1)S(1)}, u32[]{:S(2)}) copy-start(bf16[256,768]{1,0:T(8,128)(2,1)S(1)} %collective-permute-done.2.c2) | copy-start | bytes 1179652
  27.4 17.4 %collective-permute-start.3 = (bf16[256,768]{1,0:T(8,128)(2,1)S(1)}, bf16[256,768]{1,0:T(8,128)(2,1)S(1)}, u32[]{:S(2)}, u32[]{:S(2)}) collective-permute-start(bf16[256,768]{1,0:T(8,128)(2,1)S(1)} %collective-permute-done.2.c2), channel_id=1, source_target_pairs={{0,32},{32,0},{64,96},{96,64},{1,33},{33,1},{65,97},{97,65},{2,34}... | collective-permute-start | bytes 1179656 | tf_op jit(solution)/shard_map/ppermute | solution.py:594
  28.2 1.4 copy-start.15
  29.5 0.8 copy-start.16
  29.5 0.9 copy-start.19
  44.7 0.7 copy-start.21
  44.7 0.9 copy-start.22
  71.1 11.7 %collective-permute-start.9 = (bf16[512,768]{1,0:T(8,128)(2,1)}, bf16[512,768]{1,0:T(8,128)(2,1)S(1)}, u32[]{:S(2)}, u32[]{:S(2)}) collective-permute-start(bf16[512,768]{1,0:T(8,128)(2,1)} %get-tuple-element.101), channel_id=1, source_target_pairs={{0,32},{32,0},{64,96},{96,64},{1,33},{33,1},{65,97},{97,65},{2,34}... | collective-permute-start | bytes 2359304 | tf_op jit(solution)/shard_map/ppermute | solution.py:594
  72.4 30.7 %all-to-all-start = ((bf16[32,144,128]{2,1,0:T(8,128)(2,1)}), bf16[32,144,128]{2,1,0:T(8,128)(2,1)S(1)}, u32[]{:S(2)}, u32[]{:S(2)}) async-start(bf16[32,144,128]{2,1,0:T(8,128)(2,1)} %bitcast.47), calls=%async_computation | async-start | bytes 2359296 | tf_op jit(solution)/shard_map/all_to_all | solution.py:742
  82.7 1.0 copy-start.5
  83.8 20.5 %collective-permute-start.10 = (bf16[256,768]{1,0:T(8,128)(2,1)S(1)}, bf16[256,768]{1,0:T(8,128)(2,1)S(1)}, u32[]{:S(2)}, u32[]{:S(2)}) collective-permute-start(bf16[256,768]{1,0:T(8,128)(2,1)S(1)} %fusion.6), channel_id=1, source_target_pairs={{0,64},{32,96},{64,0},{96,32},{1,65},{33,97},{65,1},{97,33},{2,66}... | collective-permute-start | bytes 1179656 | tf_op jit(solution)/shard_map/ppermute | solution.py:594
  104.3 1.2 copy-start.9
  105.5 30.0 %all-to-all-start.1 = ((bf16[32,144,128]{2,1,0:T(8,128)(2,1)}), bf16[32,144,128]{2,1,0:T(8,128)(2,1)S(1)}, u32[]{:S(2)}, u32[]{:S(2)}) async-start(bf16[32,144,128]{2,1,0:T(8,128)(2,1)} %broadcast_in_dim.9), calls=%async_computation.1 | async-start | bytes 2359296 | tf_op jit(solution)/shard_map/all_to_all | solution.py:742
  131.0 3.3 %collective-permute-start.14 = (bf16[512,768]{1,0:T(8,128)(2,1)}, bf16[512,768]{1,0:T(8,128)(2,1)S(1)}, u32[]{:S(2)}, u32[]{:S(2)}) collective-permute-start(bf16[512,768]{1,0:T(8,128)(2,1)} %get-tuple-element.118), channel_id=1, source_target_pairs={{0,32},{32,0},{64,96},{96,64},{1,33},{33,1},{65,97},{97,65},{2,34}... | collective-permute-start | bytes 2359304 | tf_op jit(solution)/shard_map/ppermute | solution.py:594
  135.5 9.7 %copy-start.4 = (bf16[256,768]{1,0:T(8,128)(2,1)S(1)}, bf16[256,768]{1,0:T(8,128)(2,1)}, u32[]{:S(2)}) copy-start(bf16[256,768]{1,0:T(8,128)(2,1)} %get-tuple-element.119) | copy-start | bytes 1179652
  135.5 27.4 %all-to-all-start.2 = ((bf16[32,128,128]{2,1,0:T(8,128)(2,1)}), bf16[32,128,128]{2,1,0:T(8,128)(2,1)S(1)}, u32[]{:S(2)}, u32[]{:S(2)}) async-start(bf16[32,128,128]{2,1,0:T(8,128)(2,1)} %get-tuple-element.115), calls=%async_computation.2 | async-start | bytes 2097152 | tf_op jit(solution)/shard_map/all_to_all | solution.py:742
  147.1 4.2 %copy-start.25 = (bf16[192]{0:T(256)(128)(2,1)S(1)}, bf16[192]{0:T(256)(128)(2,1)}, u32[]{:S(2)}) copy-start(bf16[192]{0:T(256)(128)(2,1)} %gain_in.1) | copy-start | bytes 1156
  147.1 4.7 %copy-start.11 = (f32[1,768]{1,0:T(1,128)S(1)}, f32[1,768]{1,0:T(1,128)}, u32[]{:S(2)}) copy-start(f32[1,768]{1,0:T(1,128)} %get-tuple-element.123) | copy-start | bytes 9220
  147.1 18.1 %collective-permute-start.15 = (bf16[256,768]{1,0:T(8,128)(2,1)}, bf16[256,768]{1,0:T(8,128)(2,1)S(1)}, u32[]{:S(2)}, u32[]{:S(2)}) collective-permute-start(bf16[256,768]{1,0:T(8,128)(2,1)} %fusion.5), channel_id=1, source_target_pairs={{0,64},{32,96},{64,0},{96,32},{1,65},{33,97},{65,1},{97,33},{2,66}... | collective-permute-start | bytes 1179656 | tf_op jit(solution)/shard_map/ppermute | solution.py:594
  148.8 16.4 %collective-permute-start.11 = (bf16[576,128]{1,0:T(8,128)(2,1)}, bf16[576,128]{1,0:T(8,128)(2,1)}, u32[]{:S(2)}, u32[]{:S(2)}) collective-permute-start(bf16[576,128]{1,0:T(8,128)(2,1)} %get-tuple-element.154), channel_id=1, source_target_pairs={{0,32},{32,0},{64,96},{96,64},{1,33},{33,1},{65,97},{97,65},{2,34}... | collective-permute-start | bytes 442376 | tf_op jit(solution)/shard_map/ppermute | solution.py:594
  149.7 18.8 %collective-permute-start.12 = (bf16[576,128]{1,0:T(8,128)(2,1)S(1)}, bf16[576,128]{1,0:T(8,128)(2,1)}, u32[]{:S(2)}, u32[]{:S(2)}) collective-permute-start(bf16[576,128]{1,0:T(8,128)(2,1)S(1)} %get-tuple-element.153), channel_id=1, source_target_pairs={{0,64},{32,96},{64,0},{96,32},{1,65},{33,97},{65,1},{97,33},{2,66}... | collective-permute-start | bytes 442376 | tf_op jit(solution)/shard_map/ppermute | solution.py:594
  151.2 21.0 %collective-permute-start.13 = (bf16[576,128]{1,0:T(8,128)(2,1)S(1)}, bf16[576,128]{1,0:T(8,128)(2,1)}, u32[]{:S(2)}, u32[]{:S(2)}) collective-permute-start(bf16[576,128]{1,0:T(8,128)(2,1)S(1)} %get-tuple-element.152), channel_id=1, source_target_pairs={{0,96},{32,64},{64,32},{96,0},{1,97},{33,65},{65,33},{97,1},{2,98}... | collective-permute-start | bytes 442376 | tf_op jit(solution)/shard_map/ppermute | solution.py:594
  172.2 11.7 %copy-start.1 = (bf16[2304,128]{1,0:T(8,128)(2,1)S(1)}, bf16[2304,128]{1,0:T(8,128)(2,1)}, u32[]{:S(2)}) copy-start(bf16[2304,128]{1,0:T(8,128)(2,1)} %get-tuple-element.150) | copy-start | bytes 1769476
  173.3 29.3 %all-to-all-start.3 = ((bf16[128,32,128]{2,1,0:T(8,128)(2,1)}), bf16[128,32,128]{2,1,0:T(8,128)(2,1)}, u32[]{:S(2)}, u32[]{:S(2)}) async-start(bf16[128,32,128]{2,1,0:T(8,128)(2,1)} %bitcast.16), calls=%async_computation.3 | async-start | bytes 2097152 | tf_op jit(solution)/shard_map/all_to_all | solution.py:818
  184.3 1.4 copy-start.2
  184.3 1.4 copy-start.3
  185.7 1.1 copy-start
  185.7 1.2 copy-start.7
  185.7 1.3 copy-start.8
  185.7 1.4 copy-start.10

commit v3 on v2

--- a/solution.py
+++ b/solution.py
@@ -18,6 +18,7 @@
 XW = HL * HP
 CL = XW + 2 * NS
 PW = XW + CL + 128
+CUT = 640
 epsilon = 1e-05
 f32 = jnp.float32
 bf16 = jnp.bfloat16
@@ -97,9 +98,11 @@
             target[...] = value
 
 
-def columns_kernel(me, w_in, tok, taps, bias, gain_in, seg, w0, w1, w2, w3, out, rows):
+def columns_kernel(
+    me, w_in, tok, taps, bias, gain_in, seg, w0, w1, w2, w3a, w3b, out, rows, last
+):
     g = me[0]
-    for d, send in enumerate((w0, w1, w2, w3)):
+    for d, send in enumerate((w0, w1, w2, last)):
         start = (g ^ d) * XW
         send[:, :XW] = w_in[:, pl.ds(pl.multiple_of(start, 128), XW)]
         send[:, XW : 2 * XW] = w_in[:, pl.ds(pl.multiple_of(DI + start, 128), XW)]
@@ -107,6 +110,8 @@
         send[:, XW + CL :] = jnp.concatenate(
             [w_in[:, DI + CW :], jnp.zeros((192, 128 - NH), bf16)], axis=1
         )
+    w3a[...] = last[:, :CUT]
+    w3b[...] = last[:, CUT:]
     out[0:ROWS, :] = tok[...]
     rows[...] = jnp.zeros_like(rows)
     rows[0:4, 0:448] = taps[...].astype(f32)
@@ -158,7 +163,7 @@
 
 
 def forward_kernel(
-    me, t0, t1, t2, t3, w0, w1, w2, w3, dtb, rate, skip,
+    me, t0, t1, t2, t3, w0, w1, w2, w3a, w3b, dtb, rate, skip,
     w_full, normed, proj, v_out, states, y_out, pos, taps, gain_in,
     tok, state, ext, wide, seg,
 ):
@@ -170,10 +175,14 @@
         row_at = lax.broadcasted_iota(jnp.int32, (128, 128), 0)
         lane_at = lax.broadcasted_iota(jnp.int32, (128, 128), 1)
         chosen = ((row_at == lane_at + g * HL) & (lane_at < HL)).astype(bf16)
-        for d, part in enumerate((w0, w1, w2, w3)):
+        for d, part in enumerate((w0, w1, w2)):
             rows = pl.ds(pl.multiple_of((g ^ d) * 192, 64), 192)
             w_full[rows, : XW + CL] = part[:, : XW + CL]
             w_full[rows, XW + CL :] = mm(part[:, XW + CL :], chosen, NN).astype(bf16)
+        rows = pl.ds(pl.multiple_of((g ^ 3) * 192, 64), 192)
+        w_full[rows, :CUT] = w3a[...]
+        w_full[rows, CUT : XW + CL] = w3b[:, : XW + CL - CUT]
+        w_full[rows, XW + CL :] = mm(w3b[:, XW + CL - CUT :], chosen, NN).astype(bf16)
         state[...] = jnp.zeros_like(state)
         ext[0:8, :] = jnp.zeros((8, CL), f32)
         gather_short(g, (t0, t1, t2, t3), taps, gain_in, pos, wide, seg)
@@ -248,21 +257,28 @@
     stats[0] = both.T[0:8, :]
 
 
+def branch_kernel(me, gate_in, y_in, gain_out, w_out, o_own, o_pair, o_across):
+    gate = gate_in[...].astype(f32)
+    gated = y_in[...] * (gate * jax.nn.sigmoid(gate)) * gain_out[...]
+    value = mm(gated, w_out[...], NN).astype(bf16)
+    put(me[0] ^ pl.program_id(0), o_own, o_pair, o_across, value)
+
+
 def out_kernel(
-    me, c0, c1, c2, c3, gate_in, y_in, dno_in, stats, gain_out, w_out, normed,
-    bundle, d_gate, dy_out, sums, o_own, o_pair, o_across,
-    cot, acc_out, acc_gate, acc_sum, normed_out,
+    me, c0, c1, c2, c3, gate_in, y_in, dno_in, s0, s1, s2, s3, gain_out,
+    bundle, d_gate, dy_out, sums,
+    cot, acc_out, acc_sum, normed_out,
 ):
     i = pl.program_id(0)
     g = me[0]
 
     @pl.when(i == 0)
     def _():
-        for ref in (acc_out, acc_gate, acc_sum):
+        for ref in (acc_out, acc_sum):
             ref[...] = jnp.zeros_like(ref)
 
     pick(g ^ i, (c0, c1, c2, c3), cot)
-    totals = to_columns(stats[0])
+    totals = to_columns((s0[0] + s1[0]) + (s2[0] + s3[0]))
     for s in range(ROWS // SPAN):
         rows = slice(s * SPAN, (s + 1) * SPAN)
         rms = lax.rsqrt(totals[:, 2 * s : 2 * s + 1] * (1.0 / DI) + epsilon)
@@ -280,21 +296,12 @@
         dy_out[rows, :] = d_gated * silu
         d_gate[rows, :] = (d_gated * y * (sig * (1.0 + gate * (1.0 - sig)))).astype(bf16)
     acc_out[...] += mm(normed_out[...], cot[...], TN)
-    acc_gate[...] += mm(normed[...], d_gate[...], TN)
-    put(g ^ i, o_own, o_pair, o_across, mm(normed_out[...], w_out[...], NN).astype(bf16))
 
     @pl.when(i == pl.num_programs(0) - 1)
     def _():
         sums[...] = acc_sum[...]
-        for k in range(4):
-            for t in range(3):
-                at = 576 * k + 192 * t
-                bundle[at : at + 192, :] = acc_gate[
-                    192 * k : 192 * k + 192, 128 * t : 128 * t + 128
-                ].astype(bf16)
         for t in range(6):
-            at = 2304 + XW * t
-            bundle[at : at + XW, :] = acc_out[:, 128 * t : 128 * t + 128].astype(bf16)
+            bundle[XW * t : XW * t + XW, :] = acc_out[:, 128 * t : 128 * t + 128].astype(bf16)
 
 
 def split_sum(rows, ones):
@@ -403,32 +410,13 @@
     ext[ROWS:, :] = ext[0:8, :]
     d_normed = mm(d_proj[...], w_full[...], NT)
     add(9, down(d_normed * normed[...].astype(f32)))
-    acc_in[...] += mm(normed[...], d_proj[:, XW : XW + CL], TN)
+    acc_in[...] += mm(normed[...], d_proj[:, : XW + CL], TN)
     acc_dt[...] += mm(d_proj[:, XW + CL :], normed[...], TN)[0:8, :]
     return d_normed.astype(bf16)
 
 
-def late_kernel(
-    w_full, normed, proj, v_in, states, dy_in, d_gate, pos, taps, dtb, rate, skip, ones,
-    d_state, edge, acc_in, acc_dt, acc_small, d_normed,
-    ext, d_proj,
-):
-    @pl.when(pl.program_id(0) == 0)
-    def _():
-        for ref in (d_state, acc_in, acc_dt, acc_small):
-            ref[...] = jnp.zeros_like(ref)
-        ext[ROWS:, :] = jnp.zeros((8, CL), f32)
-
-    d_normed[...] = backward_block(
-        w_full, normed, proj, v_in, states, dy_in, d_gate, pos, taps, dtb, rate, skip, ones,
-        d_state, ext, acc_in, acc_dt, acc_small, d_proj,
-    )
-    edge[...] = ext[ROWS:, :]
-
-
-def early_kernel(
-    me, w_full, normed, proj, v_in, states, dy_in, d_gate, pos, taps, dtb, rate, skip, ones,
-    d_state_in, edge, acc_in_in, acc_dt_in, acc_small_in, d_normed_in, sums,
+def backward_kernel(
+    me, w_full, normed, proj, v_in, states, dy_in, d_gate, pos, taps, dtb, rate, skip, ones, sums,
     bundle, n_own, n_pair, n_across,
     d_state, ext, acc_in, acc_dt, acc_small, d_proj, small,
 ):
@@ -437,14 +425,9 @@
 
     @pl.when(pl.program_id(0) == 0)
     def _():
-        d_state[...] = d_state_in[...]
-        ext[ROWS:, :] = edge[...]
-        acc_in[...] = acc_in_in[...]
-        acc_dt[...] = acc_dt_in[...]
-        acc_small[...] = acc_small_in[...]
-        small[...] = jnp.zeros_like(small)
-        for j in range(2):
-            put(g ^ (2 + j), n_own, n_pair, n_across, d_normed_in[ROWS * j : ROWS * j + ROWS, :])
+        for ref in (d_state, acc_in, acc_dt, acc_small, small):
+            ref[...] = jnp.zeros_like(ref)
+        ext[ROWS:, :] = jnp.zeros((8, CL), f32)
 
     value = backward_block(
         w_full, normed, proj, v_in, states, dy_in, d_gate, pos, taps, dtb, rate, skip, ones,
@@ -454,74 +437,75 @@
 
     @pl.when(i == 0)
     def _():
-        def place(k, piece, value):
-            at = 32 * k + 16 * (piece % 2)
-            bundle[piece // 2, at : at + 16, :] = value.astype(bf16)
-
-        def lay(start, source, row, first, tiles):
-            for t in range(tiles):
-                lanes = slice(first + 128 * t, first + 128 * t + 128)
-                small[start + t : start + t + 1, :] = source[row : row + 1, lanes]
+        def lay(start, source, row, tiles):
+            for k in range(4):
+                for t in range(tiles):
+                    small[k, start + t : start + t + 1, :] = source[
+                        row : row + 1, 128 * t : 128 * t + 128
+                    ]
 
         for j in range(4):
-            lay(16 + 5 * j, acc_small, 5 + j, 0, 5)
-        lay(36, acc_small, 4, 0, 5)
-        lay(43, sums, 0, 0, 3)
-        lay(46, acc_small, 1, 0, 3)
-        lay(49, acc_small, 2, 0, 1)
-        lay(50, acc_small, 3, 0, 1)
+            lay(16 + 5 * j, acc_small, 5 + j, 5)
+        lay(36, acc_small, 4, 5)
+        lay(43, sums, 0, 3)
+        lay(46, acc_small, 1, 3)
+        lay(49, acc_small, 2, 1)
+        lay(50, acc_small, 3, 1)
         for k in range(4):
-            for tile in range(5):
-                for q in range(12):
-                    place(
-                        k,
-                        12 * tile + q,
-                        acc_in[
-                            192 * k + 16 * q : 192 * k + 16 * q + 16,
-                            128 * tile : 128 * tile + 128,
-                        ],
-                    )
+            for tile in range(8):
+                for q in range(4):
+                    bundle[4 * tile + q, 48 * k : 48 * k + 48, :] = acc_in[
+                        192 * k + 48 * q : 192 * k + 48 * q + 48, 128 * tile : 128 * tile + 128
+                    ].astype(bf16)
+            first, second = 192 * k, 192 * k + 128
             for h in range(HL):
-                small[2 * h : 2 * h + 1, :] = acc_dt[h : h + 1, 192 * k : 192 * k + 128]
-                small[2 * h + 1 : 2 * h + 2, 0:64] = acc_dt[
-                    h : h + 1, 192 * k + 128 : 192 * k + 192
-                ]
-            small[41:42, :] = acc_small[9:10, 192 * k : 192 * k + 128]
-            small[42:43, 0:64] = acc_small[9:10, 192 * k + 128 : 192 * k + 192]
-            for q in range(4):
-                place(k, 60 + q, small[16 * q : 16 * q + 16, :])
+                small[k, 2 * h : 2 * h + 1, :] = acc_dt[h : h + 1, first : first + 128]
+                small[k, 2 * h + 1 : 2 * h + 2, 0:64] = acc_dt[h : h + 1, second : second + 64]
+            small[k, 41:42, :] = acc_small[9:10, first : first + 128]
+            small[k, 42:43, 0:64] = acc_small[9:10, second : second + 64]
+        for r in range(32):
+            if r < 16:
+                value = jnp.concatenate([small[k, 4 * r : 4 * r + 4, :] for k in range(4)], axis=0)
+            else:
+                value = jnp.zeros((16, 128), f32)
+            bundle[r, 192:208, :] = value.astype(bf16)
+
+
+def w_out_kernel(place, p0, p1, p2, p3, grad_out):
+    for d, part in enumerate((p0, p1, p2, p3)):
+        source = (place[0] + 4 - d) % 4
+        for j in range(3):
+            half = 3 * source + j
+            rows = pl.ds(pl.multiple_of((half % 2) * 192, 64), 192)
+            lanes = pl.ds(pl.multiple_of((half // 2) * 128, 128), 128)
+            grad_out[rows, lanes] = part[192 * j : 192 * j + 192, :].astype(f32)
 
 
 def assemble_kernel(
-    me, gates0, gates1, gates2, gates3, parts, gain_in,
-    grad_in, grad_kernel, grad_bias, grad_gain_in, grad_gain_out, grad_skip,
-    grad_dt, grad_log,
+    me, parts, shorts, gain_in,
+    grad_in, grad_kernel, grad_bias, grad_gain_in, grad_gain_out, grad_skip, grad_dt, grad_log,
     wide, turned,
 ):
     g = me[0]
-
-    def piece(k, row, count=192):
-        return parts[k, row : row + count, :].astype(f32)
-
-    for d, gates in enumerate((gates0, gates1, gates2, gates3)):
-        for t in range(3):
-            start = pl.multiple_of((g ^ d) * XW + 128 * t, 128)
-            grad_in[:, pl.ds(start, 128)] = gates[192 * t : 192 * t + 192, :].astype(f32)
-    for k in range(4):
-        for t in range(3):
-            lanes = slice(DI + k * XW + 128 * t, DI + k * XW + 128 * t + 128)
-            grad_in[:, lanes] = piece(k, 192 * t)
-    for t in range(3, 5):
-        lanes = slice(2 * DI + 128 * (t - 3), 2 * DI + 128 * (t - 2))
-        grad_in[:, lanes] = (piece(0, 192 * t) + piece(1, 192 * t)) + (
-            piece(2, 192 * t) + piece(3, 192 * t)
-        )
+    for tile in range(8):
+        for q in range(4):
+            pieces = [parts[32 * k + 4 * tile + q, 0:48, :].astype(f32) for k in range(4)]
+            rows = slice(48 * q, 48 * q + 48)
+            if tile < 6:
+                for k in range(4):
+                    start = (tile // 3) * DI + k * XW + (tile % 3) * 128
+                    grad_in[rows, start : start + 128] = pieces[k]
+            else:
+                start = 2 * DI + 128 * (tile - 6)
+                grad_in[rows, start : start + 128] = (pieces[0] + pieces[1]) + (
+                    pieces[2] + pieces[3]
+                )
 
     turned[...] = jnp.zeros_like(turned)
     wide[...] = jnp.zeros_like(wide)
     gain = jnp.zeros((2, 128), f32)
     for k in range(4):
-        rest = piece(k, 960, 64)
+        rest = shorts[k]
         for h in range(HL):
             at = HL * k + h
             turned[at : at + 1, 0:128] = rest[2 * h : 2 * h + 1, :]
@@ -544,9 +528,8 @@
             grad_kernel[...] = wide[0:4, 448 * k : 448 * k + 448]
             grad_bias[...] = wide[4:5, 448 * k : 448 * k + 448]
 
-    own = parts[g, 960:1024, :].astype(f32)
-    for t in range(3):
-        grad_gain_out[:, 128 * t : 128 * t + 128] = own[43 + t : 44 + t, :]
+    own = shorts[g]
+    grad_gain_out[...] = jnp.concatenate([own[43 + t : 44 + t, :] for t in range(3)], axis=1).reshape(XW)
     lane_at = lax.broadcasted_iota(jnp.int32, (1, 128), 1)
     skips = jnp.zeros((1, 128), f32)
     for t in range(3):
@@ -606,14 +589,15 @@
     part = whole((ROWS, D))
     blocks = 4
 
-    w0, w1, w2, w3, both0 = call(
+    w0, w1, w2, w3a, w3b, both0 = call(
         columns_kernel,
         "columns",
         2,
         in_specs=[scalar_spec] + [vmem_spec] * 6,
-        out_specs=[vmem_spec] * 5,
-        out_shape=(shape((192, PW), bf16),) * 4 + (shape((ROWS + 16, D), bf16),),
-        scratch_shapes=[pltpu.VMEM((16, D), f32)],
+        out_specs=[vmem_spec] * 6,
+        out_shape=(shape((192, PW), bf16),) * 3
+        + (shape((192, CUT), bf16), shape((192, PW - CUT), bf16), shape((ROWS + 16, D), bf16)),
+        scratch_shapes=[pltpu.VMEM((16, D), f32), pltpu.VMEM((192, PW), bf16)],
     )(
         me, w_in, tok, kernel, conv_bias, gain_in,
         segments.reshape(1, ROWS),
@@ -625,14 +609,15 @@
 
     w2 = across(w2, 2)
     both2 = among(both0, 2)
-    w3 = across(w3, 3)
+    w3b = across(w3b, 3)
+    w3a = among(w3a, 3)
+    both2, both0, cot_late, w1 = lax.optimization_barrier((both2, both0, cot, w1))
     w1 = among(w1, 1)
     both1 = among(both0, 1)
-    both2, cot_late = lax.optimization_barrier((both2, cot))
     both3 = among(both2, 1)
     c2 = among(cot_late, 2)
     c1 = among(cot_late, 1)
-    c3 = among(c2, 1)
+    c3 = among(cot_late, 3)
     length = blocks * ROWS
     spans = length // SPAN
 
@@ -647,10 +632,13 @@
     by_owner_specs = [part, whole((2 * ROWS, D)), part]
     by_owner_shapes = tuple(shape((n * ROWS, D), bf16) for n in (1, 2, 1))
 
-    def to_owner(own, pair, over):
-        got = among(pair, 1).astype(f32)
-        other = (over.astype(f32) + got[ROWS:]).astype(bf16)
-        return own, got[:ROWS], among(other, 2)
+    def to_core(own, pair, over):
+        got = among(pair, 1)
+        other = (over.astype(f32) + got[ROWS:].astype(f32)).astype(bf16)
+        return own, got[:ROWS], other
+
+    def to_owner(own, got, other):
+        return own, got, among(other, 2)
 
     w_full, normed, proj, v_rows, states, y_rows, pos, taps, gain_in_all = call(
         forward_kernel,
@@ -659,7 +647,8 @@
         grid=(blocks,),
         in_specs=[scalar_spec]
         + [whole((ROWS + 16, D))] * 4
-        + [whole((192, PW))] * 4
+        + [whole((192, PW))] * 3
+        + [whole((192, CUT)), whole((192, PW - CUT))]
         + [whole((1, 128)), whole((1, 128)), whole((1, XW))],
         out_specs=[
             whole((D, PW)),
@@ -691,7 +680,7 @@
             pltpu.VMEM((8, 128), f32),
         ],
     )(
-        me, both0, both1, both2, both3, w0, w1, w2, w3, dtb, rate, skip,
+        me, both0, both1, both2, both3, w0, w1, w2, w3a, w3b, dtb, rate, skip,
     )
 
     gate_spec = pl.BlockSpec((ROWS, XW), lambda i: (i, 0))
@@ -707,55 +696,65 @@
         out_shape=(shape((length, XW), f32), shape((blocks, 8, SPAN), f32)),
         scratch_shapes=[pltpu.VMEM((ROWS, D), bf16)],
     )(me, cot, c1, c2, c3, proj, y_rows, gain_o, w_out)
-    stats = lax.psum(stats, "group")
-
-    bundle1, d_gate, dy, sums, *o_parts = call(
+    all_stats = [stats] + [among(stats, d) for d in range(1, 4)]
+
+    o_parts = call(
+        branch_kernel,
+        "branch",
+        3,
+        grid=(blocks,),
+        in_specs=[
+            scalar_spec, gate_spec, blocked((ROWS, XW), up), whole((1, XW)), whole((XW, D)),
+        ],
+        out_specs=by_owner_specs,
+        out_shape=by_owner_shapes,
+    )(me, proj, y_rows, gain_o, w_out)
+    o_parts, all_stats = lax.optimization_barrier((o_parts, all_stats))
+
+    bundle1, d_gate, dy, sums = call(
         out_kernel,
         "out",
-        7,
+        6,
         grid=(blocks,),
         in_specs=[scalar_spec]
         + [part] * 4
-        + [
-            gate_spec, blocked((ROWS, XW), up), blocked((ROWS, XW), up),
-            blocked((1, 8, SPAN), up), whole((1, XW)), whole((XW, D)), blocked((ROWS, D), up),
+        + [gate_spec, blocked((ROWS, XW), up), blocked((ROWS, XW), up)]
+        + [blocked((1, 8, SPAN), up)] * 4
+        + [whole((1, XW))],
+        out_specs=[
+            whole((2304, 128)), blocked((ROWS, XW), up), blocked((ROWS, XW), up), whole((8, XW)),
         ],
-        out_specs=[
-            whole((4608, 128)), blocked((ROWS, XW), up), blocked((ROWS, XW), up), whole((8, XW)),
-        ]
-        + by_owner_specs,
         out_shape=(
-            shape((4608, 128), bf16), shape((length, XW), bf16), shape((length, XW), f32),
+            shape((2304, 128), bf16), shape((length, XW), bf16), shape((length, XW), f32),
             shape((8, XW), f32),
-        )
-        + by_owner_shapes,
+        ),
         scratch_shapes=[
             pltpu.VMEM((ROWS, D), bf16),
             pltpu.VMEM((XW, D), f32),
-            pltpu.VMEM((D, XW), f32),
             pltpu.VMEM((8, XW), f32),
             pltpu.VMEM((ROWS, XW), bf16),
         ],
-    )(me, cot, c1, c2, c3, proj, y_rows, dno, stats, gain_o, w_out, normed)
+    )(me, cot, c1, c2, c3, proj, y_rows, dno, *all_stats, gain_o)
 
     def spread(value):
         return lax.all_to_all(value, "rep", 0, 0, tiled=True)
 
-    received1 = spread(bundle1.reshape(reps, 144, 128))
-    branches = to_owner(*o_parts)
-
+    received1 = spread(bundle1.reshape(reps, 72, 128))
+    branches = to_core(*o_parts)
+    dy, branches = lax.optimization_barrier((dy, branches))
+    branches = to_owner(*branches)
     ones = jnp.asarray(np.arange(XW)[:, None] // HP == np.arange(128)[None, :], bf16)
-    half = blocks // 2
-    shared = [
-        shape((NS, XW), f32), shape((8, CL), f32), shape((D, CL), f32), shape((8, D), f32),
-        shape((16, D), f32),
-    ]
-
-    def backward_specs(last):
-        def back(i):
-            return last - i
-
-        return [
+
+    def back(i):
+        return blocks - 1 - i
+
+    bundle2, *n_parts = call(
+        backward_kernel,
+        "backward",
+        26,
+        grid=(blocks,),
+        in_specs=[
+            scalar_spec,
             whole((D, PW)),
             blocked((ROWS, D), back),
             blocked((ROWS, PW), back),
@@ -765,67 +764,77 @@
             blocked((ROWS, XW), back),
             blocked((2, 16, SPAN), back),
             whole((8, CL)), whole((1, 128)), whole((1, 128)), whole((1, XW)), whole((XW, 128)),
-        ]
-
-    operands = (w_full, normed, proj, v_rows, states, dy, d_gate, pos, taps, dtb, rate, skip, ones)
-    handed = call(
-        late_kernel,
-        "late",
-        12,
-        grid=(half,),
-        in_specs=backward_specs(blocks - 1),
-        out_specs=[whole(v.shape) for v in shared]
-        + [blocked((ROWS, D), lambda i: half - 1 - i)],
-        out_shape=shared + [shape((half * ROWS, D), bf16)],
-        scratch_shapes=[pltpu.VMEM((ROWS + 8, CL), f32), pltpu.VMEM((ROWS, PW), bf16)],
-    )(*operands)
-
-    def total(received):
-        return jnp.sum(received.astype(f32), axis=0).astype(bf16)
-
-    reduced1 = total(received1)
-    reduced1, handed, branches = lax.optimization_barrier((reduced1, handed, branches))
-    flat1 = spread(jnp.broadcast_to(reduced1[None], (reps, 144, 128))).reshape(4608, 128)
-    bundle2, *n_parts = call(
-        early_kernel,
-        "early",
-        12,
-        grid=(half,),
-        in_specs=[scalar_spec]
-        + backward_specs(half - 1)
-        + [whole(v.shape) for v in shared]
-        + [whole((half * ROWS, D)), whole((8, XW))],
-        out_specs=[whole((32, 128, 128))] + by_owner_specs,
-        out_shape=(shape((32, 128, 128), bf16),) + by_owner_shapes,
+            whole((8, XW)),
+        ],
+        out_specs=[whole((32, 208, 128))] + by_owner_specs,
+        out_shape=(shape((32, 208, 128), bf16),) + by_owner_shapes,
         scratch_shapes=[
             pltpu.VMEM((NS, XW), f32),
             pltpu.VMEM((ROWS + 8, CL), f32),
-            pltpu.VMEM((D, CL), f32),
+            pltpu.VMEM((D, XW + CL), f32),
             pltpu.VMEM((8, D), f32),
             pltpu.VMEM((16, D), f32),
             pltpu.VMEM((ROWS, PW), bf16),
-            pltpu.VMEM((64, 128), f32),
+            pltpu.VMEM((4, 64, 128), f32),
         ],
-    )(me, *operands, *handed, sums)
-
-    bundle2, flat1 = lax.optimization_barrier((bundle2, flat1))
+    )(
+        me, w_full, normed, proj, v_rows, states, dy, d_gate, pos, taps, dtb, rate, skip, ones,
+        sums,
+    )
+
+    def total(received):
+        return jnp.sum(received.astype(f32), axis=0).astype(bf16)
+
+    r = lax.axis_index("rep")
+
+    def along(value, step):
+        stride, by = step
+        pairs = [
+            (n, n - (n // stride % 4) * stride + ((n // stride + by) % 4) * stride)
+            for n in range(reps)
+        ]
+        return lax.ppermute(value, "rep", pairs)
+
+    bundle2, received1, branches = lax.optimization_barrier((bundle2, received1, branches))
     received2 = spread(bundle2)
-    d_parts = to_owner(*n_parts)
-    by_member = flat1[:2304].reshape(4, 576, 128)
-    gates = [lax.dynamic_index_in_dim(by_member, g ^ d, 0, keepdims=False) for d in range(4)]
-    gates = [gates[0]] + [among(gates[d], d) for d in range(1, 4)]
-    reduced2, gates, d_parts = lax.optimization_barrier((total(received2), gates, d_parts))
+    d_parts = to_core(*n_parts)
+    d_parts = to_owner(*d_parts)
+    mine = total(received1)
+    other = lax.ppermute(mine, "rep", [(n, n ^ 1) for n in range(reps)])
+    two = jnp.where(r % 2 == 0, jnp.stack([mine, other]), jnp.stack([other, mine]))
+    z_parts = [along(two, (2, by)) for by in (3, 2, 1)] + [two]
+    z_all = jnp.stack(z_parts + z_parts[:3])
+    eight = lax.dynamic_slice_in_dim(z_all, 3 - r // 2 % 4, 4, axis=0).reshape(576, 128)
+    reduced2, eight, d_parts = lax.optimization_barrier((total(received2), eight, d_parts))
+    x_parts = [eight] + [along(eight, (8, by)) for by in (1, 2, 3)]
+    payload = jnp.concatenate(
+        [
+            reduced2[:192].reshape(4, 48, 128),
+            reduced2[192:].reshape(4, 4, 128),
+            jnp.zeros((4, 4, 128), bf16),
+        ],
+        axis=1,
+    )
     parts = lax.all_to_all(
-        jnp.broadcast_to(reduced2.reshape(4, 1, 32, 128), (4, reps, 32, 128)).reshape(
-            4 * reps, 32, 128
-        ),
+        jnp.broadcast_to(payload[:, None], (4, reps, 56, 128)).reshape(4 * reps, 56, 128),
         ("group", "rep"), 0, 0, tiled=True,
-    ).reshape(4, 32 * reps, 128)
-    grad_w_out = flat1[2304:].reshape(6, XW, 128).transpose(1, 0, 2).reshape(XW, D).astype(f32)
+    )
+    shorts = parts.reshape(4, reps, 56, 128)[:, :16, 48:52].astype(f32).reshape(4, 64, 128)
+    place = (r // 8).astype(jnp.int32).reshape(1)
+    grad_w_out = call(
+        w_out_kernel,
+        "w_out",
+        2,
+        in_specs=[scalar_spec] + [vmem_spec] * 4,
+        out_specs=vmem_spec,
+        out_shape=shape((XW, D), f32),
+    )(place, *x_parts)
 
     x = tok.astype(f32)
     branch = sum(value.astype(f32) for value in branches)
-    layer_out = (x + branch).astype(bf16).reshape(tokens.shape)
+    squares = sum(lax.dynamic_index_in_dim(v, g, 0, keepdims=False) for v in all_stats)
+    rms_out = lax.rsqrt(squares[0:4:2].reshape(ROWS, 1) * (1.0 / DI) + epsilon)
+    layer_out = (x + rms_out * branch).astype(bf16).reshape(tokens.shape)
     d_normed = sum(value.astype(f32) for value in d_parts)
     rms_in = lax.rsqrt(jnp.mean(x * x, axis=-1, keepdims=True) + epsilon)
     scaled = d_normed * gain_in_all
@@ -839,15 +848,15 @@
         assemble_kernel,
         "assemble",
         4,
-        in_specs=[scalar_spec] + [vmem_spec] * 6,
+        in_specs=[scalar_spec] + [vmem_spec] * 3,
         out_specs=[vmem_spec] * 8,
         out_shape=(
             shape((192, 3352), f32), shape((4, 448), f32),
-            shape((1, 448), f32), shape((1, 192), f32), shape((1, XW), f32), shape((1, HL), f32),
+            shape((1, 448), f32), shape((1, 192), f32), shape((XW,), f32), shape((1, HL), f32),
             shape((1, HL), f32), shape((1, HL), f32),
         ),
         scratch_shapes=[pltpu.VMEM((8, CW), f32), pltpu.VMEM((128, 256), f32)],
-    )(me, *gates, parts, gain_in.astype(f32).reshape(1, 192))
+    )(me, parts, shorts, gain_in.astype(f32).reshape(1, 192))
     grad_w_in, grad_kernel, grad_bias, grad_gi, grad_go, grad_s, grad_d, grad_l = grads
     return (
         layer_out,
@@ -859,7 +868,7 @@
         grad_d.reshape(-1),
         grad_l.reshape(-1),
         grad_s.reshape(-1),
-        grad_go.reshape(-1),
+        grad_go,
         grad_w_out,
     )
 

time: 208 us -> 198 us (0.952)
  blocking collectives: 10.7 us -> 0 us
  starting transfers between devices: 57.5 us -> 65.6 us
  local copies, waits for them, and re-layouts: 12.2 us -> 7.31 us
  other arithmetic: 7.97 us -> 5.81 us
    ppermute x0 -> x7, waiting for transfers between devices: none -> 25.6 us  [the longest x6 24.4 us: along(): return lax.ppermute(value, 'rep', pairs)]
    ppermute x14 -> x15, waiting for transfers between devices: 23.8 us -> 8.45 us  [among(): return lax.ppermute(value, 'group', [(i, i ^ d) for i in range(4)])]
    ppermute x0 -> x7, starting transfers between devices: none -> 14 us  [the longest x6 10.6 us: along(): return lax.ppermute(value, 'rep', pairs)]
    all_to_all x3 -> x2, starting transfers between devices: 31 us -> 17 us  [spread(): return lax.all_to_all(value, 'rep', 0, 0, tiled=True)]
    all_to_all x1, waiting for transfers between devices: 13.9 us -> 0.01 us  [local(): lax.all_to_all(jnp.broadcast_to(payload[:, None], (4, reps, 56, 128)).res...]
    psum x1 -> x0, blocking collectives: 10.7 us -> none  [local(): stats = lax.psum(stats, 'group')]
    all_to_all x1, starting transfers between devices: 10.5 us -> 18.1 us  [local(): lax.all_to_all(jnp.broadcast_to(payload[:, None], (4, reps, 56, 128)).res...]
    convert_element_type x5 -> x2, other arithmetic: 3.46 us -> 0.93 us  [to_core(): other = (over.astype(f32) + got[ROWS:].astype(f32)).astype(bf16)]
  transfers between devices with their start and end apart: 20 -> 27, of which waited for: 11 -> 10; matrix products, arithmetic and copies ran while one was open for 6% -> 4% of each run, Pallas kernels for 20% -> 26%
where the time goes in v3:
time: 198 us; the launch traced here: 197 us
  starting transfers between devices  65.6 us (33%)
  Pallas kernels  63.1 us (32%)
  waiting for transfers between devices  53.9 us (27%)
  local copies, waits for them, and re-layouts  7.31 us (4%)
  other arithmetic  5.81 us (3%)
    ppermute x6, waiting for transfers between devices, along(): return lax.ppermute(value, 'rep', pairs)  24.4 us
    pallas_call x1, Pallas kernels, local(): call(backward_kernel, 'backward', 26, grid=(blocks,), in_specs=[scalar_sp...  23.3 us
    all_to_all x1, starting transfers between devices, local(): lax.all_to_all(jnp.broadcast_to(payload[:, None], (4, reps, 56, 128)).res...  18.1 us
    all_to_all x2, waiting for transfers between devices, spread(): return lax.all_to_all(value, 'rep', 0, 0, tiled=True)  17.4 us
    all_to_all x2, starting transfers between devices, spread(): return lax.all_to_all(value, 'rep', 0, 0, tiled=True)  17 us
    pallas_call x1, Pallas kernels, local(): call(forward_kernel, 'forward', 15, grid=(blocks,), in_specs=[scalar_spec...  14.3 us
    ppermute x15, starting transfers between devices, among(): return lax.ppermute(value, 'group', [(i, i ^ d) for i in range(4)])  12.9 us
    ppermute x6, starting transfers between devices, along(): return lax.ppermute(value, 'rep', pairs)  10.6 us
  transfers between devices with their start and end apart: 27, of which 10 were waited for; matrix products, arithmetic and copies ran while one was open for 4% of the time, Pallas kernels for 26%

profile of v3, /device:TPU:1, one launch (start us, length us, event | category | flops | bytes accessed | tf_op | source)
XLA Modules:
  0.0 196.8 jit_solution(8690671611429537726)
XLA Ops:
  0.7 2.9 %columns.1 = (bf16[192,1152]{1,0:T(8,128)(2,1)}, bf16[192,1152]{1,0:T(8,128)(2,1)}, bf16[192,1152]{1,0:T(8,128)(2,1)}, bf16[192,640]{1,0:T(8,128)(2,1)}, bf16[19...) custom-call(s32[1]{0:T(128)} %bitcast.1.me, bf16[192,3352]{1,0:T(8,128)(2,1)} %w_in.1, bf16[256,768]{1,0:T(8,128)(2,1)} %bitcast.49, ...), custom_call_target="tpu_custom_call" | custom-call | flops 2000000000 | bytes 1048576 | tf_op jit(solution)/shard_map/columns/pallas_call | solution.py:592
  3.6 2.1 %collective-permute-start = (bf16[272,768]{1,0:T(8,128)(2,1)}, bf16[272,768]{1,0:T(8,128)(2,1)S(1)}, u32[]{:S(2)}, u32[]{:S(2)}) collective-permute-start(bf16[272,768]{1,0:T(8,128)(2,1)} %get-tuple-element.74.t0), channel_id=1, source_target_pairs={{0,64},{32,96},{64,0},{96,32},{1,65},{33,97},{65,1},{97,33},{2,66}... | collective-permute-start | bytes 1253384 | tf_op jit(solution)/shard_map/ppermute | solution.py:577
  5.8 2.7 %collective-permute-start.6 = (bf16[192,512]{1,0:T(8,128)(2,1)}, bf16[192,512]{1,0:T(8,128)(2,1)S(1)}, u32[]{:S(2)}, u32[]{:S(2)}) collective-permute-start(bf16[192,512]{1,0:T(8,128)(2,1)} %get-tuple-element.80), channel_id=1, source_target_pairs={{0,97},{32,65},{64,33},{96,1},{1,96},{33,64},{65,32},{97,0},{2,99}... | collective-permute-start | bytes 589832 | tf_op jit(solution)/shard_map/ppermute | solution.py:608
  8.5 0.8 collective-permute-start.4
  9.3 5.6 %collective-permute-done.t2 = bf16[272,768]{1,0:T(8,128)(2,1)S(1)} collective-permute-done((bf16[272,768]{1,0:T(8,128)(2,1)}, bf16[272,768]{1,0:T(8,128)(2,1)S(1)}, u32[]{:S(2)}, u32[]{:S(2)}) %collective-permute-start) | collective-permute-done | bytes 417824 | tf_op jit(solution)/shard_map/ppermute | solution.py:577
  14.9 2.9 %collective-permute-start.1 = (bf16[272,768]{1,0:T(8,128)(2,1)}, bf16[272,768]{1,0:T(8,128)(2,1)S(1)}, u32[]{:S(2)}, u32[]{:S(2)}) collective-permute-start(bf16[272,768]{1,0:T(8,128)(2,1)} %get-tuple-element.74.t0), channel_id=1, source_target_pairs={{0,32},{32,0},{64,96},{96,64},{1,33},{33,1},{65,97},{97,65},{2,34}... | collective-permute-start | bytes 1253384 | tf_op jit(solution)/shard_map/ppermute | solution.py:577
  18.4 0.6 reshape_reshape.3.skip
  19.1 0.6 reshape.225.gain_out
  20.1 0.5 bitcast_convert_fusion.dtb
  20.7 0.8 collective-permute-done.5.w3a
  21.4 2.4 %collective-permute-done.4.w2 = bf16[192,1152]{1,0:T(8,128)(2,1)S(1)} collective-permute-done((bf16[192,1152]{1,0:T(8,128)(2,1)}, bf16[192,1152]{1,0:T(8,128)(2,1)S(1)}, u32[]{:S(2)}, u32[]{:S(2)}) %collective-permute-start.4) | collective-permute-done | bytes 442400 | tf_op jit(solution)/shard_map/ppermute | solution.py:608
  23.9 2.0 %collective-permute-start.9 = (bf16[256,768]{1,0:T(8,128)(2,1)S(1)}, bf16[256,768]{1,0:T(8,128)(2,1)S(1)}, u32[]{:S(2)}, u32[]{:S(2)}) collective-permute-start(bf16[256,768]{1,0:T(8,128)(2,1)S(1)} %bitcast.55), channel_id=1, source_target_pairs={{0,96},{32,64},{64,32},{96,0},{1,97},{33,65},{65,33},{97,1},{2,98}... | collective-permute-start | bytes 1179656 | tf_op jit(solution)/shard_map/ppermute | solution.py:577
  26.0 0.7 copy-done.21
  26.8 14.3 %forward.1 = (bf16[768,1152]{1,0:T(8,128)(2,1)}, bf16[1024,768]{1,0:T(8,128)(2,1)}, bf16[1024,1152]{1,0:T(8,128)(2,1)}, f32[1024,640]{1,0:T(8,128)}, f32[8,128,3...) custom-call(s32[1]{0:T(128)} %bitcast.1.me, ...), custom_call_target="tpu_custom_call" | custom-call | flops 15000000512 | bytes 1048576 | tf_op jit(solution)/shard_map/forward/pallas_call | solution.py:643
  41.2 2.0 %collective-permute-done.9.c3 = bf16[256,768]{1,0:T(8,128)(2,1)S(1)} collective-permute-done((bf16[256,768]{1,0:T(8,128)(2,1)S(1)}, bf16[256,768]{1,0:T(8,128)(2,1)S(1)}, u32[]{:S(2)}, u32[]{:S(2)}) %collective-permute-start.9) | collective-permute-done | bytes 393248 | tf_op jit(solution)/shard_map/ppermute | solution.py:577
  43.2 0.7 copy-done.24
  43.9 5.2 %sums.1 = (f32[1024,384]{1,0:T(8,128)}, f32[4,8,128]{2,1,0:T(8,128)}) custom-call(s32[1]{0:T(128)} %bitcast.1.me, bf16[256,768]{1,0:T(8,128)(2,1)} %bitcast.51, bf16[256,768]{1,0:T(8,128)(2,1)} %copy-done.22, bf16[256,768]{1,0:T(8,128)(2,1)} %copy-done.23, bf16[256,768]{1,0:T(8,128)(2,1)} %copy-done.24, bf16[1024,1152]{1,0:T(8,128)(2,1)} %get-tuple-element.81.gate_in.proj, ...), custom_call_target="tpu_custom_call" | custom-call | flops 4000000000 | bytes 1048576 | tf_op jit(solution)/shard_map/sums/pallas_call | solution.py:687
  49.3 2.0 collective-permute-start.12
  51.3 4.9 %branch.1 = (bf16[256,768]{1,0:T(8,128)(2,1)}, bf16[512,768]{1,0:T(8,128)(2,1)}, bf16[256,768]{1,0:T(8,128)(2,1)}) custom-call(s32[1]{0:T(128)} %bitcast.1.me, bf16[1024,1152]{1,0:T(8,128)(2,1)} %get-tuple-element.81.gate_in.proj, f32[1024,384]{1,0:T(8,128)} %get-tuple-element.82.y_in, f32[1,384]{1,0:T(1,128)} %reshape.225.gain_out, bf16[384,768]{1,0:T(8,128)(2,1)} %w_out.4), custom_call_target="tpu_custom_call" | custom-call | flops 3000000000 | bytes 1048576 | tf_op jit(solution)/shard_map/branch/pallas_call | solution.py:701
  56.8 6.7 %out.1 = (bf16[2304,128]{1,0:T(8,128)(2,1)}, bf16[1024,384]{1,0:T(8,128)(2,1)}, f32[1024,384]{1,0:T(8,128)}, f32[8,384]{1,0:T(8,128)}) custom-call(s32[1]{0:T(128)} %bitcast.1.me, bf16[256,768]{1,0:T(8,128)(2,1)} %bitcast.52, bf16[256,768]{1,0:T(8,128)(2,1)} %copy-done.22, bf16[256,768]{1,0:T(8,128)(2,1)} %copy-done.23, bf16[256,768]{1,0:T(8,128)(2,1)} %copy-done.24, ...), custom_call_target="tpu_custom_call" | custom-call | flops 6000000000 | bytes 1048576 | tf_op jit(solution)/shard_map/out/pallas_call | solution.py:714
  63.5 9.4 %all-to-all-start = ((bf16[32,72,128]{2,1,0:T(8,128)(2,1)}), bf16[32,72,128]{2,1,0:T(8,128)(2,1)S(1)}, u32[]{:S(2)}, u32[]{:S(2)}) async-start(bf16[32,72,128]{2,1,0:T(8,128)(2,1)} %bitcast.50), calls=%async_computation | async-start | bytes 1179648 | tf_op jit(solution)/shard_map/all_to_all | solution.py:740
  73.1 1.1 collective-permute-start.14
  74.2 23.3 %backward.1 = (bf16[32,208,128]{2,1,0:T(8,128)(2,1)}, bf16[256,768]{1,0:T(8,128)(2,1)}, bf16[512,768]{1,0:T(8,128)(2,1)}, bf16[256,768]{1,0:T(8,128)(2,1)}) custom-call(s32[1]{0:T(128)} %bitcast.1.me, bf16[768,1152]{1,0:T(8,128)(2,1)} %get-tuple-element.92.w_full, bf16[1024,768]{1,0:T(8,128)(2,1)} %get-tuple-element.93.normed, ...), custom_call_target="tpu_custom_call" | custom-call | flops 25999998976 | bytes 1048576 | tf_op jit(solution)/shard_map/backward/pallas_call | solution.py:751
  97.6 3.4 %collective-permute-start.15 = (bf16[72,128]{1,0:T(8,128)(2,1)S(1)}, bf16[72,128]{1,0:T(8,128)(2,1)S(1)}, u32[]{:S(2)}, u32[]{:S(2)}) collective-permute-start(bf16[72,128]{1,0:T(8,128)(2,1)S(1)} %reduce_sum.44), channel_id=1, source_target_pairs={{0,1},{1,0},{2,3},{3,2},{4,5},{5,4},{6,7},{7,6},{8,9},{9,8},{10,11... | collective-permute-start | bytes 55304 | tf_op jit(solution)/shard_map/ppermute | solution.py:803
  101.1 1.2 collective-permute-done.15
  102.2 2.5 %collective-permute-start.16 = (bf16[2,72,128]{2,1,0:T(8,128)(2,1)S(1)}, bf16[2,72,128]{2,1,0:T(8,128)(2,1)S(1)}, u32[]{:S(2)}, u32[]{:S(2)}) collective-permute-start(bf16[2,72,128]{2,1,0:T(8,128)(2,1)S(1)} %maximum_select_fusion), channel_id=1, source_target_pairs={{0,6},{1,7},{2,0},{3,1},{4,2},{5,3},{6,4},{7,5},{8,14},{9,15},{10,... | collective-permute-start | bytes 110600 | tf_op jit(solution)/shard_map/ppermute | solution.py:796
  104.8 2.0 %collective-permute-start.19 = (bf16[512,768]{1,0:T(8,128)(2,1)}, bf16[512,768]{1,0:T(8,128)(2,1)S(1)}, u32[]{:S(2)}, u32[]{:S(2)}) collective-permute-start(bf16[512,768]{1,0:T(8,128)(2,1)} %get-tuple-element.117), channel_id=1, source_target_pairs={{0,32},{32,0},{64,96},{96,64},{1,33},{33,1},{65,97},{97,65},{2,34}... | collective-permute-start | bytes 2359304 | tf_op jit(solution)/shard_map/ppermute | solution.py:577
  106.8 7.6 %all-to-all-start.1 = ((bf16[32,208,128]{2,1,0:T(8,128)(2,1)}), bf16[32,208,128]{2,1,0:T(8,128)(2,1)S(1)}, u32[]{:S(2)}, u32[]{:S(2)}) async-start(bf16[32,208,128]{2,1,0:T(8,128)(2,1)} %get-tuple-element.114), calls=%async_computation.1 | async-start | bytes 3407872 | tf_op jit(solution)/shard_map/all_to_all | solution.py:740
  114.4 2.8 %collective-permute-start.17 = (bf16[2,72,128]{2,1,0:T(8,128)(2,1)S(1)}, bf16[2,72,128]{2,1,0:T(8,128)(2,1)S(1)}, u32[]{:S(2)}, u32[]{:S(2)}) collective-permute-start(bf16[2,72,128]{2,1,0:T(8,128)(2,1)S(1)} %maximum_select_fusion), channel_id=1, source_target_pairs={{0,4},{1,5},{2,6},{3,7},{4,0},{5,1},{6,2},{7,3},{8,12},{9,13},{10,... | collective-permute-start | bytes 110600 | tf_op jit(solution)/shard_map/ppermute | solution.py:796
  117.5 3.2 %collective-permute-done.17 = bf16[2,72,128]{2,1,0:T(8,128)(2,1)S(1)} collective-permute-done((bf16[2,72,128]{2,1,0:T(8,128)(2,1)S(1)}, bf16[2,72,128]{2,1,0:T(8,128)(2,1)S(1)}, u32[]{:S(2)}, u32[]{:S(2)}) %collective-permute-start.17) | collective-permute-done | bytes 36896 | tf_op jit(solution)/shard_map/ppermute | solution.py:796
  120.7 1.1 collective-permute-done.18
  121.9 0.8 add_convert_fusion
  122.8 17.4 %all-to-all-done.1 = bf16[32,208,128]{2,1,0:T(8,128)(2,1)S(1)} async-done(((bf16[32,208,128]{2,1,0:T(8,128)(2,1)}), bf16[32,208,128]{2,1,0:T(8,128)(2,1)S(1)}, u32[]{:S(2)}, u32[]{:S(2)}) %all-to-all-start.1) | async-done | bytes 1703968 | tf_op jit(solution)/shard_map/all_to_all | solution.py:740
  140.5 1.5 broadcast_in_dim.16
  142.0 18.1 %all-to-all-start.2 = ((bf16[128,56,128]{2,1,0:T(8,128)(2,1)}), bf16[128,56,128]{2,1,0:T(8,128)(2,1)}, u32[]{:S(2)}, u32[]{:S(2)}) async-start(bf16[128,56,128]{2,1,0:T(8,128)(2,1)} %bitcast.21), calls=%async_computation.2 | async-start | bytes 3670016 | tf_op jit(solution)/shard_map/all_to_all | solution.py:818
  160.2 0.6 reshape.228
  160.8 0.7 add_bitcast_fusion
  161.6 1.4 collective-permute-start.21
  163.0 2.4 %collective-permute-start.22 = (bf16[576,128]{1,0:T(8,128)(2,1)S(1)}, bf16[576,128]{1,0:T(8,128)(2,1)S(1)}, u32[]{:S(2)}, u32[]{:S(2)}) collective-permute-start(bf16[576,128]{1,0:T(8,128)(2,1)S(1)} %bitcast.61), channel_id=1, source_target_pairs={{0,16},{1,17},{2,18},{3,19},{4,20},{5,21},{6,22},{7,23},{8,24},{9,... | collective-permute-start | bytes 442376 | tf_op jit(solution)/shard_map/ppermute | solution.py:796
  165.4 1.2 collective-permute-start.23
  167.0 1.6 fusion.4
  168.6 17.0 %collective-permute-done.21.p1 = bf16[576,128]{1,0:T(8,128)(2,1)S(1)} collective-permute-done((bf16[576,128]{1,0:T(8,128)(2,1)S(1)}, bf16[576,128]{1,0:T(8,128)(2,1)S(1)}, u32[]{:S(2)}, u32[]{:S(2)}) %collective-permute-start.21) | collective-permute-done | bytes 147488 | tf_op jit(solution)/shard_map/ppermute | solution.py:796
  185.5 3.2 %collective-permute-done.22.p2 = bf16[576,128]{1,0:T(8,128)(2,1)S(1)} collective-permute-done((bf16[576,128]{1,0:T(8,128)(2,1)S(1)}, bf16[576,128]{1,0:T(8,128)(2,1)S(1)}, u32[]{:S(2)}, u32[]{:S(2)}) %collective-permute-start.22) | collective-permute-done | bytes 147488 | tf_op jit(solution)/shard_map/ppermute | solution.py:796
  188.8 0.6 copy-done.28
  189.5 2.2 %w_out.5 = f32[384,768]{1,0:T(8,128)} custom-call(s32[1]{0:T(128)} %bitcast.30.place, bf16[576,128]{1,0:T(8,128)(2,1)} %bitcast.63, bf16[576,128]{1,0:T(8,128)(2,1)} %copy-done.27, bf16[576,128]{1,0:T(8,128)(2,1)} %copy-done.28, bf16[576,128]{1,0:T(8,128)(2,1)} %copy-done.29), custom_call_target="tpu_custom_call" | custom-call | flops 2000000000 | bytes 1048576 | tf_op jit(solution)/shard_map/w_out/pallas_call | solution.py:824
  191.7 0.9 slice.36
  192.6 0.7 convert.9.shorts
  193.3 3.5 %assemble.1 = (f32[192,3352]{1,0:T(8,128)}, f32[4,448]{1,0:T(4,128)}, f32[1,448]{1,0:T(1,128)}, f32[1,192]{1,0:T(1,128)}, f32[384]{0:T(512)}, /*index=5*/f32[1,6]{1,0:T(1,128)}, f32[1,6]{1,0:T(1,128)}, f32[1,6]{1,0:T(1,128)}) custom-call(s32[1]{0:T(128)} %bitcast.1.me, bf16[128,56,128]{2,1,0:T(8,128)(2,1)} %all-to-all-done.2.parts, ...), custom_call_target="tpu_custom_call" | custom-call | flops 4000000000 | bytes 1048576 | tf_op jit(solution)/shard_map/assemble/pallas_call | solution.py:847
  (118 shorter events, 3.7 us)
Async XLA Ops:
  0.7 17.7 %copy-start.30 = (bf16[6]{0:T(256)(128)(2,1)S(1)}, bf16[6]{0:T(256)(128)(2,1)}, u32[]{:S(2)}) copy-start(bf16[6]{0:T(256)(128)(2,1)} %param.21) | copy-start | bytes 40
  0.7 17.7 %copy-start.16 = (bf16[6]{0:T(256)(128)(2,1)S(1)}, bf16[6]{0:T(256)(128)(2,1)}, u32[]{:S(2)}) copy-start(bf16[6]{0:T(256)(128)(2,1)} %param.22) | copy-start | bytes 40
  0.7 18.4 %copy-start.12 = (bf16[384]{0:T(512)(128)(2,1)S(1)}, bf16[384]{0:T(512)(128)(2,1)}, u32[]{:S(2)}) copy-start(bf16[384]{0:T(512)(128)(2,1)} %param.23) | copy-start | bytes 2308
  0.7 19.5 %copy-start.31 = (bf16[6]{0:T(256)(128)(2,1)S(1)}, bf16[6]{0:T(256)(128)(2,1)}, u32[]{:S(2)}) copy-start(bf16[6]{0:T(256)(128)(2,1)} %param.20) | copy-start | bytes 40
  0.7 20.7 %copy-start.3 = (bf16[1,256,768]{2,1,0:T(8,128)(2,1)S(1)}, bf16[1,256,768]{2,1,0:T(8,128)(2,1)}, u32[]{:S(2)}) copy-start(bf16[1,256,768]{2,1,0:T(8,128)(2,1)} %param.15) | copy-start | bytes 1179652
  3.6 11.3 %collective-permute-start = (bf16[272,768]{1,0:T(8,128)(2,1)}, bf16[272,768]{1,0:T(8,128)(2,1)S(1)}, u32[]{:S(2)}, u32[]{:S(2)}) collective-permute-start(bf16[272,768]{1,0:T(8,128)(2,1)} %get-tuple-element.74.t0), channel_id=1, source_target_pairs={{0,64},{32,96},{64,0},{96,32},{1,65},{33,97},{65,1},{97,33},{2,66}... | collective-permute-start | bytes 1253384 | tf_op jit(solution)/shard_map/ppermute | solution.py:577
  5.8 12.1 %collective-permute-start.6 = (bf16[192,512]{1,0:T(8,128)(2,1)}, bf16[192,512]{1,0:T(8,128)(2,1)S(1)}, u32[]{:S(2)}, u32[]{:S(2)}) collective-permute-start(bf16[192,512]{1,0:T(8,128)(2,1)} %get-tuple-element.80), channel_id=1, source_target_pairs={{0,97},{32,65},{64,33},{96,1},{1,96},{33,64},{65,32},{97,0},{2,99}... | collective-permute-start | bytes 589832 | tf_op jit(solution)/shard_map/ppermute | solution.py:608
  8.5 15.4 %collective-permute-start.4 = (bf16[192,1152]{1,0:T(8,128)(2,1)}, bf16[192,1152]{1,0:T(8,128)(2,1)S(1)}, u32[]{:S(2)}, u32[]{:S(2)}) collective-permute-start(bf16[192,1152]{1,0:T(8,128)(2,1)} %get-tuple-element.78), channel_id=1, source_target_pairs={{0,65},{32,97},{64,1},{96,33},{1,64},{33,96},{65,0},{97,32},{2,67}... | collective-permute-start | bytes 1327112 | tf_op jit(solution)/shard_map/ppermute | solution.py:608
  9.3 12.2 %collective-permute-start.5 = (bf16[192,640]{1,0:T(8,128)(2,1)}, bf16[192,640]{1,0:T(8,128)(2,1)S(1)}, u32[]{:S(2)}, u32[]{:S(2)}) collective-permute-start(bf16[192,640]{1,0:T(8,128)(2,1)} %get-tuple-element.79), channel_id=1, source_target_pairs={{0,96},{32,64},{64,32},{96,0},{1,97},{33,65},{65,33},{97,1},{2,98}... | collective-permute-start | bytes 737288 | tf_op jit(solution)/shard_map/ppermute | solution.py:577
  14.9 11.0 %copy-start.19 = (bf16[272,768]{1,0:T(8,128)(2,1)}, bf16[272,768]{1,0:T(8,128)(2,1)S(1)}, u32[]{:S(2)}) copy-start(bf16[272,768]{1,0:T(8,128)(2,1)S(1)} %collective-permute-done.t2) | copy-start | bytes 1253380
  14.9 9.0 %collective-permute-start.1 = (bf16[272,768]{1,0:T(8,128)(2,1)}, bf16[272,768]{1,0:T(8,128)(2,1)S(1)}, u32[]{:S(2)}, u32[]{:S(2)}) collective-permute-start(bf16[272,768]{1,0:T(8,128)(2,1)} %get-tuple-element.74.t0), channel_id=1, source_target_pairs={{0,32},{32,0},{64,96},{96,64},{1,33},{33,1},{65,97},{97,65},{2,34}... | collective-permute-start | bytes 1253384 | tf_op jit(solution)/shard_map/ppermute | solution.py:577
  17.8 8.1 %collective-permute-start.2 = (bf16[272,768]{1,0:T(8,128)(2,1)S(1)}, bf16[272,768]{1,0:T(8,128)(2,1)S(1)}, u32[]{:S(2)}, u32[]{:S(2)}) collective-permute-start(bf16[272,768]{1,0:T(8,128)(2,1)S(1)} %collective-permute-done.t2), channel_id=1, source_target_pairs={{0,32},{32,0},{64,96},{96,64},{1,33},{33,1},{65,97},{97,65},{2,34}... | collective-permute-start | bytes 1253384 | tf_op jit(solution)/shard_map/ppermute | solution.py:577
  17.8 8.1 %copy-start.26 = (bf16[192,512]{1,0:T(8,128)(2,1)}, bf16[192,512]{1,0:T(8,128)(2,1)S(1)}, u32[]{:S(2)}) copy-start(bf16[192,512]{1,0:T(8,128)(2,1)S(1)} %collective-permute-done.6.w3b) | copy-start | bytes 589828
  17.8 8.1 %collective-permute-start.3 = (bf16[192,1152]{1,0:T(8,128)(2,1)}, bf16[192,1152]{1,0:T(8,128)(2,1)S(1)}, u32[]{:S(2)}, u32[]{:S(2)}) collective-permute-start(bf16[192,1152]{1,0:T(8,128)(2,1)} %get-tuple-element.77), channel_id=1, source_target_pairs={{0,32},{32,0},{64,96},{96,64},{1,33},{33,1},{65,97},{97,65},{2,34}... | collective-permute-start | bytes 1327112 | tf_op jit(solution)/shard_map/ppermute | solution.py:577
  21.4 4.5 %copy-start.25 = (bf16[192,640]{1,0:T(8,128)(2,1)}, bf16[192,640]{1,0:T(8,128)(2,1)S(1)}, u32[]{:S(2)}) copy-start(bf16[192,640]{1,0:T(8,128)(2,1)S(1)} %collective-permute-done.5.w3a) | copy-start | bytes 737284
  21.4 19.7 %collective-permute-start.7 = (bf16[256,768]{1,0:T(8,128)(2,1)S(1)}, bf16[256,768]{1,0:T(8,128)(2,1)S(1)}, u32[]{:S(2)}, u32[]{:S(2)}) collective-permute-start(bf16[256,768]{1,0:T(8,128)(2,1)S(1)} %bitcast.53), channel_id=1, source_target_pairs={{0,32},{32,0},{64,96},{96,64},{1,33},{33,1},{65,97},{97,65},{2,34}... | collective-permute-start | bytes 1179656 | tf_op jit(solution)/shard_map/ppermute | solution.py:577
  23.9 17.2 %collective-permute-start.8 = (bf16[256,768]{1,0:T(8,128)(2,1)S(1)}, bf16[256,768]{1,0:T(8,128)(2,1)S(1)}, u32[]{:S(2)}, u32[]{:S(2)}) collective-permute-start(bf16[256,768]{1,0:T(8,128)(2,1)S(1)} %bitcast.54), channel_id=1, source_target_pairs={{0,64},{32,96},{64,0},{96,32},{1,65},{33,97},{65,1},{97,33},{2,66}... | collective-permute-start | bytes 1179656 | tf_op jit(solution)/shard_map/ppermute | solution.py:577
  23.9 19.2 %collective-permute-start.9 = (bf16[256,768]{1,0:T(8,128)(2,1)S(1)}, bf16[256,768]{1,0:T(8,128)(2,1)S(1)}, u32[]{:S(2)}, u32[]{:S(2)}) collective-permute-start(bf16[256,768]{1,0:T(8,128)(2,1)S(1)} %bitcast.55), channel_id=1, source_target_pairs={{0,96},{32,64},{64,32},{96,0},{1,97},{33,65},{65,33},{97,1},{2,98}... | collective-permute-start | bytes 1179656 | tf_op jit(solution)/shard_map/ppermute | solution.py:577
  49.1 7.0 %collective-permute-start.10 = (f32[4,8,128]{2,1,0:T(8,128)}, f32[4,8,128]{2,1,0:T(8,128)S(1)}, u32[]{:S(2)}, u32[]{:S(2)}) collective-permute-start(f32[4,8,128]{2,1,0:T(8,128)} %get-tuple-element.88.s0), channel_id=1, source_target_pairs={{0,32},{32,0},{64,96},{96,64},{1,33},{33,1},{65,97},{97,65},{2,34}... | collective-permute-start | bytes 49160 | tf_op jit(solution)/shard_map/ppermute | solution.py:577
  49.2 7.0 %collective-permute-start.11 = (f32[4,8,128]{2,1,0:T(8,128)}, f32[4,8,128]{2,1,0:T(8,128)S(1)}, u32[]{:S(2)}, u32[]{:S(2)}) collective-permute-start(f32[4,8,128]{2,1,0:T(8,128)} %get-tuple-element.88.s0), channel_id=1, source_target_pairs={{0,64},{32,96},{64,0},{96,32},{1,65},{33,97},{65,1},{97,33},{2,66}... | collective-permute-start | bytes 49160 | tf_op jit(solution)/shard_map/ppermute | solution.py:577
  49.3 6.9 %collective-permute-start.12 = (f32[4,8,128]{2,1,0:T(8,128)}, f32[4,8,128]{2,1,0:T(8,128)S(1)}, u32[]{:S(2)}, u32[]{:S(2)}) collective-permute-start(f32[4,8,128]{2,1,0:T(8,128)} %get-tuple-element.88.s0), channel_id=1, source_target_pairs={{0,96},{32,64},{64,32},{96,0},{1,97},{33,65},{65,33},{97,1},{2,98}... | collective-permute-start | bytes 49160 | tf_op jit(solution)/shard_map/ppermute | solution.py:577
  56.2 16.7 %collective-permute-start.13 = (bf16[512,768]{1,0:T(8,128)(2,1)}, bf16[512,768]{1,0:T(8,128)(2,1)S(1)}, u32[]{:S(2)}, u32[]{:S(2)}) collective-permute-start(bf16[512,768]{1,0:T(8,128)(2,1)} %get-tuple-element.99), channel_id=1, source_target_pairs={{0,32},{32,0},{64,96},{96,64},{1,33},{33,1},{65,97},{97,65},{2,34}... | collective-permute-start | bytes 2359304 | tf_op jit(solution)/shard_map/ppermute | solution.py:577
  63.5 9.4 %copy-start.9 = (bf16[256,768]{1,0:T(8,128)(2,1)S(1)}, bf16[256,768]{1,0:T(8,128)(2,1)}, u32[]{:S(2)}) copy-start(bf16[256,768]{1,0:T(8,128)(2,1)} %get-tuple-element.100) | copy-start | bytes 1179652
  63.5 34.0 %all-to-all-start = ((bf16[32,72,128]{2,1,0:T(8,128)(2,1)}), bf16[32,72,128]{2,1,0:T(8,128)(2,1)S(1)}, u32[]{:S(2)}, u32[]{:S(2)}) async-start(bf16[32,72,128]{2,1,0:T(8,128)(2,1)} %bitcast.50), calls=%async_computation | async-start | bytes 1179648 | tf_op jit(solution)/shard_map/all_to_all | solution.py:740
  73.0 24.5 %copy-start.1 = (bf16[512,768]{1,0:T(8,128)(2,1)}, bf16[512,768]{1,0:T(8,128)(2,1)S(1)}, u32[]{:S(2)}) copy-start(bf16[512,768]{1,0:T(8,128)(2,1)S(1)} %collective-permute-done.13) | copy-start | bytes 2359300
  73.1 24.4 %collective-permute-start.14 = (bf16[256,768]{1,0:T(8,128)(2,1)S(1)}, bf16[256,768]{1,0:T(8,128)(2,1)S(1)}, u32[]{:S(2)}, u32[]{:S(2)}) collective-permute-start(bf16[256,768]{1,0:T(8,128)(2,1)S(1)} %add_convert_fusion.1), channel_id=1, source_target_pairs={{0,64},{32,96},{64,0},{96,32},{1,65},{33,97},{65,1},{97,33},{2,66}... | collective-permute-start | bytes 1179656 | tf_op jit(solution)/shard_map/ppermute | solution.py:577
  97.5 9.3 %copy-start.6 = (bf16[256,768]{1,0:T(8,128)(2,1)}, bf16[256,768]{1,0:T(8,128)(2,1)S(1)}, u32[]{:S(2)}) copy-start(bf16[256,768]{1,0:T(8,128)(2,1)S(1)} %collective-permute-done.14) | copy-start | bytes 1179652
  97.6 4.6 %collective-permute-start.15 = (bf16[72,128]{1,0:T(8,128)(2,1)S(1)}, bf16[72,128]{1,0:T(8,128)(2,1)S(1)}, u32[]{:S(2)}, u32[]{:S(2)}) collective-permute-start(bf16[72,128]{1,0:T(8,128)(2,1)S(1)} %reduce_sum.44), channel_id=1, source_target_pairs={{0,1},{1,0},{2,3},{3,2},{4,5},{5,4},{6,7},{7,6},{8,9},{9,8},{10,11... | collective-permute-start | bytes 55304 | tf_op jit(solution)/shard_map/ppermute | solution.py:803
  102.2 15.3 %collective-permute-start.16 = (bf16[2,72,128]{2,1,0:T(8,128)(2,1)S(1)}, bf16[2,72,128]{2,1,0:T(8,128)(2,1)S(1)}, u32[]{:S(2)}, u32[]{:S(2)}) collective-permute-start(bf16[2,72,128]{2,1,0:T(8,128)(2,1)S(1)} %maximum_select_fusion), channel_id=1, source_target_pairs={{0,6},{1,7},{2,0},{3,1},{4,2},{5,3},{6,4},{7,5},{8,14},{9,15},{10,... | collective-permute-start | bytes 110600 | tf_op jit(solution)/shard_map/ppermute | solution.py:796
  104.8 17.1 %copy-start.8 = (bf16[256,768]{1,0:T(8,128)(2,1)S(1)}, bf16[256,768]{1,0:T(8,128)(2,1)}, u32[]{:S(2)}) copy-start(bf16[256,768]{1,0:T(8,128)(2,1)} %get-tuple-element.118) | copy-start | bytes 1179652
  104.8 17.1 %collective-permute-start.19 = (bf16[512,768]{1,0:T(8,128)(2,1)}, bf16[512,768]{1,0:T(8,128)(2,1)S(1)}, u32[]{:S(2)}, u32[]{:S(2)}) collective-permute-start(bf16[512,768]{1,0:T(8,128)(2,1)} %get-tuple-element.117), channel_id=1, source_target_pairs={{0,32},{32,0},{64,96},{96,64},{1,33},{33,1},{65,97},{97,65},{2,34}... | collective-permute-start | bytes 2359304 | tf_op jit(solution)/shard_map/ppermute | solution.py:577
  106.8 33.4 %all-to-all-start.1 = ((bf16[32,208,128]{2,1,0:T(8,128)(2,1)}), bf16[32,208,128]{2,1,0:T(8,128)(2,1)S(1)}, u32[]{:S(2)}, u32[]{:S(2)}) async-start(bf16[32,208,128]{2,1,0:T(8,128)(2,1)} %get-tuple-element.114), calls=%async_computation.1 | async-start | bytes 3407872 | tf_op jit(solution)/shard_map/all_to_all | solution.py:740
  114.4 6.3 %collective-permute-start.17 = (bf16[2,72,128]{2,1,0:T(8,128)(2,1)S(1)}, bf16[2,72,128]{2,1,0:T(8,128)(2,1)S(1)}, u32[]{:S(2)}, u32[]{:S(2)}) collective-permute-start(bf16[2,72,128]{2,1,0:T(8,128)(2,1)S(1)} %maximum_select_fusion), channel_id=1, source_target_pairs={{0,4},{1,5},{2,6},{3,7},{4,0},{5,1},{6,2},{7,3},{8,12},{9,13},{10,... | collective-permute-start | bytes 110600 | tf_op jit(solution)/shard_map/ppermute | solution.py:796
  117.2 4.6 %collective-permute-start.18 = (bf16[2,72,128]{2,1,0:T(8,128)(2,1)S(1)}, bf16[2,72,128]{2,1,0:T(8,128)(2,1)S(1)}, u32[]{:S(2)}, u32[]{:S(2)}) collective-permute-start(bf16[2,72,128]{2,1,0:T(8,128)(2,1)S(1)} %maximum_select_fusion), channel_id=1, source_target_pairs={{0,2},{1,3},{2,4},{3,5},{4,6},{5,7},{6,0},{7,1},{8,10},{9,11},{10,... | collective-permute-start | bytes 110600 | tf_op jit(solution)/shard_map/ppermute | solution.py:796
  122.7 17.7 %collective-permute-start.20 = (bf16[256,768]{1,0:T(8,128)(2,1)}, bf16[256,768]{1,0:T(8,128)(2,1)S(1)}, u32[]{:S(2)}, u32[]{:S(2)}) collective-permute-start(bf16[256,768]{1,0:T(8,128)(2,1)} %add_convert_fusion), channel_id=1, source_target_pairs={{0,64},{32,96},{64,0},{96,32},{1,65},{33,97},{65,1},{97,33},{2,66}... | collective-permute-start | bytes 1179656 | tf_op jit(solution)/shard_map/ppermute | solution.py:577
  122.8 42.6 %copy-start.10 = (bf16[4,2,72,128]{3,2,1,0:T(8,128)(2,1)}, bf16[4,2,72,128]{3,2,1,0:T(8,128)(2,1)S(1)}, u32[]{:S(2)}) copy-start(bf16[4,2,72,128]{3,2,1,0:T(8,128)(2,1)S(1)} %constant_dynamic-slice_fusion) | copy-start | bytes 442372
  142.0 18.2 %copy-start.32 = (bf16[192]{0:T(256)(128)(2,1)S(1)}, bf16[192]{0:T(256)(128)(2,1)}, u32[]{:S(2)}) copy-start(bf16[192]{0:T(256)(128)(2,1)} %gain_in.1) | copy-start | bytes 1156
  142.0 18.8 %copy-start.11 = (f32[1,768]{1,0:T(1,128)S(1)}, f32[1,768]{1,0:T(1,128)}, u32[]{:S(2)}) copy-start(f32[1,768]{1,0:T(1,128)} %get-tuple-element.122) | copy-start | bytes 9220
  142.0 24.6 %copy-start = (bf16[1,256,768]{2,1,0:T(8,128)(2,1)S(1)}, bf16[1,256,768]{2,1,0:T(8,128)(2,1)}, u32[]{:S(2)}) copy-start(bf16[1,256,768]{2,1,0:T(8,128)(2,1)} %param.13) | copy-start | bytes 1179652
  142.0 24.6 %copy-start.2 = (bf16[256,768]{1,0:T(8,128)(2,1)S(1)}, bf16[256,768]{1,0:T(8,128)(2,1)}, u32[]{:S(2)}) copy-start(bf16[256,768]{1,0:T(8,128)(2,1)} %get-tuple-element.119) | copy-start | bytes 1179652
  142.0 49.7 %all-to-all-start.2 = ((bf16[128,56,128]{2,1,0:T(8,128)(2,1)}), bf16[128,56,128]{2,1,0:T(8,128)(2,1)}, u32[]{:S(2)}, u32[]{:S(2)}) async-start(bf16[128,56,128]{2,1,0:T(8,128)(2,1)} %bitcast.21), calls=%async_computation.2 | async-start | bytes 3670016 | tf_op jit(solution)/shard_map/all_to_all | solution.py:818
  160.2 6.8 %slice-start = ((bf16[512,768]{1,0:T(8,128)(2,1)}), bf16[256,768]{1,0:T(8,128)(2,1)S(1)}, s32[]{:S(2)}) async-start(bf16[512,768]{1,0:T(8,128)(2,1)} %copy-done.1), calls=%async_computation.3 | async-start | bytes 786432 | tf_op jit(solution)/shard_map/slice | solution.py:638
  160.2 6.8 %copy-start.4 = (bf16[1,256,768]{2,1,0:T(8,128)(2,1)S(1)}, bf16[1,256,768]{2,1,0:T(8,128)(2,1)}, u32[]{:S(2)}) copy-start(bf16[1,256,768]{2,1,0:T(8,128)(2,1)} %param.15) | copy-start | bytes 1179652
  160.2 6.8 %copy-start.5 = (bf16[256,768]{1,0:T(8,128)(2,1)S(1)}, bf16[256,768]{1,0:T(8,128)(2,1)}, u32[]{:S(2)}) copy-start(bf16[256,768]{1,0:T(8,128)(2,1)} %get-tuple-element.111) | copy-start | bytes 1179652
  160.2 6.8 %copy-start.7 = (bf16[256,768]{1,0:T(8,128)(2,1)S(1)}, bf16[256,768]{1,0:T(8,128)(2,1)}, u32[]{:S(2)}) copy-start(bf16[256,768]{1,0:T(8,128)(2,1)} %copy-done.6) | copy-start | bytes 1179652
  161.6 24.0 %collective-permute-start.21 = (bf16[576,128]{1,0:T(8,128)(2,1)S(1)}, bf16[576,128]{1,0:T(8,128)(2,1)S(1)}, u32[]{:S(2)}, u32[]{:S(2)}) collective-permute-start(bf16[576,128]{1,0:T(8,128)(2,1)S(1)} %bitcast.60), channel_id=1, source_target_pairs={{0,8},{1,9},{2,10},{3,11},{4,12},{5,13},{6,14},{7,15},{8,16},{9,17... | collective-permute-start | bytes 442376 | tf_op jit(solution)/shard_map/ppermute | solution.py:796
  163.0 25.7 %collective-permute-start.22 = (bf16[576,128]{1,0:T(8,128)(2,1)S(1)}, bf16[576,128]{1,0:T(8,128)(2,1)S(1)}, u32[]{:S(2)}, u32[]{:S(2)}) collective-permute-start(bf16[576,128]{1,0:T(8,128)(2,1)S(1)} %bitcast.61), channel_id=1, source_target_pairs={{0,16},{1,17},{2,18},{3,19},{4,20},{5,21},{6,22},{7,23},{8,24},{9,... | collective-permute-start | bytes 442376 | tf_op jit(solution)/shard_map/ppermute | solution.py:796
  165.4 23.3 %collective-permute-start.23 = (bf16[576,128]{1,0:T(8,128)(2,1)S(1)}, bf16[576,128]{1,0:T(8,128)(2,1)S(1)}, u32[]{:S(2)}, u32[]{:S(2)}) collective-permute-start(bf16[576,128]{1,0:T(8,128)(2,1)S(1)} %bitcast.62), channel_id=1, source_target_pairs={{0,24},{1,25},{2,26},{3,27},{4,28},{5,29},{6,30},{7,31},{8,0},{9,1... | collective-permute-start | bytes 442376 | tf_op jit(solution)/shard_map/ppermute | solution.py:796
  (13 other events, 17.0 us)

commit v4 on v3

--- a/solution.py
+++ b/solution.py
@@ -471,35 +471,38 @@
             bundle[r, 192:208, :] = value.astype(bf16)
 
 
-def w_out_kernel(place, p0, p1, p2, p3, grad_out):
-    for d, part in enumerate((p0, p1, p2, p3)):
-        source = (place[0] + 4 - d) % 4
-        for j in range(3):
-            half = 3 * source + j
-            rows = pl.ds(pl.multiple_of((half % 2) * 192, 64), 192)
-            lanes = pl.ds(pl.multiple_of((half // 2) * 128, 128), 128)
-            grad_out[rows, lanes] = part[192 * j : 192 * j + 192, :].astype(f32)
-
-
 def assemble_kernel(
-    me, parts, shorts, gain_in,
-    grad_in, grad_kernel, grad_bias, grad_gain_in, grad_gain_out, grad_skip, grad_dt, grad_log,
-    wide, turned,
+    me, parts, gain_in,
+    grad_in, grad_out, grad_kernel, grad_bias, grad_gain_in, grad_gain_out, grad_skip, grad_dt,
+    grad_log,
+    wide, turned, shorts,
 ):
     g = me[0]
-    for tile in range(8):
-        for q in range(4):
-            pieces = [parts[32 * k + 4 * tile + q, 0:48, :].astype(f32) for k in range(4)]
-            rows = slice(48 * q, 48 * q + 48)
-            if tile < 6:
-                for k in range(4):
-                    start = (tile // 3) * DI + k * XW + (tile % 3) * 128
-                    grad_in[rows, start : start + 128] = pieces[k]
-            else:
-                start = 2 * DI + 128 * (tile - 6)
-                grad_in[rows, start : start + 128] = (pieces[0] + pieces[1]) + (
-                    pieces[2] + pieces[3]
-                )
+    for r in range(32):
+        tile, q = r // 4, r % 4
+        chunks = [parts[32 * k + r].astype(f32) for k in range(4)]
+        rows = slice(48 * q, 48 * q + 48)
+        if tile < 6:
+            for k in range(4):
+                start = (tile // 3) * DI + k * XW + (tile % 3) * 128
+                grad_in[rows, start : start + 128] = chunks[k][:48]
+        else:
+            start = 2 * DI + 128 * (tile - 6)
+            grad_in[rows, start : start + 128] = (chunks[0][:48] + chunks[1][:48]) + (
+                chunks[2][:48] + chunks[3][:48]
+            )
+        for k in range(4):
+            first = 72 * r + 18 * k
+            done = 0
+            while done < 18:
+                column, row = divmod(first + done, XW)
+                count = min(18 - done, XW - row)
+                grad_out[row : row + count, 128 * column : 128 * column + 128] = chunks[k][
+                    48 + done : 48 + done + count
+                ]
+                done += count
+            if r < 16:
+                shorts[k, 4 * r : 4 * r + 4, :] = chunks[k][66:70]
 
     turned[...] = jnp.zeros_like(turned)
     wide[...] = jnp.zeros_like(wide)
@@ -785,50 +788,28 @@
     def total(received):
         return jnp.sum(received.astype(f32), axis=0).astype(bf16)
 
-    r = lax.axis_index("rep")
-
-    def along(value, step):
-        stride, by = step
-        pairs = [
-            (n, n - (n // stride % 4) * stride + ((n // stride + by) % 4) * stride)
-            for n in range(reps)
-        ]
-        return lax.ppermute(value, "rep", pairs)
-
     bundle2, received1, branches = lax.optimization_barrier((bundle2, received1, branches))
     received2 = spread(bundle2)
     d_parts = to_core(*n_parts)
     d_parts = to_owner(*d_parts)
-    mine = total(received1)
-    other = lax.ppermute(mine, "rep", [(n, n ^ 1) for n in range(reps)])
-    two = jnp.where(r % 2 == 0, jnp.stack([mine, other]), jnp.stack([other, mine]))
-    z_parts = [along(two, (2, by)) for by in (3, 2, 1)] + [two]
-    z_all = jnp.stack(z_parts + z_parts[:3])
-    eight = lax.dynamic_slice_in_dim(z_all, 3 - r // 2 % 4, 4, axis=0).reshape(576, 128)
-    reduced2, eight, d_parts = lax.optimization_barrier((total(received2), eight, d_parts))
-    x_parts = [eight] + [along(eight, (8, by)) for by in (1, 2, 3)]
+    by_member = total(received1).reshape(4, 18, 128)
+    turns = [lax.dynamic_index_in_dim(by_member, g ^ d, 0, keepdims=False) for d in range(4)]
+    turns = jnp.stack([turns[0]] + [among(turns[d], d) for d in range(1, 4)])
+    outs = jnp.stack([lax.dynamic_index_in_dim(turns, g ^ k, 0, keepdims=False) for k in range(4)])
+    reduced2, outs = lax.optimization_barrier((total(received2), outs))
     payload = jnp.concatenate(
         [
             reduced2[:192].reshape(4, 48, 128),
+            outs,
             reduced2[192:].reshape(4, 4, 128),
-            jnp.zeros((4, 4, 128), bf16),
+            jnp.zeros((4, 2, 128), bf16),
         ],
         axis=1,
     )
     parts = lax.all_to_all(
-        jnp.broadcast_to(payload[:, None], (4, reps, 56, 128)).reshape(4 * reps, 56, 128),
+        jnp.broadcast_to(payload[:, None], (4, reps, 72, 128)).reshape(4 * reps, 72, 128),
         ("group", "rep"), 0, 0, tiled=True,
     )
-    shorts = parts.reshape(4, reps, 56, 128)[:, :16, 48:52].astype(f32).reshape(4, 64, 128)
-    place = (r // 8).astype(jnp.int32).reshape(1)
-    grad_w_out = call(
-        w_out_kernel,
-        "w_out",
-        2,
-        in_specs=[scalar_spec] + [vmem_spec] * 4,
-        out_specs=vmem_spec,
-        out_shape=shape((XW, D), f32),
-    )(place, *x_parts)
 
     x = tok.astype(f32)
     branch = sum(value.astype(f32) for value in branches)
@@ -848,16 +829,20 @@
         assemble_kernel,
         "assemble",
         4,
-        in_specs=[scalar_spec] + [vmem_spec] * 3,
-        out_specs=[vmem_spec] * 8,
+        in_specs=[scalar_spec] + [vmem_spec] * 2,
+        out_specs=[vmem_spec] * 9,
         out_shape=(
-            shape((192, 3352), f32), shape((4, 448), f32),
+            shape((192, 3352), f32), shape((XW, D), f32), shape((4, 448), f32),
             shape((1, 448), f32), shape((1, 192), f32), shape((XW,), f32), shape((1, HL), f32),
             shape((1, HL), f32), shape((1, HL), f32),
         ),
-        scratch_shapes=[pltpu.VMEM((8, CW), f32), pltpu.VMEM((128, 256), f32)],
-    )(me, parts, shorts, gain_in.astype(f32).reshape(1, 192))
-    grad_w_in, grad_kernel, grad_bias, grad_gi, grad_go, grad_s, grad_d, grad_l = grads
+        scratch_shapes=[
+            pltpu.VMEM((8, CW), f32),
+            pltpu.VMEM((128, 256), f32),
+            pltpu.VMEM((4, 64, 128), f32),
+        ],
+    )(me, parts, gain_in.astype(f32).reshape(1, 192))
+    grad_w_in, grad_w_out, grad_kernel, grad_bias, grad_gi, grad_go, grad_s, grad_d, grad_l = grads
     return (
         layer_out,
         grad_tokens,

time: 198 us -> 188 us (0.949)
  starting transfers between devices: 65.6 us -> 46.2 us
  waiting for transfers between devices: 53.9 us -> 61.8 us
  other arithmetic: 5.81 us -> 8.35 us
    ppermute x15 -> x18, waiting for transfers between devices: 8.45 us -> 51.9 us  [among(): return lax.ppermute(value, 'group', [(i, i ^ d) for i in range(4)])]
    ppermute x7 -> x0, waiting for transfers between devices: 25.6 us -> none  [the longest x6 24.4 us: along(): return lax.ppermute(value, 'rep', pairs)]
    ppermute x7 -> x0, starting transfers between devices: 14 us -> none  [the longest x6 10.6 us: along(): return lax.ppermute(value, 'rep', pairs)]
    all_to_all x1, starting transfers between devices: 18.1 us -> 7.78 us  [local(): lax.all_to_all(jnp.broadcast_to(payload[:, None], (4, reps, 72, 128)).res...]
    all_to_all x2, waiting for transfers between devices: 17.4 us -> 7.53 us  [spread(): return lax.all_to_all(value, 'rep', 0, 0, tiled=True)]
    ppermute x15 -> x18, starting transfers between devices: 12.9 us -> 15.7 us  [among(): return lax.ppermute(value, 'group', [(i, i ^ d) for i in range(4)])]
    pallas_call x1 -> x0, Pallas kernels: 2.23 us -> none  [local(): call(w_out_kernel, 'w_out', 2, in_specs=[scalar_spec] + [vmem_spec] * 4,...]
    all_to_all x2, starting transfers between devices: 17 us -> 19.2 us  [spread(): return lax.all_to_all(value, 'rep', 0, 0, tiled=True)]
  transfers between devices with their start and end apart: 27 -> 23, of which waited for: 10 -> 9; matrix products, arithmetic and copies ran while one was open for 4% -> 5% of each run, Pallas kernels for 26% -> 26%
where the time goes in v4:
time: 188 us; the launch traced here: 187 us
  waiting for transfers between devices  61.8 us (33%)
  Pallas kernels  61.4 us (33%)
  starting transfers between devices  46.2 us (25%)
  other arithmetic  8.35 us (4%)
  local copies, waits for them, and re-layouts  7.96 us (4%)
    ppermute x18, waiting for transfers between devices, among(): return lax.ppermute(value, 'group', [(i, i ^ d) for i in range(4)])  51.9 us
    pallas_call x1, Pallas kernels, local(): call(backward_kernel, 'backward', 26, grid=(blocks,), in_specs=[scalar_sp...  23.3 us
    all_to_all x2, starting transfers between devices, spread(): return lax.all_to_all(value, 'rep', 0, 0, tiled=True)  19.2 us
    ppermute x18, starting transfers between devices, among(): return lax.ppermute(value, 'group', [(i, i ^ d) for i in range(4)])  15.7 us
    pallas_call x1, Pallas kernels, local(): call(forward_kernel, 'forward', 15, grid=(blocks,), in_specs=[scalar_spec...  14.3 us
    all_to_all x1, starting transfers between devices, local(): lax.all_to_all(jnp.broadcast_to(payload[:, None], (4, reps, 72, 128)).res...  7.78 us
    all_to_all x2, waiting for transfers between devices, spread(): return lax.all_to_all(value, 'rep', 0, 0, tiled=True)  7.53 us
    pallas_call x1, Pallas kernels, local(): call(out_kernel, 'out', 6, grid=(blocks,), in_specs=[scalar_spec] + [part...  6.74 us
  transfers between devices with their start and end apart: 23, of which 9 were waited for; matrix products, arithmetic and copies ran while one was open for 5% of the time, Pallas kernels for 26%

profile of v4, /device:TPU:1, one launch (start us, length us, event | category | flops | bytes accessed | tf_op | source)
XLA Modules:
  0.0 186.9 jit_solution(11842384046349132073)
XLA Ops:
  0.7 2.9 %columns.1 = (bf16[192,1152]{1,0:T(8,128)(2,1)}, bf16[192,1152]{1,0:T(8,128)(2,1)}, bf16[192,1152]{1,0:T(8,128)(2,1)}, bf16[192,640]{1,0:T(8,128)(2,1)}, bf16[19...) custom-call(s32[1]{0:T(128)} %bitcast.1.me, bf16[192,3352]{1,0:T(8,128)(2,1)} %w_in.1, bf16[256,768]{1,0:T(8,128)(2,1)} %bitcast.40, ...), custom_call_target="tpu_custom_call" | custom-call | flops 2000000000 | bytes 1048576 | tf_op jit(solution)/shard_map/columns/pallas_call | solution.py:595
  3.6 2.1 %collective-permute-start = (bf16[272,768]{1,0:T(8,128)(2,1)}, bf16[272,768]{1,0:T(8,128)(2,1)S(1)}, u32[]{:S(2)}, u32[]{:S(2)}) collective-permute-start(bf16[272,768]{1,0:T(8,128)(2,1)} %get-tuple-element.72.t0), channel_id=1, source_target_pairs={{0,64},{32,96},{64,0},{96,32},{1,65},{33,97},{65,1},{97,33},{2,66}... | collective-permute-start | bytes 1253384 | tf_op jit(solution)/shard_map/ppermute | solution.py:580
  5.7 2.7 %collective-permute-start.6 = (bf16[192,512]{1,0:T(8,128)(2,1)}, bf16[192,512]{1,0:T(8,128)(2,1)S(1)}, u32[]{:S(2)}, u32[]{:S(2)}) collective-permute-start(bf16[192,512]{1,0:T(8,128)(2,1)} %get-tuple-element.78), channel_id=1, source_target_pairs={{0,97},{32,65},{64,33},{96,1},{1,96},{33,64},{65,32},{97,0},{2,99}... | collective-permute-start | bytes 589832 | tf_op jit(solution)/shard_map/ppermute | solution.py:611
  8.5 0.8 collective-permute-start.4
  9.3 5.6 %collective-permute-done.t2 = bf16[272,768]{1,0:T(8,128)(2,1)S(1)} collective-permute-done((bf16[272,768]{1,0:T(8,128)(2,1)}, bf16[272,768]{1,0:T(8,128)(2,1)S(1)}, u32[]{:S(2)}, u32[]{:S(2)}) %collective-permute-start) | collective-permute-done | bytes 417824 | tf_op jit(solution)/shard_map/ppermute | solution.py:580
  14.9 2.9 %collective-permute-start.1 = (bf16[272,768]{1,0:T(8,128)(2,1)}, bf16[272,768]{1,0:T(8,128)(2,1)S(1)}, u32[]{:S(2)}, u32[]{:S(2)}) collective-permute-start(bf16[272,768]{1,0:T(8,128)(2,1)} %get-tuple-element.72.t0), channel_id=1, source_target_pairs={{0,32},{32,0},{64,96},{96,64},{1,33},{33,1},{65,97},{97,65},{2,34}... | collective-permute-start | bytes 1253384 | tf_op jit(solution)/shard_map/ppermute | solution.py:580
  17.8 0.5 collective-permute-start.3
  18.4 0.6 reshape_reshape.3.skip
  19.0 0.6 reshape.151.gain_out
  19.6 0.5 pad_bitcast_fusion.rate
  20.1 0.5 bitcast_convert_fusion.dtb
  20.6 0.8 collective-permute-done.5.w3a
  21.4 2.4 %collective-permute-done.4.w2 = bf16[192,1152]{1,0:T(8,128)(2,1)S(1)} collective-permute-done((bf16[192,1152]{1,0:T(8,128)(2,1)}, bf16[192,1152]{1,0:T(8,128)(2,1)S(1)}, u32[]{:S(2)}, u32[]{:S(2)}) %collective-permute-start.4) | collective-permute-done | bytes 442400 | tf_op jit(solution)/shard_map/ppermute | solution.py:611
  23.9 2.0 %collective-permute-start.9 = (bf16[256,768]{1,0:T(8,128)(2,1)S(1)}, bf16[256,768]{1,0:T(8,128)(2,1)S(1)}, u32[]{:S(2)}, u32[]{:S(2)}) collective-permute-start(bf16[256,768]{1,0:T(8,128)(2,1)S(1)} %bitcast.46), channel_id=1, source_target_pairs={{0,96},{32,64},{64,32},{96,0},{1,97},{33,65},{65,33},{97,1},{2,98}... | collective-permute-start | bytes 1179656 | tf_op jit(solution)/shard_map/ppermute | solution.py:580
  26.0 0.7 copy-done.19
  26.8 14.3 %forward.1 = (bf16[768,1152]{1,0:T(8,128)(2,1)}, bf16[1024,768]{1,0:T(8,128)(2,1)}, bf16[1024,1152]{1,0:T(8,128)(2,1)}, f32[1024,640]{1,0:T(8,128)}, f32[8,128,3...) custom-call(s32[1]{0:T(128)} %bitcast.1.me, ...), custom_call_target="tpu_custom_call" | custom-call | flops 15000000512 | bytes 1048576 | tf_op jit(solution)/shard_map/forward/pallas_call | solution.py:646
  41.1 2.0 %collective-permute-done.9.c3 = bf16[256,768]{1,0:T(8,128)(2,1)S(1)} collective-permute-done((bf16[256,768]{1,0:T(8,128)(2,1)S(1)}, bf16[256,768]{1,0:T(8,128)(2,1)S(1)}, u32[]{:S(2)}, u32[]{:S(2)}) %collective-permute-start.9) | collective-permute-done | bytes 393248 | tf_op jit(solution)/shard_map/ppermute | solution.py:580
  43.2 0.7 copy-done.22
  43.9 5.2 %sums.1 = (f32[1024,384]{1,0:T(8,128)}, f32[4,8,128]{2,1,0:T(8,128)}) custom-call(s32[1]{0:T(128)} %bitcast.1.me, bf16[256,768]{1,0:T(8,128)(2,1)} %bitcast.42, bf16[256,768]{1,0:T(8,128)(2,1)} %copy-done.20, bf16[256,768]{1,0:T(8,128)(2,1)} %copy-done.21, bf16[256,768]{1,0:T(8,128)(2,1)} %copy-done.22, bf16[1024,1152]{1,0:T(8,128)(2,1)} %get-tuple-element.79.gate_in.proj, ...), custom_call_target="tpu_custom_call" | custom-call | flops 4000000000 | bytes 1048576 | tf_op jit(solution)/shard_map/sums/pallas_call | solution.py:690
  49.1 0.2 collective-permute-start.11
  49.3 2.0 %collective-permute-start.12 = (f32[4,8,128]{2,1,0:T(8,128)}, f32[4,8,128]{2,1,0:T(8,128)S(1)}, u32[]{:S(2)}, u32[]{:S(2)}) collective-permute-start(f32[4,8,128]{2,1,0:T(8,128)} %get-tuple-element.86.s0), channel_id=1, source_target_pairs={{0,96},{32,64},{64,32},{96,0},{1,97},{33,65},{65,33},{97,1},{2,98}... | collective-permute-start | bytes 49160 | tf_op jit(solution)/shard_map/ppermute | solution.py:580
  51.3 4.9 %branch.1 = (bf16[256,768]{1,0:T(8,128)(2,1)}, bf16[512,768]{1,0:T(8,128)(2,1)}, bf16[256,768]{1,0:T(8,128)(2,1)}) custom-call(s32[1]{0:T(128)} %bitcast.1.me, bf16[1024,1152]{1,0:T(8,128)(2,1)} %get-tuple-element.79.gate_in.proj, f32[1024,384]{1,0:T(8,128)} %get-tuple-element.80.y_in, f32[1,384]{1,0:T(1,128)} %reshape.151.gain_out, bf16[384,768]{1,0:T(8,128)(2,1)} %w_out.3), custom_call_target="tpu_custom_call" | custom-call | flops 3000000000 | bytes 1048576 | tf_op jit(solution)/shard_map/branch/pallas_call | solution.py:704
  56.3 0.5 copy-done.11
  56.8 6.7 %out.1 = (bf16[2304,128]{1,0:T(8,128)(2,1)}, bf16[1024,384]{1,0:T(8,128)(2,1)}, f32[1024,384]{1,0:T(8,128)}, f32[8,384]{1,0:T(8,128)}) custom-call(s32[1]{0:T(128)} %bitcast.1.me, bf16[256,768]{1,0:T(8,128)(2,1)} %bitcast.43, bf16[256,768]{1,0:T(8,128)(2,1)} %copy-done.20, bf16[256,768]{1,0:T(8,128)(2,1)} %copy-done.21, bf16[256,768]{1,0:T(8,128)(2,1)} %copy-done.22, ...), custom_call_target="tpu_custom_call" | custom-call | flops 6000000000 | bytes 1048576 | tf_op jit(solution)/shard_map/out/pallas_call | solution.py:717
  63.5 9.4 %all-to-all-start = ((bf16[32,72,128]{2,1,0:T(8,128)(2,1)}), bf16[32,72,128]{2,1,0:T(8,128)(2,1)S(1)}, u32[]{:S(2)}, u32[]{:S(2)}) async-start(bf16[32,72,128]{2,1,0:T(8,128)(2,1)} %bitcast.41), calls=%async_computation | async-start | bytes 1179648 | tf_op jit(solution)/shard_map/all_to_all | solution.py:743
  73.0 1.1 collective-permute-start.14
  74.2 23.3 %backward.1 = (bf16[32,208,128]{2,1,0:T(8,128)(2,1)}, bf16[256,768]{1,0:T(8,128)(2,1)}, bf16[512,768]{1,0:T(8,128)(2,1)}, bf16[256,768]{1,0:T(8,128)(2,1)}) custom-call(s32[1]{0:T(128)} %bitcast.1.me, bf16[768,1152]{1,0:T(8,128)(2,1)} %get-tuple-element.90.w_full, bf16[1024,768]{1,0:T(8,128)(2,1)} %get-tuple-element.91.normed, ...), custom_call_target="tpu_custom_call" | custom-call | flops 25999998976 | bytes 1048576 | tf_op jit(solution)/shard_map/backward/pallas_call | solution.py:754
  97.5 0.7 copy-done.7
  98.3 9.8 %all-to-all-start.1 = ((bf16[32,208,128]{2,1,0:T(8,128)(2,1)}), bf16[32,208,128]{2,1,0:T(8,128)(2,1)S(1)}, u32[]{:S(2)}, u32[]{:S(2)}) async-start(bf16[32,208,128]{2,1,0:T(8,128)(2,1)} %get-tuple-element.116), calls=%async_computation.1 | async-start | bytes 3407872 | tf_op jit(solution)/shard_map/all_to_all | solution.py:743
  108.3 1.2 collective-permute-start.17
  109.5 1.7 collective-permute-start.19
  111.3 9.4 %collective-permute-done.18 = bf16[18,128]{1,0:T(8,128)(2,1)S(1)} collective-permute-done((bf16[18,128]{1,0:T(8,128)(2,1)S(1)}, bf16[18,128]{1,0:T(8,128)(2,1)S(1)}, u32[]{:S(2)}, u32[]{:S(2)}) %collective-permute-start.18) | collective-permute-done | bytes 4640 | tf_op jit(solution)/shard_map/ppermute | solution.py:580
  120.8 3.7 %collective-permute-done.19 = bf16[18,128]{1,0:T(8,128)(2,1)S(1)} collective-permute-done((bf16[18,128]{1,0:T(8,128)(2,1)S(1)}, bf16[18,128]{1,0:T(8,128)(2,1)S(1)}, u32[]{:S(2)}, u32[]{:S(2)}) %collective-permute-start.19) | collective-permute-done | bytes 4640 | tf_op jit(solution)/shard_map/ppermute | solution.py:580
  124.5 7.5 %all-to-all-done.1 = bf16[32,208,128]{2,1,0:T(8,128)(2,1)S(1)} async-done(((bf16[32,208,128]{2,1,0:T(8,128)(2,1)}), bf16[32,208,128]{2,1,0:T(8,128)(2,1)S(1)}, u32[]{:S(2)}, u32[]{:S(2)}) %all-to-all-start.1) | async-done | bytes 1703968 | tf_op jit(solution)/shard_map/all_to_all | solution.py:743
  132.0 0.2 reduce_sum.44
  132.4 1.7 broadcast_in_dim.16
  134.1 7.8 %all-to-all-start.2 = ((bf16[128,72,128]{2,1,0:T(8,128)(2,1)}), bf16[128,72,128]{2,1,0:T(8,128)(2,1)S(1)}, u32[]{:S(2)}, u32[]{:S(2)}) async-start(bf16[128,72,128]{2,1,0:T(8,128)(2,1)} %bitcast.19), calls=%async_computation.2 | async-start | bytes 4718592 | tf_op jit(solution)/shard_map/all_to_all | solution.py:809
  141.9 1.1 collective-permute-start.15
  143.0 2.1 %collective-permute-done.15 = bf16[512,768]{1,0:T(8,128)(2,1)S(1)} collective-permute-done((bf16[512,768]{1,0:T(8,128)(2,1)}, bf16[512,768]{1,0:T(8,128)(2,1)S(1)}, u32[]{:S(2)}, u32[]{:S(2)}) %collective-permute-start.15) | collective-permute-done | bytes 786464 | tf_op jit(solution)/shard_map/ppermute | solution.py:580
  145.2 1.8 add_convert_fusion
  147.0 0.7 collective-permute-start.16
  147.7 0.5 reshape.152
  148.3 0.7 add_bitcast_fusion
  149.0 28.2 %collective-permute-done.16 = bf16[256,768]{1,0:T(8,128)(2,1)} collective-permute-done((bf16[256,768]{1,0:T(8,128)(2,1)}, bf16[256,768]{1,0:T(8,128)(2,1)}, u32[]{:S(2)}, u32[]{:S(2)}) %collective-permute-start.16) | collective-permute-done | bytes 393248 | tf_op jit(solution)/shard_map/ppermute | solution.py:580
  177.2 1.5 fusion.1
  178.7 2.7 %fusion.4 = (f32[1,256,768]{2,1,0:T(8,128)}, bf16[1,256,768]{2,1,0:T(8,128)(2,1)}) fusion(bf16[256,768]{1,0:T(8,128)(2,1)} %collective-permute-done.16, bf16[256,768]{1,0:T(8,128)(2,1)S(1)} %copy-done.3, f32[256]{0:T(256)S(1)} %get-tuple-element.142, f32[768]{0:T(1024)S(1)} %reduce.2, f32[256]{0:T(256)S(1)} %get-tuple-element.141, ...), kind=kLoop, calls=%fused_computation.8 | loop fusion | flops 3932160 | bytes 4331520 | tf_op jit(solution)/shard_map/reshape | solution.py:826
  181.4 1.4 copy-done
  182.9 4.0 %assemble.1 = (f32[192,3352]{1,0:T(8,128)}, f32[384,768]{1,0:T(8,128)}, f32[4,448]{1,0:T(4,128)}, f32[1,448]{1,0:T(1,128)}, f32[1,192]{1,0:T(1,128)}, /*index=5*...) custom-call(s32[1]{0:T(128)} %bitcast.1.me, bf16[128,72,128]{2,1,0:T(8,128)(2,1)} %copy-done, ...), custom_call_target="tpu_custom_call" | custom-call | flops 4000000000 | bytes 1048576 | tf_op jit(solution)/shard_map/assemble/pallas_call | solution.py:828
  (92 shorter events, 1.0 us)
Async XLA Ops:
  0.7 17.7 %copy-start.25 = (bf16[6]{0:T(256)(128)(2,1)S(1)}, bf16[6]{0:T(256)(128)(2,1)}, u32[]{:S(2)}) copy-start(bf16[6]{0:T(256)(128)(2,1)} %param.21) | copy-start | bytes 40
  0.7 17.7 %copy-start.14 = (bf16[6]{0:T(256)(128)(2,1)S(1)}, bf16[6]{0:T(256)(128)(2,1)}, u32[]{:S(2)}) copy-start(bf16[6]{0:T(256)(128)(2,1)} %param.22) | copy-start | bytes 40
  0.7 18.4 %copy-start.10 = (bf16[384]{0:T(512)(128)(2,1)S(1)}, bf16[384]{0:T(512)(128)(2,1)}, u32[]{:S(2)}) copy-start(bf16[384]{0:T(512)(128)(2,1)} %param.23) | copy-start | bytes 2308
  0.7 19.4 %copy-start.26 = (bf16[6]{0:T(256)(128)(2,1)S(1)}, bf16[6]{0:T(256)(128)(2,1)}, u32[]{:S(2)}) copy-start(bf16[6]{0:T(256)(128)(2,1)} %param.20) | copy-start | bytes 40
  0.7 20.7 %copy-start.4 = (bf16[1,256,768]{2,1,0:T(8,128)(2,1)S(1)}, bf16[1,256,768]{2,1,0:T(8,128)(2,1)}, u32[]{:S(2)}) copy-start(bf16[1,256,768]{2,1,0:T(8,128)(2,1)} %param.15) | copy-start | bytes 1179652
  3.6 11.3 %collective-permute-start = (bf16[272,768]{1,0:T(8,128)(2,1)}, bf16[272,768]{1,0:T(8,128)(2,1)S(1)}, u32[]{:S(2)}, u32[]{:S(2)}) collective-permute-start(bf16[272,768]{1,0:T(8,128)(2,1)} %get-tuple-element.72.t0), channel_id=1, source_target_pairs={{0,64},{32,96},{64,0},{96,32},{1,65},{33,97},{65,1},{97,33},{2,66}... | collective-permute-start | bytes 1253384 | tf_op jit(solution)/shard_map/ppermute | solution.py:580
  5.7 12.1 %collective-permute-start.6 = (bf16[192,512]{1,0:T(8,128)(2,1)}, bf16[192,512]{1,0:T(8,128)(2,1)S(1)}, u32[]{:S(2)}, u32[]{:S(2)}) collective-permute-start(bf16[192,512]{1,0:T(8,128)(2,1)} %get-tuple-element.78), channel_id=1, source_target_pairs={{0,97},{32,65},{64,33},{96,1},{1,96},{33,64},{65,32},{97,0},{2,99}... | collective-permute-start | bytes 589832 | tf_op jit(solution)/shard_map/ppermute | solution.py:611
  8.5 15.4 %collective-permute-start.4 = (bf16[192,1152]{1,0:T(8,128)(2,1)}, bf16[192,1152]{1,0:T(8,128)(2,1)S(1)}, u32[]{:S(2)}, u32[]{:S(2)}) collective-permute-start(bf16[192,1152]{1,0:T(8,128)(2,1)} %get-tuple-element.76), channel_id=1, source_target_pairs={{0,65},{32,97},{64,1},{96,33},{1,64},{33,96},{65,0},{97,32},{2,67}... | collective-permute-start | bytes 1327112 | tf_op jit(solution)/shard_map/ppermute | solution.py:611
  9.3 12.2 %collective-permute-start.5 = (bf16[192,640]{1,0:T(8,128)(2,1)}, bf16[192,640]{1,0:T(8,128)(2,1)S(1)}, u32[]{:S(2)}, u32[]{:S(2)}) collective-permute-start(bf16[192,640]{1,0:T(8,128)(2,1)} %get-tuple-element.77), channel_id=1, source_target_pairs={{0,96},{32,64},{64,32},{96,0},{1,97},{33,65},{65,33},{97,1},{2,98}... | collective-permute-start | bytes 737288 | tf_op jit(solution)/shard_map/ppermute | solution.py:580
  14.9 11.0 %copy-start.17 = (bf16[272,768]{1,0:T(8,128)(2,1)}, bf16[272,768]{1,0:T(8,128)(2,1)S(1)}, u32[]{:S(2)}) copy-start(bf16[272,768]{1,0:T(8,128)(2,1)S(1)} %collective-permute-done.t2) | copy-start | bytes 1253380
  14.9 9.0 %collective-permute-start.1 = (bf16[272,768]{1,0:T(8,128)(2,1)}, bf16[272,768]{1,0:T(8,128)(2,1)S(1)}, u32[]{:S(2)}, u32[]{:S(2)}) collective-permute-start(bf16[272,768]{1,0:T(8,128)(2,1)} %get-tuple-element.72.t0), channel_id=1, source_target_pairs={{0,32},{32,0},{64,96},{96,64},{1,33},{33,1},{65,97},{97,65},{2,34}... | collective-permute-start | bytes 1253384 | tf_op jit(solution)/shard_map/ppermute | solution.py:580
  17.8 8.1 %collective-permute-start.2 = (bf16[272,768]{1,0:T(8,128)(2,1)S(1)}, bf16[272,768]{1,0:T(8,128)(2,1)S(1)}, u32[]{:S(2)}, u32[]{:S(2)}) collective-permute-start(bf16[272,768]{1,0:T(8,128)(2,1)S(1)} %collective-permute-done.t2), channel_id=1, source_target_pairs={{0,32},{32,0},{64,96},{96,64},{1,33},{33,1},{65,97},{97,65},{2,34}... | collective-permute-start | bytes 1253384 | tf_op jit(solution)/shard_map/ppermute | solution.py:580
  17.8 8.1 %copy-start.24 = (bf16[192,512]{1,0:T(8,128)(2,1)}, bf16[192,512]{1,0:T(8,128)(2,1)S(1)}, u32[]{:S(2)}) copy-start(bf16[192,512]{1,0:T(8,128)(2,1)S(1)} %collective-permute-done.6.w3b) | copy-start | bytes 589828
  17.8 8.1 %collective-permute-start.3 = (bf16[192,1152]{1,0:T(8,128)(2,1)}, bf16[192,1152]{1,0:T(8,128)(2,1)S(1)}, u32[]{:S(2)}, u32[]{:S(2)}) collective-permute-start(bf16[192,1152]{1,0:T(8,128)(2,1)} %get-tuple-element.75), channel_id=1, source_target_pairs={{0,32},{32,0},{64,96},{96,64},{1,33},{33,1},{65,97},{97,65},{2,34}... | collective-permute-start | bytes 1327112 | tf_op jit(solution)/shard_map/ppermute | solution.py:580
  21.4 4.5 %copy-start.23 = (bf16[192,640]{1,0:T(8,128)(2,1)}, bf16[192,640]{1,0:T(8,128)(2,1)S(1)}, u32[]{:S(2)}) copy-start(bf16[192,640]{1,0:T(8,128)(2,1)S(1)} %collective-permute-done.5.w3a) | copy-start | bytes 737284
  21.4 19.7 %collective-permute-start.7 = (bf16[256,768]{1,0:T(8,128)(2,1)S(1)}, bf16[256,768]{1,0:T(8,128)(2,1)S(1)}, u32[]{:S(2)}, u32[]{:S(2)}) collective-permute-start(bf16[256,768]{1,0:T(8,128)(2,1)S(1)} %bitcast.44), channel_id=1, source_target_pairs={{0,32},{32,0},{64,96},{96,64},{1,33},{33,1},{65,97},{97,65},{2,34}... | collective-permute-start | bytes 1179656 | tf_op jit(solution)/shard_map/ppermute | solution.py:580
  23.9 2.1 %copy-start.15 = (bf16[192,1152]{1,0:T(8,128)(2,1)}, bf16[192,1152]{1,0:T(8,128)(2,1)S(1)}, u32[]{:S(2)}) copy-start(bf16[192,1152]{1,0:T(8,128)(2,1)S(1)} %collective-permute-done.4.w2) | copy-start | bytes 1327108
  23.9 17.2 %collective-permute-start.8 = (bf16[256,768]{1,0:T(8,128)(2,1)S(1)}, bf16[256,768]{1,0:T(8,128)(2,1)S(1)}, u32[]{:S(2)}, u32[]{:S(2)}) collective-permute-start(bf16[256,768]{1,0:T(8,128)(2,1)S(1)} %bitcast.45), channel_id=1, source_target_pairs={{0,64},{32,96},{64,0},{96,32},{1,65},{33,97},{65,1},{97,33},{2,66}... | collective-permute-start | bytes 1179656 | tf_op jit(solution)/shard_map/ppermute | solution.py:580
  23.9 2.1 %copy-start.18 = (bf16[272,768]{1,0:T(8,128)(2,1)}, bf16[272,768]{1,0:T(8,128)(2,1)S(1)}, u32[]{:S(2)}) copy-start(bf16[272,768]{1,0:T(8,128)(2,1)S(1)} %collective-permute-done.1.t1) | copy-start | bytes 1253380
  23.9 19.2 %collective-permute-start.9 = (bf16[256,768]{1,0:T(8,128)(2,1)S(1)}, bf16[256,768]{1,0:T(8,128)(2,1)S(1)}, u32[]{:S(2)}, u32[]{:S(2)}) collective-permute-start(bf16[256,768]{1,0:T(8,128)(2,1)S(1)} %bitcast.46), channel_id=1, source_target_pairs={{0,96},{32,64},{64,32},{96,0},{1,97},{33,65},{65,33},{97,1},{2,98}... | collective-permute-start | bytes 1179656 | tf_op jit(solution)/shard_map/ppermute | solution.py:580
  25.9 0.7 copy-start.19
  25.9 0.9 copy-start.16
  41.1 2.0 %copy-start.20 = (bf16[256,768]{1,0:T(8,128)(2,1)}, bf16[256,768]{1,0:T(8,128)(2,1)S(1)}, u32[]{:S(2)}) copy-start(bf16[256,768]{1,0:T(8,128)(2,1)S(1)} %collective-permute-done.7.c1) | copy-start | bytes 1179652
  41.1 2.0 %copy-start.21 = (bf16[256,768]{1,0:T(8,128)(2,1)}, bf16[256,768]{1,0:T(8,128)(2,1)S(1)}, u32[]{:S(2)}) copy-start(bf16[256,768]{1,0:T(8,128)(2,1)S(1)} %collective-permute-done.8.c2) | copy-start | bytes 1179652
  49.1 7.0 %collective-permute-start.10 = (f32[4,8,128]{2,1,0:T(8,128)}, f32[4,8,128]{2,1,0:T(8,128)S(1)}, u32[]{:S(2)}, u32[]{:S(2)}) collective-permute-start(f32[4,8,128]{2,1,0:T(8,128)} %get-tuple-element.86.s0), channel_id=1, source_target_pairs={{0,32},{32,0},{64,96},{96,64},{1,33},{33,1},{65,97},{97,65},{2,34}... | collective-permute-start | bytes 49160 | tf_op jit(solution)/shard_map/ppermute | solution.py:580
  49.1 7.0 %collective-permute-start.11 = (f32[4,8,128]{2,1,0:T(8,128)}, f32[4,8,128]{2,1,0:T(8,128)S(1)}, u32[]{:S(2)}, u32[]{:S(2)}) collective-permute-start(f32[4,8,128]{2,1,0:T(8,128)} %get-tuple-element.86.s0), channel_id=1, source_target_pairs={{0,64},{32,96},{64,0},{96,32},{1,65},{33,97},{65,1},{97,33},{2,66}... | collective-permute-start | bytes 49160 | tf_op jit(solution)/shard_map/ppermute | solution.py:580
  49.3 6.9 %collective-permute-start.12 = (f32[4,8,128]{2,1,0:T(8,128)}, f32[4,8,128]{2,1,0:T(8,128)S(1)}, u32[]{:S(2)}, u32[]{:S(2)}) collective-permute-start(f32[4,8,128]{2,1,0:T(8,128)} %get-tuple-element.86.s0), channel_id=1, source_target_pairs={{0,96},{32,64},{64,32},{96,0},{1,97},{33,65},{65,33},{97,1},{2,98}... | collective-permute-start | bytes 49160 | tf_op jit(solution)/shard_map/ppermute | solution.py:580
  56.2 16.7 %collective-permute-start.13 = (bf16[512,768]{1,0:T(8,128)(2,1)}, bf16[512,768]{1,0:T(8,128)(2,1)S(1)}, u32[]{:S(2)}, u32[]{:S(2)}) collective-permute-start(bf16[512,768]{1,0:T(8,128)(2,1)} %get-tuple-element.97), channel_id=1, source_target_pairs={{0,32},{32,0},{64,96},{96,64},{1,33},{33,1},{65,97},{97,65},{2,34}... | collective-permute-start | bytes 2359304 | tf_op jit(solution)/shard_map/ppermute | solution.py:580
  63.5 9.4 %copy-start.8 = (bf16[256,768]{1,0:T(8,128)(2,1)S(1)}, bf16[256,768]{1,0:T(8,128)(2,1)}, u32[]{:S(2)}) copy-start(bf16[256,768]{1,0:T(8,128)(2,1)} %get-tuple-element.98) | copy-start | bytes 1179652
  63.5 34.0 %all-to-all-start = ((bf16[32,72,128]{2,1,0:T(8,128)(2,1)}), bf16[32,72,128]{2,1,0:T(8,128)(2,1)S(1)}, u32[]{:S(2)}, u32[]{:S(2)}) async-start(bf16[32,72,128]{2,1,0:T(8,128)(2,1)} %bitcast.41), calls=%async_computation | async-start | bytes 1179648 | tf_op jit(solution)/shard_map/all_to_all | solution.py:743
  72.9 24.6 %copy-start.2 = (bf16[512,768]{1,0:T(8,128)(2,1)}, bf16[512,768]{1,0:T(8,128)(2,1)S(1)}, u32[]{:S(2)}) copy-start(bf16[512,768]{1,0:T(8,128)(2,1)S(1)} %collective-permute-done.13) | copy-start | bytes 2359300
  73.0 24.5 %collective-permute-start.14 = (bf16[256,768]{1,0:T(8,128)(2,1)S(1)}, bf16[256,768]{1,0:T(8,128)(2,1)S(1)}, u32[]{:S(2)}, u32[]{:S(2)}) collective-permute-start(bf16[256,768]{1,0:T(8,128)(2,1)S(1)} %add_convert_fusion.1), channel_id=1, source_target_pairs={{0,64},{32,96},{64,0},{96,32},{1,65},{33,97},{65,1},{97,33},{2,66}... | collective-permute-start | bytes 1179656 | tf_op jit(solution)/shard_map/ppermute | solution.py:580
  97.5 0.7 copy-start.7
  98.3 33.8 %all-to-all-start.1 = ((bf16[32,208,128]{2,1,0:T(8,128)(2,1)}), bf16[32,208,128]{2,1,0:T(8,128)(2,1)S(1)}, u32[]{:S(2)}, u32[]{:S(2)}) async-start(bf16[32,208,128]{2,1,0:T(8,128)(2,1)} %get-tuple-element.116), calls=%async_computation.1 | async-start | bytes 3407872 | tf_op jit(solution)/shard_map/all_to_all | solution.py:743
  108.3 3.0 %collective-permute-start.17 = (bf16[18,128]{1,0:T(8,128)(2,1)S(1)}, bf16[18,128]{1,0:T(8,128)(2,1)S(1)}, u32[]{:S(2)}, u32[]{:S(2)}) collective-permute-start(bf16[18,128]{1,0:T(8,128)(2,1)S(1)} %get-tuple-element.140), channel_id=1, source_target_pairs={{0,32},{32,0},{64,96},{96,64},{1,33},{33,1},{65,97},{97,65},{2,34}... | collective-permute-start | bytes 13832 | tf_op jit(solution)/shard_map/ppermute | solution.py:580
  109.5 11.2 %collective-permute-start.18 = (bf16[18,128]{1,0:T(8,128)(2,1)S(1)}, bf16[18,128]{1,0:T(8,128)(2,1)S(1)}, u32[]{:S(2)}, u32[]{:S(2)}) collective-permute-start(bf16[18,128]{1,0:T(8,128)(2,1)S(1)} %get-tuple-element.139), channel_id=1, source_target_pairs={{0,64},{32,96},{64,0},{96,32},{1,65},{33,97},{65,1},{97,33},{2,66}... | collective-permute-start | bytes 13832 | tf_op jit(solution)/shard_map/ppermute | solution.py:580
  109.5 14.9 %collective-permute-start.19 = (bf16[18,128]{1,0:T(8,128)(2,1)S(1)}, bf16[18,128]{1,0:T(8,128)(2,1)S(1)}, u32[]{:S(2)}, u32[]{:S(2)}) collective-permute-start(bf16[18,128]{1,0:T(8,128)(2,1)S(1)} %get-tuple-element.138), channel_id=1, source_target_pairs={{0,96},{32,64},{64,32},{96,0},{1,97},{33,65},{65,33},{97,1},{2,98}... | collective-permute-start | bytes 13832 | tf_op jit(solution)/shard_map/ppermute | solution.py:580
  134.1 13.6 %copy-start.27 = (bf16[192]{0:T(256)(128)(2,1)S(1)}, bf16[192]{0:T(256)(128)(2,1)}, u32[]{:S(2)}) copy-start(bf16[192]{0:T(256)(128)(2,1)} %gain_in.1) | copy-start | bytes 1156
  134.1 14.1 %copy-start.9 = (f32[1,768]{1,0:T(1,128)S(1)}, f32[1,768]{1,0:T(1,128)}, u32[]{:S(2)}) copy-start(f32[1,768]{1,0:T(1,128)} %get-tuple-element.115) | copy-start | bytes 9220
  134.1 43.1 %copy-start.1 = (bf16[1,256,768]{2,1,0:T(8,128)(2,1)S(1)}, bf16[1,256,768]{2,1,0:T(8,128)(2,1)}, u32[]{:S(2)}) copy-start(bf16[1,256,768]{2,1,0:T(8,128)(2,1)} %param.13) | copy-start | bytes 1179652
  134.1 47.3 %all-to-all-start.2 = ((bf16[128,72,128]{2,1,0:T(8,128)(2,1)}), bf16[128,72,128]{2,1,0:T(8,128)(2,1)S(1)}, u32[]{:S(2)}, u32[]{:S(2)}) async-start(bf16[128,72,128]{2,1,0:T(8,128)(2,1)} %bitcast.19), calls=%async_computation.2 | async-start | bytes 4718592 | tf_op jit(solution)/shard_map/all_to_all | solution.py:809
  141.9 3.3 %collective-permute-start.15 = (bf16[512,768]{1,0:T(8,128)(2,1)}, bf16[512,768]{1,0:T(8,128)(2,1)S(1)}, u32[]{:S(2)}, u32[]{:S(2)}) collective-permute-start(bf16[512,768]{1,0:T(8,128)(2,1)} %get-tuple-element.113), channel_id=1, source_target_pairs={{0,32},{32,0},{64,96},{96,64},{1,33},{33,1},{65,97},{97,65},{2,34}... | collective-permute-start | bytes 2359304 | tf_op jit(solution)/shard_map/ppermute | solution.py:580
  147.0 30.2 %collective-permute-start.16 = (bf16[256,768]{1,0:T(8,128)(2,1)}, bf16[256,768]{1,0:T(8,128)(2,1)}, u32[]{:S(2)}, u32[]{:S(2)}) collective-permute-start(bf16[256,768]{1,0:T(8,128)(2,1)} %add_convert_fusion), channel_id=1, source_target_pairs={{0,64},{32,96},{64,0},{96,32},{1,65},{33,97},{65,1},{97,33},{2,66}... | collective-permute-start | bytes 1179656 | tf_op jit(solution)/shard_map/ppermute | solution.py:580
  149.0 29.7 %slice-start = ((bf16[512,768]{1,0:T(8,128)(2,1)}), bf16[256,768]{1,0:T(8,128)(2,1)S(1)}, s32[]{:S(2)}) async-start(bf16[512,768]{1,0:T(8,128)(2,1)} %copy-done.2), calls=%async_computation.3 | async-start | bytes 786432 | tf_op jit(solution)/shard_map/slice | solution.py:641
  149.0 29.7 %copy-start.3 = (bf16[256,768]{1,0:T(8,128)(2,1)S(1)}, bf16[256,768]{1,0:T(8,128)(2,1)}, u32[]{:S(2)}) copy-start(bf16[256,768]{1,0:T(8,128)(2,1)} %get-tuple-element.112) | copy-start | bytes 1179652
  149.0 29.7 %copy-start.5 = (bf16[1,256,768]{2,1,0:T(8,128)(2,1)S(1)}, bf16[1,256,768]{2,1,0:T(8,128)(2,1)}, u32[]{:S(2)}) copy-start(bf16[1,256,768]{2,1,0:T(8,128)(2,1)} %param.15) | copy-start | bytes 1179652
  149.0 29.7 %copy-start.6 = (bf16[256,768]{1,0:T(8,128)(2,1)S(1)}, bf16[256,768]{1,0:T(8,128)(2,1)}, u32[]{:S(2)}) copy-start(bf16[256,768]{1,0:T(8,128)(2,1)} %get-tuple-element.109) | copy-start | bytes 1179652
  181.4 1.4 copy-start
  (4 other events, 2.5 us)

commit v5 on v4

--- a/solution.py
+++ b/solution.py
@@ -199,43 +199,49 @@
     normed[...] = low_rows
     proj[...] = mm(low_rows, w_full[...], NN).astype(bf16)
     ext[8 : 8 + ROWS, :] = proj[:, XW : XW + CL].astype(f32)
+    found = []
     for s in range(ROWS // SPAN):
         at = s * SPAN
-        rows = slice(at, at + SPAN)
-        dt_rows = proj[rows, XW + CL :].astype(f32) + dtb[...]
-        pos_rows = pos[2 * i + s]
-        cols, step, step_t, cum, decay, carried, tails, low = span_decays(
-            dt_rows, rate[...], pos_rows
-        )
+        dt_rows = proj[at : at + SPAN, XW + CL :].astype(f32) + dtb[...]
+        found.append(span_decays(dt_rows, rate[...], pos[2 * i + s]))
+    convs = []
+    for s, (cols, *_) in enumerate(found):
+        at = s * SPAN
         v = taps[4:5, :] + taps[3:4, :] * ext[8 + at : 8 + at + SPAN, :]
         for lag in range(1, 4):
             window = ext[8 + at - lag : 8 + at - lag + SPAN, :]
             v = v + (taps[3 - lag : 4 - lag, :] * cols[:, lag : lag + 1]) * window
-        v_out[rows, :] = v
-        conv = v * jax.nn.sigmoid(v)
-        b_rows, c_rows = conv[:, XW : XW + NS], conv[:, XW + NS :]
-        scores = mm(c_rows, b_rows, NT)
-        states[s] = state[...]
-        from_state = mm(c_rows, state[...], NN)
-        ys, ends, decays_end = [], [], []
+        v_out[at : at + SPAN, :] = v
+        convs.append(v * jax.nn.sigmoid(v))
+    inners = []
+    for conv, (_, _, step_t, _, decay, _, _, low) in zip(convs, found):
+        scores = mm(conv[:, XW + NS :], conv[:, XW : XW + NS], NT)
+        products = []
         for p in range(HL // 2):
-            lanes = slice(p * SPAN, (p + 1) * SPAN)
-            xp = conv[:, lanes]
+            xp = conv[:, p * SPAN : (p + 1) * SPAN]
             mixing = [
                 decay(h) * scores * step_t[h : h + 1, :] for h in (2 * p, 2 * p + 1)
             ]
-            inner = mm(
-                jnp.concatenate(mixing, axis=1),
-                jnp.concatenate([jnp.where(low, xp, 0.0), jnp.where(low, 0.0, xp)], axis=0),
-                NN,
+            products.append(
+                mm(
+                    jnp.concatenate(mixing, axis=1),
+                    jnp.concatenate([jnp.where(low, xp, 0.0), jnp.where(low, 0.0, xp)], axis=0),
+                    NN,
+                )
+                + skip[:, p * SPAN : (p + 1) * SPAN] * xp
             )
-            ys.append(inner + carried[p] * from_state[:, lanes] + skip[:, lanes] * xp)
-            ends.append(tails[p] * xp)
-            decays_end.append(carried[p][SPAN - 1 :, :])
-        y_out[rows, :] = jnp.concatenate(ys, axis=1)
-        state[...] = jnp.concatenate(decays_end, axis=1) * state[...] + mm(
-            b_rows, jnp.concatenate(ends, axis=1), TN
-        )
+        inners.append(jnp.concatenate(products, axis=1))
+    for s, (conv, inner, (_, _, _, _, _, carried, tails, _)) in enumerate(
+        zip(convs, inners, found)
+    ):
+        carried_all = jnp.concatenate(carried, axis=1)
+        tails_all = jnp.concatenate(tails, axis=1)
+        now = state[...]
+        states[s] = now
+        from_state = mm(conv[:, XW + NS :], now, NN)
+        y_out[s * SPAN : (s + 1) * SPAN, :] = inner + carried_all * from_state
+        fresh = mm(conv[:, XW : XW + NS], tails_all * conv[:, :XW], TN)
+        state[...] = carried_all[SPAN - 1 :, :] * now + fresh
     ext[0:8, :] = ext[ROWS : ROWS + 8, :]
 
 
@@ -326,31 +332,26 @@
         return jnp.sum(value, axis=0, keepdims=True)
 
     d_proj[:, :XW] = d_gate[...]
+    found = {}
     for s in reversed(range(ROWS // SPAN)):
-        at = s * SPAN
-        rows = slice(at, at + SPAN)
+        rows = slice(s * SPAN, (s + 1) * SPAN)
+        dt_rows = proj[rows, XW + CL :].astype(f32) + dtb[...]
+        found[s] = (dt_rows,) + span_decays(dt_rows, rate[...], pos[s])
+    inside = {}
+    for s in reversed(range(ROWS // SPAN)):
+        rows = slice(s * SPAN, (s + 1) * SPAN)
         dy = dy_in[rows, :]
-        dt_rows = proj[rows, XW + CL :].astype(f32) + dtb[...]
-        cols, step, step_t, cum, decay, carried, tails, low = span_decays(
-            dt_rows, rate[...], pos[s]
-        )
+        _, _, _, step_t, _, decay, carried, _, low = found[s]
         v = v_in[rows, :]
         sig_v = jax.nn.sigmoid(v)
         conv = v * sig_v
         x, b_rows, c_rows = conv[:, :XW], conv[:, XW : XW + NS], conv[:, XW + NS :]
         add(1, down(dy * x))
-        state = states[s]
-        state_grad = d_state[...]
         scores = mm(c_rows, b_rows, NT)
-        from_state = mm(c_rows, state, NN)
-        from_grad = mm(b_rows, state_grad, NN)
-        carried_all = jnp.concatenate(carried, axis=1)
-        tails_all = jnp.concatenate(tails, axis=1)
-        dy_carried = dy * carried_all
-        x_tail = x * tails_all
+        from_state = mm(c_rows, states[s], NN)
         d_scores = jnp.zeros((SPAN, SPAN), f32)
         row_sums = jnp.zeros((SPAN, SPAN), f32)
-        col_sums, dxs = [], []
+        col_sums, inners = [], []
         for p in range(HL // 2):
             lanes = slice(p * SPAN, (p + 1) * SPAN)
             xp, dyp = x[:, lanes], dy[:, lanes]
@@ -368,9 +369,23 @@
                 col_sums.append(down(plain))
                 row_sum = jnp.sum(plain * step_t[h : h + 1, :], axis=1, keepdims=True)
                 row_sums = jnp.where(lane_at == h, row_sum, row_sums)
-            inner = mm(jnp.concatenate(mixing, axis=0), halves, TN)
-            dxs.append(inner + skip[:, lanes] * dyp + tails[p] * from_grad[:, lanes])
-        dx = jnp.concatenate(dxs, axis=1)
+            inners.append(mm(jnp.concatenate(mixing, axis=0), halves, TN) + skip[:, lanes] * dyp)
+        inner = jnp.concatenate(inners, axis=1)
+        inside[s] = (v, sig_v, x, b_rows, c_rows, from_state, d_scores, row_sums, col_sums, inner)
+    for s in reversed(range(ROWS // SPAN)):
+        at = s * SPAN
+        rows = slice(at, at + SPAN)
+        dy = dy_in[rows, :]
+        dt_rows, cols, step, _, cum, _, carried, tails, _ = found[s]
+        v, sig_v, x, b_rows, c_rows, from_state, d_scores, row_sums, col_sums, inner = inside[s]
+        state = states[s]
+        state_grad = d_state[...]
+        from_grad = mm(b_rows, state_grad, NN)
+        carried_all = jnp.concatenate(carried, axis=1)
+        tails_all = jnp.concatenate(tails, axis=1)
+        dy_carried = dy * carried_all
+        x_tail = x * tails_all
+        dx = inner + tails_all * from_grad
         d_c = mm(d_scores, b_rows, NN) + mm(dy_carried, state, NT)
         d_b = mm(d_scores, c_rows, TN) + mm(x_tail, state_grad, NT)
 
@@ -791,12 +806,12 @@
     bundle2, received1, branches = lax.optimization_barrier((bundle2, received1, branches))
     received2 = spread(bundle2)
     d_parts = to_core(*n_parts)
-    d_parts = to_owner(*d_parts)
     by_member = total(received1).reshape(4, 18, 128)
     turns = [lax.dynamic_index_in_dim(by_member, g ^ d, 0, keepdims=False) for d in range(4)]
     turns = jnp.stack([turns[0]] + [among(turns[d], d) for d in range(1, 4)])
     outs = jnp.stack([lax.dynamic_index_in_dim(turns, g ^ k, 0, keepdims=False) for k in range(4)])
-    reduced2, outs = lax.optimization_barrier((total(received2), outs))
+    reduced2, outs, d_parts = lax.optimization_barrier((total(received2), outs, d_parts))
+    d_parts = to_owner(*d_parts)
     payload = jnp.concatenate(
         [
             reduced2[:192].reshape(4, 48, 128),

time: 188 us -> 184 us (0.979)
  other arithmetic: 8.35 us -> 6.12 us
  local copies, waits for them, and re-layouts: 7.96 us -> 5.84 us
    unnamed x56 -> x52, local copies, waits for them, and re-layouts: 4.3 us -> 2.15 us
  transfers between devices with their start and end apart: 23 -> 23, of which waited for: 9 -> 8; matrix products, arithmetic and copies ran while one was open for 5% -> 4% of each run, Pallas kernels for 26% -> 27%
where the time goes in v5:
time: 184 us; the launch traced here: 183 us
  waiting for transfers between devices  61.7 us (34%)
  Pallas kernels  61.3 us (33%)
  starting transfers between devices  47.2 us (26%)
  other arithmetic  6.12 us (3%)
  local copies, waits for them, and re-layouts  5.84 us (3%)
    ppermute x18, waiting for transfers between devices, among(): return lax.ppermute(value, 'group', [(i, i ^ d) for i in range(4)])  53.5 us
    pallas_call x1, Pallas kernels, local(): call(backward_kernel, 'backward', 26, grid=(blocks,), in_specs=[scalar_sp...  23.6 us
    all_to_all x2, starting transfers between devices, spread(): return lax.all_to_all(value, 'rep', 0, 0, tiled=True)  19.2 us
    ppermute x18, starting transfers between devices, among(): return lax.ppermute(value, 'group', [(i, i ^ d) for i in range(4)])  15.8 us
    pallas_call x1, Pallas kernels, local(): call(forward_kernel, 'forward', 15, grid=(blocks,), in_specs=[scalar_spec...  13.9 us
    all_to_all x1, starting transfers between devices, local(): lax.all_to_all(jnp.broadcast_to(payload[:, None], (4, reps, 72, 128)).res...  8.73 us
    pallas_call x1, Pallas kernels, local(): call(out_kernel, 'out', 6, grid=(blocks,), in_specs=[scalar_spec] + [part...  6.73 us
    all_to_all x2, waiting for transfers between devices, spread(): return lax.all_to_all(value, 'rep', 0, 0, tiled=True)  5.75 us
  transfers between devices with their start and end apart: 23, of which 8 were waited for; matrix products, arithmetic and copies ran while one was open for 4% of the time, Pallas kernels for 27%

profile of v5, /device:TPU:1, one launch (start us, length us, event | category | flops | bytes accessed | tf_op | source)
XLA Modules:
  0.0 183.3 jit_solution(5235303760953409451)
XLA Ops:
  0.7 2.9 %columns.1 = (bf16[192,1152]{1,0:T(8,128)(2,1)}, bf16[192,1152]{1,0:T(8,128)(2,1)}, bf16[192,1152]{1,0:T(8,128)(2,1)}, bf16[192,640]{1,0:T(8,128)(2,1)}, bf16[19...) custom-call(s32[1]{0:T(128)} %bitcast.1.me, bf16[192,3352]{1,0:T(8,128)(2,1)} %w_in.1, bf16[256,768]{1,0:T(8,128)(2,1)} %bitcast.40, ...), custom_call_target="tpu_custom_call" | custom-call | flops 2000000000 | bytes 1048576 | tf_op jit(solution)/shard_map/columns/pallas_call | solution.py:610
  3.6 2.1 %collective-permute-start = (bf16[272,768]{1,0:T(8,128)(2,1)}, bf16[272,768]{1,0:T(8,128)(2,1)S(1)}, u32[]{:S(2)}, u32[]{:S(2)}) collective-permute-start(bf16[272,768]{1,0:T(8,128)(2,1)} %get-tuple-element.75.t0), channel_id=1, source_target_pairs={{0,64},{32,96},{64,0},{96,32},{1,65},{33,97},{65,1},{97,33},{2,66}... | collective-permute-start | bytes 1253384 | tf_op jit(solution)/shard_map/ppermute | solution.py:595
  5.7 2.7 %collective-permute-start.6 = (bf16[192,512]{1,0:T(8,128)(2,1)}, bf16[192,512]{1,0:T(8,128)(2,1)S(1)}, u32[]{:S(2)}, u32[]{:S(2)}) collective-permute-start(bf16[192,512]{1,0:T(8,128)(2,1)} %get-tuple-element.81), channel_id=1, source_target_pairs={{0,97},{32,65},{64,33},{96,1},{1,96},{33,64},{65,32},{97,0},{2,99}... | collective-permute-start | bytes 589832 | tf_op jit(solution)/shard_map/ppermute | solution.py:626
  8.5 0.8 collective-permute-start.4
  9.3 5.6 %collective-permute-done.t2 = bf16[272,768]{1,0:T(8,128)(2,1)S(1)} collective-permute-done((bf16[272,768]{1,0:T(8,128)(2,1)}, bf16[272,768]{1,0:T(8,128)(2,1)S(1)}, u32[]{:S(2)}, u32[]{:S(2)}) %collective-permute-start) | collective-permute-done | bytes 417824 | tf_op jit(solution)/shard_map/ppermute | solution.py:595
  14.9 2.9 %collective-permute-start.1 = (bf16[272,768]{1,0:T(8,128)(2,1)}, bf16[272,768]{1,0:T(8,128)(2,1)S(1)}, u32[]{:S(2)}, u32[]{:S(2)}) collective-permute-start(bf16[272,768]{1,0:T(8,128)(2,1)} %get-tuple-element.75.t0), channel_id=1, source_target_pairs={{0,32},{32,0},{64,96},{96,64},{1,33},{33,1},{65,97},{97,65},{2,34}... | collective-permute-start | bytes 1253384 | tf_op jit(solution)/shard_map/ppermute | solution.py:595
  17.8 0.5 collective-permute-start.3
  18.4 0.6 reshape_reshape.3.skip
  19.0 0.6 reshape.151.gain_out
  19.6 0.5 pad_bitcast_fusion.rate
  20.1 0.5 bitcast_convert_fusion.dtb
  20.6 0.8 collective-permute-done.5.w3a
  21.4 2.4 %collective-permute-done.4.w2 = bf16[192,1152]{1,0:T(8,128)(2,1)S(1)} collective-permute-done((bf16[192,1152]{1,0:T(8,128)(2,1)}, bf16[192,1152]{1,0:T(8,128)(2,1)S(1)}, u32[]{:S(2)}, u32[]{:S(2)}) %collective-permute-start.4) | collective-permute-done | bytes 442400 | tf_op jit(solution)/shard_map/ppermute | solution.py:626
  23.9 2.0 %collective-permute-start.9 = (bf16[256,768]{1,0:T(8,128)(2,1)S(1)}, bf16[256,768]{1,0:T(8,128)(2,1)S(1)}, u32[]{:S(2)}, u32[]{:S(2)}) collective-permute-start(bf16[256,768]{1,0:T(8,128)(2,1)S(1)} %bitcast.46), channel_id=1, source_target_pairs={{0,96},{32,64},{64,32},{96,0},{1,97},{33,65},{65,33},{97,1},{2,98}... | collective-permute-start | bytes 1179656 | tf_op jit(solution)/shard_map/ppermute | solution.py:595
  26.0 0.7 copy-done.17
  26.7 0.2 copy-done.14
  26.8 13.9 %forward.1 = (bf16[768,1152]{1,0:T(8,128)(2,1)}, bf16[1024,768]{1,0:T(8,128)(2,1)}, bf16[1024,1152]{1,0:T(8,128)(2,1)}, f32[1024,640]{1,0:T(8,128)}, f32[8,128,3...) custom-call(s32[1]{0:T(128)} %bitcast.1.me, ...), custom_call_target="tpu_custom_call" | custom-call | flops 15000000512 | bytes 1048576 | tf_op jit(solution)/shard_map/forward/pallas_call | solution.py:661
  40.7 2.4 %collective-permute-done.9.c3 = bf16[256,768]{1,0:T(8,128)(2,1)S(1)} collective-permute-done((bf16[256,768]{1,0:T(8,128)(2,1)S(1)}, bf16[256,768]{1,0:T(8,128)(2,1)S(1)}, u32[]{:S(2)}, u32[]{:S(2)}) %collective-permute-start.9) | collective-permute-done | bytes 393248 | tf_op jit(solution)/shard_map/ppermute | solution.py:595
  43.1 0.7 copy-done.20
  43.9 5.2 %sums.1 = (f32[1024,384]{1,0:T(8,128)}, f32[4,8,128]{2,1,0:T(8,128)}) custom-call(s32[1]{0:T(128)} %bitcast.1.me, bf16[256,768]{1,0:T(8,128)(2,1)} %bitcast.42, bf16[256,768]{1,0:T(8,128)(2,1)} %copy-done.18, bf16[256,768]{1,0:T(8,128)(2,1)} %copy-done.19, bf16[256,768]{1,0:T(8,128)(2,1)} %copy-done.20, bf16[1024,1152]{1,0:T(8,128)(2,1)} %get-tuple-element.82.gate_in.proj, ...), custom_call_target="tpu_custom_call" | custom-call | flops 4000000000 | bytes 1048576 | tf_op jit(solution)/shard_map/sums/pallas_call | solution.py:705
  49.1 0.2 collective-permute-start.11
  49.3 2.0 %collective-permute-start.12 = (f32[4,8,128]{2,1,0:T(8,128)}, f32[4,8,128]{2,1,0:T(8,128)S(1)}, u32[]{:S(2)}, u32[]{:S(2)}) collective-permute-start(f32[4,8,128]{2,1,0:T(8,128)} %get-tuple-element.89.s0), channel_id=1, source_target_pairs={{0,96},{32,64},{64,32},{96,0},{1,97},{33,65},{65,33},{97,1},{2,98}... | collective-permute-start | bytes 49160 | tf_op jit(solution)/shard_map/ppermute | solution.py:595
  51.2 4.9 %branch.1 = (bf16[256,768]{1,0:T(8,128)(2,1)}, bf16[512,768]{1,0:T(8,128)(2,1)}, bf16[256,768]{1,0:T(8,128)(2,1)}) custom-call(s32[1]{0:T(128)} %bitcast.1.me, bf16[1024,1152]{1,0:T(8,128)(2,1)} %get-tuple-element.82.gate_in.proj, f32[1024,384]{1,0:T(8,128)} %get-tuple-element.83.y_in, f32[1,384]{1,0:T(1,128)} %reshape.151.gain_out, bf16[384,768]{1,0:T(8,128)(2,1)} %w_out.3), custom_call_target="tpu_custom_call" | custom-call | flops 3000000000 | bytes 1048576 | tf_op jit(solution)/shard_map/branch/pallas_call | solution.py:719
  56.3 0.5 copy-done.9
  56.8 6.7 %out.1 = (bf16[2304,128]{1,0:T(8,128)(2,1)}, bf16[1024,384]{1,0:T(8,128)(2,1)}, f32[1024,384]{1,0:T(8,128)}, f32[8,384]{1,0:T(8,128)}) custom-call(s32[1]{0:T(128)} %bitcast.1.me, bf16[256,768]{1,0:T(8,128)(2,1)} %bitcast.43, bf16[256,768]{1,0:T(8,128)(2,1)} %copy-done.18, bf16[256,768]{1,0:T(8,128)(2,1)} %copy-done.19, bf16[256,768]{1,0:T(8,128)(2,1)} %copy-done.20, ...), custom_call_target="tpu_custom_call" | custom-call | flops 6000000000 | bytes 1048576 | tf_op jit(solution)/shard_map/out/pallas_call | solution.py:732
  63.5 9.4 %all-to-all-start = ((bf16[32,72,128]{2,1,0:T(8,128)(2,1)}), bf16[32,72,128]{2,1,0:T(8,128)(2,1)S(1)}, u32[]{:S(2)}, u32[]{:S(2)}) async-start(bf16[32,72,128]{2,1,0:T(8,128)(2,1)} %bitcast.41), calls=%async_computation | async-start | bytes 1179648 | tf_op jit(solution)/shard_map/all_to_all | solution.py:758
  73.0 0.1 add_convert_fusion.1
  73.1 1.1 collective-permute-start.14
  74.2 23.6 %backward.1 = (bf16[32,208,128]{2,1,0:T(8,128)(2,1)}, bf16[256,768]{1,0:T(8,128)(2,1)}, bf16[512,768]{1,0:T(8,128)(2,1)}, bf16[256,768]{1,0:T(8,128)(2,1)}) custom-call(s32[1]{0:T(128)} %bitcast.1.me, bf16[768,1152]{1,0:T(8,128)(2,1)} %get-tuple-element.93.w_full, bf16[1024,768]{1,0:T(8,128)(2,1)} %get-tuple-element.94.normed, ...), custom_call_target="tpu_custom_call" | custom-call | flops 25999998976 | bytes 1048576 | tf_op jit(solution)/shard_map/backward/pallas_call | solution.py:769
  97.8 9.8 %all-to-all-start.1 = ((bf16[32,208,128]{2,1,0:T(8,128)(2,1)}), bf16[32,208,128]{2,1,0:T(8,128)(2,1)S(1)}, u32[]{:S(2)}, u32[]{:S(2)}) async-start(bf16[32,208,128]{2,1,0:T(8,128)(2,1)} %get-tuple-element.115), calls=%async_computation.1 | async-start | bytes 3407872 | tf_op jit(solution)/shard_map/all_to_all | solution.py:758
  107.6 1.2 collective-permute-start.18
  108.8 0.1 reduce_sum.44
  109.0 0.1 collective-permute-start.15
  109.2 2.0 %collective-permute-start.17 = (bf16[18,128]{1,0:T(8,128)(2,1)S(1)}, bf16[18,128]{1,0:T(8,128)(2,1)S(1)}, u32[]{:S(2)}, u32[]{:S(2)}) collective-permute-start(bf16[18,128]{1,0:T(8,128)(2,1)S(1)} %get-tuple-element.144), channel_id=1, source_target_pairs={{0,96},{32,64},{64,32},{96,0},{1,97},{33,65},{65,33},{97,1},{2,98}... | collective-permute-start | bytes 13832 | tf_op jit(solution)/shard_map/ppermute | solution.py:595
  111.3 9.0 %collective-permute-done.16 = bf16[18,128]{1,0:T(8,128)(2,1)S(1)} collective-permute-done((bf16[18,128]{1,0:T(8,128)(2,1)S(1)}, bf16[18,128]{1,0:T(8,128)(2,1)S(1)}, u32[]{:S(2)}, u32[]{:S(2)}) %collective-permute-start.16) | collective-permute-done | bytes 4640 | tf_op jit(solution)/shard_map/ppermute | solution.py:595
  120.3 3.7 %collective-permute-done.17 = bf16[18,128]{1,0:T(8,128)(2,1)S(1)} collective-permute-done((bf16[18,128]{1,0:T(8,128)(2,1)S(1)}, bf16[18,128]{1,0:T(8,128)(2,1)S(1)}, u32[]{:S(2)}, u32[]{:S(2)}) %collective-permute-start.17) | collective-permute-done | bytes 4640 | tf_op jit(solution)/shard_map/ppermute | solution.py:595
  124.1 1.8 %add_convert_fusion = bf16[256,768]{1,0:T(8,128)(2,1)} fusion(bf16[256,768]{1,0:T(8,128)(2,1)} %get-tuple-element.119, bf16[512,768]{1,0:T(8,128)(2,1)S(1)} %collective-permute-done.18), kind=kLoop, calls=%fused_computation.10 | loop fusion | flops 786432 | bytes 1179648 | tf_op jit(solution)/shard_map/convert_element_type | solution.py:655
  125.9 5.7 %all-to-all-done.1 = bf16[32,208,128]{2,1,0:T(8,128)(2,1)S(1)} async-done(((bf16[32,208,128]{2,1,0:T(8,128)(2,1)}), bf16[32,208,128]{2,1,0:T(8,128)(2,1)S(1)}, u32[]{:S(2)}, u32[]{:S(2)}) %all-to-all-start.1) | async-done | bytes 1703968 | tf_op jit(solution)/shard_map/all_to_all | solution.py:758
  131.7 0.2 reduce_sum.43
  132.0 1.7 broadcast_in_dim.16
  133.7 8.7 %all-to-all-start.2 = ((bf16[128,72,128]{2,1,0:T(8,128)(2,1)}), bf16[128,72,128]{2,1,0:T(8,128)(2,1)}, u32[]{:S(2)}, u32[]{:S(2)}) async-start(bf16[128,72,128]{2,1,0:T(8,128)(2,1)} %bitcast.19), calls=%async_computation.2 | async-start | bytes 4718592 | tf_op jit(solution)/shard_map/all_to_all | solution.py:824
  142.5 1.5 collective-permute-start.19
  144.0 0.6 reshape.152
  144.6 0.7 add_bitcast_fusion
  145.3 32.0 %collective-permute-done.19 = bf16[256,768]{1,0:T(8,128)(2,1)S(1)} collective-permute-done((bf16[256,768]{1,0:T(8,128)(2,1)}, bf16[256,768]{1,0:T(8,128)(2,1)S(1)}, u32[]{:S(2)}, u32[]{:S(2)}) %collective-permute-start.19) | collective-permute-done | bytes 393248 | tf_op jit(solution)/shard_map/ppermute | solution.py:595
  177.3 0.4 fusion.1
  177.7 1.6 fusion.4
  179.2 4.0 %assemble.1 = (f32[192,3352]{1,0:T(8,128)}, f32[384,768]{1,0:T(8,128)}, f32[4,448]{1,0:T(4,128)}, f32[1,448]{1,0:T(1,128)}, f32[1,192]{1,0:T(1,128)}, /*index=5*...) custom-call(s32[1]{0:T(128)} %bitcast.1.me, bf16[128,72,128]{2,1,0:T(8,128)(2,1)} %all-to-all-done.2.parts, ...), custom_call_target="tpu_custom_call" | custom-call | flops 4000000000 | bytes 1048576 | tf_op jit(solution)/shard_map/assemble/pallas_call | solution.py:843
  (89 shorter events, 0.7 us)
Async XLA Ops:
  0.7 17.7 %copy-start.23 = (bf16[6]{0:T(256)(128)(2,1)S(1)}, bf16[6]{0:T(256)(128)(2,1)}, u32[]{:S(2)}) copy-start(bf16[6]{0:T(256)(128)(2,1)} %param.21) | copy-start | bytes 40
  0.7 17.7 %copy-start.12 = (bf16[6]{0:T(256)(128)(2,1)S(1)}, bf16[6]{0:T(256)(128)(2,1)}, u32[]{:S(2)}) copy-start(bf16[6]{0:T(256)(128)(2,1)} %param.22) | copy-start | bytes 40
  0.7 18.4 %copy-start.8 = (bf16[384]{0:T(512)(128)(2,1)S(1)}, bf16[384]{0:T(512)(128)(2,1)}, u32[]{:S(2)}) copy-start(bf16[384]{0:T(512)(128)(2,1)} %param.23) | copy-start | bytes 2308
  0.7 19.4 %copy-start.24 = (bf16[6]{0:T(256)(128)(2,1)S(1)}, bf16[6]{0:T(256)(128)(2,1)}, u32[]{:S(2)}) copy-start(bf16[6]{0:T(256)(128)(2,1)} %param.20) | copy-start | bytes 40
  0.7 20.7 %copy-start.3 = (bf16[1,256,768]{2,1,0:T(8,128)(2,1)S(1)}, bf16[1,256,768]{2,1,0:T(8,128)(2,1)}, u32[]{:S(2)}) copy-start(bf16[1,256,768]{2,1,0:T(8,128)(2,1)} %param.15) | copy-start | bytes 1179652
  3.6 11.3 %collective-permute-start = (bf16[272,768]{1,0:T(8,128)(2,1)}, bf16[272,768]{1,0:T(8,128)(2,1)S(1)}, u32[]{:S(2)}, u32[]{:S(2)}) collective-permute-start(bf16[272,768]{1,0:T(8,128)(2,1)} %get-tuple-element.75.t0), channel_id=1, source_target_pairs={{0,64},{32,96},{64,0},{96,32},{1,65},{33,97},{65,1},{97,33},{2,66}... | collective-permute-start | bytes 1253384 | tf_op jit(solution)/shard_map/ppermute | solution.py:595
  5.7 12.1 %collective-permute-start.6 = (bf16[192,512]{1,0:T(8,128)(2,1)}, bf16[192,512]{1,0:T(8,128)(2,1)S(1)}, u32[]{:S(2)}, u32[]{:S(2)}) collective-permute-start(bf16[192,512]{1,0:T(8,128)(2,1)} %get-tuple-element.81), channel_id=1, source_target_pairs={{0,97},{32,65},{64,33},{96,1},{1,96},{33,64},{65,32},{97,0},{2,99}... | collective-permute-start | bytes 589832 | tf_op jit(solution)/shard_map/ppermute | solution.py:626
  8.5 15.4 %collective-permute-start.4 = (bf16[192,1152]{1,0:T(8,128)(2,1)}, bf16[192,1152]{1,0:T(8,128)(2,1)S(1)}, u32[]{:S(2)}, u32[]{:S(2)}) collective-permute-start(bf16[192,1152]{1,0:T(8,128)(2,1)} %get-tuple-element.79), channel_id=1, source_target_pairs={{0,65},{32,97},{64,1},{96,33},{1,64},{33,96},{65,0},{97,32},{2,67}... | collective-permute-start | bytes 1327112 | tf_op jit(solution)/shard_map/ppermute | solution.py:626
  9.3 12.2 %collective-permute-start.5 = (bf16[192,640]{1,0:T(8,128)(2,1)}, bf16[192,640]{1,0:T(8,128)(2,1)S(1)}, u32[]{:S(2)}, u32[]{:S(2)}) collective-permute-start(bf16[192,640]{1,0:T(8,128)(2,1)} %get-tuple-element.80), channel_id=1, source_target_pairs={{0,96},{32,64},{64,32},{96,0},{1,97},{33,65},{65,33},{97,1},{2,98}... | collective-permute-start | bytes 737288 | tf_op jit(solution)/shard_map/ppermute | solution.py:595
  14.9 11.0 %copy-start.15 = (bf16[272,768]{1,0:T(8,128)(2,1)}, bf16[272,768]{1,0:T(8,128)(2,1)S(1)}, u32[]{:S(2)}) copy-start(bf16[272,768]{1,0:T(8,128)(2,1)S(1)} %collective-permute-done.t2) | copy-start | bytes 1253380
  14.9 9.0 %collective-permute-start.1 = (bf16[272,768]{1,0:T(8,128)(2,1)}, bf16[272,768]{1,0:T(8,128)(2,1)S(1)}, u32[]{:S(2)}, u32[]{:S(2)}) collective-permute-start(bf16[272,768]{1,0:T(8,128)(2,1)} %get-tuple-element.75.t0), channel_id=1, source_target_pairs={{0,32},{32,0},{64,96},{96,64},{1,33},{33,1},{65,97},{97,65},{2,34}... | collective-permute-start | bytes 1253384 | tf_op jit(solution)/shard_map/ppermute | solution.py:595
  17.8 8.1 %collective-permute-start.2 = (bf16[272,768]{1,0:T(8,128)(2,1)S(1)}, bf16[272,768]{1,0:T(8,128)(2,1)S(1)}, u32[]{:S(2)}, u32[]{:S(2)}) collective-permute-start(bf16[272,768]{1,0:T(8,128)(2,1)S(1)} %collective-permute-done.t2), channel_id=1, source_target_pairs={{0,32},{32,0},{64,96},{96,64},{1,33},{33,1},{65,97},{97,65},{2,34}... | collective-permute-start | bytes 1253384 | tf_op jit(solution)/shard_map/ppermute | solution.py:595
  17.8 8.1 %copy-start.22 = (bf16[192,512]{1,0:T(8,128)(2,1)}, bf16[192,512]{1,0:T(8,128)(2,1)S(1)}, u32[]{:S(2)}) copy-start(bf16[192,512]{1,0:T(8,128)(2,1)S(1)} %collective-permute-done.6.w3b) | copy-start | bytes 589828
  17.8 8.1 %collective-permute-start.3 = (bf16[192,1152]{1,0:T(8,128)(2,1)}, bf16[192,1152]{1,0:T(8,128)(2,1)S(1)}, u32[]{:S(2)}, u32[]{:S(2)}) collective-permute-start(bf16[192,1152]{1,0:T(8,128)(2,1)} %get-tuple-element.78), channel_id=1, source_target_pairs={{0,32},{32,0},{64,96},{96,64},{1,33},{33,1},{65,97},{97,65},{2,34}... | collective-permute-start | bytes 1327112 | tf_op jit(solution)/shard_map/ppermute | solution.py:595
  21.4 4.5 %copy-start.21 = (bf16[192,640]{1,0:T(8,128)(2,1)}, bf16[192,640]{1,0:T(8,128)(2,1)S(1)}, u32[]{:S(2)}) copy-start(bf16[192,640]{1,0:T(8,128)(2,1)S(1)} %collective-permute-done.5.w3a) | copy-start | bytes 737284
  21.4 19.3 %collective-permute-start.7 = (bf16[256,768]{1,0:T(8,128)(2,1)S(1)}, bf16[256,768]{1,0:T(8,128)(2,1)S(1)}, u32[]{:S(2)}, u32[]{:S(2)}) collective-permute-start(bf16[256,768]{1,0:T(8,128)(2,1)S(1)} %bitcast.44), channel_id=1, source_target_pairs={{0,32},{32,0},{64,96},{96,64},{1,33},{33,1},{65,97},{97,65},{2,34}... | collective-permute-start | bytes 1179656 | tf_op jit(solution)/shard_map/ppermute | solution.py:595
  23.9 2.1 %copy-start.13 = (bf16[192,1152]{1,0:T(8,128)(2,1)}, bf16[192,1152]{1,0:T(8,128)(2,1)S(1)}, u32[]{:S(2)}) copy-start(bf16[192,1152]{1,0:T(8,128)(2,1)S(1)} %collective-permute-done.4.w2) | copy-start | bytes 1327108
  23.9 16.8 %collective-permute-start.8 = (bf16[256,768]{1,0:T(8,128)(2,1)S(1)}, bf16[256,768]{1,0:T(8,128)(2,1)S(1)}, u32[]{:S(2)}, u32[]{:S(2)}) collective-permute-start(bf16[256,768]{1,0:T(8,128)(2,1)S(1)} %bitcast.45), channel_id=1, source_target_pairs={{0,64},{32,96},{64,0},{96,32},{1,65},{33,97},{65,1},{97,33},{2,66}... | collective-permute-start | bytes 1179656 | tf_op jit(solution)/shard_map/ppermute | solution.py:595
  23.9 2.1 %copy-start.16 = (bf16[272,768]{1,0:T(8,128)(2,1)}, bf16[272,768]{1,0:T(8,128)(2,1)S(1)}, u32[]{:S(2)}) copy-start(bf16[272,768]{1,0:T(8,128)(2,1)S(1)} %collective-permute-done.1.t1) | copy-start | bytes 1253380
  23.9 19.2 %collective-permute-start.9 = (bf16[256,768]{1,0:T(8,128)(2,1)S(1)}, bf16[256,768]{1,0:T(8,128)(2,1)S(1)}, u32[]{:S(2)}, u32[]{:S(2)}) collective-permute-start(bf16[256,768]{1,0:T(8,128)(2,1)S(1)} %bitcast.46), channel_id=1, source_target_pairs={{0,96},{32,64},{64,32},{96,0},{1,97},{33,65},{65,33},{97,1},{2,98}... | collective-permute-start | bytes 1179656 | tf_op jit(solution)/shard_map/ppermute | solution.py:595
  25.9 0.7 copy-start.17
  25.9 0.9 copy-start.14
  40.7 2.5 %copy-start.18 = (bf16[256,768]{1,0:T(8,128)(2,1)}, bf16[256,768]{1,0:T(8,128)(2,1)S(1)}, u32[]{:S(2)}) copy-start(bf16[256,768]{1,0:T(8,128)(2,1)S(1)} %collective-permute-done.7.c1) | copy-start | bytes 1179652
  40.7 2.4 %copy-start.19 = (bf16[256,768]{1,0:T(8,128)(2,1)}, bf16[256,768]{1,0:T(8,128)(2,1)S(1)}, u32[]{:S(2)}) copy-start(bf16[256,768]{1,0:T(8,128)(2,1)S(1)} %collective-permute-done.8.c2) | copy-start | bytes 1179652
  43.1 0.7 copy-start.20
  49.1 7.0 %collective-permute-start.10 = (f32[4,8,128]{2,1,0:T(8,128)}, f32[4,8,128]{2,1,0:T(8,128)S(1)}, u32[]{:S(2)}, u32[]{:S(2)}) collective-permute-start(f32[4,8,128]{2,1,0:T(8,128)} %get-tuple-element.89.s0), channel_id=1, source_target_pairs={{0,32},{32,0},{64,96},{96,64},{1,33},{33,1},{65,97},{97,65},{2,34}... | collective-permute-start | bytes 49160 | tf_op jit(solution)/shard_map/ppermute | solution.py:595
  49.1 7.0 %collective-permute-start.11 = (f32[4,8,128]{2,1,0:T(8,128)}, f32[4,8,128]{2,1,0:T(8,128)S(1)}, u32[]{:S(2)}, u32[]{:S(2)}) collective-permute-start(f32[4,8,128]{2,1,0:T(8,128)} %get-tuple-element.89.s0), channel_id=1, source_target_pairs={{0,64},{32,96},{64,0},{96,32},{1,65},{33,97},{65,1},{97,33},{2,66}... | collective-permute-start | bytes 49160 | tf_op jit(solution)/shard_map/ppermute | solution.py:595
  49.3 6.9 %collective-permute-start.12 = (f32[4,8,128]{2,1,0:T(8,128)}, f32[4,8,128]{2,1,0:T(8,128)S(1)}, u32[]{:S(2)}, u32[]{:S(2)}) collective-permute-start(f32[4,8,128]{2,1,0:T(8,128)} %get-tuple-element.89.s0), channel_id=1, source_target_pairs={{0,96},{32,64},{64,32},{96,0},{1,97},{33,65},{65,33},{97,1},{2,98}... | collective-permute-start | bytes 49160 | tf_op jit(solution)/shard_map/ppermute | solution.py:595
  56.2 0.6 copy-start.11
  56.2 16.7 %collective-permute-start.13 = (bf16[512,768]{1,0:T(8,128)(2,1)}, bf16[512,768]{1,0:T(8,128)(2,1)S(1)}, u32[]{:S(2)}, u32[]{:S(2)}) collective-permute-start(bf16[512,768]{1,0:T(8,128)(2,1)} %get-tuple-element.100), channel_id=1, source_target_pairs={{0,32},{32,0},{64,96},{96,64},{1,33},{33,1},{65,97},{97,65},{2,34}... | collective-permute-start | bytes 2359304 | tf_op jit(solution)/shard_map/ppermute | solution.py:595
  63.5 9.4 %copy-start.6 = (bf16[256,768]{1,0:T(8,128)(2,1)S(1)}, bf16[256,768]{1,0:T(8,128)(2,1)}, u32[]{:S(2)}) copy-start(bf16[256,768]{1,0:T(8,128)(2,1)} %get-tuple-element.101) | copy-start | bytes 1179652
  63.5 34.2 %all-to-all-start = ((bf16[32,72,128]{2,1,0:T(8,128)(2,1)}), bf16[32,72,128]{2,1,0:T(8,128)(2,1)S(1)}, u32[]{:S(2)}, u32[]{:S(2)}) async-start(bf16[32,72,128]{2,1,0:T(8,128)(2,1)} %bitcast.41), calls=%async_computation | async-start | bytes 1179648 | tf_op jit(solution)/shard_map/all_to_all | solution.py:758
  72.9 24.8 %copy-start.1 = (bf16[512,768]{1,0:T(8,128)(2,1)}, bf16[512,768]{1,0:T(8,128)(2,1)S(1)}, u32[]{:S(2)}) copy-start(bf16[512,768]{1,0:T(8,128)(2,1)S(1)} %collective-permute-done.13) | copy-start | bytes 2359300
  73.1 24.7 %collective-permute-start.14 = (bf16[256,768]{1,0:T(8,128)(2,1)S(1)}, bf16[256,768]{1,0:T(8,128)(2,1)S(1)}, u32[]{:S(2)}, u32[]{:S(2)}) collective-permute-start(bf16[256,768]{1,0:T(8,128)(2,1)S(1)} %add_convert_fusion.1), channel_id=1, source_target_pairs={{0,64},{32,96},{64,0},{96,32},{1,65},{33,97},{65,1},{97,33},{2,66}... | collective-permute-start | bytes 1179656 | tf_op jit(solution)/shard_map/ppermute | solution.py:595
  97.8 33.9 %all-to-all-start.1 = ((bf16[32,208,128]{2,1,0:T(8,128)(2,1)}), bf16[32,208,128]{2,1,0:T(8,128)(2,1)S(1)}, u32[]{:S(2)}, u32[]{:S(2)}) async-start(bf16[32,208,128]{2,1,0:T(8,128)(2,1)} %get-tuple-element.115), calls=%async_computation.1 | async-start | bytes 3407872 | tf_op jit(solution)/shard_map/all_to_all | solution.py:758
  107.6 16.4 %collective-permute-start.18 = (bf16[512,768]{1,0:T(8,128)(2,1)}, bf16[512,768]{1,0:T(8,128)(2,1)S(1)}, u32[]{:S(2)}, u32[]{:S(2)}) collective-permute-start(bf16[512,768]{1,0:T(8,128)(2,1)} %get-tuple-element.118), channel_id=1, source_target_pairs={{0,32},{32,0},{64,96},{96,64},{1,33},{33,1},{65,97},{97,65},{2,34}... | collective-permute-start | bytes 2359304 | tf_op jit(solution)/shard_map/ppermute | solution.py:595
  109.0 2.3 %collective-permute-start.15 = (bf16[18,128]{1,0:T(8,128)(2,1)S(1)}, bf16[18,128]{1,0:T(8,128)(2,1)S(1)}, u32[]{:S(2)}, u32[]{:S(2)}) collective-permute-start(bf16[18,128]{1,0:T(8,128)(2,1)S(1)} %get-tuple-element.146), channel_id=1, source_target_pairs={{0,32},{32,0},{64,96},{96,64},{1,33},{33,1},{65,97},{97,65},{2,34}... | collective-permute-start | bytes 13832 | tf_op jit(solution)/shard_map/ppermute | solution.py:595
  109.1 11.2 %collective-permute-start.16 = (bf16[18,128]{1,0:T(8,128)(2,1)S(1)}, bf16[18,128]{1,0:T(8,128)(2,1)S(1)}, u32[]{:S(2)}, u32[]{:S(2)}) collective-permute-start(bf16[18,128]{1,0:T(8,128)(2,1)S(1)} %get-tuple-element.145), channel_id=1, source_target_pairs={{0,64},{32,96},{64,0},{96,32},{1,65},{33,97},{65,1},{97,33},{2,66}... | collective-permute-start | bytes 13832 | tf_op jit(solution)/shard_map/ppermute | solution.py:595
  109.2 14.8 %collective-permute-start.17 = (bf16[18,128]{1,0:T(8,128)(2,1)S(1)}, bf16[18,128]{1,0:T(8,128)(2,1)S(1)}, u32[]{:S(2)}, u32[]{:S(2)}) collective-permute-start(bf16[18,128]{1,0:T(8,128)(2,1)S(1)} %get-tuple-element.144), channel_id=1, source_target_pairs={{0,96},{32,64},{64,32},{96,0},{1,97},{33,65},{65,33},{97,1},{2,98}... | collective-permute-start | bytes 13832 | tf_op jit(solution)/shard_map/ppermute | solution.py:595
  133.7 10.2 %copy-start.25 = (bf16[192]{0:T(256)(128)(2,1)S(1)}, bf16[192]{0:T(256)(128)(2,1)}, u32[]{:S(2)}) copy-start(bf16[192]{0:T(256)(128)(2,1)} %gain_in.1) | copy-start | bytes 1156
  133.7 10.8 %copy-start.7 = (f32[1,768]{1,0:T(1,128)S(1)}, f32[1,768]{1,0:T(1,128)}, u32[]{:S(2)}) copy-start(f32[1,768]{1,0:T(1,128)} %get-tuple-element.123) | copy-start | bytes 9220
  133.7 43.5 %copy-start = (bf16[1,256,768]{2,1,0:T(8,128)(2,1)S(1)}, bf16[1,256,768]{2,1,0:T(8,128)(2,1)}, u32[]{:S(2)}) copy-start(bf16[1,256,768]{2,1,0:T(8,128)(2,1)} %param.13) | copy-start | bytes 1179652
  133.7 43.5 %copy-start.2 = (bf16[256,768]{1,0:T(8,128)(2,1)S(1)}, bf16[256,768]{1,0:T(8,128)(2,1)}, u32[]{:S(2)}) copy-start(bf16[256,768]{1,0:T(8,128)(2,1)} %get-tuple-element.120) | copy-start | bytes 1179652
  133.7 45.5 %all-to-all-start.2 = ((bf16[128,72,128]{2,1,0:T(8,128)(2,1)}), bf16[128,72,128]{2,1,0:T(8,128)(2,1)}, u32[]{:S(2)}, u32[]{:S(2)}) async-start(bf16[128,72,128]{2,1,0:T(8,128)(2,1)} %bitcast.19), calls=%async_computation.2 | async-start | bytes 4718592 | tf_op jit(solution)/shard_map/all_to_all | solution.py:824
  142.5 35.2 %slice-start = ((bf16[512,768]{1,0:T(8,128)(2,1)}), bf16[256,768]{1,0:T(8,128)(2,1)S(1)}, s32[]{:S(2)}) async-start(bf16[512,768]{1,0:T(8,128)(2,1)} %copy-done.1), calls=%async_computation.3 | async-start | bytes 786432 | tf_op jit(solution)/shard_map/slice | solution.py:656
  142.5 35.2 %copy-start.4 = (bf16[1,256,768]{2,1,0:T(8,128)(2,1)S(1)}, bf16[1,256,768]{2,1,0:T(8,128)(2,1)}, u32[]{:S(2)}) copy-start(bf16[1,256,768]{2,1,0:T(8,128)(2,1)} %param.15) | copy-start | bytes 1179652
  142.5 35.2 %copy-start.5 = (bf16[256,768]{1,0:T(8,128)(2,1)S(1)}, bf16[256,768]{1,0:T(8,128)(2,1)}, u32[]{:S(2)}) copy-start(bf16[256,768]{1,0:T(8,128)(2,1)} %get-tuple-element.112) | copy-start | bytes 1179652
  142.5 34.8 %collective-permute-start.19 = (bf16[256,768]{1,0:T(8,128)(2,1)}, bf16[256,768]{1,0:T(8,128)(2,1)S(1)}, u32[]{:S(2)}, u32[]{:S(2)}) collective-permute-start(bf16[256,768]{1,0:T(8,128)(2,1)} %add_convert_fusion), channel_id=1, source_target_pairs={{0,64},{32,96},{64,0},{96,32},{1,65},{33,97},{65,1},{97,33},{2,66}... | collective-permute-start | bytes 1179656 | tf_op jit(solution)/shard_map/ppermute | solution.py:595
  (2 other events, 1.2 us)

commit v6 on v5

--- a/solution.py
+++ b/solution.py
@@ -271,16 +271,16 @@
 
 
 def out_kernel(
-    me, c0, c1, c2, c3, gate_in, y_in, dno_in, s0, s1, s2, s3, gain_out,
-    bundle, d_gate, dy_out, sums,
-    cot, acc_out, acc_sum, normed_out,
+    me, c0, c1, c2, c3, gate_in, y_in, dno_in, s0, s1, s2, s3, gain_out, normed,
+    bundle, left, d_gate, dy_out, sums,
+    cot, acc_out, acc_gate, acc_sum, normed_out,
 ):
     i = pl.program_id(0)
     g = me[0]
 
     @pl.when(i == 0)
     def _():
-        for ref in (acc_out, acc_sum):
+        for ref in (acc_out, acc_gate, acc_sum):
             ref[...] = jnp.zeros_like(ref)
 
     pick(g ^ i, (c0, c1, c2, c3), cot)
@@ -302,12 +302,27 @@
         dy_out[rows, :] = d_gated * silu
         d_gate[rows, :] = (d_gated * y * (sig * (1.0 + gate * (1.0 - sig)))).astype(bf16)
     acc_out[...] += mm(normed_out[...], cot[...], TN)
+    acc_gate[...] += mm(normed[...], d_gate[...], TN)
 
     @pl.when(i == pl.num_programs(0) - 1)
     def _():
         sums[...] = acc_sum[...]
-        for t in range(6):
-            bundle[XW * t : XW * t + XW, :] = acc_out[:, 128 * t : 128 * t + 128].astype(bf16)
+        for k in range(4):
+            for piece in range(36):
+                tile, row = piece // 12, 192 * k + 16 * (piece % 12)
+                value = acc_gate[row : row + 16, 128 * tile : 128 * tile + 128].astype(bf16)
+                if piece < 32:
+                    bundle[piece, 16 * k : 16 * k + 16, :] = value
+                else:
+                    left[4 * k + piece - 32] = value
+        for piece in range(160):
+            at = 64 + 16 * (piece % 5)
+            tile, row = piece // 24, 16 * (piece % 24)
+            if piece < 144:
+                value = acc_out[row : row + 16, 128 * tile : 128 * tile + 128].astype(bf16)
+            else:
+                value = jnp.zeros((16, 128), bf16)
+            bundle[piece // 5, at : at + 16, :] = value
 
 
 def split_sum(rows, ones):
@@ -425,13 +440,13 @@
     ext[ROWS:, :] = ext[0:8, :]
     d_normed = mm(d_proj[...], w_full[...], NT)
     add(9, down(d_normed * normed[...].astype(f32)))
-    acc_in[...] += mm(normed[...], d_proj[:, : XW + CL], TN)
+    acc_in[...] += mm(normed[...], d_proj[:, XW : XW + CL], TN)
     acc_dt[...] += mm(d_proj[:, XW + CL :], normed[...], TN)[0:8, :]
     return d_normed.astype(bf16)
 
 
 def backward_kernel(
-    me, w_full, normed, proj, v_in, states, dy_in, d_gate, pos, taps, dtb, rate, skip, ones, sums,
+    me, w_full, normed, proj, v_in, states, dy_in, d_gate, pos, taps, dtb, rate, skip, ones, sums, left,
     bundle, n_own, n_pair, n_across,
     d_state, ext, acc_in, acc_dt, acc_small, d_proj, small,
 ):
@@ -467,11 +482,14 @@
         lay(49, acc_small, 2, 1)
         lay(50, acc_small, 3, 1)
         for k in range(4):
-            for tile in range(8):
-                for q in range(4):
-                    bundle[4 * tile + q, 48 * k : 48 * k + 48, :] = acc_in[
-                        192 * k + 48 * q : 192 * k + 48 * q + 48, 128 * tile : 128 * tile + 128
-                    ].astype(bf16)
+            for piece in range(64):
+                at = 32 * k + 16 * (piece % 2)
+                tile, row = piece // 12, 192 * k + 16 * (piece % 12)
+                if piece < 60:
+                    value = acc_in[row : row + 16, 128 * tile : 128 * tile + 128].astype(bf16)
+                else:
+                    value = left[4 * k + piece - 60]
+                bundle[piece // 2, at : at + 16, :] = value
             first, second = 192 * k, 192 * k + 128
             for h in range(HL):
                 small[k, 2 * h : 2 * h + 1, :] = acc_dt[h : h + 1, first : first + 128]
@@ -483,7 +501,7 @@
                 value = jnp.concatenate([small[k, 4 * r : 4 * r + 4, :] for k in range(4)], axis=0)
             else:
                 value = jnp.zeros((16, 128), f32)
-            bundle[r, 192:208, :] = value.astype(bf16)
+            bundle[r, 128:144, :] = value.astype(bf16)
 
 
 def assemble_kernel(
@@ -494,30 +512,36 @@
 ):
     g = me[0]
     for r in range(32):
-        tile, q = r // 4, r % 4
         chunks = [parts[32 * k + r].astype(f32) for k in range(4)]
-        rows = slice(48 * q, 48 * q + 48)
-        if tile < 6:
-            for k in range(4):
-                start = (tile // 3) * DI + k * XW + (tile % 3) * 128
-                grad_in[rows, start : start + 128] = chunks[k][:48]
-        else:
-            start = 2 * DI + 128 * (tile - 6)
-            grad_in[rows, start : start + 128] = (chunks[0][:48] + chunks[1][:48]) + (
-                chunks[2][:48] + chunks[3][:48]
-            )
+        pieces = [(0, r)]
+        for n in (2 * r, 2 * r + 1):
+            pieces.append((16 + 16 * (n % 2), 36 + n if n < 60 else n - 28))
+        for at, piece in pieces:
+            tile, row = piece // 12, 16 * (piece % 12)
+            values = [chunk[at : at + 16] for chunk in chunks]
+            if tile < 6:
+                for k in range(4):
+                    start = (tile // 3) * DI + k * XW + (tile % 3) * 128
+                    grad_in[row : row + 16, start : start + 128] = values[k]
+            else:
+                start = 2 * DI + 128 * (tile - 6)
+                grad_in[row : row + 16, start : start + 128] = (values[0] + values[1]) + (
+                    values[2] + values[3]
+                )
         for k in range(4):
-            first = 72 * r + 18 * k
             done = 0
-            while done < 18:
-                column, row = divmod(first + done, XW)
-                count = min(18 - done, XW - row)
-                grad_out[row : row + count, 128 * column : 128 * column + 128] = chunks[k][
-                    48 + done : 48 + done + count
-                ]
+            while done < 20:
+                piece, inside = divmod(20 * k + done, 16)
+                piece += 5 * r
+                count = min(20 - done, 16 - inside)
+                if piece < 144:
+                    row, column = 16 * (piece % 24) + inside, 128 * (piece // 24)
+                    grad_out[row : row + count, column : column + 128] = chunks[k][
+                        48 + done : 48 + done + count
+                    ]
                 done += count
             if r < 16:
-                shorts[k, 4 * r : 4 * r + 4, :] = chunks[k][66:70]
+                shorts[k, 4 * r : 4 * r + 4, :] = chunks[k][68:72]
 
     turned[...] = jnp.zeros_like(turned)
     wide[...] = jnp.zeros_like(wide)
@@ -729,7 +753,7 @@
     )(me, proj, y_rows, gain_o, w_out)
     o_parts, all_stats = lax.optimization_barrier((o_parts, all_stats))
 
-    bundle1, d_gate, dy, sums = call(
+    bundle1, left, d_gate, dy, sums = call(
         out_kernel,
         "out",
         6,
@@ -738,26 +762,28 @@
         + [part] * 4
         + [gate_spec, blocked((ROWS, XW), up), blocked((ROWS, XW), up)]
         + [blocked((1, 8, SPAN), up)] * 4
-        + [whole((1, XW))],
+        + [whole((1, XW)), blocked((ROWS, D), up)],
         out_specs=[
-            whole((2304, 128)), blocked((ROWS, XW), up), blocked((ROWS, XW), up), whole((8, XW)),
+            whole((32, 144, 128)), whole((16, 16, 128)), blocked((ROWS, XW), up), blocked((ROWS, XW), up), whole((8, XW)),
         ],
         out_shape=(
-            shape((2304, 128), bf16), shape((length, XW), bf16), shape((length, XW), f32),
+            shape((32, 144, 128), bf16), shape((16, 16, 128), bf16),
+            shape((length, XW), bf16), shape((length, XW), f32),
             shape((8, XW), f32),
         ),
         scratch_shapes=[
             pltpu.VMEM((ROWS, D), bf16),
             pltpu.VMEM((XW, D), f32),
+            pltpu.VMEM((D, XW), f32),
             pltpu.VMEM((8, XW), f32),
             pltpu.VMEM((ROWS, XW), bf16),
         ],
-    )(me, cot, c1, c2, c3, proj, y_rows, dno, *all_stats, gain_o)
+    )(me, cot, c1, c2, c3, proj, y_rows, dno, *all_stats, gain_o, normed)
 
     def spread(value):
         return lax.all_to_all(value, "rep", 0, 0, tiled=True)
 
-    received1 = spread(bundle1.reshape(reps, 72, 128))
+    received1 = spread(bundle1)
     branches = to_core(*o_parts)
     dy, branches = lax.optimization_barrier((dy, branches))
     branches = to_owner(*branches)
@@ -783,13 +809,14 @@
             blocked((2, 16, SPAN), back),
             whole((8, CL)), whole((1, 128)), whole((1, 128)), whole((1, XW)), whole((XW, 128)),
             whole((8, XW)),
+            whole((16, 16, 128)),
         ],
-        out_specs=[whole((32, 208, 128))] + by_owner_specs,
-        out_shape=(shape((32, 208, 128), bf16),) + by_owner_shapes,
+        out_specs=[whole((32, 144, 128))] + by_owner_specs,
+        out_shape=(shape((32, 144, 128), bf16),) + by_owner_shapes,
         scratch_shapes=[
             pltpu.VMEM((NS, XW), f32),
             pltpu.VMEM((ROWS + 8, CL), f32),
-            pltpu.VMEM((D, XW + CL), f32),
+            pltpu.VMEM((D, CL), f32),
             pltpu.VMEM((8, D), f32),
             pltpu.VMEM((16, D), f32),
             pltpu.VMEM((ROWS, PW), bf16),
@@ -797,7 +824,7 @@
         ],
     )(
         me, w_full, normed, proj, v_rows, states, dy, d_gate, pos, taps, dtb, rate, skip, ones,
-        sums,
+        sums, left,
     )
 
     def total(received):
@@ -806,18 +833,22 @@
     bundle2, received1, branches = lax.optimization_barrier((bundle2, received1, branches))
     received2 = spread(bundle2)
     d_parts = to_core(*n_parts)
-    by_member = total(received1).reshape(4, 18, 128)
+    reduced1 = total(received1)
+    by_member = reduced1[64:].reshape(4, 20, 128)
     turns = [lax.dynamic_index_in_dim(by_member, g ^ d, 0, keepdims=False) for d in range(4)]
     turns = jnp.stack([turns[0]] + [among(turns[d], d) for d in range(1, 4)])
     outs = jnp.stack([lax.dynamic_index_in_dim(turns, g ^ k, 0, keepdims=False) for k in range(4)])
-    reduced2, outs, d_parts = lax.optimization_barrier((total(received2), outs, d_parts))
+    first = reduced1[:64].reshape(4, 16, 128)
+    reduced2, outs, first, d_parts = lax.optimization_barrier(
+        (total(received2), outs, first, d_parts)
+    )
     d_parts = to_owner(*d_parts)
     payload = jnp.concatenate(
         [
-            reduced2[:192].reshape(4, 48, 128),
+            first,
+            reduced2[:128].reshape(4, 32, 128),
             outs,
-            reduced2[192:].reshape(4, 4, 128),
-            jnp.zeros((4, 2, 128), bf16),
+            reduced2[128:].reshape(4, 4, 128),
         ],
         axis=1,
     )

time: 184 us -> 178 us (0.967)
  waiting for transfers between devices: 61.7 us -> 55.1 us
    ppermute x18, waiting for transfers between devices: 53.5 us -> 47.1 us  [among(): return lax.ppermute(value, 'group', [(i, i ^ d) for i in range(4)])]
  transfers between devices with their start and end apart: 23 -> 23, of which waited for: 8 -> 8; matrix products, arithmetic and copies ran while one was open for 4% -> 5% of each run, Pallas kernels for 27% -> 28%
where the time goes in v6:
time: 178 us; the launch traced here: 177 us
  Pallas kernels  62.1 us (35%)
  waiting for transfers between devices  55.1 us (31%)
  starting transfers between devices  45.9 us (26%)
  other arithmetic  6.63 us (4%)
  local copies, waits for them, and re-layouts  6.5 us (4%)
    ppermute x18, waiting for transfers between devices, among(): return lax.ppermute(value, 'group', [(i, i ^ d) for i in range(4)])  47.1 us
    pallas_call x1, Pallas kernels, local(): call(backward_kernel, 'backward', 26, grid=(blocks,), in_specs=[scalar_sp...  22.9 us
    all_to_all x2, starting transfers between devices, spread(): return lax.all_to_all(value, 'rep', 0, 0, tiled=True)  19.2 us
    ppermute x18, starting transfers between devices, among(): return lax.ppermute(value, 'group', [(i, i ^ d) for i in range(4)])  15.8 us
    pallas_call x1, Pallas kernels, local(): call(forward_kernel, 'forward', 15, grid=(blocks,), in_specs=[scalar_spec...  13.9 us
    pallas_call x1, Pallas kernels, local(): call(out_kernel, 'out', 6, grid=(blocks,), in_specs=[scalar_spec] + [part...  8.27 us
    all_to_all x1, starting transfers between devices, local(): lax.all_to_all(jnp.broadcast_to(payload[:, None], (4, reps, 72, 128)).res...  7.35 us
    all_to_all x2, waiting for transfers between devices, spread(): return lax.all_to_all(value, 'rep', 0, 0, tiled=True)  5.58 us
  transfers between devices with their start and end apart: 23, of which 8 were waited for; matrix products, arithmetic and copies ran while one was open for 5% of the time, Pallas kernels for 28%

profile of v6, /device:TPU:1, one launch (start us, length us, event | category | flops | bytes accessed | tf_op | source)
XLA Modules:
  0.0 177.3 jit_solution(2318841655159692461)
XLA Ops:
  0.7 2.9 %columns.1 = (bf16[192,1152]{1,0:T(8,128)(2,1)}, bf16[192,1152]{1,0:T(8,128)(2,1)}, bf16[192,1152]{1,0:T(8,128)(2,1)}, bf16[192,640]{1,0:T(8,128)(2,1)}, bf16[19...) custom-call(s32[1]{0:T(128)} %bitcast.1.me, bf16[192,3352]{1,0:T(8,128)(2,1)} %w_in.1, bf16[256,768]{1,0:T(8,128)(2,1)} %bitcast.40, ...), custom_call_target="tpu_custom_call" | custom-call | flops 2000000000 | bytes 1048576 | tf_op jit(solution)/shard_map/columns/pallas_call | solution.py:634
  3.6 2.1 %collective-permute-start = (bf16[272,768]{1,0:T(8,128)(2,1)}, bf16[272,768]{1,0:T(8,128)(2,1)S(1)}, u32[]{:S(2)}, u32[]{:S(2)}) collective-permute-start(bf16[272,768]{1,0:T(8,128)(2,1)} %get-tuple-element.77.t0), channel_id=1, source_target_pairs={{0,64},{32,96},{64,0},{96,32},{1,65},{33,97},{65,1},{97,33},{2,66}... | collective-permute-start | bytes 1253384 | tf_op jit(solution)/shard_map/ppermute | solution.py:619
  5.7 2.7 %collective-permute-start.6 = (bf16[192,512]{1,0:T(8,128)(2,1)}, bf16[192,512]{1,0:T(8,128)(2,1)S(1)}, u32[]{:S(2)}, u32[]{:S(2)}) collective-permute-start(bf16[192,512]{1,0:T(8,128)(2,1)} %get-tuple-element.83), channel_id=1, source_target_pairs={{0,97},{32,65},{64,33},{96,1},{1,96},{33,64},{65,32},{97,0},{2,99}... | collective-permute-start | bytes 589832 | tf_op jit(solution)/shard_map/ppermute | solution.py:650
  8.5 0.8 collective-permute-start.4
  9.2 5.6 %collective-permute-done.t2 = bf16[272,768]{1,0:T(8,128)(2,1)S(1)} collective-permute-done((bf16[272,768]{1,0:T(8,128)(2,1)}, bf16[272,768]{1,0:T(8,128)(2,1)S(1)}, u32[]{:S(2)}, u32[]{:S(2)}) %collective-permute-start) | collective-permute-done | bytes 417824 | tf_op jit(solution)/shard_map/ppermute | solution.py:619
  14.9 2.9 %collective-permute-start.1 = (bf16[272,768]{1,0:T(8,128)(2,1)}, bf16[272,768]{1,0:T(8,128)(2,1)S(1)}, u32[]{:S(2)}, u32[]{:S(2)}) collective-permute-start(bf16[272,768]{1,0:T(8,128)(2,1)} %get-tuple-element.77.t0), channel_id=1, source_target_pairs={{0,32},{32,0},{64,96},{96,64},{1,33},{33,1},{65,97},{97,65},{2,34}... | collective-permute-start | bytes 1253384 | tf_op jit(solution)/shard_map/ppermute | solution.py:619
  17.8 0.5 collective-permute-start.3
  18.4 0.6 reshape_reshape.3.skip
  19.0 0.6 reshape.151.gain_out
  19.6 0.5 pad_bitcast_fusion.rate
  20.1 0.5 bitcast_convert_fusion.dtb
  20.6 0.8 collective-permute-done.5.w3a
  21.4 2.4 %collective-permute-done.4.w2 = bf16[192,1152]{1,0:T(8,128)(2,1)S(1)} collective-permute-done((bf16[192,1152]{1,0:T(8,128)(2,1)}, bf16[192,1152]{1,0:T(8,128)(2,1)S(1)}, u32[]{:S(2)}, u32[]{:S(2)}) %collective-permute-start.4) | collective-permute-done | bytes 442400 | tf_op jit(solution)/shard_map/ppermute | solution.py:650
  23.9 2.0 %collective-permute-start.9 = (bf16[256,768]{1,0:T(8,128)(2,1)S(1)}, bf16[256,768]{1,0:T(8,128)(2,1)S(1)}, u32[]{:S(2)}, u32[]{:S(2)}) collective-permute-start(bf16[256,768]{1,0:T(8,128)(2,1)S(1)} %bitcast.45), channel_id=1, source_target_pairs={{0,96},{32,64},{64,32},{96,0},{1,97},{33,65},{65,33},{97,1},{2,98}... | collective-permute-start | bytes 1179656 | tf_op jit(solution)/shard_map/ppermute | solution.py:619
  26.0 0.7 copy-done.18
  26.7 0.1 copy-done.15
  26.8 13.9 %forward.1 = (bf16[768,1152]{1,0:T(8,128)(2,1)}, bf16[1024,768]{1,0:T(8,128)(2,1)}, bf16[1024,1152]{1,0:T(8,128)(2,1)}, f32[1024,640]{1,0:T(8,128)}, f32[8,128,3...) custom-call(s32[1]{0:T(128)} %bitcast.1.me, ...), custom_call_target="tpu_custom_call" | custom-call | flops 15000000512 | bytes 1048576 | tf_op jit(solution)/shard_map/forward/pallas_call | solution.py:685
  40.7 2.4 %collective-permute-done.9.c3 = bf16[256,768]{1,0:T(8,128)(2,1)S(1)} collective-permute-done((bf16[256,768]{1,0:T(8,128)(2,1)S(1)}, bf16[256,768]{1,0:T(8,128)(2,1)S(1)}, u32[]{:S(2)}, u32[]{:S(2)}) %collective-permute-start.9) | collective-permute-done | bytes 393248 | tf_op jit(solution)/shard_map/ppermute | solution.py:619
  43.1 0.7 copy-done.21
  43.9 5.2 %sums.1 = (f32[1024,384]{1,0:T(8,128)}, f32[4,8,128]{2,1,0:T(8,128)}) custom-call(s32[1]{0:T(128)} %bitcast.1.me, bf16[256,768]{1,0:T(8,128)(2,1)} %bitcast.41, bf16[256,768]{1,0:T(8,128)(2,1)} %copy-done.19, bf16[256,768]{1,0:T(8,128)(2,1)} %copy-done.20, bf16[256,768]{1,0:T(8,128)(2,1)} %copy-done.21, bf16[1024,1152]{1,0:T(8,128)(2,1)} %get-tuple-element.84.gate_in.proj, ...), custom_call_target="tpu_custom_call" | custom-call | flops 4000000000 | bytes 1048576 | tf_op jit(solution)/shard_map/sums/pallas_call | solution.py:729
  49.1 0.2 collective-permute-start.11
  49.3 2.0 %collective-permute-start.12 = (f32[4,8,128]{2,1,0:T(8,128)}, f32[4,8,128]{2,1,0:T(8,128)S(1)}, u32[]{:S(2)}, u32[]{:S(2)}) collective-permute-start(f32[4,8,128]{2,1,0:T(8,128)} %get-tuple-element.91.s0), channel_id=1, source_target_pairs={{0,96},{32,64},{64,32},{96,0},{1,97},{33,65},{65,33},{97,1},{2,98}... | collective-permute-start | bytes 49160 | tf_op jit(solution)/shard_map/ppermute | solution.py:619
  51.3 4.9 %branch.1 = (bf16[256,768]{1,0:T(8,128)(2,1)}, bf16[512,768]{1,0:T(8,128)(2,1)}, bf16[256,768]{1,0:T(8,128)(2,1)}) custom-call(s32[1]{0:T(128)} %bitcast.1.me, bf16[1024,1152]{1,0:T(8,128)(2,1)} %get-tuple-element.84.gate_in.proj, f32[1024,384]{1,0:T(8,128)} %get-tuple-element.85.y_in, f32[1,384]{1,0:T(1,128)} %reshape.151.gain_out, bf16[384,768]{1,0:T(8,128)(2,1)} %w_out.3), custom_call_target="tpu_custom_call" | custom-call | flops 3000000000 | bytes 1048576 | tf_op jit(solution)/shard_map/branch/pallas_call | solution.py:743
  56.3 0.5 copy-done.10
  56.8 8.3 %out.1 = (bf16[32,144,128]{2,1,0:T(8,128)(2,1)}, bf16[16,16,128]{2,1,0:T(8,128)(2,1)}, bf16[1024,384]{1,0:T(8,128)(2,1)}, f32[1024,384]{1,0:T(8,128)}, f32[8,384]{1,0:T(8,128)}) custom-call(s32[1]{0:T(128)} %bitcast.1.me, bf16[256,768]{1,0:T(8,128)(2,1)} %bitcast.42, bf16[256,768]{1,0:T(8,128)(2,1)} %copy-done.19, bf16[256,768]{1,0:T(8,128)(2,1)} %copy-done.20, ...), custom_call_target="tpu_custom_call" | custom-call | flops 6000000000 | bytes 1048576 | tf_op jit(solution)/shard_map/out/pallas_call | solution.py:756
  65.1 9.4 %all-to-all-start = ((bf16[32,144,128]{2,1,0:T(8,128)(2,1)}), bf16[32,144,128]{2,1,0:T(8,128)(2,1)S(1)}, u32[]{:S(2)}, u32[]{:S(2)}) async-start(bf16[32,144,128]{2,1,0:T(8,128)(2,1)} %get-tuple-element.111), calls=%async_computation | async-start | bytes 2359296 | tf_op jit(solution)/shard_map/all_to_all | solution.py:784
  74.6 1.1 collective-permute-start.14
  75.7 22.9 %backward.1 = (bf16[32,144,128]{2,1,0:T(8,128)(2,1)}, bf16[256,768]{1,0:T(8,128)(2,1)}, bf16[512,768]{1,0:T(8,128)(2,1)}, bf16[256,768]{1,0:T(8,128)(2,1)}) custom-call(s32[1]{0:T(128)} %bitcast.1.me, bf16[768,1152]{1,0:T(8,128)(2,1)} %get-tuple-element.95.w_full, bf16[1024,768]{1,0:T(8,128)(2,1)} %get-tuple-element.96.normed, ...), custom_call_target="tpu_custom_call" | custom-call | flops 25999998976 | bytes 1048576 | tf_op jit(solution)/shard_map/backward/pallas_call | solution.py:795
  98.6 9.9 %all-to-all-start.1 = ((bf16[32,144,128]{2,1,0:T(8,128)(2,1)}), bf16[32,144,128]{2,1,0:T(8,128)(2,1)S(1)}, u32[]{:S(2)}, u32[]{:S(2)}) async-start(bf16[32,144,128]{2,1,0:T(8,128)(2,1)} %get-tuple-element.118), calls=%async_computation.1 | async-start | bytes 2359296 | tf_op jit(solution)/shard_map/all_to_all | solution.py:784
  108.5 1.2 collective-permute-start.18
  109.7 0.8 reduce_sum.44
  110.5 0.7 slice.38
  111.2 0.1 collective-permute-start.15
  111.4 2.0 %collective-permute-start.17 = (bf16[20,128]{1,0:T(8,128)(2,1)S(1)}, bf16[20,128]{1,0:T(8,128)(2,1)S(1)}, u32[]{:S(2)}, u32[]{:S(2)}) collective-permute-start(bf16[20,128]{1,0:T(8,128)(2,1)S(1)} %get-tuple-element.148), channel_id=1, source_target_pairs={{0,96},{32,64},{64,32},{96,0},{1,97},{33,65},{65,33},{97,1},{2,98}... | collective-permute-start | bytes 15368 | tf_op jit(solution)/shard_map/ppermute | solution.py:619
  113.5 2.8 %collective-permute-done.16 = bf16[20,128]{1,0:T(8,128)(2,1)S(1)} collective-permute-done((bf16[20,128]{1,0:T(8,128)(2,1)S(1)}, bf16[20,128]{1,0:T(8,128)(2,1)S(1)}, u32[]{:S(2)}, u32[]{:S(2)}) %collective-permute-start.16) | collective-permute-done | bytes 5152 | tf_op jit(solution)/shard_map/ppermute | solution.py:619
  116.3 3.4 %collective-permute-done.17 = bf16[20,128]{1,0:T(8,128)(2,1)S(1)} collective-permute-done((bf16[20,128]{1,0:T(8,128)(2,1)S(1)}, bf16[20,128]{1,0:T(8,128)(2,1)S(1)}, u32[]{:S(2)}, u32[]{:S(2)}) %collective-permute-start.17) | collective-permute-done | bytes 5152 | tf_op jit(solution)/shard_map/ppermute | solution.py:619
  119.8 1.8 %add_convert_fusion = bf16[256,768]{1,0:T(8,128)(2,1)} fusion(bf16[256,768]{1,0:T(8,128)(2,1)} %get-tuple-element.122, bf16[512,768]{1,0:T(8,128)(2,1)S(1)} %collective-permute-done.18), kind=kLoop, calls=%fused_computation.10 | loop fusion | flops 786432 | bytes 1179648 | tf_op jit(solution)/shard_map/convert_element_type | solution.py:679
  121.6 5.6 %all-to-all-done.1 = bf16[32,144,128]{2,1,0:T(8,128)(2,1)S(1)} async-done(((bf16[32,144,128]{2,1,0:T(8,128)(2,1)}), bf16[32,144,128]{2,1,0:T(8,128)(2,1)S(1)}, u32[]{:S(2)}, u32[]{:S(2)}) %all-to-all-start.1) | async-done | bytes 1179680 | tf_op jit(solution)/shard_map/all_to_all | solution.py:784
  127.2 0.2 reduce_sum.43
  127.4 1.7 broadcast_in_dim.5
  129.1 7.4 %all-to-all-start.2 = ((bf16[128,72,128]{2,1,0:T(8,128)(2,1)}), bf16[128,72,128]{2,1,0:T(8,128)(2,1)}, u32[]{:S(2)}, u32[]{:S(2)}) async-start(bf16[128,72,128]{2,1,0:T(8,128)(2,1)} %bitcast.19), calls=%async_computation.2 | async-start | bytes 4718592 | tf_op jit(solution)/shard_map/all_to_all | solution.py:855
  136.5 1.5 collective-permute-start.19
  138.0 0.5 reshape.152
  138.6 0.7 add_bitcast_fusion
  139.3 32.0 %collective-permute-done.19 = bf16[256,768]{1,0:T(8,128)(2,1)S(1)} collective-permute-done((bf16[256,768]{1,0:T(8,128)(2,1)S(1)}, bf16[256,768]{1,0:T(8,128)(2,1)S(1)}, u32[]{:S(2)}, u32[]{:S(2)}) %collective-permute-start.19) | collective-permute-done | bytes 393248 | tf_op jit(solution)/shard_map/ppermute | solution.py:619
  171.3 0.4 fusion.1
  171.7 1.6 fusion.4
  173.3 4.0 %assemble.1 = (f32[192,3352]{1,0:T(8,128)}, f32[384,768]{1,0:T(8,128)}, f32[4,448]{1,0:T(4,128)}, f32[1,448]{1,0:T(1,128)}, f32[1,192]{1,0:T(1,128)}, /*index=5*...) custom-call(s32[1]{0:T(128)} %bitcast.1.me, bf16[128,72,128]{2,1,0:T(8,128)(2,1)} %all-to-all-done.2.parts, ...), custom_call_target="tpu_custom_call" | custom-call | flops 4000000000 | bytes 1048576 | tf_op jit(solution)/shard_map/assemble/pallas_call | solution.py:874
  (92 shorter events, 0.7 us)
Async XLA Ops:
  0.7 17.6 %copy-start.24 = (bf16[6]{0:T(256)(128)(2,1)S(1)}, bf16[6]{0:T(256)(128)(2,1)}, u32[]{:S(2)}) copy-start(bf16[6]{0:T(256)(128)(2,1)} %param.21) | copy-start | bytes 40
  0.7 17.6 %copy-start.13 = (bf16[6]{0:T(256)(128)(2,1)S(1)}, bf16[6]{0:T(256)(128)(2,1)}, u32[]{:S(2)}) copy-start(bf16[6]{0:T(256)(128)(2,1)} %param.22) | copy-start | bytes 40
  0.7 18.4 %copy-start.9 = (bf16[384]{0:T(512)(128)(2,1)S(1)}, bf16[384]{0:T(512)(128)(2,1)}, u32[]{:S(2)}) copy-start(bf16[384]{0:T(512)(128)(2,1)} %param.23) | copy-start | bytes 2308
  0.7 19.4 %copy-start.25 = (bf16[6]{0:T(256)(128)(2,1)S(1)}, bf16[6]{0:T(256)(128)(2,1)}, u32[]{:S(2)}) copy-start(bf16[6]{0:T(256)(128)(2,1)} %param.20) | copy-start | bytes 40
  0.7 20.7 %copy-start.3 = (bf16[1,256,768]{2,1,0:T(8,128)(2,1)S(1)}, bf16[1,256,768]{2,1,0:T(8,128)(2,1)}, u32[]{:S(2)}) copy-start(bf16[1,256,768]{2,1,0:T(8,128)(2,1)} %param.15) | copy-start | bytes 1179652
  3.6 11.3 %collective-permute-start = (bf16[272,768]{1,0:T(8,128)(2,1)}, bf16[272,768]{1,0:T(8,128)(2,1)S(1)}, u32[]{:S(2)}, u32[]{:S(2)}) collective-permute-start(bf16[272,768]{1,0:T(8,128)(2,1)} %get-tuple-element.77.t0), channel_id=1, source_target_pairs={{0,64},{32,96},{64,0},{96,32},{1,65},{33,97},{65,1},{97,33},{2,66}... | collective-permute-start | bytes 1253384 | tf_op jit(solution)/shard_map/ppermute | solution.py:619
  5.7 12.1 %collective-permute-start.6 = (bf16[192,512]{1,0:T(8,128)(2,1)}, bf16[192,512]{1,0:T(8,128)(2,1)S(1)}, u32[]{:S(2)}, u32[]{:S(2)}) collective-permute-start(bf16[192,512]{1,0:T(8,128)(2,1)} %get-tuple-element.83), channel_id=1, source_target_pairs={{0,97},{32,65},{64,33},{96,1},{1,96},{33,64},{65,32},{97,0},{2,99}... | collective-permute-start | bytes 589832 | tf_op jit(solution)/shard_map/ppermute | solution.py:650
  8.5 15.4 %collective-permute-start.4 = (bf16[192,1152]{1,0:T(8,128)(2,1)}, bf16[192,1152]{1,0:T(8,128)(2,1)S(1)}, u32[]{:S(2)}, u32[]{:S(2)}) collective-permute-start(bf16[192,1152]{1,0:T(8,128)(2,1)} %get-tuple-element.81), channel_id=1, source_target_pairs={{0,65},{32,97},{64,1},{96,33},{1,64},{33,96},{65,0},{97,32},{2,67}... | collective-permute-start | bytes 1327112 | tf_op jit(solution)/shard_map/ppermute | solution.py:650
  9.2 12.2 %collective-permute-start.5 = (bf16[192,640]{1,0:T(8,128)(2,1)}, bf16[192,640]{1,0:T(8,128)(2,1)S(1)}, u32[]{:S(2)}, u32[]{:S(2)}) collective-permute-start(bf16[192,640]{1,0:T(8,128)(2,1)} %get-tuple-element.82), channel_id=1, source_target_pairs={{0,96},{32,64},{64,32},{96,0},{1,97},{33,65},{65,33},{97,1},{2,98}... | collective-permute-start | bytes 737288 | tf_op jit(solution)/shard_map/ppermute | solution.py:619
  14.9 11.0 %copy-start.16 = (bf16[272,768]{1,0:T(8,128)(2,1)}, bf16[272,768]{1,0:T(8,128)(2,1)S(1)}, u32[]{:S(2)}) copy-start(bf16[272,768]{1,0:T(8,128)(2,1)S(1)} %collective-permute-done.t2) | copy-start | bytes 1253380
  14.9 9.0 %collective-permute-start.1 = (bf16[272,768]{1,0:T(8,128)(2,1)}, bf16[272,768]{1,0:T(8,128)(2,1)S(1)}, u32[]{:S(2)}, u32[]{:S(2)}) collective-permute-start(bf16[272,768]{1,0:T(8,128)(2,1)} %get-tuple-element.77.t0), channel_id=1, source_target_pairs={{0,32},{32,0},{64,96},{96,64},{1,33},{33,1},{65,97},{97,65},{2,34}... | collective-permute-start | bytes 1253384 | tf_op jit(solution)/shard_map/ppermute | solution.py:619
  17.8 8.1 %collective-permute-start.2 = (bf16[272,768]{1,0:T(8,128)(2,1)S(1)}, bf16[272,768]{1,0:T(8,128)(2,1)S(1)}, u32[]{:S(2)}, u32[]{:S(2)}) collective-permute-start(bf16[272,768]{1,0:T(8,128)(2,1)S(1)} %collective-permute-done.t2), channel_id=1, source_target_pairs={{0,32},{32,0},{64,96},{96,64},{1,33},{33,1},{65,97},{97,65},{2,34}... | collective-permute-start | bytes 1253384 | tf_op jit(solution)/shard_map/ppermute | solution.py:619
  17.8 8.1 %copy-start.23 = (bf16[192,512]{1,0:T(8,128)(2,1)}, bf16[192,512]{1,0:T(8,128)(2,1)S(1)}, u32[]{:S(2)}) copy-start(bf16[192,512]{1,0:T(8,128)(2,1)S(1)} %collective-permute-done.6.w3b) | copy-start | bytes 589828
  17.8 8.1 %collective-permute-start.3 = (bf16[192,1152]{1,0:T(8,128)(2,1)}, bf16[192,1152]{1,0:T(8,128)(2,1)S(1)}, u32[]{:S(2)}, u32[]{:S(2)}) collective-permute-start(bf16[192,1152]{1,0:T(8,128)(2,1)} %get-tuple-element.80), channel_id=1, source_target_pairs={{0,32},{32,0},{64,96},{96,64},{1,33},{33,1},{65,97},{97,65},{2,34}... | collective-permute-start | bytes 1327112 | tf_op jit(solution)/shard_map/ppermute | solution.py:619
  21.4 4.5 %copy-start.22 = (bf16[192,640]{1,0:T(8,128)(2,1)}, bf16[192,640]{1,0:T(8,128)(2,1)S(1)}, u32[]{:S(2)}) copy-start(bf16[192,640]{1,0:T(8,128)(2,1)S(1)} %collective-permute-done.5.w3a) | copy-start | bytes 737284
  21.4 19.3 %collective-permute-start.7 = (bf16[256,768]{1,0:T(8,128)(2,1)S(1)}, bf16[256,768]{1,0:T(8,128)(2,1)S(1)}, u32[]{:S(2)}, u32[]{:S(2)}) collective-permute-start(bf16[256,768]{1,0:T(8,128)(2,1)S(1)} %bitcast.43), channel_id=1, source_target_pairs={{0,32},{32,0},{64,96},{96,64},{1,33},{33,1},{65,97},{97,65},{2,34}... | collective-permute-start | bytes 1179656 | tf_op jit(solution)/shard_map/ppermute | solution.py:619
  23.9 2.1 %copy-start.14 = (bf16[192,1152]{1,0:T(8,128)(2,1)}, bf16[192,1152]{1,0:T(8,128)(2,1)S(1)}, u32[]{:S(2)}) copy-start(bf16[192,1152]{1,0:T(8,128)(2,1)S(1)} %collective-permute-done.4.w2) | copy-start | bytes 1327108
  23.9 16.8 %collective-permute-start.8 = (bf16[256,768]{1,0:T(8,128)(2,1)S(1)}, bf16[256,768]{1,0:T(8,128)(2,1)S(1)}, u32[]{:S(2)}, u32[]{:S(2)}) collective-permute-start(bf16[256,768]{1,0:T(8,128)(2,1)S(1)} %bitcast.44), channel_id=1, source_target_pairs={{0,64},{32,96},{64,0},{96,32},{1,65},{33,97},{65,1},{97,33},{2,66}... | collective-permute-start | bytes 1179656 | tf_op jit(solution)/shard_map/ppermute | solution.py:619
  23.9 2.1 %copy-start.17 = (bf16[272,768]{1,0:T(8,128)(2,1)}, bf16[272,768]{1,0:T(8,128)(2,1)S(1)}, u32[]{:S(2)}) copy-start(bf16[272,768]{1,0:T(8,128)(2,1)S(1)} %collective-permute-done.1.t1) | copy-start | bytes 1253380
  23.9 19.2 %collective-permute-start.9 = (bf16[256,768]{1,0:T(8,128)(2,1)S(1)}, bf16[256,768]{1,0:T(8,128)(2,1)S(1)}, u32[]{:S(2)}, u32[]{:S(2)}) collective-permute-start(bf16[256,768]{1,0:T(8,128)(2,1)S(1)} %bitcast.45), channel_id=1, source_target_pairs={{0,96},{32,64},{64,32},{96,0},{1,97},{33,65},{65,33},{97,1},{2,98}... | collective-permute-start | bytes 1179656 | tf_op jit(solution)/shard_map/ppermute | solution.py:619
  25.9 0.8 copy-start.18
  25.9 0.9 copy-start.15
  40.7 2.5 %copy-start.19 = (bf16[256,768]{1,0:T(8,128)(2,1)}, bf16[256,768]{1,0:T(8,128)(2,1)S(1)}, u32[]{:S(2)}) copy-start(bf16[256,768]{1,0:T(8,128)(2,1)S(1)} %collective-permute-done.7.c1) | copy-start | bytes 1179652
  40.7 2.4 %copy-start.20 = (bf16[256,768]{1,0:T(8,128)(2,1)}, bf16[256,768]{1,0:T(8,128)(2,1)S(1)}, u32[]{:S(2)}) copy-start(bf16[256,768]{1,0:T(8,128)(2,1)S(1)} %collective-permute-done.8.c2) | copy-start | bytes 1179652
  49.1 7.1 %collective-permute-start.10 = (f32[4,8,128]{2,1,0:T(8,128)}, f32[4,8,128]{2,1,0:T(8,128)S(1)}, u32[]{:S(2)}, u32[]{:S(2)}) collective-permute-start(f32[4,8,128]{2,1,0:T(8,128)} %get-tuple-element.91.s0), channel_id=1, source_target_pairs={{0,32},{32,0},{64,96},{96,64},{1,33},{33,1},{65,97},{97,65},{2,34}... | collective-permute-start | bytes 49160 | tf_op jit(solution)/shard_map/ppermute | solution.py:619
  49.1 7.1 %collective-permute-start.11 = (f32[4,8,128]{2,1,0:T(8,128)}, f32[4,8,128]{2,1,0:T(8,128)S(1)}, u32[]{:S(2)}, u32[]{:S(2)}) collective-permute-start(f32[4,8,128]{2,1,0:T(8,128)} %get-tuple-element.91.s0), channel_id=1, source_target_pairs={{0,64},{32,96},{64,0},{96,32},{1,65},{33,97},{65,1},{97,33},{2,66}... | collective-permute-start | bytes 49160 | tf_op jit(solution)/shard_map/ppermute | solution.py:619
  49.3 6.9 %collective-permute-start.12 = (f32[4,8,128]{2,1,0:T(8,128)}, f32[4,8,128]{2,1,0:T(8,128)S(1)}, u32[]{:S(2)}, u32[]{:S(2)}) collective-permute-start(f32[4,8,128]{2,1,0:T(8,128)} %get-tuple-element.91.s0), channel_id=1, source_target_pairs={{0,96},{32,64},{64,32},{96,0},{1,97},{33,65},{65,33},{97,1},{2,98}... | collective-permute-start | bytes 49160 | tf_op jit(solution)/shard_map/ppermute | solution.py:619
  56.2 18.2 %collective-permute-start.13 = (bf16[512,768]{1,0:T(8,128)(2,1)}, bf16[512,768]{1,0:T(8,128)(2,1)S(1)}, u32[]{:S(2)}, u32[]{:S(2)}) collective-permute-start(bf16[512,768]{1,0:T(8,128)(2,1)} %get-tuple-element.102), channel_id=1, source_target_pairs={{0,32},{32,0},{64,96},{96,64},{1,33},{33,1},{65,97},{97,65},{2,34}... | collective-permute-start | bytes 2359304 | tf_op jit(solution)/shard_map/ppermute | solution.py:619
  65.1 9.4 %copy-start.7 = (bf16[256,768]{1,0:T(8,128)(2,1)S(1)}, bf16[256,768]{1,0:T(8,128)(2,1)}, u32[]{:S(2)}) copy-start(bf16[256,768]{1,0:T(8,128)(2,1)} %get-tuple-element.103) | copy-start | bytes 1179652
  65.1 33.5 %all-to-all-start = ((bf16[32,144,128]{2,1,0:T(8,128)(2,1)}), bf16[32,144,128]{2,1,0:T(8,128)(2,1)S(1)}, u32[]{:S(2)}, u32[]{:S(2)}) async-start(bf16[32,144,128]{2,1,0:T(8,128)(2,1)} %get-tuple-element.111), calls=%async_computation | async-start | bytes 2359296 | tf_op jit(solution)/shard_map/all_to_all | solution.py:784
  74.5 24.1 %copy-start.1 = (bf16[512,768]{1,0:T(8,128)(2,1)}, bf16[512,768]{1,0:T(8,128)(2,1)S(1)}, u32[]{:S(2)}) copy-start(bf16[512,768]{1,0:T(8,128)(2,1)S(1)} %collective-permute-done.13) | copy-start | bytes 2359300
  74.6 24.0 %collective-permute-start.14 = (bf16[256,768]{1,0:T(8,128)(2,1)S(1)}, bf16[256,768]{1,0:T(8,128)(2,1)S(1)}, u32[]{:S(2)}, u32[]{:S(2)}) collective-permute-start(bf16[256,768]{1,0:T(8,128)(2,1)S(1)} %add_convert_fusion.1), channel_id=1, source_target_pairs={{0,64},{32,96},{64,0},{96,32},{1,65},{33,97},{65,1},{97,33},{2,66}... | collective-permute-start | bytes 1179656 | tf_op jit(solution)/shard_map/ppermute | solution.py:619
  98.6 28.6 %all-to-all-start.1 = ((bf16[32,144,128]{2,1,0:T(8,128)(2,1)}), bf16[32,144,128]{2,1,0:T(8,128)(2,1)S(1)}, u32[]{:S(2)}, u32[]{:S(2)}) async-start(bf16[32,144,128]{2,1,0:T(8,128)(2,1)} %get-tuple-element.118), calls=%async_computation.1 | async-start | bytes 2359296 | tf_op jit(solution)/shard_map/all_to_all | solution.py:784
  108.5 11.3 %collective-permute-start.18 = (bf16[512,768]{1,0:T(8,128)(2,1)}, bf16[512,768]{1,0:T(8,128)(2,1)S(1)}, u32[]{:S(2)}, u32[]{:S(2)}) collective-permute-start(bf16[512,768]{1,0:T(8,128)(2,1)} %get-tuple-element.121), channel_id=1, source_target_pairs={{0,32},{32,0},{64,96},{96,64},{1,33},{33,1},{65,97},{97,65},{2,34}... | collective-permute-start | bytes 2359304 | tf_op jit(solution)/shard_map/ppermute | solution.py:619
  111.2 2.2 %collective-permute-start.15 = (bf16[20,128]{1,0:T(8,128)(2,1)S(1)}, bf16[20,128]{1,0:T(8,128)(2,1)S(1)}, u32[]{:S(2)}, u32[]{:S(2)}) collective-permute-start(bf16[20,128]{1,0:T(8,128)(2,1)S(1)} %get-tuple-element.150), channel_id=1, source_target_pairs={{0,32},{32,0},{64,96},{96,64},{1,33},{33,1},{65,97},{97,65},{2,34}... | collective-permute-start | bytes 15368 | tf_op jit(solution)/shard_map/ppermute | solution.py:619
  111.4 5.0 %collective-permute-start.16 = (bf16[20,128]{1,0:T(8,128)(2,1)S(1)}, bf16[20,128]{1,0:T(8,128)(2,1)S(1)}, u32[]{:S(2)}, u32[]{:S(2)}) collective-permute-start(bf16[20,128]{1,0:T(8,128)(2,1)S(1)} %get-tuple-element.149), channel_id=1, source_target_pairs={{0,64},{32,96},{64,0},{96,32},{1,65},{33,97},{65,1},{97,33},{2,66}... | collective-permute-start | bytes 15368 | tf_op jit(solution)/shard_map/ppermute | solution.py:619
  111.4 8.2 %collective-permute-start.17 = (bf16[20,128]{1,0:T(8,128)(2,1)S(1)}, bf16[20,128]{1,0:T(8,128)(2,1)S(1)}, u32[]{:S(2)}, u32[]{:S(2)}) collective-permute-start(bf16[20,128]{1,0:T(8,128)(2,1)S(1)} %get-tuple-element.148), channel_id=1, source_target_pairs={{0,96},{32,64},{64,32},{96,0},{1,97},{33,65},{65,33},{97,1},{2,98}... | collective-permute-start | bytes 15368 | tf_op jit(solution)/shard_map/ppermute | solution.py:619
  119.7 7.7 %slice-start.1 = ((bf16[144,128]{1,0:T(8,128)(2,1)}), bf16[64,128]{1,0:T(8,128)(2,1)S(1)}, s32[]{:S(2)}) async-start(bf16[144,128]{1,0:T(8,128)(2,1)} %reduce_sum.44), calls=%async_computation.4 | async-start | bytes 32768 | tf_op jit(solution)/shard_map/slice | solution.py:841
  129.1 7.4 %copy-start.6 = (bf16[256,768]{1,0:T(8,128)(2,1)S(1)}, bf16[256,768]{1,0:T(8,128)(2,1)}, u32[]{:S(2)}) copy-start(bf16[256,768]{1,0:T(8,128)(2,1)} %add_convert_fusion) | copy-start | bytes 1179652
  129.1 8.9 %copy-start.26 = (bf16[192]{0:T(256)(128)(2,1)S(1)}, bf16[192]{0:T(256)(128)(2,1)}, u32[]{:S(2)}) copy-start(bf16[192]{0:T(256)(128)(2,1)} %gain_in.1) | copy-start | bytes 1156
  129.1 9.4 %copy-start.8 = (f32[1,768]{1,0:T(1,128)S(1)}, f32[1,768]{1,0:T(1,128)}, u32[]{:S(2)}) copy-start(f32[1,768]{1,0:T(1,128)} %get-tuple-element.126) | copy-start | bytes 9220
  129.1 42.2 %copy-start = (bf16[1,256,768]{2,1,0:T(8,128)(2,1)S(1)}, bf16[1,256,768]{2,1,0:T(8,128)(2,1)}, u32[]{:S(2)}) copy-start(bf16[1,256,768]{2,1,0:T(8,128)(2,1)} %param.13) | copy-start | bytes 1179652
  129.1 42.2 %copy-start.2 = (bf16[256,768]{1,0:T(8,128)(2,1)S(1)}, bf16[256,768]{1,0:T(8,128)(2,1)}, u32[]{:S(2)}) copy-start(bf16[256,768]{1,0:T(8,128)(2,1)} %get-tuple-element.123) | copy-start | bytes 1179652
  129.1 44.1 %all-to-all-start.2 = ((bf16[128,72,128]{2,1,0:T(8,128)(2,1)}), bf16[128,72,128]{2,1,0:T(8,128)(2,1)}, u32[]{:S(2)}, u32[]{:S(2)}) async-start(bf16[128,72,128]{2,1,0:T(8,128)(2,1)} %bitcast.19), calls=%async_computation.2 | async-start | bytes 4718592 | tf_op jit(solution)/shard_map/all_to_all | solution.py:855
  136.5 35.2 %slice-start = ((bf16[512,768]{1,0:T(8,128)(2,1)}), bf16[256,768]{1,0:T(8,128)(2,1)S(1)}, s32[]{:S(2)}) async-start(bf16[512,768]{1,0:T(8,128)(2,1)} %copy-done.1), calls=%async_computation.3 | async-start | bytes 786432 | tf_op jit(solution)/shard_map/slice | solution.py:680
  136.5 35.2 %copy-start.4 = (bf16[1,256,768]{2,1,0:T(8,128)(2,1)S(1)}, bf16[1,256,768]{2,1,0:T(8,128)(2,1)}, u32[]{:S(2)}) copy-start(bf16[1,256,768]{2,1,0:T(8,128)(2,1)} %param.15) | copy-start | bytes 1179652
  136.5 35.2 %copy-start.5 = (bf16[256,768]{1,0:T(8,128)(2,1)S(1)}, bf16[256,768]{1,0:T(8,128)(2,1)}, u32[]{:S(2)}) copy-start(bf16[256,768]{1,0:T(8,128)(2,1)} %get-tuple-element.115) | copy-start | bytes 1179652
  136.5 34.8 %collective-permute-start.19 = (bf16[256,768]{1,0:T(8,128)(2,1)S(1)}, bf16[256,768]{1,0:T(8,128)(2,1)S(1)}, u32[]{:S(2)}, u32[]{:S(2)}) collective-permute-start(bf16[256,768]{1,0:T(8,128)(2,1)S(1)} %copy-done.6), channel_id=1, source_target_pairs={{0,64},{32,96},{64,0},{96,32},{1,65},{33,97},{65,1},{97,33},{2,66}... | collective-permute-start | bytes 1179656 | tf_op jit(solution)/shard_map/ppermute | solution.py:619
  (4 other events, 2.5 us)

commit v7 on v6

--- a/solution.py
+++ b/solution.py
@@ -862,15 +862,6 @@
     squares = sum(lax.dynamic_index_in_dim(v, g, 0, keepdims=False) for v in all_stats)
     rms_out = lax.rsqrt(squares[0:4:2].reshape(ROWS, 1) * (1.0 / DI) + epsilon)
     layer_out = (x + rms_out * branch).astype(bf16).reshape(tokens.shape)
-    d_normed = sum(value.astype(f32) for value in d_parts)
-    rms_in = lax.rsqrt(jnp.mean(x * x, axis=-1, keepdims=True) + epsilon)
-    scaled = d_normed * gain_in_all
-    grad_tokens = (
-        cot.astype(f32)
-        + rms_in * scaled
-        - x * (rms_in * rms_in * rms_in * jnp.mean(x * scaled, axis=-1, keepdims=True))
-    ).reshape(tokens.shape)
-
     grads = call(
         assemble_kernel,
         "assemble",
@@ -888,6 +879,15 @@
             pltpu.VMEM((4, 64, 128), f32),
         ],
     )(me, parts, gain_in.astype(f32).reshape(1, 192))
+    grads, d_parts = lax.optimization_barrier((grads, d_parts))
+    d_normed = sum(value.astype(f32) for value in d_parts)
+    rms_in = lax.rsqrt(jnp.mean(x * x, axis=-1, keepdims=True) + epsilon)
+    scaled = d_normed * gain_in_all
+    grad_tokens = (
+        cot.astype(f32)
+        + rms_in * scaled
+        - x * (rms_in * rms_in * rms_in * jnp.mean(x * scaled, axis=-1, keepdims=True))
+    ).reshape(tokens.shape)
     grad_w_in, grad_w_out, grad_kernel, grad_bias, grad_gi, grad_go, grad_s, grad_d, grad_l = grads
     return (
         layer_out,

time: 178 us -> 177 us (level)
    ppermute x18, waiting for transfers between devices: 47.1 us -> 15 us  [among(): return lax.ppermute(value, 'group', [(i, i ^ d) for i in range(4)])]
    all_to_all x1, waiting for transfers between devices: 0.01 us -> 29.9 us  [local(): lax.all_to_all(jnp.broadcast_to(payload[:, None], (4, reps, 72, 128)).res...]
  transfers between devices with their start and end apart: 23 -> 23, of which waited for: 8 -> 7; matrix products, arithmetic and copies ran while one was open for 5% -> 4% of each run, Pallas kernels for 28% -> 31%
where the time goes in v7:
time: 177 us; the launch traced here: 176 us
  Pallas kernels  62.2 us (35%)
  waiting for transfers between devices  53.8 us (30%)
  starting transfers between devices  45.7 us (26%)
  local copies, waits for them, and re-layouts  7.28 us (4%)
  other arithmetic  5.91 us (3%)
    all_to_all x1, waiting for transfers between devices, local(): lax.all_to_all(jnp.broadcast_to(payload[:, None], (4, reps, 72, 128)).res...  29.9 us
    pallas_call x1, Pallas kernels, local(): call(backward_kernel, 'backward', 26, grid=(blocks,), in_specs=[scalar_sp...  22.9 us
    all_to_all x2, starting transfers between devices, spread(): return lax.all_to_all(value, 'rep', 0, 0, tiled=True)  19.2 us
    ppermute x18, starting transfers between devices, among(): return lax.ppermute(value, 'group', [(i, i ^ d) for i in range(4)])  15.8 us
    ppermute x18, waiting for transfers between devices, among(): return lax.ppermute(value, 'group', [(i, i ^ d) for i in range(4)])  15 us
    pallas_call x1, Pallas kernels, local(): call(forward_kernel, 'forward', 15, grid=(blocks,), in_specs=[scalar_spec...  13.9 us
    pallas_call x1, Pallas kernels, local(): call(out_kernel, 'out', 6, grid=(blocks,), in_specs=[scalar_spec] + [part...  8.28 us
    all_to_all x1, starting transfers between devices, local(): lax.all_to_all(jnp.broadcast_to(payload[:, None], (4, reps, 72, 128)).res...  7.14 us
  transfers between devices with their start and end apart: 23, of which 7 were waited for; matrix products, arithmetic and copies ran while one was open for 4% of the time, Pallas kernels for 31%

profile of v7, /device:TPU:1, one launch (start us, length us, event | category | flops | bytes accessed | tf_op | source)
XLA Modules:
  0.0 175.9 jit_solution(16220444231218125746)
XLA Ops:
  0.7 2.9 %columns.1 = (bf16[192,1152]{1,0:T(8,128)(2,1)}, bf16[192,1152]{1,0:T(8,128)(2,1)}, bf16[192,1152]{1,0:T(8,128)(2,1)}, bf16[192,640]{1,0:T(8,128)(2,1)}, bf16[19...) custom-call(s32[1]{0:T(128)} %bitcast.1.me, bf16[192,3352]{1,0:T(8,128)(2,1)} %w_in.1, bf16[256,768]{1,0:T(8,128)(2,1)} %bitcast.40, ...), custom_call_target="tpu_custom_call" | custom-call | flops 2000000000 | bytes 1048576 | tf_op jit(solution)/shard_map/columns/pallas_call | solution.py:634
  3.6 2.1 %collective-permute-start = (bf16[272,768]{1,0:T(8,128)(2,1)}, bf16[272,768]{1,0:T(8,128)(2,1)S(1)}, u32[]{:S(2)}, u32[]{:S(2)}) collective-permute-start(bf16[272,768]{1,0:T(8,128)(2,1)} %get-tuple-element.89.t0), channel_id=1, source_target_pairs={{0,64},{32,96},{64,0},{96,32},{1,65},{33,97},{65,1},{97,33},{2,66}... | collective-permute-start | bytes 1253384 | tf_op jit(solution)/shard_map/ppermute | solution.py:619
  5.7 2.7 %collective-permute-start.6 = (bf16[192,512]{1,0:T(8,128)(2,1)}, bf16[192,512]{1,0:T(8,128)(2,1)S(1)}, u32[]{:S(2)}, u32[]{:S(2)}) collective-permute-start(bf16[192,512]{1,0:T(8,128)(2,1)} %get-tuple-element.95), channel_id=1, source_target_pairs={{0,97},{32,65},{64,33},{96,1},{1,96},{33,64},{65,32},{97,0},{2,99}... | collective-permute-start | bytes 589832 | tf_op jit(solution)/shard_map/ppermute | solution.py:650
  8.5 0.8 collective-permute-start.4
  9.3 5.6 %collective-permute-done.t2 = bf16[272,768]{1,0:T(8,128)(2,1)S(1)} collective-permute-done((bf16[272,768]{1,0:T(8,128)(2,1)}, bf16[272,768]{1,0:T(8,128)(2,1)S(1)}, u32[]{:S(2)}, u32[]{:S(2)}) %collective-permute-start) | collective-permute-done | bytes 417824 | tf_op jit(solution)/shard_map/ppermute | solution.py:619
  14.9 2.9 %collective-permute-start.1 = (bf16[272,768]{1,0:T(8,128)(2,1)}, bf16[272,768]{1,0:T(8,128)(2,1)S(1)}, u32[]{:S(2)}, u32[]{:S(2)}) collective-permute-start(bf16[272,768]{1,0:T(8,128)(2,1)} %get-tuple-element.89.t0), channel_id=1, source_target_pairs={{0,32},{32,0},{64,96},{96,64},{1,33},{33,1},{65,97},{97,65},{2,34}... | collective-permute-start | bytes 1253384 | tf_op jit(solution)/shard_map/ppermute | solution.py:619
  17.8 0.5 collective-permute-start.3
  18.4 0.6 reshape_reshape.3.skip
  19.0 0.6 reshape.151.gain_out
  19.6 0.5 bitcast_convert_fusion.dtb
  20.1 0.5 pad_bitcast_fusion.rate
  20.6 0.8 collective-permute-done.5.w3a
  21.4 2.4 %collective-permute-done.4.w2 = bf16[192,1152]{1,0:T(8,128)(2,1)S(1)} collective-permute-done((bf16[192,1152]{1,0:T(8,128)(2,1)}, bf16[192,1152]{1,0:T(8,128)(2,1)S(1)}, u32[]{:S(2)}, u32[]{:S(2)}) %collective-permute-start.4) | collective-permute-done | bytes 442400 | tf_op jit(solution)/shard_map/ppermute | solution.py:650
  23.9 2.0 %collective-permute-start.9 = (bf16[256,768]{1,0:T(8,128)(2,1)S(1)}, bf16[256,768]{1,0:T(8,128)(2,1)S(1)}, u32[]{:S(2)}, u32[]{:S(2)}) collective-permute-start(bf16[256,768]{1,0:T(8,128)(2,1)S(1)} %bitcast.45), channel_id=1, source_target_pairs={{0,96},{32,64},{64,32},{96,0},{1,97},{33,65},{65,33},{97,1},{2,98}... | collective-permute-start | bytes 1179656 | tf_op jit(solution)/shard_map/ppermute | solution.py:619
  26.0 0.7 copy-done.17
  26.7 0.1 copy-done.14
  26.8 13.9 %forward.1 = (bf16[768,1152]{1,0:T(8,128)(2,1)}, bf16[1024,768]{1,0:T(8,128)(2,1)}, bf16[1024,1152]{1,0:T(8,128)(2,1)}, f32[1024,640]{1,0:T(8,128)}, f32[8,128,3...) custom-call(s32[1]{0:T(128)} %bitcast.1.me, ...), custom_call_target="tpu_custom_call" | custom-call | flops 15000000512 | bytes 1048576 | tf_op jit(solution)/shard_map/forward/pallas_call | solution.py:685
  40.7 2.4 %collective-permute-done.9.c3 = bf16[256,768]{1,0:T(8,128)(2,1)S(1)} collective-permute-done((bf16[256,768]{1,0:T(8,128)(2,1)S(1)}, bf16[256,768]{1,0:T(8,128)(2,1)S(1)}, u32[]{:S(2)}, u32[]{:S(2)}) %collective-permute-start.9) | collective-permute-done | bytes 393248 | tf_op jit(solution)/shard_map/ppermute | solution.py:619
  43.1 0.7 copy-done.20
  43.9 5.2 %sums.1 = (f32[1024,384]{1,0:T(8,128)}, f32[4,8,128]{2,1,0:T(8,128)}) custom-call(s32[1]{0:T(128)} %bitcast.1.me, bf16[256,768]{1,0:T(8,128)(2,1)} %bitcast.41, bf16[256,768]{1,0:T(8,128)(2,1)} %copy-done.18, bf16[256,768]{1,0:T(8,128)(2,1)} %copy-done.19, bf16[256,768]{1,0:T(8,128)(2,1)} %copy-done.20, bf16[1024,1152]{1,0:T(8,128)(2,1)} %get-tuple-element.96.gate_in.proj, ...), custom_call_target="tpu_custom_call" | custom-call | flops 4000000000 | bytes 1048576 | tf_op jit(solution)/shard_map/sums/pallas_call | solution.py:729
  49.1 0.2 collective-permute-start.11
  49.3 2.0 %collective-permute-start.12 = (f32[4,8,128]{2,1,0:T(8,128)}, f32[4,8,128]{2,1,0:T(8,128)S(1)}, u32[]{:S(2)}, u32[]{:S(2)}) collective-permute-start(f32[4,8,128]{2,1,0:T(8,128)} %get-tuple-element.103.s0), channel_id=1, source_target_pairs={{0,96},{32,64},{64,32},{96,0},{1,97},{33,65},{65,33},{97,1},{2,98}... | collective-permute-start | bytes 49160 | tf_op jit(solution)/shard_map/ppermute | solution.py:619
  51.2 4.9 %branch.1 = (bf16[256,768]{1,0:T(8,128)(2,1)}, bf16[512,768]{1,0:T(8,128)(2,1)}, bf16[256,768]{1,0:T(8,128)(2,1)}) custom-call(s32[1]{0:T(128)} %bitcast.1.me, bf16[1024,1152]{1,0:T(8,128)(2,1)} %get-tuple-element.96.gate_in.proj, f32[1024,384]{1,0:T(8,128)} %get-tuple-element.97.y_in, f32[1,384]{1,0:T(1,128)} %reshape.151.gain_out, bf16[384,768]{1,0:T(8,128)(2,1)} %w_out.3), custom_call_target="tpu_custom_call" | custom-call | flops 3000000000 | bytes 1048576 | tf_op jit(solution)/shard_map/branch/pallas_call | solution.py:743
  56.3 0.5 copy-done.9
  56.8 8.3 %out.1 = (bf16[32,144,128]{2,1,0:T(8,128)(2,1)}, bf16[16,16,128]{2,1,0:T(8,128)(2,1)}, bf16[1024,384]{1,0:T(8,128)(2,1)}, f32[1024,384]{1,0:T(8,128)}, f32[8,384]{1,0:T(8,128)}) custom-call(s32[1]{0:T(128)} %bitcast.1.me, bf16[256,768]{1,0:T(8,128)(2,1)} %bitcast.42, bf16[256,768]{1,0:T(8,128)(2,1)} %copy-done.18, bf16[256,768]{1,0:T(8,128)(2,1)} %copy-done.19, ...), custom_call_target="tpu_custom_call" | custom-call | flops 6000000000 | bytes 1048576 | tf_op jit(solution)/shard_map/out/pallas_call | solution.py:756
  65.1 9.4 %all-to-all-start = ((bf16[32,144,128]{2,1,0:T(8,128)(2,1)}), bf16[32,144,128]{2,1,0:T(8,128)(2,1)S(1)}, u32[]{:S(2)}, u32[]{:S(2)}) async-start(bf16[32,144,128]{2,1,0:T(8,128)(2,1)} %get-tuple-element.123), calls=%async_computation | async-start | bytes 2359296 | tf_op jit(solution)/shard_map/all_to_all | solution.py:784
  74.6 1.1 collective-permute-start.14
  75.7 22.9 %backward.1 = (bf16[32,144,128]{2,1,0:T(8,128)(2,1)}, bf16[256,768]{1,0:T(8,128)(2,1)}, bf16[512,768]{1,0:T(8,128)(2,1)}, bf16[256,768]{1,0:T(8,128)(2,1)}) custom-call(s32[1]{0:T(128)} %bitcast.1.me, bf16[768,1152]{1,0:T(8,128)(2,1)} %get-tuple-element.107.w_full, bf16[1024,768]{1,0:T(8,128)(2,1)} %get-tuple-element.108.normed, ...), custom_call_target="tpu_custom_call" | custom-call | flops 25999998976 | bytes 1048576 | tf_op jit(solution)/shard_map/backward/pallas_call | solution.py:795
  98.6 9.8 %all-to-all-start.1 = ((bf16[32,144,128]{2,1,0:T(8,128)(2,1)}), bf16[32,144,128]{2,1,0:T(8,128)(2,1)S(1)}, u32[]{:S(2)}, u32[]{:S(2)}) async-start(bf16[32,144,128]{2,1,0:T(8,128)(2,1)} %get-tuple-element.130), calls=%async_computation.1 | async-start | bytes 2359296 | tf_op jit(solution)/shard_map/all_to_all | solution.py:784
  108.5 1.2 collective-permute-start.18
  109.7 0.8 reduce_sum.44
  110.5 0.7 slice.38
  111.3 1.4 collective-permute-start.16
  112.7 0.8 collective-permute-start.15
  113.5 6.2 %collective-permute-done.17 = bf16[20,128]{1,0:T(8,128)(2,1)S(1)} collective-permute-done((bf16[20,128]{1,0:T(8,128)(2,1)S(1)}, bf16[20,128]{1,0:T(8,128)(2,1)S(1)}, u32[]{:S(2)}, u32[]{:S(2)}) %collective-permute-start.17) | collective-permute-done | bytes 5152 | tf_op jit(solution)/shard_map/ppermute | solution.py:619
  119.7 1.1 add_convert_fusion
  120.8 6.4 %all-to-all-done.1 = bf16[32,144,128]{2,1,0:T(8,128)(2,1)S(1)} async-done(((bf16[32,144,128]{2,1,0:T(8,128)(2,1)}), bf16[32,144,128]{2,1,0:T(8,128)(2,1)S(1)}, u32[]{:S(2)}, u32[]{:S(2)}) %all-to-all-start.1) | async-done | bytes 1179680 | tf_op jit(solution)/shard_map/all_to_all | solution.py:784
  127.2 0.2 reduce_sum.43
  127.4 1.7 broadcast_in_dim.5
  129.2 7.1 %all-to-all-start.2 = ((bf16[128,72,128]{2,1,0:T(8,128)(2,1)}), bf16[128,72,128]{2,1,0:T(8,128)(2,1)}, u32[]{:S(2)}, u32[]{:S(2)}) async-start(bf16[128,72,128]{2,1,0:T(8,128)(2,1)} %bitcast.18), calls=%async_computation.2 | async-start | bytes 4718592 | tf_op jit(solution)/shard_map/all_to_all | solution.py:855
  136.3 0.6 reshape.152
  136.9 0.7 add_bitcast_fusion
  137.6 1.5 collective-permute-start.19
  139.1 29.9 %all-to-all-done.2.parts = bf16[128,72,128]{2,1,0:T(8,128)(2,1)} async-done(((bf16[128,72,128]{2,1,0:T(8,128)(2,1)}), bf16[128,72,128]{2,1,0:T(8,128)(2,1)}, u32[]{:S(2)}, u32[]{:S(2)}) %all-to-all-start.2) | async-done | bytes 2359328 | tf_op jit(solution)/shard_map/all_to_all | solution.py:855
  169.1 4.1 %assemble.1 = (f32[192,3352]{1,0:T(8,128)}, f32[384,768]{1,0:T(8,128)}, f32[4,448]{1,0:T(4,128)}, f32[1,448]{1,0:T(1,128)}, f32[1,192]{1,0:T(1,128)}, /*index=5*...) custom-call(s32[1]{0:T(128)} %bitcast.1.me, bf16[128,72,128]{2,1,0:T(8,128)(2,1)} %all-to-all-done.2.parts, ...), custom_call_target="tpu_custom_call" | custom-call | flops 4000000000 | bytes 1048576 | tf_op jit(solution)/shard_map/assemble/pallas_call | solution.py:865
  173.2 0.4 fusion.1
  173.6 0.6 slice-done
  174.4 1.6 fusion.4
  (90 shorter events, 0.9 us)
Async XLA Ops:
  0.7 17.7 %copy-start.23 = (bf16[6]{0:T(256)(128)(2,1)S(1)}, bf16[6]{0:T(256)(128)(2,1)}, u32[]{:S(2)}) copy-start(bf16[6]{0:T(256)(128)(2,1)} %param.21) | copy-start | bytes 40
  0.7 17.7 %copy-start.12 = (bf16[6]{0:T(256)(128)(2,1)S(1)}, bf16[6]{0:T(256)(128)(2,1)}, u32[]{:S(2)}) copy-start(bf16[6]{0:T(256)(128)(2,1)} %param.22) | copy-start | bytes 40
  0.7 18.4 %copy-start.8 = (bf16[384]{0:T(512)(128)(2,1)S(1)}, bf16[384]{0:T(512)(128)(2,1)}, u32[]{:S(2)}) copy-start(bf16[384]{0:T(512)(128)(2,1)} %param.23) | copy-start | bytes 2308
  0.7 18.9 %copy-start.24 = (bf16[6]{0:T(256)(128)(2,1)S(1)}, bf16[6]{0:T(256)(128)(2,1)}, u32[]{:S(2)}) copy-start(bf16[6]{0:T(256)(128)(2,1)} %param.20) | copy-start | bytes 40
  0.7 20.7 %copy-start.3 = (bf16[1,256,768]{2,1,0:T(8,128)(2,1)S(1)}, bf16[1,256,768]{2,1,0:T(8,128)(2,1)}, u32[]{:S(2)}) copy-start(bf16[1,256,768]{2,1,0:T(8,128)(2,1)} %param.15) | copy-start | bytes 1179652
  3.6 11.3 %collective-permute-start = (bf16[272,768]{1,0:T(8,128)(2,1)}, bf16[272,768]{1,0:T(8,128)(2,1)S(1)}, u32[]{:S(2)}, u32[]{:S(2)}) collective-permute-start(bf16[272,768]{1,0:T(8,128)(2,1)} %get-tuple-element.89.t0), channel_id=1, source_target_pairs={{0,64},{32,96},{64,0},{96,32},{1,65},{33,97},{65,1},{97,33},{2,66}... | collective-permute-start | bytes 1253384 | tf_op jit(solution)/shard_map/ppermute | solution.py:619
  5.7 12.1 %collective-permute-start.6 = (bf16[192,512]{1,0:T(8,128)(2,1)}, bf16[192,512]{1,0:T(8,128)(2,1)S(1)}, u32[]{:S(2)}, u32[]{:S(2)}) collective-permute-start(bf16[192,512]{1,0:T(8,128)(2,1)} %get-tuple-element.95), channel_id=1, source_target_pairs={{0,97},{32,65},{64,33},{96,1},{1,96},{33,64},{65,32},{97,0},{2,99}... | collective-permute-start | bytes 589832 | tf_op jit(solution)/shard_map/ppermute | solution.py:650
  8.5 15.4 %collective-permute-start.4 = (bf16[192,1152]{1,0:T(8,128)(2,1)}, bf16[192,1152]{1,0:T(8,128)(2,1)S(1)}, u32[]{:S(2)}, u32[]{:S(2)}) collective-permute-start(bf16[192,1152]{1,0:T(8,128)(2,1)} %get-tuple-element.93), channel_id=1, source_target_pairs={{0,65},{32,97},{64,1},{96,33},{1,64},{33,96},{65,0},{97,32},{2,67}... | collective-permute-start | bytes 1327112 | tf_op jit(solution)/shard_map/ppermute | solution.py:650
  9.3 12.2 %collective-permute-start.5 = (bf16[192,640]{1,0:T(8,128)(2,1)}, bf16[192,640]{1,0:T(8,128)(2,1)S(1)}, u32[]{:S(2)}, u32[]{:S(2)}) collective-permute-start(bf16[192,640]{1,0:T(8,128)(2,1)} %get-tuple-element.94), channel_id=1, source_target_pairs={{0,96},{32,64},{64,32},{96,0},{1,97},{33,65},{65,33},{97,1},{2,98}... | collective-permute-start | bytes 737288 | tf_op jit(solution)/shard_map/ppermute | solution.py:619
  14.9 11.0 %copy-start.15 = (bf16[272,768]{1,0:T(8,128)(2,1)}, bf16[272,768]{1,0:T(8,128)(2,1)S(1)}, u32[]{:S(2)}) copy-start(bf16[272,768]{1,0:T(8,128)(2,1)S(1)} %collective-permute-done.t2) | copy-start | bytes 1253380
  14.9 9.0 %collective-permute-start.1 = (bf16[272,768]{1,0:T(8,128)(2,1)}, bf16[272,768]{1,0:T(8,128)(2,1)S(1)}, u32[]{:S(2)}, u32[]{:S(2)}) collective-permute-start(bf16[272,768]{1,0:T(8,128)(2,1)} %get-tuple-element.89.t0), channel_id=1, source_target_pairs={{0,32},{32,0},{64,96},{96,64},{1,33},{33,1},{65,97},{97,65},{2,34}... | collective-permute-start | bytes 1253384 | tf_op jit(solution)/shard_map/ppermute | solution.py:619
  17.8 8.1 %collective-permute-start.2 = (bf16[272,768]{1,0:T(8,128)(2,1)S(1)}, bf16[272,768]{1,0:T(8,128)(2,1)S(1)}, u32[]{:S(2)}, u32[]{:S(2)}) collective-permute-start(bf16[272,768]{1,0:T(8,128)(2,1)S(1)} %collective-permute-done.t2), channel_id=1, source_target_pairs={{0,32},{32,0},{64,96},{96,64},{1,33},{33,1},{65,97},{97,65},{2,34}... | collective-permute-start | bytes 1253384 | tf_op jit(solution)/shard_map/ppermute | solution.py:619
  17.8 8.1 %copy-start.22 = (bf16[192,512]{1,0:T(8,128)(2,1)}, bf16[192,512]{1,0:T(8,128)(2,1)S(1)}, u32[]{:S(2)}) copy-start(bf16[192,512]{1,0:T(8,128)(2,1)S(1)} %collective-permute-done.6.w3b) | copy-start | bytes 589828
  17.8 8.1 %collective-permute-start.3 = (bf16[192,1152]{1,0:T(8,128)(2,1)}, bf16[192,1152]{1,0:T(8,128)(2,1)S(1)}, u32[]{:S(2)}, u32[]{:S(2)}) collective-permute-start(bf16[192,1152]{1,0:T(8,128)(2,1)} %get-tuple-element.92), channel_id=1, source_target_pairs={{0,32},{32,0},{64,96},{96,64},{1,33},{33,1},{65,97},{97,65},{2,34}... | collective-permute-start | bytes 1327112 | tf_op jit(solution)/shard_map/ppermute | solution.py:619
  21.4 4.5 %copy-start.21 = (bf16[192,640]{1,0:T(8,128)(2,1)}, bf16[192,640]{1,0:T(8,128)(2,1)S(1)}, u32[]{:S(2)}) copy-start(bf16[192,640]{1,0:T(8,128)(2,1)S(1)} %collective-permute-done.5.w3a) | copy-start | bytes 737284
  21.4 19.3 %collective-permute-start.7 = (bf16[256,768]{1,0:T(8,128)(2,1)S(1)}, bf16[256,768]{1,0:T(8,128)(2,1)S(1)}, u32[]{:S(2)}, u32[]{:S(2)}) collective-permute-start(bf16[256,768]{1,0:T(8,128)(2,1)S(1)} %bitcast.43), channel_id=1, source_target_pairs={{0,32},{32,0},{64,96},{96,64},{1,33},{33,1},{65,97},{97,65},{2,34}... | collective-permute-start | bytes 1179656 | tf_op jit(solution)/shard_map/ppermute | solution.py:619
  23.9 2.1 %copy-start.13 = (bf16[192,1152]{1,0:T(8,128)(2,1)}, bf16[192,1152]{1,0:T(8,128)(2,1)S(1)}, u32[]{:S(2)}) copy-start(bf16[192,1152]{1,0:T(8,128)(2,1)S(1)} %collective-permute-done.4.w2) | copy-start | bytes 1327108
  23.9 16.8 %collective-permute-start.8 = (bf16[256,768]{1,0:T(8,128)(2,1)S(1)}, bf16[256,768]{1,0:T(8,128)(2,1)S(1)}, u32[]{:S(2)}, u32[]{:S(2)}) collective-permute-start(bf16[256,768]{1,0:T(8,128)(2,1)S(1)} %bitcast.44), channel_id=1, source_target_pairs={{0,64},{32,96},{64,0},{96,32},{1,65},{33,97},{65,1},{97,33},{2,66}... | collective-permute-start | bytes 1179656 | tf_op jit(solution)/shard_map/ppermute | solution.py:619
  23.9 2.1 %copy-start.16 = (bf16[272,768]{1,0:T(8,128)(2,1)}, bf16[272,768]{1,0:T(8,128)(2,1)S(1)}, u32[]{:S(2)}) copy-start(bf16[272,768]{1,0:T(8,128)(2,1)S(1)} %collective-permute-done.1.t1) | copy-start | bytes 1253380
  23.9 19.2 %collective-permute-start.9 = (bf16[256,768]{1,0:T(8,128)(2,1)S(1)}, bf16[256,768]{1,0:T(8,128)(2,1)S(1)}, u32[]{:S(2)}, u32[]{:S(2)}) collective-permute-start(bf16[256,768]{1,0:T(8,128)(2,1)S(1)} %bitcast.45), channel_id=1, source_target_pairs={{0,96},{32,64},{64,32},{96,0},{1,97},{33,65},{65,33},{97,1},{2,98}... | collective-permute-start | bytes 1179656 | tf_op jit(solution)/shard_map/ppermute | solution.py:619
  25.9 0.8 copy-start.17
  25.9 0.9 copy-start.14
  40.7 2.5 %copy-start.18 = (bf16[256,768]{1,0:T(8,128)(2,1)}, bf16[256,768]{1,0:T(8,128)(2,1)S(1)}, u32[]{:S(2)}) copy-start(bf16[256,768]{1,0:T(8,128)(2,1)S(1)} %collective-permute-done.7.c1) | copy-start | bytes 1179652
  40.7 2.4 %copy-start.19 = (bf16[256,768]{1,0:T(8,128)(2,1)}, bf16[256,768]{1,0:T(8,128)(2,1)S(1)}, u32[]{:S(2)}) copy-start(bf16[256,768]{1,0:T(8,128)(2,1)S(1)} %collective-permute-done.8.c2) | copy-start | bytes 1179652
  43.1 0.7 copy-start.20
  49.1 7.1 %collective-permute-start.10 = (f32[4,8,128]{2,1,0:T(8,128)}, f32[4,8,128]{2,1,0:T(8,128)S(1)}, u32[]{:S(2)}, u32[]{:S(2)}) collective-permute-start(f32[4,8,128]{2,1,0:T(8,128)} %get-tuple-element.103.s0), channel_id=1, source_target_pairs={{0,32},{32,0},{64,96},{96,64},{1,33},{33,1},{65,97},{97,65},{2,34}... | collective-permute-start | bytes 49160 | tf_op jit(solution)/shard_map/ppermute | solution.py:619
  49.1 7.1 %collective-permute-start.11 = (f32[4,8,128]{2,1,0:T(8,128)}, f32[4,8,128]{2,1,0:T(8,128)S(1)}, u32[]{:S(2)}, u32[]{:S(2)}) collective-permute-start(f32[4,8,128]{2,1,0:T(8,128)} %get-tuple-element.103.s0), channel_id=1, source_target_pairs={{0,64},{32,96},{64,0},{96,32},{1,65},{33,97},{65,1},{97,33},{2,66}... | collective-permute-start | bytes 49160 | tf_op jit(solution)/shard_map/ppermute | solution.py:619
  49.3 6.9 %collective-permute-start.12 = (f32[4,8,128]{2,1,0:T(8,128)}, f32[4,8,128]{2,1,0:T(8,128)S(1)}, u32[]{:S(2)}, u32[]{:S(2)}) collective-permute-start(f32[4,8,128]{2,1,0:T(8,128)} %get-tuple-element.103.s0), channel_id=1, source_target_pairs={{0,96},{32,64},{64,32},{96,0},{1,97},{33,65},{65,33},{97,1},{2,98}... | collective-permute-start | bytes 49160 | tf_op jit(solution)/shard_map/ppermute | solution.py:619
  56.2 18.3 %collective-permute-start.13 = (bf16[512,768]{1,0:T(8,128)(2,1)}, bf16[512,768]{1,0:T(8,128)(2,1)S(1)}, u32[]{:S(2)}, u32[]{:S(2)}) collective-permute-start(bf16[512,768]{1,0:T(8,128)(2,1)} %get-tuple-element.114), channel_id=1, source_target_pairs={{0,32},{32,0},{64,96},{96,64},{1,33},{33,1},{65,97},{97,65},{2,34}... | collective-permute-start | bytes 2359304 | tf_op jit(solution)/shard_map/ppermute | solution.py:619
  65.1 9.4 %copy-start.6 = (bf16[256,768]{1,0:T(8,128)(2,1)S(1)}, bf16[256,768]{1,0:T(8,128)(2,1)}, u32[]{:S(2)}) copy-start(bf16[256,768]{1,0:T(8,128)(2,1)} %get-tuple-element.115) | copy-start | bytes 1179652
  65.1 33.5 %all-to-all-start = ((bf16[32,144,128]{2,1,0:T(8,128)(2,1)}), bf16[32,144,128]{2,1,0:T(8,128)(2,1)S(1)}, u32[]{:S(2)}, u32[]{:S(2)}) async-start(bf16[32,144,128]{2,1,0:T(8,128)(2,1)} %get-tuple-element.123), calls=%async_computation | async-start | bytes 2359296 | tf_op jit(solution)/shard_map/all_to_all | solution.py:784
  74.5 24.1 %copy-start.1 = (bf16[512,768]{1,0:T(8,128)(2,1)}, bf16[512,768]{1,0:T(8,128)(2,1)S(1)}, u32[]{:S(2)}) copy-start(bf16[512,768]{1,0:T(8,128)(2,1)S(1)} %collective-permute-done.13) | copy-start | bytes 2359300
  74.6 24.0 %collective-permute-start.14 = (bf16[256,768]{1,0:T(8,128)(2,1)S(1)}, bf16[256,768]{1,0:T(8,128)(2,1)S(1)}, u32[]{:S(2)}, u32[]{:S(2)}) collective-permute-start(bf16[256,768]{1,0:T(8,128)(2,1)S(1)} %add_convert_fusion.1), channel_id=1, source_target_pairs={{0,64},{32,96},{64,0},{96,32},{1,65},{33,97},{65,1},{97,33},{2,66}... | collective-permute-start | bytes 1179656 | tf_op jit(solution)/shard_map/ppermute | solution.py:619
  98.6 28.6 %all-to-all-start.1 = ((bf16[32,144,128]{2,1,0:T(8,128)(2,1)}), bf16[32,144,128]{2,1,0:T(8,128)(2,1)S(1)}, u32[]{:S(2)}, u32[]{:S(2)}) async-start(bf16[32,144,128]{2,1,0:T(8,128)(2,1)} %get-tuple-element.130), calls=%async_computation.1 | async-start | bytes 2359296 | tf_op jit(solution)/shard_map/all_to_all | solution.py:784
  108.5 11.2 %collective-permute-start.18 = (bf16[512,768]{1,0:T(8,128)(2,1)}, bf16[512,768]{1,0:T(8,128)(2,1)S(1)}, u32[]{:S(2)}, u32[]{:S(2)}) collective-permute-start(bf16[512,768]{1,0:T(8,128)(2,1)} %get-tuple-element.133), channel_id=1, source_target_pairs={{0,32},{32,0},{64,96},{96,64},{1,33},{33,1},{65,97},{97,65},{2,34}... | collective-permute-start | bytes 2359304 | tf_op jit(solution)/shard_map/ppermute | solution.py:619
  111.2 8.4 %collective-permute-start.17 = (bf16[20,128]{1,0:T(8,128)(2,1)S(1)}, bf16[20,128]{1,0:T(8,128)(2,1)S(1)}, u32[]{:S(2)}, u32[]{:S(2)}) collective-permute-start(bf16[20,128]{1,0:T(8,128)(2,1)S(1)} %get-tuple-element.172), channel_id=1, source_target_pairs={{0,96},{32,64},{64,32},{96,0},{1,97},{33,65},{65,33},{97,1},{2,98}... | collective-permute-start | bytes 15368 | tf_op jit(solution)/shard_map/ppermute | solution.py:619
  111.3 8.3 %collective-permute-start.16 = (bf16[20,128]{1,0:T(8,128)(2,1)S(1)}, bf16[20,128]{1,0:T(8,128)(2,1)S(1)}, u32[]{:S(2)}, u32[]{:S(2)}) collective-permute-start(bf16[20,128]{1,0:T(8,128)(2,1)S(1)} %get-tuple-element.173), channel_id=1, source_target_pairs={{0,64},{32,96},{64,0},{96,32},{1,65},{33,97},{65,1},{97,33},{2,66}... | collective-permute-start | bytes 15368 | tf_op jit(solution)/shard_map/ppermute | solution.py:619
  112.7 6.9 %collective-permute-start.15 = (bf16[20,128]{1,0:T(8,128)(2,1)S(1)}, bf16[20,128]{1,0:T(8,128)(2,1)S(1)}, u32[]{:S(2)}, u32[]{:S(2)}) collective-permute-start(bf16[20,128]{1,0:T(8,128)(2,1)S(1)} %get-tuple-element.174), channel_id=1, source_target_pairs={{0,32},{32,0},{64,96},{96,64},{1,33},{33,1},{65,97},{97,65},{2,34}... | collective-permute-start | bytes 15368 | tf_op jit(solution)/shard_map/ppermute | solution.py:619
  119.7 7.7 %slice-start.1 = ((bf16[144,128]{1,0:T(8,128)(2,1)}), bf16[64,128]{1,0:T(8,128)(2,1)S(1)}, s32[]{:S(2)}) async-start(bf16[144,128]{1,0:T(8,128)(2,1)} %reduce_sum.44), calls=%async_computation.4 | async-start | bytes 32768 | tf_op jit(solution)/shard_map/slice | solution.py:841
  129.2 7.2 %copy-start.25 = (bf16[192]{0:T(256)(128)(2,1)S(1)}, bf16[192]{0:T(256)(128)(2,1)}, u32[]{:S(2)}) copy-start(bf16[192]{0:T(256)(128)(2,1)} %gain_in.1) | copy-start | bytes 1156
  129.2 7.7 %copy-start.7 = (f32[1,768]{1,0:T(1,128)S(1)}, f32[1,768]{1,0:T(1,128)}, u32[]{:S(2)}) copy-start(f32[1,768]{1,0:T(1,128)} %get-tuple-element.153) | copy-start | bytes 9220
  129.2 39.9 %all-to-all-start.2 = ((bf16[128,72,128]{2,1,0:T(8,128)(2,1)}), bf16[128,72,128]{2,1,0:T(8,128)(2,1)}, u32[]{:S(2)}, u32[]{:S(2)}) async-start(bf16[128,72,128]{2,1,0:T(8,128)(2,1)} %bitcast.18), calls=%async_computation.2 | async-start | bytes 4718592 | tf_op jit(solution)/shard_map/all_to_all | solution.py:855
  137.6 35.6 %collective-permute-start.19 = (bf16[256,768]{1,0:T(8,128)(2,1)S(1)}, bf16[256,768]{1,0:T(8,128)(2,1)S(1)}, u32[]{:S(2)}, u32[]{:S(2)}) collective-permute-start(bf16[256,768]{1,0:T(8,128)(2,1)S(1)} %add_convert_fusion), channel_id=1, source_target_pairs={{0,64},{32,96},{64,0},{96,32},{1,65},{33,97},{65,1},{97,33},{2,66}... | collective-permute-start | bytes 1179656 | tf_op jit(solution)/shard_map/ppermute | solution.py:619
  169.1 4.1 %copy-start = (bf16[1,256,768]{2,1,0:T(8,128)(2,1)S(1)}, bf16[1,256,768]{2,1,0:T(8,128)(2,1)}, u32[]{:S(2)}) copy-start(bf16[1,256,768]{2,1,0:T(8,128)(2,1)} %param.13) | copy-start | bytes 1179652
  169.1 4.1 %copy-start.2 = (bf16[256,768]{1,0:T(8,128)(2,1)S(1)}, bf16[256,768]{1,0:T(8,128)(2,1)}, u32[]{:S(2)}) copy-start(bf16[256,768]{1,0:T(8,128)(2,1)} %get-tuple-element.150) | copy-start | bytes 1179652
  173.2 1.0 slice-start
  173.2 1.1 copy-start.4
  173.2 1.2 copy-start.5
  (3 other events, 1.8 us)
